TPU v7x, 32 devices: a whole 2x2x4 slice. The times are simulated.
32 devices in a mesh: seq: 4 (over y, x), exp: 8 (over z, core).
Axes of the slice: x: 2, y: 2, z: 4, core: 2. Of those that a mesh axis runs over, the one named last changes fastest.
Arguments:
- residual: bfloat16 [512, 2, 3072], P(('seq', 'exp')), may hold values from -6 to 6
- queries: bfloat16 [2, 512, 4096], P(None, 'seq', 'exp'), may hold values from -6 to 6
- key_vecs: bfloat16 [2, 512, 4096], P(None, 'seq', 'exp'), may hold values from -0.52734375 to 0.52734375
- value_vecs: bfloat16 [2, 512, 4096], P(None, 'seq', 'exp'), may hold values from -6 to 6
- log_decay: float32 [2, 32, 512], P(None, 'exp', 'seq'), may hold values from -2 to 0
- head_gain: float32 [4096], P('exp'), may hold values from 0.1 to 1.9
- out_proj: bfloat16 [4096, 3072], P('exp'), may hold values from -0.09375 to 0.09375
- norm_gain: float32 [3072], replicated, may hold values from 0.1 to 1.9
- routes: int32 [512, 2, 2], replicated, may hold values from 0 to 7, all different within a row; in each aligned block of 256 rows (0 to 255, 256 to 511, ..., all dimensions but the last counted through in order) at most 128 rows name the same one
- route_weight: float32 [512, 2, 2], replicated, may hold values from 0.1 to 1
- w_gate: bfloat16 [8, 4608, 3072], P('exp', 'seq'), may hold values from -0.109375 to 0.109375
- w_up: bfloat16 [8, 4608, 3072], P('exp', 'seq'), may hold values from -0.109375 to 0.109375
Outputs:
- attn_out: float32 [512, 2, 3072], P(('seq', 'exp'))
- expert_hidden: float32 [8, 4608, 512], P('exp', 'seq')
Inputs may be any that keep to these rules, and one draw needn't show every extreme that they name: Each aligned block of 256 rows of routes (positions c * 128 .. (c + 1) * 128 - 1 of both sequences) names one expert at most 128 times, a bound that some block reaches; the 2 entries of a row differ.
All inputs are finite; a program needn't handle non-finite values.
Results may differ from a plain program's by a relative error of at most 0.0052.
Values may be sent and summed in bfloat16 or wider, within the bound.
No kernel may reach another device: no remote copies, remote signals or barrier semaphores. Data moves between devices by JAX's collectives and lax.ppermute only.
A program may use at most 64 MiB of HBM per device.

v0:
```python
import jax
import jax.numpy as jnp
from jax import lax
from jax.sharding import PartitionSpec as P

PRECISE = lax.Precision.HIGHEST


def passed_along(block, axis, distance):
    devices = range(lax.axis_size(axis))
    route = [(i - distance, i) for i in devices if i - distance in devices]
    return lax.ppermute(block, axis, route)


def row_norm(values_in, gain_vec):
    meansq = jnp.mean(values_in * values_in, axis=-1, keepdims=True)
    return values_in * lax.rsqrt(meansq + 1e-06) * gain_vec


def per_device(
    residual,
    queries,
    key_vecs,
    value_vecs,
    log_decay,
    head_gain,
    out_proj,
    norm_gain,
    routes,
    route_weight,
    w_gate,
    w_up,
):
    seq_total, group_len, feat_width = queries.shape
    head_count = log_decay.shape[1]
    head_size = feat_width // head_count
    query_t = queries.reshape(seq_total, group_len, head_count, head_size)
    key_t = key_vecs.reshape(seq_total, group_len, head_count, head_size)
    value_t = value_vecs.reshape(seq_total, group_len, head_count, head_size).astype(jnp.float32)
    running = jnp.cumsum(log_decay, axis=-1)
    causal_mask = jnp.tril(jnp.ones((group_len, group_len), dtype=bool))
    spread_log = running[..., :, None] - running[..., None, :]
    decay_mat = jnp.where(causal_mask, jnp.exp(jnp.where(causal_mask, spread_log, 0.0)), 0.0)
    scores = (
        jnp.einsum("bthc,bjhc->bhtj", query_t, key_t, preferred_element_type=jnp.float32)
        * decay_mat
    )
    inner_part = jnp.einsum("bhtj,bjhd->bhtd", scores, value_t, precision=PRECISE)
    block_total = running[..., -1]
    tail_decay = jnp.exp(block_total[..., None] - running)
    weighted_keys = key_t.astype(jnp.float32) * jnp.swapaxes(tail_decay, 1, 2)[..., None]
    fresh_state = jnp.einsum("bjhc,bjhd->bhcd", weighted_keys, value_t, precision=PRECISE)

    def advance(turn_index, incoming):
        outgoing = jnp.exp(block_total)[..., None, None] * incoming + fresh_state
        return passed_along(outgoing, "seq", 1)

    incoming = lax.fori_loop(0, lax.axis_size("seq") - 1, advance, jnp.zeros_like(fresh_state))
    outer_part = jnp.exp(running)[..., None] * jnp.einsum(
        "bthc,bhcd->bhtd", query_t.astype(jnp.float32), incoming, precision=PRECISE
    )
    gain_grid = head_gain.reshape(head_count, head_size)[None, :, None, :]
    normed_heads = row_norm(inner_part + outer_part, gain_grid)
    attention = (
        jnp.transpose(normed_heads, (2, 0, 1, 3))
        .reshape(group_len, seq_total, feat_width)
        .astype(jnp.bfloat16)
    )
    own_rows = residual.shape[0]
    model_width = residual.shape[2]
    offset = lax.axis_index("exp") * own_rows
    seq_count = lax.axis_size("seq")
    owner_count = lax.axis_size("exp")
    row_count = group_len * seq_total
    top_count = routes.shape[-1]
    route_blocks = routes.reshape(seq_count, row_count, top_count)
    weight_blocks = route_weight.reshape(seq_count, row_count, top_count)
    placed = lax.dynamic_update_slice_in_dim(
        jnp.zeros((group_len, seq_total, model_width), jnp.float32),
        residual.astype(jnp.float32),
        offset,
        0,
    )
    mixed_all = lax.psum(
        jnp.einsum("tbk,kd->tbd", attention, out_proj, preferred_element_type=jnp.float32) + placed,
        "exp",
    )
    normed_all = row_norm(mixed_all, norm_gain).astype(jnp.bfloat16).reshape(row_count, model_width)
    mixed_rows = lax.dynamic_slice_in_dim(mixed_all, offset, own_rows, 0)
    capacity = 8 * group_len // owner_count
    expert_id = lax.axis_index("exp")
    route_hits = route_blocks == expert_id
    chosen = jnp.any(route_hits, axis=-1)
    token_weight = jnp.sum(jnp.where(route_hits, weight_blocks, 0.0), axis=-1)
    slot_rank = jnp.cumsum(chosen.astype(jnp.int32), axis=1) - 1
    slot_ids = jnp.arange(capacity, dtype=jnp.int32)
    pick_table = ((slot_rank[:, None, :] == slot_ids[None, :, None]) & chosen[:, None, :]).astype(
        jnp.float32
    )
    slot_weight = jnp.einsum("csj,cj->cs", pick_table, token_weight, precision=PRECISE).reshape(-1)
    own_picks = lax.dynamic_index_in_dim(pick_table, lax.axis_index("seq"), 0, keepdims=False)
    slot_rows = jnp.dot(
        own_picks.astype(jnp.bfloat16), normed_all, preferred_element_type=jnp.float32
    ).astype(jnp.bfloat16)
    row_piece = lax.all_gather(slot_rows, "seq", axis=0, tiled=True)
    gate_val = lax.dot_general(
        w_gate[0], row_piece, (((1,), (1,)), ((), ())), preferred_element_type=jnp.float32
    )
    up_val = lax.dot_general(
        w_up[0], row_piece, (((1,), (1,)), ((), ())), preferred_element_type=jnp.float32
    )
    hidden = slot_weight[None, :] * jax.nn.silu(gate_val) * up_val
    return (mixed_rows, hidden[None])


def solution(mesh):
    placed = (
        P(("seq", "exp"), None, None),
        P(None, "seq", "exp"),
        P(None, "seq", "exp"),
        P(None, "seq", "exp"),
        P(None, "exp", "seq"),
        P("exp"),
        P("exp", None),
        P(),
        P(),
        P(),
        P("exp", "seq", None),
        P("exp", "seq", None),
    )
    return jax.shard_map(
        per_device,
        mesh=mesh,
        in_specs=placed,
        out_specs=(P(("seq", "exp"), None, None), P("exp", "seq", None)),
        check_vma=False,
    )
```

profile of v0, /device:TPU:0, one launch (start us, length us, event | category | flops | bytes accessed | tf_op | source)
XLA Modules:
  0.0 241.6 jit_solution(10774314924628445739)
XLA Ops:
  7.2 1.4 reduce_window_sum.28
  8.9 1.1 copy.56
  10.1 2.2 fusion.24
  13.1 51.7 %while.12 = (s32[]{:T(128)}, f32[2,4,128,128]{3,2,1,0:T(8,128)}, f32[2,4,1,1]{1,0,3,2:T(2,128)S(1)}, f32[2,4,128,128]{3,2,1,0:T(8,128)}, s32[]{:T(128)}) while((s32[]{:T(128)}, f32[2,4,128,128]{3,2,1,0:T(8,128)}, f32[2,4,1,1]{1,0,3,2:T(2,128)S(1)}, f32[2,4,128,128]{3,2,1,0:T(8,128)}, s32[]{:T(128)}) %tuple.43), condition=%wide.region_2.3_spmd, body=%wide.region_1.2_spmd.sunk | while | flops 262146 | bytes 3670149 | solution.py:58
  13.1 2.1 multiply_add_fusion.2
  15.2 5.7 %collective-permute-start = (f32[2,4,128,128]{3,2,1,0:T(8,128)}, f32[2,4,128,128]{3,2,1,0:T(8,128)}, u32[]{:S(2)}, u32[]{:S(2)}) collective-permute-start(f32[2,4,128,128]{3,2,1,0:T(8,128)} %multiply_add_fusion.2), channel_id=1, source_target_pairs={{0,8},{8,16},{16,24},{1,9},{9,17},{17,25},{2,10},{10,18},{18,26},{... | collective-permute-start | bytes 1572872 | tf_op jit(solution)/shard_map/while/body/eval_jaxpr/ppermute | solution.py:12
  20.9 10.7 %collective-permute-done = f32[2,4,128,128]{3,2,1,0:T(8,128)} collective-permute-done((f32[2,4,128,128]{3,2,1,0:T(8,128)}, f32[2,4,128,128]{3,2,1,0:T(8,128)}, u32[]{:S(2)}, u32[]{:S(2)}) %collective-permute-start) | collective-permute-done | bytes 524320 | tf_op jit(solution)/shard_map/while/body/eval_jaxpr/ppermute | solution.py:12
  31.6 2.1 multiply_add_fusion.2
  33.7 5.2 %collective-permute-start = (f32[2,4,128,128]{3,2,1,0:T(8,128)}, f32[2,4,128,128]{3,2,1,0:T(8,128)}, u32[]{:S(2)}, u32[]{:S(2)}) collective-permute-start(f32[2,4,128,128]{3,2,1,0:T(8,128)} %multiply_add_fusion.2), channel_id=1, source_target_pairs={{0,8},{8,16},{16,24},{1,9},{9,17},{17,25},{2,10},{10,18},{18,26},{... | collective-permute-start | bytes 1572872 | tf_op jit(solution)/shard_map/while/body/eval_jaxpr/ppermute | solution.py:12
  38.9 9.8 %collective-permute-done = f32[2,4,128,128]{3,2,1,0:T(8,128)} collective-permute-done((f32[2,4,128,128]{3,2,1,0:T(8,128)}, f32[2,4,128,128]{3,2,1,0:T(8,128)}, u32[]{:S(2)}, u32[]{:S(2)}) %collective-permute-start) | collective-permute-done | bytes 524320 | tf_op jit(solution)/shard_map/while/body/eval_jaxpr/ppermute | solution.py:12
  48.6 2.1 multiply_add_fusion.2
  50.8 5.2 %collective-permute-start = (f32[2,4,128,128]{3,2,1,0:T(8,128)}, f32[2,4,128,128]{3,2,1,0:T(8,128)}, u32[]{:S(2)}, u32[]{:S(2)}) collective-permute-start(f32[2,4,128,128]{3,2,1,0:T(8,128)} %multiply_add_fusion.2), channel_id=1, source_target_pairs={{0,8},{8,16},{16,24},{1,9},{9,17},{17,25},{2,10},{10,18},{18,26},{... | collective-permute-start | bytes 1572872 | tf_op jit(solution)/shard_map/while/body/eval_jaxpr/ppermute | solution.py:12
  55.9 8.9 %collective-permute-done = f32[2,4,128,128]{3,2,1,0:T(8,128)} collective-permute-done((f32[2,4,128,128]{3,2,1,0:T(8,128)}, f32[2,4,128,128]{3,2,1,0:T(8,128)}, u32[]{:S(2)}, u32[]{:S(2)}) %collective-permute-start) | collective-permute-done | bytes 524320 | tf_op jit(solution)/shard_map/while/body/eval_jaxpr/ppermute | solution.py:12
  64.8 1.7 fusion.31
  66.6 1.5 convolution_multiply_fusion
  68.0 1.5 fusion.19
  69.5 1.3 fusion.23
  70.9 2.7 %fusion.16 = f32[128,2,3072]{2,0,1:T(8,128)} fusion(bf16[128,2,512]{0,2,1:T(8,128)(2,1)S(1)} %bitcast.106, bf16[512,3072]{1,0:T(8,128)(2,1)S(1)} %copy-done), kind=kOutput, calls=%fused_computation.10 | convolution fusion | flops 805306368 | bytes 6553600 | tf_op jit(solution)/shard_map/tbk,kd->tbd/dot_general | solution.py:85
  73.6 1.8 add_dynamic-update-slice_fusion
  76.1 1.4 reduce-window.6
  78.2 78.4 %all-reduce.2.cloned.1.call-done = f32[128,2,3072]{2,0,1:T(8,128)} async-done(((f32[128,2,3072]{2,0,1:T(8,128)}), f32[128,2,3072]{2,0,1:T(8,128)}) %all-reduce.2.cloned.1.call-update) | async-done | bytes 3145744 | tf_op jit(solution)/shard_map/psum | solution.py:84
  156.6 2.3 multiply_reduce_fusion
  159.4 1.2 multiply_convert_fusion
  160.6 2.8 %copy.49 = bf16[128,2,3072]{2,1,0:T(2,128)(2,1)} copy(bf16[128,2,3072]{2,0,1:T(8,128)(2,1)S(1)} %multiply_convert_fusion) | data formatting | bytes 3145728 | tf_op jit(solution)/shard_map/convert_element_type | solution.py:88
  163.3 4.6 %reshape.92 = bf16[256,3072]{1,0:T(8,128)(2,1)} reshape(bf16[128,2,3072]{2,1,0:T(2,128)(2,1)} %copy.49) | data formatting | bytes 3145728 | tf_op jit(solution)/shard_map/reshape | solution.py:88
  168.0 2.7 %convolution_convert_fusion = bf16[128,3072]{1,0:T(8,128)(2,1)} fusion(bf16[256,3072]{1,0:T(8,128)(2,1)} %reshape.92, pred[4,128,256]{2,1,0:T(32,128)(4,1)S(1)} %fusion.27, s32[]{:T(128)S(6)} %select_n.26), kind=kOutput, calls=%fused_computation.5 | convolution fusion | flops 201785344 | bytes 2392068 | tf_op jit(solution)/shard_map/dot_general | solution.py:102
  171.3 1.0 constant_dynamic-slice_fusion
  172.4 1.1 copy.50
  173.4 41.2 %all-gather.2.cloned.1.call-done = bf16[512,3072]{1,0:T(8,128)(2,1)} async-done(((bf16[128,3072]{1,0:T(8,128)(2,1)}), bf16[512,3072]{1,0:T(8,128)(2,1)}) %all-gather.2.cloned.1.call-update) | async-done | bytes 3145744 | tf_op jit(solution)/shard_map/all_gather | solution.py:105
  214.6 8.4 %fusion.4 = f32[1152,512]{0,1:T(8,128)S(1)} fusion(bf16[512,3072]{1,0:T(8,128)(2,1)} %all-gather.2.cloned.1.call-done, bf16[1,1152,3072]{2,1,0:T(8,128)(2,1)} %param.24), kind=kOutput, calls=%fused_computation.6 | convolution fusion | flops 3623878656 | bytes 12582912 | tf_op jit(solution)/shard_map/dot_general | solution.py:106
  223.0 8.7 %fusion.13 = f32[1,1152,512]{1,2,0:T(8,128)} fusion(bf16[512,3072]{1,0:T(8,128)(2,1)S(1)} %copy-done.9, bf16[1,1152,3072]{2,1,0:T(8,128)(2,1)} %param.25, f32[1152,512]{0,1:T(8,128)S(1)} %fusion.4, f32[512]{0:T(512)S(1)} %bitcast.114), kind=kOutput, calls=%fused_computation.9 | convolution fusion | flops 3627417600 | bytes 14944256 | tf_op jit(solution)/shard_map/dot_general | solution.py:109
  231.8 3.0 %copy.51 = f32[1,1152,512]{2,1,0:T(8,128)} copy(f32[1,1152,512]{1,2,0:T(8,128)} %fusion.13) | data formatting | bytes 4718592
  (48 shorter events, 3.7 us)
Async XLA Ops:
  7.2 63.7 %copy-start = (bf16[512,3072]{1,0:T(8,128)(2,1)S(1)}, bf16[512,3072]{1,0:T(8,128)(2,1)}, u32[]{:S(2)}) copy-start(bf16[512,3072]{1,0:T(8,128)(2,1)} %param.20) | copy-start | bytes 9437188
  7.2 149.4 %all-reduce.2.cloned.1.call-start = ((), (), s32[]{:S(2)}) async-start(), calls=%async_computation | async-start | bytes 6291456 | tf_op jit(solution)/shard_map/psum | solution.py:84
  10.0 3.1 %copy-start.4 = (bf16[2,128,512]{1,2,0:T(8,128)(2,1)}, bf16[2,128,512]{1,2,0:T(8,128)(2,1)S(1)}, u32[]{:S(2)}) copy-start(bf16[2,128,512]{1,2,0:T(8,128)(2,1)S(1)} %copy.56) | copy-start | bytes 786436
  13.1 54.9 %copy-start.3 = (bf16[2,128,512]{2,1,0:T(8,128)(2,1)S(1)}, bf16[2,128,512]{2,1,0:T(8,128)(2,1)}, u32[]{:S(2)}) copy-start(bf16[2,128,512]{2,1,0:T(8,128)(2,1)} %param.17) | copy-start | bytes 786436
  15.2 16.3 %collective-permute-start = (f32[2,4,128,128]{3,2,1,0:T(8,128)}, f32[2,4,128,128]{3,2,1,0:T(8,128)}, u32[]{:S(2)}, u32[]{:S(2)}) collective-permute-start(f32[2,4,128,128]{3,2,1,0:T(8,128)} %multiply_add_fusion.2), channel_id=1, source_target_pairs={{0,8},{8,16},{16,24},{1,9},{9,17},{17,25},{2,10},{10,18},{18,26},{... | collective-permute-start | bytes 1572872 | tf_op jit(solution)/shard_map/while/body/eval_jaxpr/ppermute | solution.py:12
  33.7 15.0 %collective-permute-start = (f32[2,4,128,128]{3,2,1,0:T(8,128)}, f32[2,4,128,128]{3,2,1,0:T(8,128)}, u32[]{:S(2)}, u32[]{:S(2)}) collective-permute-start(f32[2,4,128,128]{3,2,1,0:T(8,128)} %multiply_add_fusion.2), channel_id=1, source_target_pairs={{0,8},{8,16},{16,24},{1,9},{9,17},{17,25},{2,10},{10,18},{18,26},{... | collective-permute-start | bytes 1572872 | tf_op jit(solution)/shard_map/while/body/eval_jaxpr/ppermute | solution.py:12
  50.8 14.1 %collective-permute-start = (f32[2,4,128,128]{3,2,1,0:T(8,128)}, f32[2,4,128,128]{3,2,1,0:T(8,128)}, u32[]{:S(2)}, u32[]{:S(2)}) collective-permute-start(f32[2,4,128,128]{3,2,1,0:T(8,128)} %multiply_add_fusion.2), channel_id=1, source_target_pairs={{0,8},{8,16},{16,24},{1,9},{9,17},{17,25},{2,10},{10,18},{18,26},{... | collective-permute-start | bytes 1572872 | tf_op jit(solution)/shard_map/while/body/eval_jaxpr/ppermute | solution.py:12
  64.8 4.7 %copy-start.8 = (f32[512]{0:T(512)S(1)}, f32[512]{0:T(512)}, u32[]{:S(2)}) copy-start(f32[512]{0:T(512)} %param.19) | copy-start | bytes 6148
  66.5 1.5 copy-start.2
  70.9 2.7 %copy-start.5 = (bf16[16,2,3072]{2,1,0:T(2,128)(2,1)S(1)}, bf16[16,2,3072]{2,1,0:T(2,128)(2,1)}, u32[]{:S(2)}) copy-start(bf16[16,2,3072]{2,1,0:T(2,128)(2,1)} %param.14) | copy-start | bytes 589828
  73.6 1.9 copy-start.6
  75.5 139.2 %all-gather.2.cloned.1.call-start = ((), (), s32[]{:S(2)}) async-start(), calls=%async_computation.1 | async-start | bytes 3932160 | tf_op jit(solution)/shard_map/all_gather | solution.py:105
  156.6 2.8 %copy-start.1 = (f32[128,2,3072]{2,0,1:T(8,128)S(1)}, f32[128,2,3072]{2,0,1:T(8,128)}, u32[]{:S(2)}) copy-start(f32[128,2,3072]{2,0,1:T(8,128)} %all-reduce.2.cloned.1.call-done) | copy-start | bytes 9437188
  163.3 7.3 %copy-start.7 = (f32[512,2,2]{0,2,1:T(2,128)S(1)}, f32[512,2,2]{0,2,1:T(2,128)}, u32[]{:S(2)}) copy-start(f32[512,2,2]{0,2,1:T(2,128)} %param.23) | copy-start | bytes 24580
  214.6 8.4 %copy-start.9 = (bf16[512,3072]{1,0:T(8,128)(2,1)S(1)}, bf16[512,3072]{1,0:T(8,128)(2,1)}, u32[]{:S(2)}) copy-start(bf16[512,3072]{1,0:T(8,128)(2,1)} %all-gather.2.cloned.1.call-done) | copy-start | bytes 9437188
Sparse Core Ops, SparseCore 0:
  75.6 80.9 all-reduce.1
  170.8 43.8 all-gather.1
where the time goes:
time: 242 us
  waiting for transfers between devices  149 us (62%)
  matrix products  29.6 us (12%)
  local copies, waits for them, and re-layouts  16.5 us (7%)
  other arithmetic  16.2 us (7%)
  starting transfers between devices  16.1 us (7%)
  between operations  14.2 us (6%)
    psum x1, waiting for transfers between devices, per_device(): lax.psum(jnp.einsum('tbk,kd->tbd', attention, out_proj, preferred_element...  78.4 us
    all_gather x1, waiting for transfers between devices, per_device(): row_piece = lax.all_gather(slot_rows, 'seq', axis=0, tiled=True)  41.2 us
    ppermute x3, waiting for transfers between devices, passed_along(): return lax.ppermute(block, axis, route)  29.3 us
    ppermute x3, starting transfers between devices, passed_along(): return lax.ppermute(block, axis, route)  16 us
    dot_general x1, matrix products, per_device(): lax.dot_general(w_up[0], row_piece, (((1,), (1,)), ((), ())), preferred_e...  8.74 us
    dot_general x1, matrix products, per_device(): lax.dot_general(w_gate[0], row_piece, (((1,), (1,)), ((), ())), preferred...  8.36 us
    add x3, other arithmetic, advance(): outgoing = jnp.exp(block_total)[..., None, None] * incoming + fresh_state  6.35 us
  transfers between devices with their start and end apart: 5, of which 5 were waited for; matrix products, arithmetic and copies ran while one was open for 2% of the time, Pallas kernels for 0%

commit v1 on v0

v1 whole, which is shorter than its diff:
```python
import functools

import jax
import jax.numpy as jnp
from jax import lax
from jax.experimental import pallas as pl
from jax.experimental.pallas import tpu as pltpu
from jax.sharding import PartitionSpec as P

BF, F32 = jnp.bfloat16, jnp.float32
PRECISE = lax.Precision.HIGHEST
VMEM_BYTES = 48 * 1024 * 1024
NT = (((1,), (1,)), ((), ()))
TN = (((0,), (0,)), ((), ()))


def swap(block, axis, distance, forward_only=False):
    devices = range(lax.axis_size(axis))
    route = [(i, i ^ distance) for i in devices if not forward_only or i < i ^ distance]
    return lax.ppermute(block, axis, route)


def mm(a, b, dims=(((1,), (0,)), ((), ()))):
    return lax.dot_general(a, b, dims, preferred_element_type=F32)


def halves(x):
    high = x.astype(BF)
    return high, (x - high.astype(F32)).astype(BF)


def thirds(x):
    high, rest = x.astype(BF), None
    rest = x - high.astype(F32)
    middle = rest.astype(BF)
    return high, middle, (rest - middle.astype(F32)).astype(BF)


def lower_triangle(size):
    return (
        lax.broadcasted_iota(jnp.int32, (size, size), 0) >= lax.broadcasted_iota(jnp.int32, (size, size), 1)
    )


def running_columns(log_decay):
    tri = lower_triangle(log_decay.shape[1]).astype(F32)
    return lax.dot_general(tri, log_decay, NT, precision=PRECISE, preferred_element_type=F32)


def running_rows(log_decay):
    tri = lower_triangle(log_decay.shape[1]).astype(F32)
    return lax.dot_general(log_decay, tri, NT, precision=PRECISE, preferred_element_type=F32)


def state_kernel(k_ref, v_ref, decay_ref, out_ref):
    seqs, heads, size = decay_ref.shape
    width = k_ref.shape[2] // heads
    totals = []
    for b in range(seqs):
        columns = running_columns(decay_ref[b])
        tail = jnp.exp(columns[size - 1 : size, :] - columns)
        totals.append(jnp.broadcast_to(running_rows(decay_ref[b])[:, size - 1 : size], (heads, width)))
        for h in range(heads):
            part = slice(h * width, (h + 1) * width)
            value = v_ref[b, :, part]
            high, low = halves(k_ref[b, :, part].astype(F32) * tail[:, h : h + 1])
            at = (b * heads + h) * width
            out_ref[at : at + width, :] = (mm(high, value, TN) + mm(low, value, TN)).astype(BF)
    total = jnp.concatenate(totals, axis=0)
    pieces = [piece.astype(F32) for piece in thirds(total)]
    pieces.append(jnp.zeros_like(total))
    out_ref[seqs * heads * width :, :] = jnp.concatenate(pieces, axis=0).astype(BF)


def inner_kernel(q_ref, k_ref, v_ref, decay_ref, out_ref):
    seqs, heads, size = decay_ref.shape
    width = k_ref.shape[2] // heads
    causal = lower_triangle(size)
    for b in range(seqs):
        columns = running_columns(decay_ref[b])
        rows = running_rows(decay_ref[b])
        for h in range(heads):
            part = slice(h * width, (h + 1) * width)
            spread = columns[:, h : h + 1] - rows[h : h + 1, :]
            decay = jnp.where(causal, jnp.exp(jnp.where(causal, spread, 0.0)), 0.0)
            scores = mm(q_ref[b, :, part], k_ref[b, :, part], NT) * decay
            high, low = halves(scores)
            value = v_ref[b, :, part]
            out_ref[b, :, part] = mm(high, value) + mm(low, value)


def project_kernel(count, line, *refs):
    q_ref, inner_ref, decay_ref, gain_ref = refs[:4]
    states = refs[4 : 3 + count]
    proj_ref, own_ref, partner_ref, att_ref = refs[3 + count :]
    seqs, heads, size = decay_ref.shape
    width = q_ref.shape[2] // heads

    @pl.when(pl.program_id(0) == 0)
    def _():
        me = lax.axis_index("seq")
        index = lax.axis_index("exp")
        base = seqs * heads * width
        each = seqs * heads
        totals = []
        for state in states:
            three = state[base : base + 4 * each, :].astype(F32)
            totals.append(three[:each] + three[each : 2 * each] + three[2 * each : 3 * each])
        factors = []
        for first in range(1, count):
            later = jnp.zeros_like(totals[0])
            for second in range(1, count):
                between = ((me ^ first) < (me ^ second)) & ((me ^ second) < me)
                later = later + jnp.where(between, totals[second - 1], 0.0)
            factors.append(jnp.where((me ^ first) < me, jnp.exp(later), 0.0))
        rows = []
        for b in range(seqs):
            grown = jnp.exp(running_columns(decay_ref[b]))
            parts = []
            for h in range(heads):
                part = slice(h * width, (h + 1) * width)
                n = b * heads + h
                incoming = jnp.zeros((width, width), F32)
                for state, factor in zip(states, factors):
                    incoming = incoming + factor[n : n + 1, :] * state[n * width : (n + 1) * width, :].astype(F32)
                high, low = halves(incoming)
                query = q_ref[b, :, part]
                raw = inner_ref[b, :, part] + grown[:, h : h + 1] * (mm(query, high) + mm(query, low))
                meansq = jnp.mean(raw * raw, axis=-1, keepdims=True)
                parts.append((raw * lax.rsqrt(meansq + 1e-06) * gain_ref[:, part]).astype(BF))
            rows.append(jnp.concatenate(parts, axis=1))
        attention = jnp.concatenate(rows, axis=0)
        total = seqs * size
        own = size // (2 * line)
        to = lax.broadcasted_iota(jnp.int32, (total, total), 0)
        source = source_position(to // (total // 2), (to // (seqs * own)) % line, to % own, index, own)
        source = source + size * ((to // own) % seqs)
        pick = (source == lax.broadcasted_iota(jnp.int32, (total, total), 1)).astype(BF)
        att_ref[...] = mm(pick, attention).astype(BF)

    half = att_ref.shape[0] // 2
    own_ref[...] = mm(att_ref[:half, :], proj_ref[...])
    partner_ref[...] = mm(att_ref[half:, :], proj_ref[...]).astype(BF)


def source_position(flip, distance, place, index, own):
    return own * (2 * ((index // 2) ^ distance) + ((index % 2) ^ flip)) + place


def pair_sum_kernel(own_ref, got_ref, first_ref, *send_refs):
    rows = first_ref.shape[0]
    first_ref[...] = own_ref[:rows, :] + got_ref[:rows, :].astype(F32)
    for d, send_ref in enumerate(send_refs, start=1):
        part = slice(d * rows, (d + 1) * rows)
        send_ref[...] = (own_ref[part, :] + got_ref[part, :].astype(F32)).astype(BF)


def mix_kernel(first_ref, residual_ref, gain_ref, *refs):
    mixed_ref, normed_ref = refs[-2:]
    mixed = residual_ref[...].astype(F32) + first_ref[...]
    for got_ref in refs[:-2]:
        mixed = mixed + got_ref[...].astype(F32)
    mixed_ref[...] = mixed
    meansq = jnp.mean(mixed * mixed, axis=-1, keepdims=True)
    normed_ref[...] = (mixed * lax.rsqrt(meansq + 1e-06) * gain_ref[...]).astype(BF)


def route_kernel(capacity, own, seqs, first_ref, second_ref, first_weight, second_weight, slot_ref, weight_ref, a_ref, b_ref):
    count, total = first_ref.shape
    me = lax.axis_index("seq")
    index = lax.axis_index("exp")
    line = total // (2 * own * seqs)
    hit_a, hit_b = first_ref[...] == index, second_ref[...] == index
    chosen = jnp.where(hit_a | hit_b, 1.0, 0.0).astype(BF)
    weight = jnp.where(hit_a, first_weight[...], 0.0) + jnp.where(hit_b, second_weight[...], 0.0)
    to = lax.broadcasted_iota(jnp.int32, (total, total), 1)
    piece = total // 4
    distance = (to // (2 * piece)) * (line // 2) + (to // (seqs * own)) % (line // 2)
    row = source_position((to // piece) % 2, distance, to % own, index, own) * seqs + (to // own) % seqs
    origin = lax.broadcasted_iota(jnp.int32, (total, total), 0)
    rank = mm(chosen, (origin <= row).astype(BF)) - 1.0
    same = (origin == row).astype(BF)
    picked = mm(chosen, same) > 0.5
    block = lax.broadcasted_iota(jnp.int32, (count, total), 0) % (count // 2)
    a_ref[...] = jnp.where(picked, rank.astype(jnp.int32) + block * capacity, -1)
    high, middle, low = thirds(weight)
    b_ref[...] = mm(high, same) + mm(middle, same) + mm(low, same)
    for d in range(count):
        slot_ref[d : d + 1, :] = a_ref[pl.ds(me ^ d, 1), :]
        weight_ref[d : d + 1, :] = b_ref[pl.ds(me ^ d, 1), :]


def expert_kernel(pieces, side_ref, slot_ref, weight_ref, gate_ref, up_ref, *refs):
    refs = list(refs)
    piece_refs, out_ref, rows_ref, scale_ref = refs[:pieces], *refs[-3:]

    @pl.when(pl.program_id(0) == 0)
    def _():
        blocks, total = slot_ref.shape
        slots = rows_ref.shape[0]
        each = pieces // blocks
        gathered, scale = None, None
        for n in range(blocks):
            pick = (
                slot_ref[n : n + 1, :] == lax.broadcasted_iota(jnp.int32, (slots, total), 0)
            ).astype(BF)
            rows = jnp.concatenate([ref[...] for ref in piece_refs[n * each : (n + 1) * each]], axis=0)
            part = mm(pick, rows)
            gathered = part if n == 0 else gathered + part
            share = sum(mm(jnp.broadcast_to(w, (8, total)), pick, NT) for w in thirds(weight_ref[n : n + 1, :]))
            scale = share if n == 0 else scale + share
        rows_ref[...] = gathered.astype(BF)
        scale_ref[...] = scale

    gate = mm(gate_ref[0], rows_ref[...], NT)
    up = mm(up_ref[0], rows_ref[...], NT)
    out_ref[0] = scale_ref[0:1, :] * (gate / (1.0 + jnp.exp(-gate))) * up


def params():
    return pltpu.CompilerParams(vmem_limit_bytes=VMEM_BYTES)


def cost(flops, bytes_accessed, transcendentals=0):
    return pl.CostEstimate(flops=int(flops), bytes_accessed=int(bytes_accessed), transcendentals=int(transcendentals))


def whole(shape):
    return pl.BlockSpec(shape, lambda *_: (0,) * len(shape))


def expert_half(side, slot, weight, w_gate, w_up, pieces, previous):
    units, width = w_gate.shape[1:]
    tile = max(size for size in range(16, 385, 16) if units % size == 0)
    rows = [piece for block in pieces for piece in block]
    slots = previous[1]
    total = slot.shape[1]
    aliases = {} if previous[0] is None else {5 + len(rows): 0}
    carried = [] if previous[0] is None else [previous[0]]
    weights_spec = pl.BlockSpec((1, tile, width), lambda i, side: (0, i, 0))
    grid_spec = pltpu.PrefetchScalarGridSpec(
        num_scalar_prefetch=1,
        grid=(units // tile,),
        in_specs=[
            whole(slot.shape),
            whole(weight.shape),
            weights_spec,
            weights_spec,
        ]
        + [whole(piece.shape) for piece in rows]
        + [pl.BlockSpec(memory_space=pl.ANY) for _ in carried],
        out_specs=pl.BlockSpec((1, tile, slots), lambda i, side: (0, i, side[0])),
        scratch_shapes=[pltpu.VMEM((slots, width), BF), pltpu.VMEM((8, slots), F32)],
    )
    return pl.pallas_call(
        functools.partial(expert_kernel, len(rows)),
        grid_spec=grid_spec,
        out_shape=jax.ShapeDtypeStruct((1, units, 2 * slots), F32),
        input_output_aliases=aliases,
        compiler_params=params(),
        cost_estimate=cost(4 * units * width * slots + 2 * slots * total * width * len(pieces), 4 * units * width),
        name="expert_half",
    )(side, slot, weight, w_gate, w_up, *rows, *carried)


def per_device(
    residual,
    queries,
    key_vecs,
    value_vecs,
    log_decay,
    head_gain,
    out_proj,
    norm_gain,
    routes,
    route_weight,
    w_gate,
    w_up,
):
    count, owners = lax.axis_size("seq"), lax.axis_size("exp")
    line = owners // 2
    me = lax.axis_index("seq")
    seqs, size, feat = queries.shape
    heads = log_decay.shape[1]
    width = feat // heads
    own, _, model = residual.shape
    unit = own * seqs
    total = size * seqs
    capacity = 8 * size // owners

    states = pl.pallas_call(
        state_kernel,
        out_shape=jax.ShapeDtypeStruct((seqs * heads * (width + 4), width), BF),
        compiler_params=params(),
        cost_estimate=cost(4 * total * feat * width, 6 * total * feat),
        name="states",
    )(key_vecs, value_vecs, log_decay)
    arrived = [swap(states, "seq", d, forward_only=True) for d in range(1, count)]
    inner = pl.pallas_call(
        inner_kernel,
        out_shape=jax.ShapeDtypeStruct((seqs, size, feat), F32),
        compiler_params=params(),
        cost_estimate=cost(6 * total * feat * size, 10 * total * feat),
        name="inner",
    )(queries, key_vecs, value_vecs, log_decay)

    tile = next(t for t in (1024, 512, 256, 128) if model % t == 0)
    own_sum, partner_sum = pl.pallas_call(
        functools.partial(project_kernel, count, line),
        grid=(model // tile,),
        in_specs=[whole(queries.shape), whole(inner.shape), whole(log_decay.shape), whole((1, feat))]
        + [whole(states.shape)] * (count - 1)
        + [pl.BlockSpec((feat, tile), lambda i: (0, i))],
        out_specs=[pl.BlockSpec((total // 2, tile), lambda i: (0, i))] * 2,
        out_shape=[
            jax.ShapeDtypeStruct((total // 2, model), F32),
            jax.ShapeDtypeStruct((total // 2, model), BF),
        ],
        scratch_shapes=[pltpu.VMEM((total, feat), BF)],
        compiler_params=params(),
        cost_estimate=cost(2 * total * feat * model, 2 * feat * model + 3 * total * model),
        name="project",
    )(queries, inner, log_decay, head_gain.reshape(1, feat), *arrived, out_proj)

    from_partner = swap(partner_sum, "exp", 1)
    tiles = model // tile
    first, *sends = pl.pallas_call(
        pair_sum_kernel,
        grid=(tiles,),
        in_specs=[pl.BlockSpec((total // 2, tile), lambda i: (0, i))] * 2,
        out_specs=[pl.BlockSpec((unit, tile), lambda i: (0, i))] * line,
        out_shape=[jax.ShapeDtypeStruct((unit, model), F32)] + [jax.ShapeDtypeStruct((unit, model), BF)] * (line - 1),
        compiler_params=params(),
        cost_estimate=cost(total * model, 4 * total * model),
        name="pair_sum",
    )(own_sum, from_partner)
    got = [swap(send, "exp", 2 * d) for d, send in enumerate(sends, start=1)]

    residual_rows = jnp.transpose(residual, (1, 0, 2)).reshape(unit, model)
    mixed, normed = pl.pallas_call(
        mix_kernel,
        out_shape=[jax.ShapeDtypeStruct((unit, model), F32), jax.ShapeDtypeStruct((unit, model), BF)],
        compiler_params=params(),
        cost_estimate=cost(10 * unit * model, 16 * unit * model),
        name="mix",
    )(first, residual_rows, norm_gain.reshape(1, model), *got)
    mixed_rows = jnp.transpose(mixed.reshape(seqs, own, model), (1, 0, 2))

    block_routes = routes.reshape(count, total, routes.shape[-1])
    block_weights = route_weight.reshape(count, total, routes.shape[-1])
    slot, weight = pl.pallas_call(
        functools.partial(route_kernel, capacity, own, seqs),
        out_shape=[jax.ShapeDtypeStruct((count, total), jnp.int32), jax.ShapeDtypeStruct((count, total), F32)],
        scratch_shapes=[pltpu.VMEM((count, total), jnp.int32), pltpu.VMEM((count, total), F32)],
        compiler_params=params(),
        cost_estimate=cost(10 * count * total * total, 16 * count * total),
        name="route",
    )(block_routes[..., 0], block_routes[..., 1], block_weights[..., 0], block_weights[..., 1])

    along = [normed] + [swap(normed, "exp", 2 * d) for d in range(1, line)]
    parts = [jnp.concatenate(along[: line // 2], axis=0), jnp.concatenate(along[line // 2 :], axis=0)]
    blocks = []
    for d in range(count):
        pieces = []
        for part in parts:
            here = part if d == 0 else swap(part, "seq", d)
            pieces += [here, swap(here, "exp", 1)]
        blocks.append(pieces)
    half = count // 2
    slots = half * capacity
    side = (me // half).astype(jnp.int32).reshape(1)
    hidden = expert_half(side, slot[:half], weight[:half], w_gate, w_up, blocks[:half], (None, slots))
    hidden = expert_half(1 - side, slot[half:], weight[half:], w_gate, w_up, blocks[half:], (hidden, slots))
    return (mixed_rows, hidden)


def solution(mesh):
    placed = (
        P(("seq", "exp"), None, None),
        P(None, "seq", "exp"),
        P(None, "seq", "exp"),
        P(None, "seq", "exp"),
        P(None, "exp", "seq"),
        P("exp"),
        P("exp", None),
        P(),
        P(),
        P(),
        P("exp", "seq", None),
        P("exp", "seq", None),
    )
    return jax.shard_map(
        per_device,
        mesh=mesh,
        in_specs=placed,
        out_specs=(P(("seq", "exp"), None, None), P("exp", "seq", None)),
        check_vma=False,
    )
```

time: 242 us -> 124 us (0.51)
  waiting for transfers between devices: 149 us -> 53 us
  matrix products: 29.6 us -> 0 us
  Pallas kernels: 0 us -> 27.2 us
  starting transfers between devices: 16.1 us -> 33.9 us
  other arithmetic: 16.2 us -> 0 us
  between operations: 14.2 us -> 0.83 us
  local copies, waits for them, and re-layouts: 16.5 us -> 9 us
    psum x1 -> x0, waiting for transfers between devices: 78.4 us -> none  [per_device(): lax.psum(jnp.einsum('tbk,kd->tbd', attention, out_proj, preferred_element...]
    all_gather x1 -> x0, waiting for transfers between devices: 41.2 us -> none  [per_device(): row_piece = lax.all_gather(slot_rows, 'seq', axis=0, tiled=True)]
    dot_general x9 -> x0, matrix products: 29.6 us -> none  [the longest x1 8.74 us: per_device(): lax.dot_general(w_up[0], row_piece, (((1,), (1,)), ((), ())), preferred_e...]
    pallas_call x0 -> x8, Pallas kernels: none -> 27.2 us  [the longest x2 19.7 us: expert_half(): pl.pallas_call(functools.partial(expert_kernel, len(rows)), grid_spec=gri...]
    ppermute x3 -> x24, waiting for transfers between devices: 29.3 us -> 53 us  [swap(): return lax.ppermute(block, axis, route)]
    ppermute x3 -> x24, starting transfers between devices: 16 us -> 33.9 us  [swap(): return lax.ppermute(block, axis, route)]
    add x4 -> x0, other arithmetic: 8.18 us -> none  [the longest x3 6.35 us: advance(): outgoing = jnp.exp(block_total)[..., None, None] * incoming + fresh_state]
    reshape x2 -> x3, local copies, waits for them, and re-layouts: 5.74 us -> 1.64 us  [the longest x1 1.05 us: per_device(): mixed_rows = jnp.transpose(mixed.reshape(seqs, own, model), (1, 0, 2))]
  transfers between devices with their start and end apart: 5 -> 24, of which waited for: 5 -> 13; matrix products, arithmetic and copies ran while one was open for 2% -> 2% of each run, Pallas kernels for 0% -> 9%
where the time goes in v1:
time: 124 us
  waiting for transfers between devices  53 us (43%)
  starting transfers between devices  33.9 us (27%)
  Pallas kernels  27.2 us (22%)
  local copies, waits for them, and re-layouts  9 us (7%)
    ppermute x24, waiting for transfers between devices, swap(): return lax.ppermute(block, axis, route)  53 us
    ppermute x24, starting transfers between devices, swap(): return lax.ppermute(block, axis, route)  33.9 us
    pallas_call x2, Pallas kernels, expert_half(): pl.pallas_call(functools.partial(expert_kernel, len(rows)), grid_spec=gri...  19.7 us
    unnamed x28, local copies, waits for them, and re-layouts  7.28 us
    pallas_call x1, Pallas kernels, per_device(): pl.pallas_call(functools.partial(project_kernel, count, line), grid=(mode...  4.42 us
  transfers between devices with their start and end apart: 24, of which 13 were waited for; matrix products, arithmetic and copies ran while one was open for 2% of the time, Pallas kernels for 9%

profile of v1, /device:TPU:0, one launch (start us, length us, event | category | flops | bytes accessed | tf_op | source)
XLA Modules:
  0.0 123.9 jit_solution(12839914031138891678)
XLA Ops:
  1.6 0.9 copy-done.2
  4.1 5.8 %collective-permute-start.2 = (bf16[1056,128]{1,0:T(8,128)(2,1)S(1)}, bf16[1056,128]{1,0:T(8,128)(2,1)S(1)}, u32[]{:S(2)}, u32[]{:S(2)}) collective-permute-start(bf16[1056,128]{1,0:T(8,128)(2,1)S(1)} %states.1), channel_id=1, source_target_pairs={{0,24},{8,16},{1,25},{9,17},{2,26},{10,18},{3,27},{11,19},{4,28},{... | collective-permute-start | bytes 811016 | tf_op jit(solution)/shard_map/ppermute | solution.py:20
  9.9 1.3 %collective-permute-start.1 = (bf16[1056,128]{1,0:T(8,128)(2,1)S(1)}, bf16[1056,128]{1,0:T(8,128)(2,1)S(1)}, u32[]{:S(2)}, u32[]{:S(2)}) collective-permute-start(bf16[1056,128]{1,0:T(8,128)(2,1)S(1)} %states.1), channel_id=1, source_target_pairs={{0,16},{8,24},{1,17},{9,25},{2,18},{10,26},{3,19},{11,27},{4,20},{... | collective-permute-start | bytes 811016 | tf_op jit(solution)/shard_map/ppermute | solution.py:20
  11.2 2.5 %collective-permute-start = (bf16[1056,128]{1,0:T(8,128)(2,1)S(1)}, bf16[1056,128]{1,0:T(8,128)(2,1)S(1)}, u32[]{:S(2)}, u32[]{:S(2)}) collective-permute-start(bf16[1056,128]{1,0:T(8,128)(2,1)S(1)} %states.1), channel_id=1, source_target_pairs={{0,8},{16,24},{1,9},{17,25},{2,10},{18,26},{3,11},{19,27},{4,12},{... | collective-permute-start | bytes 811016 | tf_op jit(solution)/shard_map/ppermute | solution.py:20
  14.7 0.9 copy-done.3
  15.6 0.9 copy-done.4
  17.3 1.3 %inner.1.refs_1_ = f32[2,128,512]{2,1,0:T(8,128)S(1)} custom-call(bf16[2,128,512]{2,1,0:T(8,128)(2,1)S(1)} %copy-done.4, bf16[2,128,512]{2,1,0:T(8,128)(2,1)S(1)} %copy-done.1, bf16[2,128,512]{2,1,0:T(8,128)(2,1)S(1)} %copy-done.3, f32[2,4,128]{2,1,0:T(4,128)S(1)} %copy-done.6), custom_call_target="tpu_custom_call" | custom-call | flops 100663296 | bytes 1310720 | tf_op jit(solution)/shard_map/inner/pallas_call | solution.py:299
  18.6 2.8 %collective-permute-done.1.refs_5_ = bf16[1056,128]{1,0:T(8,128)(2,1)S(1)} collective-permute-done((bf16[1056,128]{1,0:T(8,128)(2,1)S(1)}, bf16[1056,128]{1,0:T(8,128)(2,1)S(1)}, u32[]{:S(2)}, u32[]{:S(2)}) %collective-permute-start.1) | collective-permute-done | bytes 270368 | tf_op jit(solution)/shard_map/ppermute | solution.py:20
  22.2 4.4 %project.1 = (f32[128,3072]{1,0:T(8,128)S(1)}, bf16[128,3072]{1,0:T(8,128)(2,1)S(1)}) custom-call(bf16[2,128,512]{2,1,0:T(8,128)(2,1)S(1)} %copy-done.4, f32[2,128,512]{2,1,0:T(8,128)S(1)} %inner.1.refs_1_, f32[2,4,128]{2,1,0:T(4,128)S(1)} %copy-done.6, f32[1,512]{1,0:T(1,128)S(1)} %bitcast.24, bf16[1056,128]{1,0:T(8,128)(2,1)S(1)} %collective-permute-done.refs_4_, ...), custom_call_target="tpu_custom_call" | custom-call | flops 805306368 | bytes 5505024 | tf_op jit(solution)/shard_map/project/pallas_call | solution.py:308
  26.7 2.3 %collective-permute-done.3.got_ref = bf16[128,3072]{1,0:T(8,128)(2,1)S(1)} collective-permute-done((bf16[128,3072]{1,0:T(8,128)(2,1)S(1)}, bf16[128,3072]{1,0:T(8,128)(2,1)S(1)}, u32[]{:S(2)}, u32[]{:S(2)}) %collective-permute-start.3) | collective-permute-done | bytes 786464 | tf_op jit(solution)/shard_map/ppermute | solution.py:20
  29.4 1.6 %collective-permute-start.4 = (bf16[32,3072]{1,0:T(8,128)(2,1)S(1)}, bf16[32,3072]{1,0:T(8,128)(2,1)S(1)}, u32[]{:S(2)}, u32[]{:S(2)}) collective-permute-start(bf16[32,3072]{1,0:T(8,128)(2,1)S(1)} %get-tuple-element.15), channel_id=1, source_target_pairs={{0,2},{1,3},{2,0},{3,1},{4,6},{5,7},{6,4},{7,5},{8,10},{9,11},{10,... | collective-permute-start | bytes 589832 | tf_op jit(solution)/shard_map/ppermute | solution.py:20
  31.0 2.6 %collective-permute-start.5 = (bf16[32,3072]{1,0:T(8,128)(2,1)S(1)}, bf16[32,3072]{1,0:T(8,128)(2,1)S(1)}, u32[]{:S(2)}, u32[]{:S(2)}) collective-permute-start(bf16[32,3072]{1,0:T(8,128)(2,1)S(1)} %get-tuple-element.16), channel_id=1, source_target_pairs={{0,4},{1,5},{2,6},{3,7},{4,0},{5,1},{6,2},{7,3},{8,12},{9,13},{10,... | collective-permute-start | bytes 589832 | tf_op jit(solution)/shard_map/ppermute | solution.py:20
  35.0 5.1 %collective-permute-done.4.refs_0_ = bf16[32,3072]{1,0:T(8,128)(2,1)S(1)} collective-permute-done((bf16[32,3072]{1,0:T(8,128)(2,1)S(1)}, bf16[32,3072]{1,0:T(8,128)(2,1)S(1)}, u32[]{:S(2)}, u32[]{:S(2)}) %collective-permute-start.4) | collective-permute-done | bytes 196640 | tf_op jit(solution)/shard_map/ppermute | solution.py:20
  40.0 8.1 %collective-permute-done.5.refs_1_ = bf16[32,3072]{1,0:T(8,128)(2,1)S(1)} collective-permute-done((bf16[32,3072]{1,0:T(8,128)(2,1)S(1)}, bf16[32,3072]{1,0:T(8,128)(2,1)S(1)}, u32[]{:S(2)}, u32[]{:S(2)}) %collective-permute-start.5) | collective-permute-done | bytes 196640 | tf_op jit(solution)/shard_map/ppermute | solution.py:20
  48.4 2.5 %collective-permute-start.11 = (bf16[32,3072]{1,0:T(8,128)(2,1)S(1)}, bf16[32,3072]{1,0:T(8,128)(2,1)S(1)}, u32[]{:S(2)}, u32[]{:S(2)}) collective-permute-start(bf16[32,3072]{1,0:T(8,128)(2,1)S(1)} %get-tuple-element.21), channel_id=1, source_target_pairs={{0,6},{1,7},{2,4},{3,5},{4,2},{5,3},{6,0},{7,1},{8,14},{9,15},{10,... | collective-permute-start | bytes 589832 | tf_op jit(solution)/shard_map/ppermute | solution.py:20
  50.9 4.9 %collective-permute-start.10 = (bf16[32,3072]{1,0:T(8,128)(2,1)S(1)}, bf16[32,3072]{1,0:T(8,128)(2,1)S(1)}, u32[]{:S(2)}, u32[]{:S(2)}) collective-permute-start(bf16[32,3072]{1,0:T(8,128)(2,1)S(1)} %get-tuple-element.21), channel_id=1, source_target_pairs={{0,4},{1,5},{2,6},{3,7},{4,0},{5,1},{6,2},{7,3},{8,12},{9,13},{10,... | collective-permute-start | bytes 589832 | tf_op jit(solution)/shard_map/ppermute | solution.py:20
  55.9 6.6 %collective-permute-done.7 = bf16[32,3072]{1,0:T(8,128)(2,1)S(1)} collective-permute-done((bf16[32,3072]{1,0:T(8,128)(2,1)S(1)}, bf16[32,3072]{1,0:T(8,128)(2,1)S(1)}, u32[]{:S(2)}, u32[]{:S(2)}) %collective-permute-start.7) | collective-permute-done | bytes 196640 | tf_op jit(solution)/shard_map/ppermute | solution.py:20
  62.6 2.5 %collective-permute-start.20 = (bf16[64,3072]{1,0:T(8,128)(2,1)S(1)}, bf16[64,3072]{1,0:T(8,128)(2,1)S(1)}, u32[]{:S(2)}, u32[]{:S(2)}) collective-permute-start(bf16[64,3072]{1,0:T(8,128)(2,1)S(1)} %constant_dynamic-update-slice_fusion.refs_0_), channel_id=1, source_target_pairs={{0,8},{8,0},{16,24},{24,16},{1,9},{9,1},{17,25},{25,17},{2,10},{10... | collective-permute-start | bytes 1179656 | tf_op jit(solution)/shard_map/ppermute | solution.py:20
  65.1 1.4 %collective-permute-start.14 = (bf16[64,3072]{1,0:T(8,128)(2,1)S(1)}, bf16[64,3072]{1,0:T(8,128)(2,1)S(1)}, u32[]{:S(2)}, u32[]{:S(2)}) collective-permute-start(bf16[64,3072]{1,0:T(8,128)(2,1)S(1)} %constant_dynamic-update-slice_fusion.refs_0_), channel_id=1, source_target_pairs={{0,24},{8,16},{16,8},{24,0},{1,25},{9,17},{17,9},{25,1},{2,26},{10... | collective-permute-start | bytes 1179656 | tf_op jit(solution)/shard_map/ppermute | solution.py:20
  66.5 1.6 %collective-permute-done.10 = bf16[32,3072]{1,0:T(8,128)(2,1)S(1)} collective-permute-done((bf16[32,3072]{1,0:T(8,128)(2,1)S(1)}, bf16[32,3072]{1,0:T(8,128)(2,1)S(1)}, u32[]{:S(2)}, u32[]{:S(2)}) %collective-permute-start.10) | collective-permute-done | bytes 196640 | tf_op jit(solution)/shard_map/ppermute | solution.py:20
  68.1 2.4 %collective-permute-start.8 = (bf16[64,3072]{1,0:T(8,128)(2,1)S(1)}, bf16[64,3072]{1,0:T(8,128)(2,1)S(1)}, u32[]{:S(2)}, u32[]{:S(2)}) collective-permute-start(bf16[64,3072]{1,0:T(8,128)(2,1)S(1)} %constant_dynamic-update-slice_fusion.refs_0_), channel_id=1, source_target_pairs={{0,16},{8,24},{16,0},{24,8},{1,17},{9,25},{17,1},{25,9},{2,18},{10... | collective-permute-start | bytes 1179656 | tf_op jit(solution)/shard_map/ppermute | solution.py:20
  70.6 1.6 %collective-permute-start.22 = (bf16[64,3072]{1,0:T(8,128)(2,1)S(1)}, bf16[64,3072]{1,0:T(8,128)(2,1)S(1)}, u32[]{:S(2)}, u32[]{:S(2)}) collective-permute-start(bf16[64,3072]{1,0:T(8,128)(2,1)S(1)} %constant_dynamic-update-slice_fusion.2.refs_2_), channel_id=1, source_target_pairs={{0,8},{8,0},{16,24},{24,16},{1,9},{9,1},{17,25},{25,17},{2,10},{10... | collective-permute-start | bytes 1179656 | tf_op jit(solution)/shard_map/ppermute | solution.py:20
  72.4 2.3 %collective-permute-done.20.refs_4_ = bf16[64,3072]{1,0:T(8,128)(2,1)S(1)} collective-permute-done((bf16[64,3072]{1,0:T(8,128)(2,1)S(1)}, bf16[64,3072]{1,0:T(8,128)(2,1)S(1)}, u32[]{:S(2)}, u32[]{:S(2)}) %collective-permute-start.20) | collective-permute-done | bytes 393248 | tf_op jit(solution)/shard_map/ppermute | solution.py:20
  74.7 3.3 %collective-permute-start.16 = (bf16[64,3072]{1,0:T(8,128)(2,1)S(1)}, bf16[64,3072]{1,0:T(8,128)(2,1)S(1)}, u32[]{:S(2)}, u32[]{:S(2)}) collective-permute-start(bf16[64,3072]{1,0:T(8,128)(2,1)S(1)} %constant_dynamic-update-slice_fusion.2.refs_2_), channel_id=1, source_target_pairs={{0,24},{8,16},{16,8},{24,0},{1,25},{9,17},{17,9},{25,1},{2,26},{10... | collective-permute-start | bytes 1179656 | tf_op jit(solution)/shard_map/ppermute | solution.py:20
  78.1 6.9 %collective-permute-done.14.refs_4_ = bf16[64,3072]{1,0:T(8,128)(2,1)S(1)} collective-permute-done((bf16[64,3072]{1,0:T(8,128)(2,1)S(1)}, bf16[64,3072]{1,0:T(8,128)(2,1)S(1)}, u32[]{:S(2)}, u32[]{:S(2)}) %collective-permute-start.14) | collective-permute-done | bytes 393248 | tf_op jit(solution)/shard_map/ppermute | solution.py:20
  85.0 3.9 %collective-permute-done.8.refs_0_ = bf16[64,3072]{1,0:T(8,128)(2,1)S(1)} collective-permute-done((bf16[64,3072]{1,0:T(8,128)(2,1)S(1)}, bf16[64,3072]{1,0:T(8,128)(2,1)S(1)}, u32[]{:S(2)}, u32[]{:S(2)}) %collective-permute-start.8) | collective-permute-done | bytes 393248 | tf_op jit(solution)/shard_map/ppermute | solution.py:20
  88.9 2.7 %collective-permute-done.22.refs_6_ = bf16[64,3072]{1,0:T(8,128)(2,1)S(1)} collective-permute-done((bf16[64,3072]{1,0:T(8,128)(2,1)S(1)}, bf16[64,3072]{1,0:T(8,128)(2,1)S(1)}, u32[]{:S(2)}, u32[]{:S(2)}) %collective-permute-start.22) | collective-permute-done | bytes 393248 | tf_op jit(solution)/shard_map/ppermute | solution.py:20
  91.6 1.1 copy.24
  93.2 5.1 %collective-permute-done.16.refs_6_ = bf16[64,3072]{1,0:T(8,128)(2,1)S(1)} collective-permute-done((bf16[64,3072]{1,0:T(8,128)(2,1)S(1)}, bf16[64,3072]{1,0:T(8,128)(2,1)S(1)}, u32[]{:S(2)}, u32[]{:S(2)}) %collective-permute-start.16) | collective-permute-done | bytes 393248 | tf_op jit(solution)/shard_map/ppermute | solution.py:20
  98.3 5.5 %collective-permute-done.12.refs_2_ = bf16[64,3072]{1,0:T(8,128)(2,1)S(1)} collective-permute-done((bf16[64,3072]{1,0:T(8,128)(2,1)S(1)}, bf16[64,3072]{1,0:T(8,128)(2,1)S(1)}, u32[]{:S(2)}, u32[]{:S(2)}) %collective-permute-start.12) | collective-permute-done | bytes 393248 | tf_op jit(solution)/shard_map/ppermute | solution.py:20
  104.3 9.8 %expert_half.2.refs_8_ = f32[1,1152,512]{2,1,0:T(8,128)} custom-call(s32[1]{0:T(128)} %bitcast.6.side_ref, s32[2,256]{1,0:T(2,128)S(1)} %get-tuple-element.28.slot_ref, f32[2,256]{1,0:T(2,128)S(1)} %get-tuple-element.26.weight_ref, bf16[1,1152,3072]{2,1,0:T(8,128)(2,1)} %gate_ref.3, bf16[1,1152,3072]{2,1,0:T(8,128)(2,1)} %up_ref.3, ...), custom_call_target="tpu_custom_call" | custom-call | flops 4429185024 | bytes 14155776 | tf_op jit(solution)/shard_map/expert_half/pallas_call | solution.py:255
  114.1 9.8 %expert_half.3 = f32[1,1152,512]{2,1,0:T(8,128)} custom-call(s32[1]{0:T(128)S(6)} %sub.8.side_ref, s32[2,256]{1,0:T(2,128)S(1)} %get-tuple-element.29.slot_ref, f32[2,256]{1,0:T(2,128)S(1)} %get-tuple-element.27.weight_ref, bf16[1,1152,3072]{2,1,0:T(8,128)(2,1)} %gate_ref.3, bf16[1,1152,3072]{2,1,0:T(8,128)(2,1)} %up_ref.3, ...), custom_call_target="tpu_custom_call", output_to_operand_aliasing={{}: (13, {})} | custom-call | flops 4429185024 | bytes 14155776 | tf_op jit(solution)/shard_map/expert_half/pallas_call | solution.py:255
  (62 shorter events, 8.4 us)
Async XLA Ops:
  0.6 1.0 copy-start
  1.6 0.9 copy-start.2
  4.1 14.5 %collective-permute-start.2 = (bf16[1056,128]{1,0:T(8,128)(2,1)S(1)}, bf16[1056,128]{1,0:T(8,128)(2,1)S(1)}, u32[]{:S(2)}, u32[]{:S(2)}) collective-permute-start(bf16[1056,128]{1,0:T(8,128)(2,1)S(1)} %states.1), channel_id=1, source_target_pairs={{0,24},{8,16},{1,25},{9,17},{2,26},{10,18},{3,27},{11,19},{4,28},{... | collective-permute-start | bytes 811016 | tf_op jit(solution)/shard_map/ppermute | solution.py:20
  9.9 11.5 %collective-permute-start.1 = (bf16[1056,128]{1,0:T(8,128)(2,1)S(1)}, bf16[1056,128]{1,0:T(8,128)(2,1)S(1)}, u32[]{:S(2)}, u32[]{:S(2)}) collective-permute-start(bf16[1056,128]{1,0:T(8,128)(2,1)S(1)} %states.1), channel_id=1, source_target_pairs={{0,16},{8,24},{1,17},{9,25},{2,18},{10,26},{3,19},{11,27},{4,20},{... | collective-permute-start | bytes 811016 | tf_op jit(solution)/shard_map/ppermute | solution.py:20
  11.2 10.2 %collective-permute-start = (bf16[1056,128]{1,0:T(8,128)(2,1)S(1)}, bf16[1056,128]{1,0:T(8,128)(2,1)S(1)}, u32[]{:S(2)}, u32[]{:S(2)}) collective-permute-start(bf16[1056,128]{1,0:T(8,128)(2,1)S(1)} %states.1), channel_id=1, source_target_pairs={{0,8},{16,24},{1,9},{17,25},{2,10},{18,26},{3,11},{19,27},{4,12},{... | collective-permute-start | bytes 811016 | tf_op jit(solution)/shard_map/ppermute | solution.py:20
  13.7 1.0 copy-start.1
  14.7 0.9 copy-start.3
  22.2 11.7 %copy-start.9 = (bf16[16,2,3072]{2,1,0:T(2,128)(2,1)S(1)}, bf16[16,2,3072]{2,1,0:T(2,128)(2,1)}, u32[]{:S(2)}) copy-start(bf16[16,2,3072]{2,1,0:T(2,128)(2,1)} %param.12) | copy-start | bytes 589828
  22.2 11.7 %copy-start.10 = (s32[512,2,2]{0,2,1:T(2,128)S(1)}, s32[512,2,2]{0,2,1:T(2,128)}, u32[]{:S(2)}) copy-start(s32[512,2,2]{0,2,1:T(2,128)} %param.20) | copy-start | bytes 24580
  22.2 12.3 %copy-start.11 = (f32[512,2,2]{0,2,1:T(2,128)S(1)}, f32[512,2,2]{0,2,1:T(2,128)}, u32[]{:S(2)}) copy-start(f32[512,2,2]{0,2,1:T(2,128)} %param.21) | copy-start | bytes 24580
  26.6 21.6 %copy-start.7 = (f32[3072]{0:T(1024)S(1)}, f32[3072]{0:T(1024)}, u32[]{:S(2)}) copy-start(f32[3072]{0:T(1024)} %param.19) | copy-start | bytes 36868
  26.6 2.4 %collective-permute-start.3 = (bf16[128,3072]{1,0:T(8,128)(2,1)S(1)}, bf16[128,3072]{1,0:T(8,128)(2,1)S(1)}, u32[]{:S(2)}, u32[]{:S(2)}) collective-permute-start(bf16[128,3072]{1,0:T(8,128)(2,1)S(1)} %get-tuple-element.13), channel_id=1, source_target_pairs={{0,1},{1,0},{2,3},{3,2},{4,5},{5,4},{6,7},{7,6},{8,9},{9,8},{10,11... | collective-permute-start | bytes 2359304 | tf_op jit(solution)/shard_map/ppermute | solution.py:20
  29.4 10.6 %collective-permute-start.4 = (bf16[32,3072]{1,0:T(8,128)(2,1)S(1)}, bf16[32,3072]{1,0:T(8,128)(2,1)S(1)}, u32[]{:S(2)}, u32[]{:S(2)}) collective-permute-start(bf16[32,3072]{1,0:T(8,128)(2,1)S(1)} %get-tuple-element.15), channel_id=1, source_target_pairs={{0,2},{1,3},{2,0},{3,1},{4,6},{5,7},{6,4},{7,5},{8,10},{9,11},{10,... | collective-permute-start | bytes 589832 | tf_op jit(solution)/shard_map/ppermute | solution.py:20
  31.0 17.1 %collective-permute-start.5 = (bf16[32,3072]{1,0:T(8,128)(2,1)S(1)}, bf16[32,3072]{1,0:T(8,128)(2,1)S(1)}, u32[]{:S(2)}, u32[]{:S(2)}) collective-permute-start(bf16[32,3072]{1,0:T(8,128)(2,1)S(1)} %get-tuple-element.16), channel_id=1, source_target_pairs={{0,4},{1,5},{2,6},{3,7},{4,0},{5,1},{6,2},{7,3},{8,12},{9,13},{10,... | collective-permute-start | bytes 589832 | tf_op jit(solution)/shard_map/ppermute | solution.py:20
  33.6 14.5 %collective-permute-start.6 = (bf16[32,3072]{1,0:T(8,128)(2,1)S(1)}, bf16[32,3072]{1,0:T(8,128)(2,1)S(1)}, u32[]{:S(2)}, u32[]{:S(2)}) collective-permute-start(bf16[32,3072]{1,0:T(8,128)(2,1)S(1)} %get-tuple-element.17), channel_id=1, source_target_pairs={{0,6},{1,7},{2,4},{3,5},{4,2},{5,3},{6,0},{7,1},{8,14},{9,15},{10,... | collective-permute-start | bytes 589832 | tf_op jit(solution)/shard_map/ppermute | solution.py:20
  48.4 22.2 %collective-permute-start.11 = (bf16[32,3072]{1,0:T(8,128)(2,1)S(1)}, bf16[32,3072]{1,0:T(8,128)(2,1)S(1)}, u32[]{:S(2)}, u32[]{:S(2)}) collective-permute-start(bf16[32,3072]{1,0:T(8,128)(2,1)S(1)} %get-tuple-element.21), channel_id=1, source_target_pairs={{0,6},{1,7},{2,4},{3,5},{4,2},{5,3},{6,0},{7,1},{8,14},{9,15},{10,... | collective-permute-start | bytes 589832 | tf_op jit(solution)/shard_map/ppermute | solution.py:20
  50.9 17.2 %collective-permute-start.10 = (bf16[32,3072]{1,0:T(8,128)(2,1)S(1)}, bf16[32,3072]{1,0:T(8,128)(2,1)S(1)}, u32[]{:S(2)}, u32[]{:S(2)}) collective-permute-start(bf16[32,3072]{1,0:T(8,128)(2,1)S(1)} %get-tuple-element.21), channel_id=1, source_target_pairs={{0,4},{1,5},{2,6},{3,7},{4,0},{5,1},{6,2},{7,3},{8,12},{9,13},{10,... | collective-permute-start | bytes 589832 | tf_op jit(solution)/shard_map/ppermute | solution.py:20
  55.8 6.8 %collective-permute-start.7 = (bf16[32,3072]{1,0:T(8,128)(2,1)S(1)}, bf16[32,3072]{1,0:T(8,128)(2,1)S(1)}, u32[]{:S(2)}, u32[]{:S(2)}) collective-permute-start(bf16[32,3072]{1,0:T(8,128)(2,1)S(1)} %get-tuple-element.21), channel_id=1, source_target_pairs={{0,2},{1,3},{2,0},{3,1},{4,6},{5,7},{6,4},{7,5},{8,10},{9,11},{10,... | collective-permute-start | bytes 589832 | tf_op jit(solution)/shard_map/ppermute | solution.py:20
  62.6 12.1 %collective-permute-start.20 = (bf16[64,3072]{1,0:T(8,128)(2,1)S(1)}, bf16[64,3072]{1,0:T(8,128)(2,1)S(1)}, u32[]{:S(2)}, u32[]{:S(2)}) collective-permute-start(bf16[64,3072]{1,0:T(8,128)(2,1)S(1)} %constant_dynamic-update-slice_fusion.refs_0_), channel_id=1, source_target_pairs={{0,8},{8,0},{16,24},{24,16},{1,9},{9,1},{17,25},{25,17},{2,10},{10... | collective-permute-start | bytes 1179656 | tf_op jit(solution)/shard_map/ppermute | solution.py:20
  65.1 9.6 %collective-permute-start.18 = (bf16[64,3072]{1,0:T(8,128)(2,1)S(1)}, bf16[64,3072]{1,0:T(8,128)(2,1)S(1)}, u32[]{:S(2)}, u32[]{:S(2)}) collective-permute-start(bf16[64,3072]{1,0:T(8,128)(2,1)S(1)} %constant_dynamic-update-slice_fusion.refs_0_), channel_id=1, source_target_pairs={{0,1},{1,0},{2,3},{3,2},{4,5},{5,4},{6,7},{7,6},{8,9},{9,8},{10,11... | collective-permute-start | bytes 1179656 | tf_op jit(solution)/shard_map/ppermute | solution.py:20
  65.1 19.8 %collective-permute-start.14 = (bf16[64,3072]{1,0:T(8,128)(2,1)S(1)}, bf16[64,3072]{1,0:T(8,128)(2,1)S(1)}, u32[]{:S(2)}, u32[]{:S(2)}) collective-permute-start(bf16[64,3072]{1,0:T(8,128)(2,1)S(1)} %constant_dynamic-update-slice_fusion.refs_0_), channel_id=1, source_target_pairs={{0,24},{8,16},{16,8},{24,0},{1,25},{9,17},{17,9},{25,1},{2,26},{10... | collective-permute-start | bytes 1179656 | tf_op jit(solution)/shard_map/ppermute | solution.py:20
  68.1 20.8 %collective-permute-start.8 = (bf16[64,3072]{1,0:T(8,128)(2,1)S(1)}, bf16[64,3072]{1,0:T(8,128)(2,1)S(1)}, u32[]{:S(2)}, u32[]{:S(2)}) collective-permute-start(bf16[64,3072]{1,0:T(8,128)(2,1)S(1)} %constant_dynamic-update-slice_fusion.refs_0_), channel_id=1, source_target_pairs={{0,16},{8,24},{16,0},{24,8},{1,17},{9,25},{17,1},{25,9},{2,18},{10... | collective-permute-start | bytes 1179656 | tf_op jit(solution)/shard_map/ppermute | solution.py:20
  70.6 21.0 %collective-permute-start.22 = (bf16[64,3072]{1,0:T(8,128)(2,1)S(1)}, bf16[64,3072]{1,0:T(8,128)(2,1)S(1)}, u32[]{:S(2)}, u32[]{:S(2)}) collective-permute-start(bf16[64,3072]{1,0:T(8,128)(2,1)S(1)} %constant_dynamic-update-slice_fusion.2.refs_2_), channel_id=1, source_target_pairs={{0,8},{8,0},{16,24},{24,16},{1,9},{9,1},{17,25},{25,17},{2,10},{10... | collective-permute-start | bytes 1179656 | tf_op jit(solution)/shard_map/ppermute | solution.py:20
  74.7 17.9 %collective-permute-start.19 = (bf16[64,3072]{1,0:T(8,128)(2,1)S(1)}, bf16[64,3072]{1,0:T(8,128)(2,1)S(1)}, u32[]{:S(2)}, u32[]{:S(2)}) collective-permute-start(bf16[64,3072]{1,0:T(8,128)(2,1)S(1)} %constant_dynamic-update-slice_fusion.2.refs_2_), channel_id=1, source_target_pairs={{0,1},{1,0},{2,3},{3,2},{4,5},{5,4},{6,7},{7,6},{8,9},{9,8},{10,11... | collective-permute-start | bytes 1179656 | tf_op jit(solution)/shard_map/ppermute | solution.py:20
  74.7 23.5 %collective-permute-start.16 = (bf16[64,3072]{1,0:T(8,128)(2,1)S(1)}, bf16[64,3072]{1,0:T(8,128)(2,1)S(1)}, u32[]{:S(2)}, u32[]{:S(2)}) collective-permute-start(bf16[64,3072]{1,0:T(8,128)(2,1)S(1)} %constant_dynamic-update-slice_fusion.2.refs_2_), channel_id=1, source_target_pairs={{0,24},{8,16},{16,8},{24,0},{1,25},{9,17},{17,9},{25,1},{2,26},{10... | collective-permute-start | bytes 1179656 | tf_op jit(solution)/shard_map/ppermute | solution.py:20
  85.0 18.8 %collective-permute-start.12 = (bf16[64,3072]{1,0:T(8,128)(2,1)S(1)}, bf16[64,3072]{1,0:T(8,128)(2,1)S(1)}, u32[]{:S(2)}, u32[]{:S(2)}) collective-permute-start(bf16[64,3072]{1,0:T(8,128)(2,1)S(1)} %constant_dynamic-update-slice_fusion.2.refs_2_), channel_id=1, source_target_pairs={{0,16},{8,24},{16,0},{24,8},{1,17},{9,25},{17,1},{25,9},{2,18},{10... | collective-permute-start | bytes 1179656 | tf_op jit(solution)/shard_map/ppermute | solution.py:20
  88.9 14.8 %collective-permute-start.21 = (bf16[64,3072]{1,0:T(8,128)(2,1)S(1)}, bf16[64,3072]{1,0:T(8,128)(2,1)S(1)}, u32[]{:S(2)}, u32[]{:S(2)}) collective-permute-start(bf16[64,3072]{1,0:T(8,128)(2,1)S(1)} %collective-permute-done.20.refs_4_), channel_id=1, source_target_pairs={{0,1},{1,0},{2,3},{3,2},{4,5},{5,4},{6,7},{7,6},{8,9},{9,8},{10,11... | collective-permute-start | bytes 1179656 | tf_op jit(solution)/shard_map/ppermute | solution.py:20
  91.6 12.7 %collective-permute-start.23 = (bf16[64,3072]{1,0:T(8,128)(2,1)S(1)}, bf16[64,3072]{1,0:T(8,128)(2,1)S(1)}, u32[]{:S(2)}, u32[]{:S(2)}) collective-permute-start(bf16[64,3072]{1,0:T(8,128)(2,1)S(1)} %collective-permute-done.22.refs_6_), channel_id=1, source_target_pairs={{0,1},{1,0},{2,3},{3,2},{4,5},{5,4},{6,7},{7,6},{8,9},{9,8},{10,11... | collective-permute-start | bytes 1179656 | tf_op jit(solution)/shard_map/ppermute | solution.py:20
  92.7 21.4 %collective-permute-start.15 = (bf16[64,3072]{1,0:T(8,128)(2,1)S(1)}, bf16[64,3072]{1,0:T(8,128)(2,1)S(1)}, u32[]{:S(2)}, u32[]{:S(2)}) collective-permute-start(bf16[64,3072]{1,0:T(8,128)(2,1)S(1)} %collective-permute-done.14.refs_4_), channel_id=1, source_target_pairs={{0,1},{1,0},{2,3},{3,2},{4,5},{5,4},{6,7},{7,6},{8,9},{9,8},{10,11... | collective-permute-start | bytes 1179656 | tf_op jit(solution)/shard_map/ppermute | solution.py:20
  98.3 15.8 %collective-permute-start.9 = (bf16[64,3072]{1,0:T(8,128)(2,1)S(1)}, bf16[64,3072]{1,0:T(8,128)(2,1)S(1)}, u32[]{:S(2)}, u32[]{:S(2)}) collective-permute-start(bf16[64,3072]{1,0:T(8,128)(2,1)S(1)} %collective-permute-done.8.refs_0_), channel_id=1, source_target_pairs={{0,1},{1,0},{2,3},{3,2},{4,5},{5,4},{6,7},{7,6},{8,9},{9,8},{10,11... | collective-permute-start | bytes 1179656 | tf_op jit(solution)/shard_map/ppermute | solution.py:20
  103.7 10.3 %collective-permute-start.17 = (bf16[64,3072]{1,0:T(8,128)(2,1)S(1)}, bf16[64,3072]{1,0:T(8,128)(2,1)S(1)}, u32[]{:S(2)}, u32[]{:S(2)}) collective-permute-start(bf16[64,3072]{1,0:T(8,128)(2,1)S(1)} %collective-permute-done.16.refs_6_), channel_id=1, source_target_pairs={{0,1},{1,0},{2,3},{3,2},{4,5},{5,4},{6,7},{7,6},{8,9},{9,8},{10,11... | collective-permute-start | bytes 1179656 | tf_op jit(solution)/shard_map/ppermute | solution.py:20
  103.7 10.4 %collective-permute-start.13 = (bf16[64,3072]{1,0:T(8,128)(2,1)S(1)}, bf16[64,3072]{1,0:T(8,128)(2,1)S(1)}, u32[]{:S(2)}, u32[]{:S(2)}) collective-permute-start(bf16[64,3072]{1,0:T(8,128)(2,1)S(1)} %collective-permute-done.12.refs_2_), channel_id=1, source_target_pairs={{0,1},{1,0},{2,3},{3,2},{4,5},{5,4},{6,7},{7,6},{8,9},{9,8},{10,11... | collective-permute-start | bytes 1179656 | tf_op jit(solution)/shard_map/ppermute | solution.py:20
  (4 other events, 3.0 us)

commit v2 on v1

v2 whole, which is shorter than its diff:
```python
import functools

import jax
import jax.numpy as jnp
from jax import lax
from jax.experimental import pallas as pl
from jax.experimental.pallas import tpu as pltpu
from jax.sharding import PartitionSpec as P

BF, F32 = jnp.bfloat16, jnp.float32
PRECISE = lax.Precision.HIGHEST
VMEM_BYTES = 16 * 1024 * 1024
NT = (((1,), (1,)), ((), ()))
TN = (((0,), (0,)), ((), ()))


def in_hbm(*arrays):
    return [pltpu.with_memory_space_constraint(array, pltpu.HBM) for array in arrays]


def in_vmem(*arrays):
    return [pltpu.with_memory_space_constraint(array, pltpu.VMEM) for array in arrays]


def swap(block, axis, distance, forward_only=False):
    devices = range(lax.axis_size(axis))
    route = [(i, i ^ distance) for i in devices if not forward_only or i < i ^ distance]
    return lax.ppermute(block, axis, route)


def mm(a, b, dims=(((1,), (0,)), ((), ()))):
    return lax.dot_general(a, b, dims, preferred_element_type=F32)


def halves(x):
    high = x.astype(BF)
    return high, (x - high.astype(F32)).astype(BF)


def thirds(x):
    high, rest = x.astype(BF), None
    rest = x - high.astype(F32)
    middle = rest.astype(BF)
    return high, middle, (rest - middle.astype(F32)).astype(BF)


def lower_triangle(size):
    return (
        lax.broadcasted_iota(jnp.int32, (size, size), 0) >= lax.broadcasted_iota(jnp.int32, (size, size), 1)
    )


def running_columns(log_decay):
    tri = lower_triangle(log_decay.shape[1]).astype(F32)
    return lax.dot_general(tri, log_decay, NT, precision=PRECISE, preferred_element_type=F32)


def running_rows(log_decay):
    tri = lower_triangle(log_decay.shape[1]).astype(F32)
    return lax.dot_general(log_decay, tri, NT, precision=PRECISE, preferred_element_type=F32)


def state_kernel(k_hbm, v_hbm, decay_hbm, *refs):
    out_refs, (k_ref, v_ref, decay_ref, sems) = refs[:-4], refs[-4:]
    copies = [
        pltpu.make_async_copy(source, to, sems.at[n])
        for n, (source, to) in enumerate(((decay_hbm, decay_ref), (k_hbm, k_ref), (v_hbm, v_ref)))
    ]
    for copy in copies:
        copy.start()
    for copy in copies:
        copy.wait()
    seqs, heads, size = decay_ref.shape
    width = k_ref.shape[2] // heads
    group = seqs // len(out_refs)
    for g, out_ref in enumerate(out_refs):
        totals = []
        for b in range(group):
            log_decay = decay_ref[g * group + b]
            columns = running_columns(log_decay)
            tail = jnp.exp(columns[size - 1 : size, :] - columns)
            totals.append(jnp.broadcast_to(running_rows(log_decay)[:, size - 1 : size], (heads, width)))
            for h in range(heads):
                part = slice(h * width, (h + 1) * width)
                value = v_ref[g * group + b, :, part]
                high, low = halves(k_ref[g * group + b, :, part].astype(F32) * tail[:, h : h + 1])
                at = (b * heads + h) * width
                out_ref[at : at + width, :] = (mm(high, value, TN) + mm(low, value, TN)).astype(BF)
        total = jnp.concatenate(totals, axis=0)
        pieces = [piece.astype(F32) for piece in thirds(total)]
        pieces.append(jnp.zeros_like(total))
        out_ref[group * heads * width :, :] = jnp.concatenate(pieces, axis=0).astype(BF)


def inner_kernel(q_hbm, k_hbm, v_hbm, decay_hbm, proj_hbm, residual_hbm, out_ref, q_ref, proj_ref, rows_ref, *scratch):
    k_ref, v_ref, decay_ref, residual_ref, sems = scratch
    pairs = (
        (decay_hbm, decay_ref),
        (q_hbm, q_ref),
        (k_hbm, k_ref),
        (v_hbm, v_ref),
        (residual_hbm, residual_ref),
        (proj_hbm, proj_ref),
    )
    copies = [pltpu.make_async_copy(source, to, sems.at[n]) for n, (source, to) in enumerate(pairs)]
    for copy in copies:
        copy.start()
    for copy in copies[:-1]:
        copy.wait()
    own, seqs, _ = residual_ref.shape
    for b in range(seqs):
        rows_ref[b * own : (b + 1) * own, :] = residual_ref[:, b, :].astype(F32)
    _, heads, size = decay_ref.shape
    width = k_ref.shape[2] // heads
    causal = lower_triangle(size)
    for b in range(seqs):
        columns = running_columns(decay_ref[b])
        rows = running_rows(decay_ref[b])
        for h in range(heads):
            part = slice(h * width, (h + 1) * width)
            spread = columns[:, h : h + 1] - rows[h : h + 1, :]
            decay = jnp.where(causal, jnp.exp(jnp.where(causal, spread, 0.0)), 0.0)
            scores = mm(q_ref[b, :, part], k_ref[b, :, part], NT) * decay
            high, low = halves(scores)
            value = v_ref[b, :, part]
            out_ref[b, :, part] = mm(high, value) + mm(low, value)
    copies[-1].wait()


def project_kernel(count, line, *refs):
    q_ref, inner_ref, decay_ref, gain_ref = refs[:4]
    states = refs[4 : 3 + count]
    proj_ref, own_ref, partner_ref = refs[3 + count :]
    seqs, size, feat = q_ref.shape
    heads = decay_ref.shape[1]
    width = feat // heads
    me = lax.axis_index("seq")
    index = lax.axis_index("exp")
    each = seqs * heads
    base = each * width
    totals = []
    for state in states:
        three = state[base : base + 4 * each, :].astype(F32)
        totals.append(three[:each] + three[each : 2 * each] + three[2 * each : 3 * each])
    factors = []
    for first in range(1, count):
        later = jnp.zeros_like(totals[0])
        for second in range(1, count):
            between = ((me ^ first) < (me ^ second)) & ((me ^ second) < me)
            later = later + jnp.where(between, totals[second - 1], 0.0)
        factors.append(jnp.where((me ^ first) < me, jnp.exp(later), 0.0))
    rows = []
    for b in range(seqs):
        grown = jnp.exp(running_columns(decay_ref[b]))
        parts = []
        for h in range(heads):
            part = slice(h * width, (h + 1) * width)
            n = b * heads + h
            incoming = jnp.zeros((width, width), F32)
            for state, factor in zip(states, factors):
                incoming = incoming + factor[n : n + 1, :] * state[n * width : (n + 1) * width, :].astype(F32)
            high, low = halves(incoming)
            query = q_ref[b, :, part]
            raw = inner_ref[b, :, part] + grown[:, h : h + 1] * (mm(query, high) + mm(query, low))
            meansq = jnp.mean(raw * raw, axis=-1, keepdims=True)
            parts.append((raw * lax.rsqrt(meansq + 1e-06) * gain_ref[:, part]).astype(BF))
        rows.append(jnp.concatenate(parts, axis=1))
    attention = jnp.concatenate(rows, axis=0)
    total = seqs * size
    own = size // (2 * line)
    to = lax.broadcasted_iota(jnp.int32, (total, total), 0)
    source = source_position(to // (total // 2), (to // (seqs * own)) % line, to % own, index, own)
    source = source + size * ((to // own) % seqs)
    pick = (source == lax.broadcasted_iota(jnp.int32, (total, total), 1)).astype(BF)
    attention = mm(pick, attention).astype(BF)
    model = proj_ref.shape[1]
    tile = column_tile(model)
    for n in range(model // tile):
        columns = slice(n * tile, (n + 1) * tile)
        product = mm(attention, proj_ref[:, columns])
        own_ref[:, columns] = product[: total // 2, :]
        partner_ref[:, columns] = product[total // 2 :, :].astype(BF)


def column_tile(model):
    return max(t for t in range(128, 1025, 128) if model % t == 0)


def source_position(flip, distance, place, index, own):
    return own * (2 * ((index // 2) ^ distance) + ((index % 2) ^ flip)) + place


def fold_kernel(kept_ref, got_ref, keep_ref, *send_refs):
    rows = keep_ref.shape[0]
    keep_ref[...] = kept_ref[:rows, :] + got_ref[:rows, :].astype(F32)
    for d, send_ref in enumerate(send_refs, start=1):
        part = slice(d * rows, (d + 1) * rows)
        send_ref[...] = (kept_ref[part, :] + got_ref[part, :].astype(F32)).astype(BF)


def mix_kernel(kept_ref, residual_ref, gain_ref, *refs):
    mixed_ref, normed_ref = refs[-2:]
    mixed = residual_ref[...] + kept_ref[...]
    for got_ref in refs[:-2]:
        mixed = mixed + got_ref[...].astype(F32)
    mixed_ref[...] = mixed
    meansq = jnp.mean(mixed * mixed, axis=-1, keepdims=True)
    normed_ref[...] = (mixed * lax.rsqrt(meansq + 1e-06) * gain_ref[...]).astype(BF)


def place_kernel(mixed_ref, out_ref):
    own, seqs, _ = out_ref.shape
    for b in range(seqs):
        out_ref[:, b, :] = mixed_ref[b * own : (b + 1) * own, :]


def load_kernel(gate_hbm, up_hbm, after, gate_ref, up_ref, sems):
    parts = sems.shape[1]
    rows = gate_ref.shape[1] // parts
    copies = []
    for m, (source, to) in enumerate(((gate_hbm, gate_ref), (up_hbm, up_ref))):
        for n in range(parts):
            part = pl.ds(n * rows, rows)
            copies.append(pltpu.make_async_copy(source.at[0, part], to.at[0, part], sems.at[m, n]))
            copies[-1].start()
    for copy in copies:
        copy.wait()


def gather_kernel(first, second, *refs):
    for to, sources in zip(refs[-2:], (refs[:first], refs[first : first + second])):
        at = 0
        for source in sources:
            to[at : at + source.shape[0], :] = source[...]
            at += source.shape[0]


def halves_kernel(one_ref, two_ref, after, low_ref, high_ref):
    half = low_ref.shape[0]
    low_ref[...] = one_ref[:half, :]
    high_ref[...] = two_ref[half:, :]


def exchanged(block, count, after):
    if count != 4 or block.shape[0] % 32 != 0:
        return [[swap(block, "seq", d)] for d in range(1, count)]
    half = block.shape[0] // 2
    one, two = swap(block, "seq", 1), swap(block, "seq", 2)
    vmem, anywhere = pl.BlockSpec(memory_space=pltpu.VMEM), pl.BlockSpec(memory_space=pl.ANY)
    low, high = pl.pallas_call(
        halves_kernel,
        in_specs=[vmem] * 2 + [anywhere],
        out_specs=[vmem] * 2,
        out_shape=[jax.ShapeDtypeStruct((half, block.shape[1]), block.dtype)] * 2,
        compiler_params=params(VMEM_BYTES // 8),
        cost_estimate=cost(1, 4 * block.size),
        name="halves",
    )(one, two, after)
    one, two, low, high = lax.optimization_barrier((one, two, low, high))
    return [[one], [two], [swap(low, "seq", 2), swap(high, "seq", 1)]]


def route_kernel(capacity, own, routes_ref, weights_ref, slot_ref, weight_ref, a_ref, b_ref):
    seqs, tops, _ = routes_ref.shape
    count, total = slot_ref.shape
    size = total // seqs
    me = lax.axis_index("seq")
    index = lax.axis_index("exp")
    line = size // (2 * own)
    lines, shares = [], []
    for c in range(count):
        part = slice(c * size, (c + 1) * size)
        hit, share = [], []
        for b in range(seqs):
            hits = [routes_ref[b, k : k + 1, part] == index for k in range(tops)]
            hit.append(sum(jnp.where(one, 1.0, 0.0) for one in hits))
            share.append(sum(jnp.where(one, weights_ref[b, k : k + 1, part], 0.0) for k, one in enumerate(hits)))
        lines.append(jnp.concatenate(hit, axis=1))
        shares.append(jnp.concatenate(share, axis=1))
    chosen = jnp.concatenate(lines, axis=0).astype(BF)
    weight = jnp.concatenate(shares, axis=0)
    to = lax.broadcasted_iota(jnp.int32, (total, total), 1)
    row = source_position(to // (total // 2), (to // (seqs * own)) % line, to % own, index, own) * seqs
    row = row + (to // own) % seqs
    origin = lax.broadcasted_iota(jnp.int32, (total, total), 0)
    origin = (origin % size) * seqs + origin // size
    rank = mm(chosen, (origin <= row).astype(BF)) - 1.0
    same = (origin == row).astype(BF)
    picked = mm(chosen, same) > 0.5
    block = lax.broadcasted_iota(jnp.int32, (count, total), 0) % (count // 2)
    a_ref[...] = jnp.where(picked, rank.astype(jnp.int32) + block * capacity, -1)
    high, middle, low = thirds(weight)
    b_ref[...] = mm(high, same) + mm(middle, same) + mm(low, same)
    for d in range(count):
        slot_ref[d : d + 1, :] = a_ref[pl.ds(me ^ d, 1), :]
        weight_ref[d : d + 1, :] = b_ref[pl.ds(me ^ d, 1), :]


def expert_kernel(plan, arrays, later, slot_ref, weight_ref, gate_ref, up_ref, *refs):
    array_refs, (out_hbm, rows_ref, out_ref, sems) = refs[:arrays], refs[-4:]
    count, total = slot_ref.shape
    blocks = count // 2
    first_block = later * blocks
    slots, width = rows_ref.shape
    tile = out_ref.shape[1]
    numbers = lax.broadcasted_iota(jnp.int32, (slots, total), 0)
    lines = range(first_block, first_block + blocks)
    pick = jnp.concatenate([(slot_ref[n : n + 1, :] == numbers).astype(BF) for n in lines], axis=1)
    weight = jnp.concatenate([weight_ref[n : n + 1, :] for n in lines], axis=1)
    parts = [part.astype(F32) for part in thirds(weight)] + [jnp.zeros((5, blocks * total), F32)]
    scale = jnp.sum(mm(jnp.concatenate(parts, axis=0).astype(BF), pick, NT), axis=0, keepdims=True)

    step = column_tile(width)
    for n in range(width // step):
        part = slice(n * step, (n + 1) * step)
        rows = [array_refs[number][first : first + height, part] for number, first, height in plan]
        rows_ref[:, part] = mm(pick, jnp.concatenate(rows, axis=0)).astype(BF)
    side = (lax.axis_index("seq") // blocks) ^ later
    columns = pl.ds(pl.multiple_of(side * slots, slots), slots)
    copies = []
    for step in range(out_ref.shape[0]):
        part = slice(step * tile, (step + 1) * tile)
        gate = mm(gate_ref[0, part, :], rows_ref[...], NT)
        up = mm(up_ref[0, part, :], rows_ref[...], NT)
        out_ref[step] = scale * (gate / (1.0 + jnp.exp(-gate))) * up
        copies.append(pltpu.make_async_copy(out_ref.at[step], out_hbm.at[0, part, columns], sems.at[step]))
        copies[-1].start()
    for copy in copies:
        copy.wait()


def params(vmem=VMEM_BYTES):
    return pltpu.CompilerParams(vmem_limit_bytes=vmem)


def cost(flops, bytes_accessed, transcendentals=0):
    return pl.CostEstimate(flops=int(flops), bytes_accessed=int(bytes_accessed), transcendentals=int(transcendentals))


def whole(shape):
    return pl.BlockSpec(shape, lambda *_: (0,) * len(shape))


def expert_half(later, slot, weight, w_gate, w_up, plan, arrays, previous, slots):
    units, width = w_gate.shape[1:]
    tile = max(size for size in range(16, 385, 16) if units % size == 0)
    steps = units // tile
    carried = [] if previous is None else [previous]
    vmem, hbm = pl.BlockSpec(memory_space=pltpu.VMEM), pl.BlockSpec(memory_space=pltpu.HBM)
    return pl.pallas_call(
        functools.partial(expert_kernel, plan, len(arrays), later),
        in_specs=[vmem] * (4 + len(arrays)) + [hbm] * len(carried),
        out_specs=hbm,
        out_shape=jax.ShapeDtypeStruct((1, units, 2 * slots), F32),
        scratch_shapes=[
            pltpu.VMEM((slots, width), BF),
            pltpu.VMEM((steps, tile, slots), F32),
            pltpu.SemaphoreType.DMA((steps,)),
        ],
        input_output_aliases={4 + len(arrays): 0} if carried else {},
        compiler_params=params(),
        cost_estimate=cost(4 * units * width * slots, 2 * slots * width),
        name="experts",
    )(slot, weight, *in_vmem(w_gate, w_up), *arrays, *carried)


def per_device(
    residual,
    queries,
    key_vecs,
    value_vecs,
    log_decay,
    head_gain,
    out_proj,
    norm_gain,
    routes,
    route_weight,
    w_gate,
    w_up,
):
    count, owners = lax.axis_size("seq"), lax.axis_size("exp")
    line = owners // 2
    me = lax.axis_index("seq")
    seqs, size, feat = queries.shape
    heads = log_decay.shape[1]
    width = feat // heads
    own, _, model = residual.shape
    unit = own * seqs
    total = size * seqs
    capacity = 8 * size // owners

    vmem, hbm, anywhere = (pl.BlockSpec(memory_space=space) for space in (pltpu.VMEM, pltpu.HBM, pl.ANY))

    states = pl.pallas_call(
        state_kernel,
        in_specs=[hbm] * 3,
        out_shape=jax.ShapeDtypeStruct((seqs * heads * (width + 4), width), BF),
        scratch_shapes=[
            pltpu.VMEM(key_vecs.shape, BF),
            pltpu.VMEM(value_vecs.shape, BF),
            pltpu.VMEM(log_decay.shape, F32),
            pltpu.SemaphoreType.DMA((3,)),
        ],
        compiler_params=params(),
        cost_estimate=cost(4 * total * feat * width, 6 * total * feat),
        name="states",
    )(*in_hbm(key_vecs, value_vecs, log_decay))
    arrived = [swap(states, "seq", d, forward_only=True) for d in range(1, count)]

    inner, query, proj, residual_rows = pl.pallas_call(
        inner_kernel,
        in_specs=[hbm] * 6,
        out_specs=[vmem] * 4,
        out_shape=[
            pltpu.VMEM((seqs, size, feat), F32),
            pltpu.VMEM(queries.shape, BF),
            pltpu.VMEM(out_proj.shape, BF),
            pltpu.VMEM((unit, model), F32),
        ],
        scratch_shapes=[
            pltpu.VMEM(key_vecs.shape, BF),
            pltpu.VMEM(value_vecs.shape, BF),
            pltpu.VMEM(log_decay.shape, F32),
            pltpu.VMEM(residual.shape, BF),
            pltpu.SemaphoreType.DMA((6,)),
        ],
        compiler_params=params(),
        cost_estimate=cost(6 * total * feat * size, 10 * total * feat),
        name="inner",
    )(*in_hbm(queries, key_vecs, value_vecs, log_decay, out_proj, residual))

    own_sum, partner_sum = pl.pallas_call(
        functools.partial(project_kernel, count, line),
        in_specs=[vmem] * (5 + count - 1),
        out_specs=[vmem] * 2,
        out_shape=[jax.ShapeDtypeStruct((total // 2, model), F32), jax.ShapeDtypeStruct((total // 2, model), BF)],
        compiler_params=params(),
        cost_estimate=cost(2 * total * feat * model, 2 * feat * model + 3 * total * model),
        name="project",
    )(*in_vmem(query, inner), log_decay, head_gain.reshape(1, feat), *arrived, *in_vmem(proj))

    tile = column_tile(model)

    def column_blocks(count):
        return pl.BlockSpec((count, tile), lambda i: (0, i))

    keep, *sends = pl.pallas_call(
        fold_kernel,
        grid=(model // tile,),
        in_specs=[column_blocks(total // 2)] * 2,
        out_specs=[column_blocks(unit)] * line,
        out_shape=[jax.ShapeDtypeStruct((unit, model), F32)]
        + [jax.ShapeDtypeStruct((unit, model), BF)] * (line - 1),
        compiler_params=params(),
        cost_estimate=cost(total * model, 4 * total * model),
        name="fold",
    )(own_sum, swap(partner_sum, "exp", 1))
    got = [swap(send, "exp", 2 * d) for d, send in enumerate(sends, start=1)]

    routes, route_weight, keep = lax.optimization_barrier((routes, route_weight, keep))
    slot, weight = pl.pallas_call(
        functools.partial(route_kernel, capacity, own),
        out_shape=[jax.ShapeDtypeStruct((count, total), jnp.int32), jax.ShapeDtypeStruct((count, total), F32)],
        scratch_shapes=[pltpu.VMEM((count, total), jnp.int32), pltpu.VMEM((count, total), F32)],
        compiler_params=params(),
        cost_estimate=cost(10 * count * total * total, 16 * count * total),
        name="route",
    )(jnp.transpose(routes, (1, 2, 0)), jnp.transpose(route_weight, (1, 2, 0)))

    keep, slot, weight = lax.optimization_barrier((keep, slot, weight))
    mixed, normed = pl.pallas_call(
        mix_kernel,
        out_shape=[jax.ShapeDtypeStruct((unit, model), F32), jax.ShapeDtypeStruct((unit, model), BF)],
        compiler_params=params(),
        cost_estimate=cost(10 * unit * model, 16 * unit * model),
        name="mix",
    )(keep, residual_rows, norm_gain.reshape(1, model), *got)
    attn_out = pl.pallas_call(
        place_kernel,
        out_shape=jax.ShapeDtypeStruct((own, seqs, model), F32),
        compiler_params=params(VMEM_BYTES // 8),
        cost_estimate=cost(1, 8 * unit * model),
        name="place",
    )(mixed)

    along = [swap(normed, "exp", 2 * d) for d in range(1, line)]
    across = [normed] + [swap(normed, "seq", d) for d in range(1, count)]
    rows = [len(arrays) * unit for arrays in (across, along)]
    near, rest = pl.pallas_call(
        functools.partial(gather_kernel, count, line - 1),
        in_specs=[vmem] * (count + line - 1) + [anywhere],
        out_specs=[vmem] * 2,
        out_shape=[jax.ShapeDtypeStruct((n, model), BF) for n in rows],
        compiler_params=params(VMEM_BYTES // 8),
        cost_estimate=cost(1, 4 * sum(rows) * model),
        name="gather",
    )(*across, *along, *in_hbm(attn_out))
    gate, up = pl.pallas_call(
        load_kernel,
        in_specs=[hbm, hbm, anywhere],
        out_specs=[vmem] * 2,
        out_shape=[pltpu.VMEM(w_gate.shape, BF), pltpu.VMEM(w_up.shape, BF)],
        scratch_shapes=[pltpu.SemaphoreType.DMA((2, 4))],
        compiler_params=params(VMEM_BYTES // 8),
        cost_estimate=cost(1, 4 * w_gate.size),
        name="load",
    )(*in_hbm(w_gate, w_up), rest)
    rests = [[rest]] + exchanged(rest, count, *in_vmem(gate))
    half = count // 2
    slots = half * capacity

    def planned(first, parts):
        plan, arrays = [], [near, near_partner]
        for n, pieces in enumerate(parts):
            partners = [swap(piece, "exp", 1) for piece in pieces]
            for k, share in enumerate((pieces, partners)):
                plan.append((k, (first + n) * unit, unit))
                for piece in share:
                    plan.append((len(arrays), 0, piece.shape[0]))
                    arrays.append(piece)
        return plan, arrays

    near_partner = swap(near, "exp", 1)
    plan, arrays = planned(0, rests[:half])
    hidden = expert_half(0, slot, weight, gate, up, plan, arrays, None, slots)
    late = [len(pieces) for pieces in rests[half:]]
    *pieces, hidden = lax.optimization_barrier((*(piece for part in rests[half:] for piece in part), hidden))
    pieces = iter(pieces)
    plan, arrays = planned(half, [[next(pieces) for _ in range(n)] for n in late])
    hidden = expert_half(1, slot, weight, gate, up, plan, arrays, hidden, slots)
    return (attn_out, hidden)


def solution(mesh):
    placed = (
        P(("seq", "exp"), None, None),
        P(None, "seq", "exp"),
        P(None, "seq", "exp"),
        P(None, "seq", "exp"),
        P(None, "exp", "seq"),
        P("exp"),
        P("exp", None),
        P(),
        P(),
        P(),
        P("exp", "seq", None),
        P("exp", "seq", None),
    )
    return jax.shard_map(
        per_device,
        mesh=mesh,
        in_specs=placed,
        out_specs=(P(("seq", "exp"), None, None), P("exp", "seq", None)),
        check_vma=False,
    )
```

time: 124 us -> 99 us (0.80)
  waiting for transfers between devices: 53 us -> 40.2 us
  local copies, waits for them, and re-layouts: 9 us -> 0.02 us
  Pallas kernels: 27.2 us -> 24.7 us
    ppermute x24 -> x23, waiting for transfers between devices: 53 us -> 40.2 us  [swap(): return lax.ppermute(block, axis, route)]
    unnamed x28 -> x10, local copies, waits for them, and re-layouts: 7.28 us -> 0.02 us
    pallas_call x7 -> x11, Pallas kernels: 27 us -> 24.5 us  [the longest x2 11.2 us: expert_half(): pl.pallas_call(functools.partial(expert_kernel, plan, len(arrays), later)...]
    reshape x3 -> x0, local copies, waits for them, and re-layouts: 1.64 us -> none  [the longest x1 1.05 us: per_device(): mixed_rows = jnp.transpose(mixed.reshape(seqs, own, model), (1, 0, 2))]
    ppermute x24 -> x23, starting transfers between devices: 33.9 us -> 32.8 us  [swap(): return lax.ppermute(block, axis, route)]
  transfers between devices with their start and end apart: 24 -> 23, of which waited for: 13 -> 13; matrix products, arithmetic and copies ran while one was open for 2% -> 0% of each run, Pallas kernels for 9% -> 15%
where the time goes in v2:
time: 99 us; the launch traced here: 98.7 us
  waiting for transfers between devices  40.2 us (41%)
  starting transfers between devices  32.8 us (33%)
  Pallas kernels  24.7 us (25%)
    ppermute x23, waiting for transfers between devices, swap(): return lax.ppermute(block, axis, route)  40.2 us
    ppermute x23, starting transfers between devices, swap(): return lax.ppermute(block, axis, route)  32.8 us
    pallas_call x2, Pallas kernels, expert_half(): pl.pallas_call(functools.partial(expert_kernel, plan, len(arrays), later)...  11.2 us
    pallas_call x1, Pallas kernels, per_device(): pl.pallas_call(load_kernel, in_specs=[hbm, hbm, anywhere], out_specs=[vme...  5.15 us
    pallas_call x1, Pallas kernels, per_device(): pl.pallas_call(inner_kernel, in_specs=[hbm] * 6, out_specs=[vmem] * 4, ou...  2.71 us
    pallas_call x1, Pallas kernels, per_device(): pl.pallas_call(state_kernel, in_specs=[hbm] * 3, out_shape=jax.ShapeDtype...  1.98 us
  transfers between devices with their start and end apart: 23, of which 13 were waited for; matrix products, arithmetic and copies ran while one was open for 0% of the time, Pallas kernels for 15%

profile of v2, /device:TPU:0, one launch (start us, length us, event | category | flops | bytes accessed | tf_op | source)
XLA Modules:
  0.0 98.7 jit_solution(10927451379709681054)
XLA Ops:
  0.7 2.0 %states.1 = bf16[1056,128]{1,0:T(8,128)(2,1)S(1)} custom-call(bf16[2,128,512]{2,1,0:T(8,128)(2,1)} %k_hbm.3, bf16[2,128,512]{2,1,0:T(8,128)(2,1)} %v_hbm.3, f32[2,4,128]{2,1,0:T(4,128)} %refs_2_.1), custom_call_target="tpu_custom_call" | custom-call | flops 67108864 | bytes 786432 | tf_op jit(solution)/shard_map/states/pallas_call | solution.py:394
  2.6 5.8 %collective-permute-start.2 = (bf16[1056,128]{1,0:T(8,128)(2,1)S(1)}, bf16[1056,128]{1,0:T(8,128)(2,1)S(1)}, u32[]{:S(2)}, u32[]{:S(2)}) collective-permute-start(bf16[1056,128]{1,0:T(8,128)(2,1)S(1)} %states.1), channel_id=1, source_target_pairs={{0,24},{8,16},{1,25},{9,17},{2,26},{10,18},{3,27},{11,19},{4,28},{... | collective-permute-start | bytes 811016 | tf_op jit(solution)/shard_map/ppermute | solution.py:28
  8.5 1.3 %collective-permute-start.1 = (bf16[1056,128]{1,0:T(8,128)(2,1)S(1)}, bf16[1056,128]{1,0:T(8,128)(2,1)S(1)}, u32[]{:S(2)}, u32[]{:S(2)}) collective-permute-start(bf16[1056,128]{1,0:T(8,128)(2,1)S(1)} %states.1), channel_id=1, source_target_pairs={{0,16},{8,24},{1,17},{9,25},{2,18},{10,26},{3,19},{11,27},{4,20},{... | collective-permute-start | bytes 811016 | tf_op jit(solution)/shard_map/ppermute | solution.py:28
  9.8 2.5 %collective-permute-start = (bf16[1056,128]{1,0:T(8,128)(2,1)S(1)}, bf16[1056,128]{1,0:T(8,128)(2,1)S(1)}, u32[]{:S(2)}, u32[]{:S(2)}) collective-permute-start(bf16[1056,128]{1,0:T(8,128)(2,1)S(1)} %states.1), channel_id=1, source_target_pairs={{0,8},{16,24},{1,9},{17,25},{2,10},{18,26},{3,11},{19,27},{4,12},{... | collective-permute-start | bytes 811016 | tf_op jit(solution)/shard_map/ppermute | solution.py:28
  12.3 2.7 %inner.1 = (f32[2,128,512]{2,1,0:T(8,128)S(1)}, bf16[2,128,512]{2,1,0:T(8,128)(2,1)S(1)}, bf16[512,3072]{1,0:T(8,128)(2,1)S(1)}, f32[32,3072]{1,0:T(8,128)S(1)}) custom-call(bf16[2,128,512]{2,1,0:T(8,128)(2,1)} %q_hbm.1, bf16[2,128,512]{2,1,0:T(8,128)(2,1)} %k_hbm.3, bf16[2,128,512]{2,1,0:T(8,128)(2,1)} %v_hbm.3, f32[2,4,128]{2,1,0:T(4,128)} %refs_2_.1, ...), custom_call_target="tpu_custom_call" | custom-call | flops 100663296 | bytes 1310720 | tf_op jit(solution)/shard_map/inner/pallas_call | solution.py:410
  15.4 4.6 %collective-permute-done.1.refs_5_ = bf16[1056,128]{1,0:T(8,128)(2,1)S(1)} collective-permute-done((bf16[1056,128]{1,0:T(8,128)(2,1)S(1)}, bf16[1056,128]{1,0:T(8,128)(2,1)S(1)}, u32[]{:S(2)}, u32[]{:S(2)}) %collective-permute-start.1) | collective-permute-done | bytes 270368 | tf_op jit(solution)/shard_map/ppermute | solution.py:28
  20.0 1.8 %project.1 = (f32[128,3072]{1,0:T(8,128)S(1)}, bf16[128,3072]{1,0:T(8,128)(2,1)S(1)}) custom-call(bf16[2,128,512]{2,1,0:T(8,128)(2,1)S(1)} %get-tuple-element.36.refs_0_, f32[2,128,512]{2,1,0:T(8,128)S(1)} %get-tuple-element.37.refs_1_, f32[2,4,128]{2,1,0:T(4,128)S(1)} %copy-done, f32[1,512]{1,0:T(1,128)S(1)} %bitcast.7, ...), custom_call_target="tpu_custom_call" | custom-call | flops 805306368 | bytes 5505024 | tf_op jit(solution)/shard_map/project/pallas_call | solution.py:432
  21.9 2.3 %collective-permute-done.3.got_ref = bf16[128,3072]{1,0:T(8,128)(2,1)S(1)} collective-permute-done((bf16[128,3072]{1,0:T(8,128)(2,1)S(1)}, bf16[128,3072]{1,0:T(8,128)(2,1)S(1)}, u32[]{:S(2)}, u32[]{:S(2)}) %collective-permute-start.3) | collective-permute-done | bytes 786464 | tf_op jit(solution)/shard_map/ppermute | solution.py:28
  24.2 0.4 fold.1
  24.6 1.6 %collective-permute-start.4 = (bf16[32,3072]{1,0:T(8,128)(2,1)S(1)}, bf16[32,3072]{1,0:T(8,128)(2,1)S(1)}, u32[]{:S(2)}, u32[]{:S(2)}) collective-permute-start(bf16[32,3072]{1,0:T(8,128)(2,1)S(1)} %get-tuple-element.49), channel_id=1, source_target_pairs={{0,2},{1,3},{2,0},{3,1},{4,6},{5,7},{6,4},{7,5},{8,10},{9,11},{10,... | collective-permute-start | bytes 589832 | tf_op jit(solution)/shard_map/ppermute | solution.py:28
  26.3 2.6 %collective-permute-start.5 = (bf16[32,3072]{1,0:T(8,128)(2,1)S(1)}, bf16[32,3072]{1,0:T(8,128)(2,1)S(1)}, u32[]{:S(2)}, u32[]{:S(2)}) collective-permute-start(bf16[32,3072]{1,0:T(8,128)(2,1)S(1)} %get-tuple-element.50), channel_id=1, source_target_pairs={{0,4},{1,5},{2,6},{3,7},{4,0},{5,1},{6,2},{7,3},{8,12},{9,13},{10,... | collective-permute-start | bytes 589832 | tf_op jit(solution)/shard_map/ppermute | solution.py:28
  29.3 5.9 %collective-permute-done.4.refs_0_ = bf16[32,3072]{1,0:T(8,128)(2,1)S(1)} collective-permute-done((bf16[32,3072]{1,0:T(8,128)(2,1)S(1)}, bf16[32,3072]{1,0:T(8,128)(2,1)S(1)}, u32[]{:S(2)}, u32[]{:S(2)}) %collective-permute-start.4) | collective-permute-done | bytes 196640 | tf_op jit(solution)/shard_map/ppermute | solution.py:28
  35.3 8.1 %collective-permute-done.5.refs_1_ = bf16[32,3072]{1,0:T(8,128)(2,1)S(1)} collective-permute-done((bf16[32,3072]{1,0:T(8,128)(2,1)S(1)}, bf16[32,3072]{1,0:T(8,128)(2,1)S(1)}, u32[]{:S(2)}, u32[]{:S(2)}) %collective-permute-start.5) | collective-permute-done | bytes 196640 | tf_op jit(solution)/shard_map/ppermute | solution.py:28
  43.6 2.5 %collective-permute-start.12 = (bf16[32,3072]{1,0:T(8,128)(2,1)S(1)}, bf16[32,3072]{1,0:T(8,128)(2,1)S(1)}, u32[]{:S(2)}, u32[]{:S(2)}) collective-permute-start(bf16[32,3072]{1,0:T(8,128)(2,1)S(1)} %get-tuple-element.55.refs_0_), channel_id=1, source_target_pairs={{0,6},{1,7},{2,4},{3,5},{4,2},{5,3},{6,0},{7,1},{8,14},{9,15},{10,... | collective-permute-start | bytes 589832 | tf_op jit(solution)/shard_map/ppermute | solution.py:28
  46.2 4.9 %collective-permute-start.11 = (bf16[32,3072]{1,0:T(8,128)(2,1)S(1)}, bf16[32,3072]{1,0:T(8,128)(2,1)S(1)}, u32[]{:S(2)}, u32[]{:S(2)}) collective-permute-start(bf16[32,3072]{1,0:T(8,128)(2,1)S(1)} %get-tuple-element.55.refs_0_), channel_id=1, source_target_pairs={{0,4},{1,5},{2,6},{3,7},{4,0},{5,1},{6,2},{7,3},{8,12},{9,13},{10,... | collective-permute-start | bytes 589832 | tf_op jit(solution)/shard_map/ppermute | solution.py:28
  51.2 3.4 %collective-permute-start.9 = (bf16[32,3072]{1,0:T(8,128)(2,1)S(1)}, bf16[32,3072]{1,0:T(8,128)(2,1)S(1)}, u32[]{:S(2)}, u32[]{:S(2)}) collective-permute-start(bf16[32,3072]{1,0:T(8,128)(2,1)S(1)} %get-tuple-element.55.refs_0_), channel_id=1, source_target_pairs={{0,24},{8,16},{16,8},{24,0},{1,25},{9,17},{17,9},{25,1},{2,26},{10... | collective-permute-start | bytes 589832 | tf_op jit(solution)/shard_map/ppermute | solution.py:28
  54.5 0.6 collective-permute-start.8
  55.1 0.8 place.1.refs_7_
  55.9 7.4 %collective-permute-done.11.refs_5_ = bf16[32,3072]{1,0:T(8,128)(2,1)S(1)} collective-permute-done((bf16[32,3072]{1,0:T(8,128)(2,1)S(1)}, bf16[32,3072]{1,0:T(8,128)(2,1)S(1)}, u32[]{:S(2)}, u32[]{:S(2)}) %collective-permute-start.11) | collective-permute-done | bytes 196640 | tf_op jit(solution)/shard_map/ppermute | solution.py:28
  63.5 2.5 %collective-permute-start.15 = (bf16[96,3072]{1,0:T(8,128)(2,1)S(1)}, bf16[96,3072]{1,0:T(8,128)(2,1)S(1)}, u32[]{:S(2)}, u32[]{:S(2)}) collective-permute-start(bf16[96,3072]{1,0:T(8,128)(2,1)S(1)} %get-tuple-element.56.after.refs_2_), channel_id=1, source_target_pairs={{0,16},{8,24},{16,0},{24,8},{1,17},{9,25},{17,1},{25,9},{2,18},{10... | collective-permute-start | bytes 1769480 | tf_op jit(solution)/shard_map/ppermute | solution.py:28
  66.0 1.5 %collective-permute-start.14 = (bf16[96,3072]{1,0:T(8,128)(2,1)S(1)}, bf16[96,3072]{1,0:T(8,128)(2,1)S(1)}, u32[]{:S(2)}, u32[]{:S(2)}) collective-permute-start(bf16[96,3072]{1,0:T(8,128)(2,1)S(1)} %get-tuple-element.56.after.refs_2_), channel_id=1, source_target_pairs={{0,8},{8,0},{16,24},{24,16},{1,9},{9,1},{17,25},{25,17},{2,10},{10... | collective-permute-start | bytes 1769480 | tf_op jit(solution)/shard_map/ppermute | solution.py:28
  67.5 0.5 collective-permute-start.18
  68.0 5.2 %load.1 = (bf16[1,1152,3072]{2,1,0:T(8,128)(2,1)S(1)}, bf16[1,1152,3072]{2,1,0:T(8,128)(2,1)S(1)}) custom-call(bf16[1,1152,3072]{2,1,0:T(8,128)(2,1)} %gate_hbm.1, bf16[1,1152,3072]{2,1,0:T(8,128)(2,1)} %up_hbm.1, bf16[96,3072]{1,0:T(8,128)(2,1)S(1)} %get-tuple-element.56.after.refs_2_), custom_call_target="tpu_custom_call" | custom-call | flops 1 | bytes 14155776 | tf_op jit(solution)/shard_map/load/pallas_call | solution.py:498
  73.2 5.9 %collective-permute-done.15.two_ref.refs_2_ = bf16[96,3072]{1,0:T(8,128)(2,1)S(1)} collective-permute-done((bf16[96,3072]{1,0:T(8,128)(2,1)S(1)}, bf16[96,3072]{1,0:T(8,128)(2,1)S(1)}, u32[]{:S(2)}, u32[]{:S(2)}) %collective-permute-start.15) | collective-permute-done | bytes 589856 | tf_op jit(solution)/shard_map/ppermute | solution.py:28
  79.0 1.5 %collective-permute-done.14.one_ref.refs_4_ = bf16[96,3072]{1,0:T(8,128)(2,1)S(1)} collective-permute-done((bf16[96,3072]{1,0:T(8,128)(2,1)S(1)}, bf16[96,3072]{1,0:T(8,128)(2,1)S(1)}, u32[]{:S(2)}, u32[]{:S(2)}) %collective-permute-start.14) | collective-permute-done | bytes 589856 | tf_op jit(solution)/shard_map/ppermute | solution.py:28
  80.6 0.4 collective-permute-start.16
  81.0 1.7 %collective-permute-start.17 = (bf16[48,3072]{1,0:T(8,128)(2,1)S(1)}, bf16[48,3072]{1,0:T(8,128)(2,1)S(1)}, u32[]{:S(2)}, u32[]{:S(2)}) collective-permute-start(bf16[48,3072]{1,0:T(8,128)(2,1)S(1)} %get-tuple-element.64), channel_id=1, source_target_pairs={{0,8},{8,0},{16,24},{24,16},{1,9},{9,1},{17,25},{25,17},{2,10},{10... | collective-permute-start | bytes 884744 | tf_op jit(solution)/shard_map/ppermute | solution.py:28
  82.7 5.6 %experts.2.refs_8_ = f32[1,1152,512]{2,1,0:T(8,128)} custom-call(s32[4,256]{1,0:T(4,128)S(1)} %get-tuple-element.53.slot_ref, f32[4,256]{1,0:T(4,128)S(1)} %get-tuple-element.54.weight_ref, bf16[1,1152,3072]{2,1,0:T(8,128)(2,1)S(1)} %get-tuple-element.57.after.gate_ref, bf16[1,1152,3072]{2,1,0:T(8,128)(2,1)S(1)} %get-tuple-element.58.up_ref, ...), custom_call_target="tpu_custom_call" | custom-call | flops 3623878656 | bytes 1572864 | tf_op jit(solution)/shard_map/experts/pallas_call | solution.py:350
  88.3 1.7 %collective-permute-done.16.refs_4_ = bf16[48,3072]{1,0:T(8,128)(2,1)S(1)} collective-permute-done((bf16[48,3072]{1,0:T(8,128)(2,1)S(1)}, bf16[48,3072]{1,0:T(8,128)(2,1)S(1)}, u32[]{:S(2)}, u32[]{:S(2)}) %collective-permute-start.16) | collective-permute-done | bytes 294944 | tf_op jit(solution)/shard_map/ppermute | solution.py:28
  90.1 0.5 collective-permute-start.21
  90.6 1.9 %collective-permute-done.21.refs_6_ = bf16[48,3072]{1,0:T(8,128)(2,1)S(1)} collective-permute-done((bf16[48,3072]{1,0:T(8,128)(2,1)S(1)}, bf16[48,3072]{1,0:T(8,128)(2,1)S(1)}, u32[]{:S(2)}, u32[]{:S(2)}) %collective-permute-start.21) | collective-permute-done | bytes 294944 | tf_op jit(solution)/shard_map/ppermute | solution.py:28
  93.0 5.6 %experts.3 = f32[1,1152,512]{2,1,0:T(8,128)} custom-call(s32[4,256]{1,0:T(4,128)S(1)} %get-tuple-element.53.slot_ref, f32[4,256]{1,0:T(4,128)S(1)} %get-tuple-element.54.weight_ref, bf16[1,1152,3072]{2,1,0:T(8,128)(2,1)S(1)} %get-tuple-element.57.after.gate_ref, ...), custom_call_target="tpu_custom_call", output_to_operand_aliasing={{}: (12, {})} | custom-call | flops 3623878656 | bytes 1572864 | tf_op jit(solution)/shard_map/experts/pallas_call | solution.py:350
  (36 shorter events, 2.1 us)
Async XLA Ops:
  0.6 19.4 %copy-start = (f32[2,4,128]{2,1,0:T(4,128)S(1)}, f32[2,4,128]{2,1,0:T(4,128)}, u32[]{:S(2)}) copy-start(f32[2,4,128]{2,1,0:T(4,128)} %refs_2_.1) | copy-start | bytes 12292
  0.6 19.4 %copy-start.4 = (f32[512]{0:T(512)S(1)}, f32[512]{0:T(512)}, u32[]{:S(2)}) copy-start(f32[512]{0:T(512)} %param.17) | copy-start | bytes 6148
  2.6 12.7 %collective-permute-start.2 = (bf16[1056,128]{1,0:T(8,128)(2,1)S(1)}, bf16[1056,128]{1,0:T(8,128)(2,1)S(1)}, u32[]{:S(2)}, u32[]{:S(2)}) collective-permute-start(bf16[1056,128]{1,0:T(8,128)(2,1)S(1)} %states.1), channel_id=1, source_target_pairs={{0,24},{8,16},{1,25},{9,17},{2,26},{10,18},{3,27},{11,19},{4,28},{... | collective-permute-start | bytes 811016 | tf_op jit(solution)/shard_map/ppermute | solution.py:28
  8.5 11.5 %collective-permute-start.1 = (bf16[1056,128]{1,0:T(8,128)(2,1)S(1)}, bf16[1056,128]{1,0:T(8,128)(2,1)S(1)}, u32[]{:S(2)}, u32[]{:S(2)}) collective-permute-start(bf16[1056,128]{1,0:T(8,128)(2,1)S(1)} %states.1), channel_id=1, source_target_pairs={{0,16},{8,24},{1,17},{9,25},{2,18},{10,26},{3,19},{11,27},{4,20},{... | collective-permute-start | bytes 811016 | tf_op jit(solution)/shard_map/ppermute | solution.py:28
  9.8 10.2 %collective-permute-start = (bf16[1056,128]{1,0:T(8,128)(2,1)S(1)}, bf16[1056,128]{1,0:T(8,128)(2,1)S(1)}, u32[]{:S(2)}, u32[]{:S(2)}) collective-permute-start(bf16[1056,128]{1,0:T(8,128)(2,1)S(1)} %states.1), channel_id=1, source_target_pairs={{0,8},{16,24},{1,9},{17,25},{2,10},{18,26},{3,11},{19,27},{4,12},{... | collective-permute-start | bytes 811016 | tf_op jit(solution)/shard_map/ppermute | solution.py:28
  20.0 9.1 %copy-start.2 = (s32[512,2,2]{0,2,1:T(2,128)S(1)}, s32[512,2,2]{0,2,1:T(2,128)}, u32[]{:S(2)}) copy-start(s32[512,2,2]{0,2,1:T(2,128)} %param.20) | copy-start | bytes 24580
  20.0 9.1 %copy-start.3 = (f32[512,2,2]{0,2,1:T(2,128)S(1)}, f32[512,2,2]{0,2,1:T(2,128)}, u32[]{:S(2)}) copy-start(f32[512,2,2]{0,2,1:T(2,128)} %param.21) | copy-start | bytes 24580
  20.0 23.4 %copy-start.1 = (f32[3072]{0:T(1024)S(1)}, f32[3072]{0:T(1024)}, u32[]{:S(2)}) copy-start(f32[3072]{0:T(1024)} %param.19) | copy-start | bytes 36868
  21.8 2.4 %collective-permute-start.3 = (bf16[128,3072]{1,0:T(8,128)(2,1)S(1)}, bf16[128,3072]{1,0:T(8,128)(2,1)S(1)}, u32[]{:S(2)}, u32[]{:S(2)}) collective-permute-start(bf16[128,3072]{1,0:T(8,128)(2,1)S(1)} %get-tuple-element.40), channel_id=1, source_target_pairs={{0,1},{1,0},{2,3},{3,2},{4,5},{5,4},{6,7},{7,6},{8,9},{9,8},{10,11... | collective-permute-start | bytes 2359304 | tf_op jit(solution)/shard_map/ppermute | solution.py:28
  24.6 10.6 %collective-permute-start.4 = (bf16[32,3072]{1,0:T(8,128)(2,1)S(1)}, bf16[32,3072]{1,0:T(8,128)(2,1)S(1)}, u32[]{:S(2)}, u32[]{:S(2)}) collective-permute-start(bf16[32,3072]{1,0:T(8,128)(2,1)S(1)} %get-tuple-element.49), channel_id=1, source_target_pairs={{0,2},{1,3},{2,0},{3,1},{4,6},{5,7},{6,4},{7,5},{8,10},{9,11},{10,... | collective-permute-start | bytes 589832 | tf_op jit(solution)/shard_map/ppermute | solution.py:28
  26.3 17.1 %collective-permute-start.5 = (bf16[32,3072]{1,0:T(8,128)(2,1)S(1)}, bf16[32,3072]{1,0:T(8,128)(2,1)S(1)}, u32[]{:S(2)}, u32[]{:S(2)}) collective-permute-start(bf16[32,3072]{1,0:T(8,128)(2,1)S(1)} %get-tuple-element.50), channel_id=1, source_target_pairs={{0,4},{1,5},{2,6},{3,7},{4,0},{5,1},{6,2},{7,3},{8,12},{9,13},{10,... | collective-permute-start | bytes 589832 | tf_op jit(solution)/shard_map/ppermute | solution.py:28
  28.9 14.5 %collective-permute-start.6 = (bf16[32,3072]{1,0:T(8,128)(2,1)S(1)}, bf16[32,3072]{1,0:T(8,128)(2,1)S(1)}, u32[]{:S(2)}, u32[]{:S(2)}) collective-permute-start(bf16[32,3072]{1,0:T(8,128)(2,1)S(1)} %get-tuple-element.51), channel_id=1, source_target_pairs={{0,6},{1,7},{2,4},{3,5},{4,2},{5,3},{6,0},{7,1},{8,14},{9,15},{10,... | collective-permute-start | bytes 589832 | tf_op jit(solution)/shard_map/ppermute | solution.py:28
  43.6 11.5 %collective-permute-start.12 = (bf16[32,3072]{1,0:T(8,128)(2,1)S(1)}, bf16[32,3072]{1,0:T(8,128)(2,1)S(1)}, u32[]{:S(2)}, u32[]{:S(2)}) collective-permute-start(bf16[32,3072]{1,0:T(8,128)(2,1)S(1)} %get-tuple-element.55.refs_0_), channel_id=1, source_target_pairs={{0,6},{1,7},{2,4},{3,5},{4,2},{5,3},{6,0},{7,1},{8,14},{9,15},{10,... | collective-permute-start | bytes 589832 | tf_op jit(solution)/shard_map/ppermute | solution.py:28
  46.2 17.2 %collective-permute-start.11 = (bf16[32,3072]{1,0:T(8,128)(2,1)S(1)}, bf16[32,3072]{1,0:T(8,128)(2,1)S(1)}, u32[]{:S(2)}, u32[]{:S(2)}) collective-permute-start(bf16[32,3072]{1,0:T(8,128)(2,1)S(1)} %get-tuple-element.55.refs_0_), channel_id=1, source_target_pairs={{0,4},{1,5},{2,6},{3,7},{4,0},{5,1},{6,2},{7,3},{8,12},{9,13},{10,... | collective-permute-start | bytes 589832 | tf_op jit(solution)/shard_map/ppermute | solution.py:28
  51.1 12.3 %collective-permute-start.10 = (bf16[32,3072]{1,0:T(8,128)(2,1)S(1)}, bf16[32,3072]{1,0:T(8,128)(2,1)S(1)}, u32[]{:S(2)}, u32[]{:S(2)}) collective-permute-start(bf16[32,3072]{1,0:T(8,128)(2,1)S(1)} %get-tuple-element.55.refs_0_), channel_id=1, source_target_pairs={{0,2},{1,3},{2,0},{3,1},{4,6},{5,7},{6,4},{7,5},{8,10},{9,11},{10,... | collective-permute-start | bytes 589832 | tf_op jit(solution)/shard_map/ppermute | solution.py:28
  51.2 12.2 %collective-permute-start.9 = (bf16[32,3072]{1,0:T(8,128)(2,1)S(1)}, bf16[32,3072]{1,0:T(8,128)(2,1)S(1)}, u32[]{:S(2)}, u32[]{:S(2)}) collective-permute-start(bf16[32,3072]{1,0:T(8,128)(2,1)S(1)} %get-tuple-element.55.refs_0_), channel_id=1, source_target_pairs={{0,24},{8,16},{16,8},{24,0},{1,25},{9,17},{17,9},{25,1},{2,26},{10... | collective-permute-start | bytes 589832 | tf_op jit(solution)/shard_map/ppermute | solution.py:28
  54.5 8.8 %collective-permute-start.8 = (bf16[32,3072]{1,0:T(8,128)(2,1)S(1)}, bf16[32,3072]{1,0:T(8,128)(2,1)S(1)}, u32[]{:S(2)}, u32[]{:S(2)}) collective-permute-start(bf16[32,3072]{1,0:T(8,128)(2,1)S(1)} %get-tuple-element.55.refs_0_), channel_id=1, source_target_pairs={{0,16},{8,24},{16,0},{24,8},{1,17},{9,25},{17,1},{25,9},{2,18},{10... | collective-permute-start | bytes 589832 | tf_op jit(solution)/shard_map/ppermute | solution.py:28
  55.1 8.3 %collective-permute-start.7 = (bf16[32,3072]{1,0:T(8,128)(2,1)S(1)}, bf16[32,3072]{1,0:T(8,128)(2,1)S(1)}, u32[]{:S(2)}, u32[]{:S(2)}) collective-permute-start(bf16[32,3072]{1,0:T(8,128)(2,1)S(1)} %get-tuple-element.55.refs_0_), channel_id=1, source_target_pairs={{0,8},{8,0},{16,24},{24,16},{1,9},{9,1},{17,25},{25,17},{2,10},{10... | collective-permute-start | bytes 589832 | tf_op jit(solution)/shard_map/ppermute | solution.py:28
  63.5 15.5 %collective-permute-start.15 = (bf16[96,3072]{1,0:T(8,128)(2,1)S(1)}, bf16[96,3072]{1,0:T(8,128)(2,1)S(1)}, u32[]{:S(2)}, u32[]{:S(2)}) collective-permute-start(bf16[96,3072]{1,0:T(8,128)(2,1)S(1)} %get-tuple-element.56.after.refs_2_), channel_id=1, source_target_pairs={{0,16},{8,24},{16,0},{24,8},{1,17},{9,25},{17,1},{25,9},{2,18},{10... | collective-permute-start | bytes 1769480 | tf_op jit(solution)/shard_map/ppermute | solution.py:28
  66.0 14.5 %collective-permute-start.14 = (bf16[96,3072]{1,0:T(8,128)(2,1)S(1)}, bf16[96,3072]{1,0:T(8,128)(2,1)S(1)}, u32[]{:S(2)}, u32[]{:S(2)}) collective-permute-start(bf16[96,3072]{1,0:T(8,128)(2,1)S(1)} %get-tuple-element.56.after.refs_2_), channel_id=1, source_target_pairs={{0,8},{8,0},{16,24},{24,16},{1,9},{9,1},{17,25},{25,17},{2,10},{10... | collective-permute-start | bytes 1769480 | tf_op jit(solution)/shard_map/ppermute | solution.py:28
  67.5 15.3 %collective-permute-start.13 = (bf16[128,3072]{1,0:T(8,128)(2,1)S(1)}, bf16[128,3072]{1,0:T(8,128)(2,1)S(1)}, u32[]{:S(2)}, u32[]{:S(2)}) collective-permute-start(bf16[128,3072]{1,0:T(8,128)(2,1)S(1)} %get-tuple-element.59.refs_0_), channel_id=1, source_target_pairs={{0,1},{1,0},{2,3},{3,2},{4,5},{5,4},{6,7},{7,6},{8,9},{9,8},{10,11... | collective-permute-start | bytes 2359304 | tf_op jit(solution)/shard_map/ppermute | solution.py:28
  67.5 15.2 %collective-permute-start.18 = (bf16[96,3072]{1,0:T(8,128)(2,1)S(1)}, bf16[96,3072]{1,0:T(8,128)(2,1)S(1)}, u32[]{:S(2)}, u32[]{:S(2)}) collective-permute-start(bf16[96,3072]{1,0:T(8,128)(2,1)S(1)} %get-tuple-element.56.after.refs_2_), channel_id=1, source_target_pairs={{0,1},{1,0},{2,3},{3,2},{4,5},{5,4},{6,7},{7,6},{8,9},{9,8},{10,11... | collective-permute-start | bytes 1769480 | tf_op jit(solution)/shard_map/ppermute | solution.py:28
  80.5 2.2 %collective-permute-start.19 = (bf16[96,3072]{1,0:T(8,128)(2,1)S(1)}, bf16[96,3072]{1,0:T(8,128)(2,1)S(1)}, u32[]{:S(2)}, u32[]{:S(2)}) collective-permute-start(bf16[96,3072]{1,0:T(8,128)(2,1)S(1)} %collective-permute-done.14.one_ref.refs_4_), channel_id=1, source_target_pairs={{0,1},{1,0},{2,3},{3,2},{4,5},{5,4},{6,7},{7,6},{8,9},{9,8},{10,11... | collective-permute-start | bytes 1769480 | tf_op jit(solution)/shard_map/ppermute | solution.py:28
  80.6 9.4 %collective-permute-start.16 = (bf16[48,3072]{1,0:T(8,128)(2,1)S(1)}, bf16[48,3072]{1,0:T(8,128)(2,1)S(1)}, u32[]{:S(2)}, u32[]{:S(2)}) collective-permute-start(bf16[48,3072]{1,0:T(8,128)(2,1)S(1)} %get-tuple-element.63), channel_id=1, source_target_pairs={{0,16},{8,24},{16,0},{24,8},{1,17},{9,25},{17,1},{25,9},{2,18},{10... | collective-permute-start | bytes 884744 | tf_op jit(solution)/shard_map/ppermute | solution.py:28
  81.0 9.1 %collective-permute-start.17 = (bf16[48,3072]{1,0:T(8,128)(2,1)S(1)}, bf16[48,3072]{1,0:T(8,128)(2,1)S(1)}, u32[]{:S(2)}, u32[]{:S(2)}) collective-permute-start(bf16[48,3072]{1,0:T(8,128)(2,1)S(1)} %get-tuple-element.64), channel_id=1, source_target_pairs={{0,8},{8,0},{16,24},{24,16},{1,9},{9,1},{17,25},{25,17},{2,10},{10... | collective-permute-start | bytes 884744 | tf_op jit(solution)/shard_map/ppermute | solution.py:28
  90.1 2.9 %collective-permute-start.20 = (bf16[96,3072]{1,0:T(8,128)(2,1)S(1)}, bf16[96,3072]{1,0:T(8,128)(2,1)S(1)}, u32[]{:S(2)}, u32[]{:S(2)}) collective-permute-start(bf16[96,3072]{1,0:T(8,128)(2,1)S(1)} %collective-permute-done.15.two_ref.refs_2_), channel_id=1, source_target_pairs={{0,1},{1,0},{2,3},{3,2},{4,5},{5,4},{6,7},{7,6},{8,9},{9,8},{10,11... | collective-permute-start | bytes 1769480 | tf_op jit(solution)/shard_map/ppermute | solution.py:28
  90.1 2.4 %collective-permute-start.21 = (bf16[48,3072]{1,0:T(8,128)(2,1)S(1)}, bf16[48,3072]{1,0:T(8,128)(2,1)S(1)}, u32[]{:S(2)}, u32[]{:S(2)}) collective-permute-start(bf16[48,3072]{1,0:T(8,128)(2,1)S(1)} %collective-permute-done.16.refs_4_), channel_id=1, source_target_pairs={{0,1},{1,0},{2,3},{3,2},{4,5},{5,4},{6,7},{7,6},{8,9},{9,8},{10,11... | collective-permute-start | bytes 884744 | tf_op jit(solution)/shard_map/ppermute | solution.py:28
  90.6 2.3 %collective-permute-start.22 = (bf16[48,3072]{1,0:T(8,128)(2,1)S(1)}, bf16[48,3072]{1,0:T(8,128)(2,1)S(1)}, u32[]{:S(2)}, u32[]{:S(2)}) collective-permute-start(bf16[48,3072]{1,0:T(8,128)(2,1)S(1)} %collective-permute-done.17.refs_5_), channel_id=1, source_target_pairs={{0,1},{1,0},{2,3},{3,2},{4,5},{5,4},{6,7},{7,6},{8,9},{9,8},{10,11... | collective-permute-start | bytes 884744 | tf_op jit(solution)/shard_map/ppermute | solution.py:28

commit v3 on v2

--- a/solution.py
+++ b/solution.py
@@ -60,39 +60,34 @@
     return lax.dot_general(log_decay, tri, NT, precision=PRECISE, preferred_element_type=F32)
 
 
-def state_kernel(k_hbm, v_hbm, decay_hbm, *refs):
-    out_refs, (k_ref, v_ref, decay_ref, sems) = refs[:-4], refs[-4:]
-    copies = [
-        pltpu.make_async_copy(source, to, sems.at[n])
-        for n, (source, to) in enumerate(((decay_hbm, decay_ref), (k_hbm, k_ref), (v_hbm, v_ref)))
-    ]
+def state_kernel(k_hbm, v_hbm, decay_hbm, proj_hbm, out_ref, proj_ref, k_ref, v_ref, decay_ref, sems):
+    pairs = ((decay_hbm, decay_ref), (k_hbm, k_ref), (v_hbm, v_ref), (proj_hbm, proj_ref))
+    copies = [pltpu.make_async_copy(source, to, sems.at[n]) for n, (source, to) in enumerate(pairs)]
     for copy in copies:
         copy.start()
-    for copy in copies:
+    for copy in copies[:-1]:
         copy.wait()
     seqs, heads, size = decay_ref.shape
     width = k_ref.shape[2] // heads
-    group = seqs // len(out_refs)
-    for g, out_ref in enumerate(out_refs):
-        totals = []
-        for b in range(group):
-            log_decay = decay_ref[g * group + b]
-            columns = running_columns(log_decay)
-            tail = jnp.exp(columns[size - 1 : size, :] - columns)
-            totals.append(jnp.broadcast_to(running_rows(log_decay)[:, size - 1 : size], (heads, width)))
-            for h in range(heads):
-                part = slice(h * width, (h + 1) * width)
-                value = v_ref[g * group + b, :, part]
-                high, low = halves(k_ref[g * group + b, :, part].astype(F32) * tail[:, h : h + 1])
-                at = (b * heads + h) * width
-                out_ref[at : at + width, :] = (mm(high, value, TN) + mm(low, value, TN)).astype(BF)
-        total = jnp.concatenate(totals, axis=0)
-        pieces = [piece.astype(F32) for piece in thirds(total)]
-        pieces.append(jnp.zeros_like(total))
-        out_ref[group * heads * width :, :] = jnp.concatenate(pieces, axis=0).astype(BF)
-
-
-def inner_kernel(q_hbm, k_hbm, v_hbm, decay_hbm, proj_hbm, residual_hbm, out_ref, q_ref, proj_ref, rows_ref, *scratch):
+    totals = []
+    for b in range(seqs):
+        columns = running_columns(decay_ref[b])
+        tail = jnp.exp(columns[size - 1 : size, :] - columns)
+        totals.append(jnp.broadcast_to(running_rows(decay_ref[b])[:, size - 1 : size], (heads, width)))
+        for h in range(heads):
+            part = slice(h * width, (h + 1) * width)
+            value = v_ref[b, :, part]
+            high, low = halves(k_ref[b, :, part].astype(F32) * tail[:, h : h + 1])
+            at = (b * heads + h) * width
+            out_ref[at : at + width, :] = (mm(high, value, TN) + mm(low, value, TN)).astype(BF)
+    total = jnp.concatenate(totals, axis=0)
+    pieces = [piece.astype(F32) for piece in thirds(total)]
+    pieces.append(jnp.zeros_like(total))
+    out_ref[seqs * heads * width :, :] = jnp.concatenate(pieces, axis=0).astype(BF)
+    copies[-1].wait()
+
+
+def inner_kernel(q_hbm, k_hbm, v_hbm, decay_hbm, residual_hbm, after, out_ref, q_ref, rows_ref, *scratch):
     k_ref, v_ref, decay_ref, residual_ref, sems = scratch
     pairs = (
         (decay_hbm, decay_ref),
@@ -100,12 +95,11 @@
         (k_hbm, k_ref),
         (v_hbm, v_ref),
         (residual_hbm, residual_ref),
-        (proj_hbm, proj_ref),
     )
     copies = [pltpu.make_async_copy(source, to, sems.at[n]) for n, (source, to) in enumerate(pairs)]
     for copy in copies:
         copy.start()
-    for copy in copies[:-1]:
+    for copy in copies:
         copy.wait()
     own, seqs, _ = residual_ref.shape
     for b in range(seqs):
@@ -124,13 +118,12 @@
             high, low = halves(scores)
             value = v_ref[b, :, part]
             out_ref[b, :, part] = mm(high, value) + mm(low, value)
-    copies[-1].wait()
-
-
-def project_kernel(count, line, *refs):
+
+
+def attend_kernel(count, line, *refs):
     q_ref, inner_ref, decay_ref, gain_ref = refs[:4]
     states = refs[4 : 3 + count]
-    proj_ref, own_ref, partner_ref = refs[3 + count :]
+    own_ref, partner_ref = refs[3 + count :]
     seqs, size, feat = q_ref.shape
     heads = decay_ref.shape[1]
     width = feat // heads
@@ -173,13 +166,19 @@
     source = source + size * ((to // own) % seqs)
     pick = (source == lax.broadcasted_iota(jnp.int32, (total, total), 1)).astype(BF)
     attention = mm(pick, attention).astype(BF)
-    model = proj_ref.shape[1]
+    own_ref[...] = attention[: total // 2, :]
+    partner_ref[...] = attention[total // 2 :, :]
+
+
+def project_kernel(own_ref, partner_ref, proj_ref, partner_proj_ref, keep_ref, *send_refs):
+    rows, model = keep_ref.shape
     tile = column_tile(model)
     for n in range(model // tile):
         columns = slice(n * tile, (n + 1) * tile)
-        product = mm(attention, proj_ref[:, columns])
-        own_ref[:, columns] = product[: total // 2, :]
-        partner_ref[:, columns] = product[total // 2 :, :].astype(BF)
+        product = mm(own_ref[...], proj_ref[:, columns]) + mm(partner_ref[...], partner_proj_ref[:, columns])
+        keep_ref[:, columns] = product[:rows, :]
+        for d, send_ref in enumerate(send_refs, start=1):
+            send_ref[:, columns] = product[d * rows : (d + 1) * rows, :].astype(BF)
 
 
 def column_tile(model):
@@ -188,14 +187,6 @@
 
 def source_position(flip, distance, place, index, own):
     return own * (2 * ((index // 2) ^ distance) + ((index % 2) ^ flip)) + place
-
-
-def fold_kernel(kept_ref, got_ref, keep_ref, *send_refs):
-    rows = keep_ref.shape[0]
-    keep_ref[...] = kept_ref[:rows, :] + got_ref[:rows, :].astype(F32)
-    for d, send_ref in enumerate(send_refs, start=1):
-        part = slice(d * rows, (d + 1) * rows)
-        send_ref[...] = (kept_ref[part, :] + got_ref[part, :].astype(F32)).astype(BF)
 
 
 def mix_kernel(kept_ref, residual_ref, gain_ref, *refs):
@@ -228,36 +219,40 @@
 
 
 def gather_kernel(first, second, *refs):
-    for to, sources in zip(refs[-2:], (refs[:first], refs[first : first + second])):
+    near_ref, rest_ref, corner_ref = refs[-3:]
+    for to, sources in ((near_ref, refs[:first]), (rest_ref, refs[first : first + second])):
         at = 0
         for source in sources:
             to[at : at + source.shape[0], :] = source[...]
             at += source.shape[0]
-
-
-def halves_kernel(one_ref, two_ref, after, low_ref, high_ref):
+    corner_ref[...] = refs[first - 1][...]
+
+
+def halves_kernel(one_ref, two_ref, corner_ref, after, low_ref, high_ref):
     half = low_ref.shape[0]
-    low_ref[...] = one_ref[:half, :]
-    high_ref[...] = two_ref[half:, :]
-
-
-def exchanged(block, count, after):
-    if count != 4 or block.shape[0] % 32 != 0:
+    first = one_ref.shape[0] - 2 * half
+    low_ref[...] = one_ref[first : first + half, :]
+    high_ref[...] = two_ref[first + half :, :]
+
+
+def exchanged(block, corner, count, after):
+    rows, unit = block.shape[0], corner.shape[0]
+    if count != 4 or unit % 16 != 0 or (rows - unit) % 32 != 0 or rows == unit:
         return [[swap(block, "seq", d)] for d in range(1, count)]
-    half = block.shape[0] // 2
     one, two = swap(block, "seq", 1), swap(block, "seq", 2)
+    corner = swap(corner, "exp", 2)
     vmem, anywhere = pl.BlockSpec(memory_space=pltpu.VMEM), pl.BlockSpec(memory_space=pl.ANY)
     low, high = pl.pallas_call(
         halves_kernel,
-        in_specs=[vmem] * 2 + [anywhere],
+        in_specs=[vmem] * 3 + [anywhere],
         out_specs=[vmem] * 2,
-        out_shape=[jax.ShapeDtypeStruct((half, block.shape[1]), block.dtype)] * 2,
+        out_shape=[jax.ShapeDtypeStruct(((rows - unit) // 2, block.shape[1]), block.dtype)] * 2,
         compiler_params=params(VMEM_BYTES // 8),
         cost_estimate=cost(1, 4 * block.size),
         name="halves",
-    )(one, two, after)
+    )(one, two, corner, after)
     one, two, low, high = lax.optimization_barrier((one, two, low, high))
-    return [[one], [two], [swap(low, "seq", 2), swap(high, "seq", 1)]]
+    return [[one], [two], [corner, swap(low, "seq", 2), swap(high, "seq", 1)]]
 
 
 def route_kernel(capacity, own, routes_ref, weights_ref, slot_ref, weight_ref, a_ref, b_ref):
@@ -391,30 +386,33 @@
 
     vmem, hbm, anywhere = (pl.BlockSpec(memory_space=space) for space in (pltpu.VMEM, pltpu.HBM, pl.ANY))
 
-    states = pl.pallas_call(
+    states, proj = pl.pallas_call(
         state_kernel,
-        in_specs=[hbm] * 3,
-        out_shape=jax.ShapeDtypeStruct((seqs * heads * (width + 4), width), BF),
+        in_specs=[hbm] * 4,
+        out_specs=[vmem] * 2,
+        out_shape=[
+            pltpu.VMEM((seqs * heads * (width + 4), width), BF),
+            pltpu.VMEM(out_proj.shape, BF),
+        ],
         scratch_shapes=[
             pltpu.VMEM(key_vecs.shape, BF),
             pltpu.VMEM(value_vecs.shape, BF),
             pltpu.VMEM(log_decay.shape, F32),
-            pltpu.SemaphoreType.DMA((3,)),
+            pltpu.SemaphoreType.DMA((4,)),
         ],
         compiler_params=params(),
         cost_estimate=cost(4 * total * feat * width, 6 * total * feat),
         name="states",
-    )(*in_hbm(key_vecs, value_vecs, log_decay))
-    arrived = [swap(states, "seq", d, forward_only=True) for d in range(1, count)]
-
-    inner, query, proj, residual_rows = pl.pallas_call(
+    )(*in_hbm(key_vecs, value_vecs, log_decay, out_proj))
+    arrived = [swap(states, "seq", d) for d in range(1, count)]
+
+    inner, query, residual_rows = pl.pallas_call(
         inner_kernel,
-        in_specs=[hbm] * 6,
-        out_specs=[vmem] * 4,
+        in_specs=[hbm] * 5 + [anywhere],
+        out_specs=[vmem] * 3,
         out_shape=[
             pltpu.VMEM((seqs, size, feat), F32),
             pltpu.VMEM(queries.shape, BF),
-            pltpu.VMEM(out_proj.shape, BF),
             pltpu.VMEM((unit, model), F32),
         ],
         scratch_shapes=[
@@ -422,39 +420,33 @@
             pltpu.VMEM(value_vecs.shape, BF),
             pltpu.VMEM(log_decay.shape, F32),
             pltpu.VMEM(residual.shape, BF),
-            pltpu.SemaphoreType.DMA((6,)),
+            pltpu.SemaphoreType.DMA((5,)),
         ],
         compiler_params=params(),
         cost_estimate=cost(6 * total * feat * size, 10 * total * feat),
         name="inner",
-    )(*in_hbm(queries, key_vecs, value_vecs, log_decay, out_proj, residual))
-
-    own_sum, partner_sum = pl.pallas_call(
-        functools.partial(project_kernel, count, line),
-        in_specs=[vmem] * (5 + count - 1),
+    )(*in_hbm(queries, key_vecs, value_vecs, log_decay, residual), *in_vmem(states))
+
+    mine, theirs = pl.pallas_call(
+        functools.partial(attend_kernel, count, line),
+        in_specs=[vmem] * (4 + count - 1),
         out_specs=[vmem] * 2,
-        out_shape=[jax.ShapeDtypeStruct((total // 2, model), F32), jax.ShapeDtypeStruct((total // 2, model), BF)],
-        compiler_params=params(),
-        cost_estimate=cost(2 * total * feat * model, 2 * feat * model + 3 * total * model),
-        name="project",
-    )(*in_vmem(query, inner), log_decay, head_gain.reshape(1, feat), *arrived, *in_vmem(proj))
-
-    tile = column_tile(model)
-
-    def column_blocks(count):
-        return pl.BlockSpec((count, tile), lambda i: (0, i))
+        out_shape=[jax.ShapeDtypeStruct((total // 2, feat), BF)] * 2,
+        compiler_params=params(),
+        cost_estimate=cost(6 * total * feat * width, 10 * total * feat),
+        name="attend",
+    )(*in_vmem(query, inner), log_decay, head_gain.reshape(1, feat), *arrived)
 
     keep, *sends = pl.pallas_call(
-        fold_kernel,
-        grid=(model // tile,),
-        in_specs=[column_blocks(total // 2)] * 2,
-        out_specs=[column_blocks(unit)] * line,
+        project_kernel,
+        in_specs=[vmem] * 4,
+        out_specs=[vmem] * line,
         out_shape=[jax.ShapeDtypeStruct((unit, model), F32)]
         + [jax.ShapeDtypeStruct((unit, model), BF)] * (line - 1),
         compiler_params=params(),
-        cost_estimate=cost(total * model, 4 * total * model),
-        name="fold",
-    )(own_sum, swap(partner_sum, "exp", 1))
+        cost_estimate=cost(2 * total * feat * model, 4 * feat * model + 3 * total * model),
+        name="project",
+    )(mine, swap(theirs, "exp", 1), *in_vmem(proj), swap(proj, "exp", 1))
     got = [swap(send, "exp", 2 * d) for d, send in enumerate(sends, start=1)]
 
     routes, route_weight, keep = lax.optimization_barrier((routes, route_weight, keep))
@@ -486,11 +478,11 @@
     along = [swap(normed, "exp", 2 * d) for d in range(1, line)]
     across = [normed] + [swap(normed, "seq", d) for d in range(1, count)]
     rows = [len(arrays) * unit for arrays in (across, along)]
-    near, rest = pl.pallas_call(
+    near, rest, corner = pl.pallas_call(
         functools.partial(gather_kernel, count, line - 1),
         in_specs=[vmem] * (count + line - 1) + [anywhere],
-        out_specs=[vmem] * 2,
-        out_shape=[jax.ShapeDtypeStruct((n, model), BF) for n in rows],
+        out_specs=[vmem] * 3,
+        out_shape=[jax.ShapeDtypeStruct((n, model), BF) for n in (*rows, unit)],
         compiler_params=params(VMEM_BYTES // 8),
         cost_estimate=cost(1, 4 * sum(rows) * model),
         name="gather",
@@ -505,7 +497,7 @@
         cost_estimate=cost(1, 4 * w_gate.size),
         name="load",
     )(*in_hbm(w_gate, w_up), rest)
-    rests = [[rest]] + exchanged(rest, count, *in_vmem(gate))
+    rests = [[rest]] + exchanged(rest, corner, count, *in_vmem(gate))
     half = count // 2
     slots = half * capacity
 
@@ -523,10 +515,8 @@
     near_partner = swap(near, "exp", 1)
     plan, arrays = planned(0, rests[:half])
     hidden = expert_half(0, slot, weight, gate, up, plan, arrays, None, slots)
-    late = [len(pieces) for pieces in rests[half:]]
-    *pieces, hidden = lax.optimization_barrier((*(piece for part in rests[half:] for piece in part), hidden))
-    pieces = iter(pieces)
-    plan, arrays = planned(half, [[next(pieces) for _ in range(n)] for n in late])
+    *rests[-1][-2:], hidden = lax.optimization_barrier((*rests[-1][-2:], hidden))
+    plan, arrays = planned(half, rests[half:])
     hidden = expert_half(1, slot, weight, gate, up, plan, arrays, hidden, slots)
     return (attn_out, hidden)
 

time: 99 us -> 94.2 us (0.952)
  starting transfers between devices: 32.8 us -> 29 us
    ppermute x23 -> x26, starting transfers between devices: 32.8 us -> 29 us  [swap(): return lax.ppermute(block, axis, route)]
    ppermute x23 -> x26, waiting for transfers between devices: 40.2 us -> 39.7 us  [swap(): return lax.ppermute(block, axis, route)]
  transfers between devices with their start and end apart: 23 -> 26, of which waited for: 13 -> 11; matrix products, arithmetic and copies ran while one was open for 0% -> 0% of each run, Pallas kernels for 15% -> 16%
where the time goes in v3:
time: 94.2 us; the launch traced here: 94 us
  waiting for transfers between devices  39.7 us (42%)
  starting transfers between devices  29 us (31%)
  Pallas kernels  24.5 us (26%)
    ppermute x26, waiting for transfers between devices, swap(): return lax.ppermute(block, axis, route)  39.7 us
    ppermute x26, starting transfers between devices, swap(): return lax.ppermute(block, axis, route)  29 us
    pallas_call x2, Pallas kernels, expert_half(): pl.pallas_call(functools.partial(expert_kernel, plan, len(arrays), later)...  11.2 us
    pallas_call x1, Pallas kernels, per_device(): pl.pallas_call(load_kernel, in_specs=[hbm, hbm, anywhere], out_specs=[vme...  5.15 us
    pallas_call x1, Pallas kernels, per_device(): pl.pallas_call(inner_kernel, in_specs=[hbm] * 5 + [anywhere], out_specs=[...  2.69 us
    pallas_call x1, Pallas kernels, per_device(): pl.pallas_call(state_kernel, in_specs=[hbm] * 4, out_specs=[vmem] * 2, ou...  2.12 us
  transfers between devices with their start and end apart: 26, of which 11 were waited for; matrix products, arithmetic and copies ran while one was open for 0% of the time, Pallas kernels for 16%

profile of v3, /device:TPU:0, one launch (start us, length us, event | category | flops | bytes accessed | tf_op | source)
XLA Modules:
  0.0 94.0 jit_solution(16484390054767928523)
XLA Ops:
  0.7 2.1 %states.1 = (bf16[1056,128]{1,0:T(8,128)(2,1)S(1)}, bf16[512,3072]{1,0:T(8,128)(2,1)S(1)}) custom-call(bf16[2,128,512]{2,1,0:T(8,128)(2,1)} %k_hbm.3, bf16[2,128,512]{2,1,0:T(8,128)(2,1)} %v_hbm.3, f32[2,4,128]{2,1,0:T(4,128)} %refs_2_.1, bf16[512,3072]{1,0:T(8,128)(2,1)} %proj_hbm.1), custom_call_target="tpu_custom_call" | custom-call | flops 67108864 | bytes 786432 | tf_op jit(solution)/shard_map/states/pallas_call | solution.py:389
  2.8 0.5 collective-permute-start.4
  3.3 3.5 %collective-permute-start.2 = (bf16[1056,128]{1,0:T(8,128)(2,1)S(1)}, bf16[1056,128]{1,0:T(8,128)(2,1)S(1)}, u32[]{:S(2)}, u32[]{:S(2)}) collective-permute-start(bf16[1056,128]{1,0:T(8,128)(2,1)S(1)} %get-tuple-element.37.after), channel_id=1, source_target_pairs={{0,24},{8,16},{16,8},{24,0},{1,25},{9,17},{17,9},{25,1},{2,26},{10... | collective-permute-start | bytes 811016 | tf_op jit(solution)/shard_map/ppermute | solution.py:28
  7.5 2.7 %inner.1 = (f32[2,128,512]{2,1,0:T(8,128)S(1)}, bf16[2,128,512]{2,1,0:T(8,128)(2,1)S(1)}, f32[32,3072]{1,0:T(8,128)S(1)}) custom-call(bf16[2,128,512]{2,1,0:T(8,128)(2,1)} %q_hbm.1, bf16[2,128,512]{2,1,0:T(8,128)(2,1)} %k_hbm.3, bf16[2,128,512]{2,1,0:T(8,128)(2,1)} %v_hbm.3, f32[2,4,128]{2,1,0:T(4,128)} %refs_2_.1, bf16[16,2,3072]{2,1,0:T(2,128)(2,1)} %residual_hbm.1, ...), custom_call_target="tpu_custom_call" | custom-call | flops 100663296 | bytes 1310720 | tf_op jit(solution)/shard_map/inner/pallas_call | solution.py:409
  10.2 4.0 %collective-permute-done.2.refs_6_ = bf16[1056,128]{1,0:T(8,128)(2,1)S(1)} collective-permute-done((bf16[1056,128]{1,0:T(8,128)(2,1)S(1)}, bf16[1056,128]{1,0:T(8,128)(2,1)S(1)}, u32[]{:S(2)}, u32[]{:S(2)}) %collective-permute-start.2) | collective-permute-done | bytes 270368 | tf_op jit(solution)/shard_map/ppermute | solution.py:28
  14.2 5.5 %collective-permute-done.1.refs_5_ = bf16[1056,128]{1,0:T(8,128)(2,1)S(1)} collective-permute-done((bf16[1056,128]{1,0:T(8,128)(2,1)S(1)}, bf16[1056,128]{1,0:T(8,128)(2,1)S(1)}, u32[]{:S(2)}, u32[]{:S(2)}) %collective-permute-start.1) | collective-permute-done | bytes 270368 | tf_op jit(solution)/shard_map/ppermute | solution.py:28
  20.0 0.9 attend.1
  21.0 1.3 %collective-permute-done.3.partner_ref = bf16[128,512]{1,0:T(8,128)(2,1)S(1)} collective-permute-done((bf16[128,512]{1,0:T(8,128)(2,1)S(1)}, bf16[128,512]{1,0:T(8,128)(2,1)S(1)}, u32[]{:S(2)}, u32[]{:S(2)}) %collective-permute-start.3) | collective-permute-done | bytes 131104 | tf_op jit(solution)/shard_map/ppermute | solution.py:28
  22.4 1.0 %project.1 = (f32[32,3072]{1,0:T(8,128)S(1)}, bf16[32,3072]{1,0:T(8,128)(2,1)S(1)}, bf16[32,3072]{1,0:T(8,128)(2,1)S(1)}, bf16[32,3072]{1,0:T(8,128)(2,1)S(1)}) custom-call(bf16[128,512]{1,0:T(8,128)(2,1)S(1)} %get-tuple-element.40.own_ref, bf16[128,512]{1,0:T(8,128)(2,1)S(1)} %collective-permute-done.3.partner_ref, ...), custom_call_target="tpu_custom_call" | custom-call | flops 805306368 | bytes 8650752 | tf_op jit(solution)/shard_map/project/pallas_call | solution.py:440
  23.4 1.6 %collective-permute-start.5 = (bf16[32,3072]{1,0:T(8,128)(2,1)S(1)}, bf16[32,3072]{1,0:T(8,128)(2,1)S(1)}, u32[]{:S(2)}, u32[]{:S(2)}) collective-permute-start(bf16[32,3072]{1,0:T(8,128)(2,1)S(1)} %get-tuple-element.51), channel_id=1, source_target_pairs={{0,2},{1,3},{2,0},{3,1},{4,6},{5,7},{6,4},{7,5},{8,10},{9,11},{10,... | collective-permute-start | bytes 589832 | tf_op jit(solution)/shard_map/ppermute | solution.py:28
  25.0 2.6 %collective-permute-start.6 = (bf16[32,3072]{1,0:T(8,128)(2,1)S(1)}, bf16[32,3072]{1,0:T(8,128)(2,1)S(1)}, u32[]{:S(2)}, u32[]{:S(2)}) collective-permute-start(bf16[32,3072]{1,0:T(8,128)(2,1)S(1)} %get-tuple-element.52), channel_id=1, source_target_pairs={{0,4},{1,5},{2,6},{3,7},{4,0},{5,1},{6,2},{7,3},{8,12},{9,13},{10,... | collective-permute-start | bytes 589832 | tf_op jit(solution)/shard_map/ppermute | solution.py:28
  28.1 5.9 %collective-permute-done.5.refs_0_ = bf16[32,3072]{1,0:T(8,128)(2,1)S(1)} collective-permute-done((bf16[32,3072]{1,0:T(8,128)(2,1)S(1)}, bf16[32,3072]{1,0:T(8,128)(2,1)S(1)}, u32[]{:S(2)}, u32[]{:S(2)}) %collective-permute-start.5) | collective-permute-done | bytes 196640 | tf_op jit(solution)/shard_map/ppermute | solution.py:28
  34.0 8.1 %collective-permute-done.6.refs_1_ = bf16[32,3072]{1,0:T(8,128)(2,1)S(1)} collective-permute-done((bf16[32,3072]{1,0:T(8,128)(2,1)S(1)}, bf16[32,3072]{1,0:T(8,128)(2,1)S(1)}, u32[]{:S(2)}, u32[]{:S(2)}) %collective-permute-start.6) | collective-permute-done | bytes 196640 | tf_op jit(solution)/shard_map/ppermute | solution.py:28
  42.4 2.5 %collective-permute-start.13 = (bf16[32,3072]{1,0:T(8,128)(2,1)S(1)}, bf16[32,3072]{1,0:T(8,128)(2,1)S(1)}, u32[]{:S(2)}, u32[]{:S(2)}) collective-permute-start(bf16[32,3072]{1,0:T(8,128)(2,1)S(1)} %get-tuple-element.57.refs_0_), channel_id=1, source_target_pairs={{0,6},{1,7},{2,4},{3,5},{4,2},{5,3},{6,0},{7,1},{8,14},{9,15},{10,... | collective-permute-start | bytes 589832 | tf_op jit(solution)/shard_map/ppermute | solution.py:28
  44.9 4.9 %collective-permute-start.12 = (bf16[32,3072]{1,0:T(8,128)(2,1)S(1)}, bf16[32,3072]{1,0:T(8,128)(2,1)S(1)}, u32[]{:S(2)}, u32[]{:S(2)}) collective-permute-start(bf16[32,3072]{1,0:T(8,128)(2,1)S(1)} %get-tuple-element.57.refs_0_), channel_id=1, source_target_pairs={{0,4},{1,5},{2,6},{3,7},{4,0},{5,1},{6,2},{7,3},{8,12},{9,13},{10,... | collective-permute-start | bytes 589832 | tf_op jit(solution)/shard_map/ppermute | solution.py:28
  49.9 1.7 %collective-permute-start.10 = (bf16[32,3072]{1,0:T(8,128)(2,1)S(1)}, bf16[32,3072]{1,0:T(8,128)(2,1)S(1)}, u32[]{:S(2)}, u32[]{:S(2)}) collective-permute-start(bf16[32,3072]{1,0:T(8,128)(2,1)S(1)} %get-tuple-element.57.refs_0_), channel_id=1, source_target_pairs={{0,24},{8,16},{16,8},{24,0},{1,25},{9,17},{17,9},{25,1},{2,26},{10... | collective-permute-start | bytes 589832 | tf_op jit(solution)/shard_map/ppermute | solution.py:28
  51.6 1.3 %collective-permute-start.9 = (bf16[32,3072]{1,0:T(8,128)(2,1)S(1)}, bf16[32,3072]{1,0:T(8,128)(2,1)S(1)}, u32[]{:S(2)}, u32[]{:S(2)}) collective-permute-start(bf16[32,3072]{1,0:T(8,128)(2,1)S(1)} %get-tuple-element.57.refs_0_), channel_id=1, source_target_pairs={{0,16},{8,24},{16,0},{24,8},{1,17},{9,25},{17,1},{25,9},{2,18},{10... | collective-permute-start | bytes 589832 | tf_op jit(solution)/shard_map/ppermute | solution.py:28
  52.9 0.5 collective-permute-start.8
  53.4 0.8 place.1.refs_7_
  54.2 7.9 %collective-permute-done.12.refs_5_ = bf16[32,3072]{1,0:T(8,128)(2,1)S(1)} collective-permute-done((bf16[32,3072]{1,0:T(8,128)(2,1)S(1)}, bf16[32,3072]{1,0:T(8,128)(2,1)S(1)}, u32[]{:S(2)}, u32[]{:S(2)}) %collective-permute-start.12) | collective-permute-done | bytes 196640 | tf_op jit(solution)/shard_map/ppermute | solution.py:28
  62.2 1.5 %collective-permute-start.16 = (bf16[96,3072]{1,0:T(8,128)(2,1)S(1)}, bf16[96,3072]{1,0:T(8,128)(2,1)S(1)}, u32[]{:S(2)}, u32[]{:S(2)}) collective-permute-start(bf16[96,3072]{1,0:T(8,128)(2,1)S(1)} %get-tuple-element.58.after.refs_2_), channel_id=1, source_target_pairs={{0,16},{8,24},{16,0},{24,8},{1,17},{9,25},{17,1},{25,9},{2,18},{10... | collective-permute-start | bytes 1769480 | tf_op jit(solution)/shard_map/ppermute | solution.py:28
  63.7 0.8 collective-permute-start.15
  64.5 2.6 %collective-permute-start.17 = (bf16[32,3072]{1,0:T(8,128)(2,1)S(1)}, bf16[32,3072]{1,0:T(8,128)(2,1)S(1)}, u32[]{:S(2)}, u32[]{:S(2)}) collective-permute-start(bf16[32,3072]{1,0:T(8,128)(2,1)S(1)} %get-tuple-element.62), channel_id=1, source_target_pairs={{0,2},{1,3},{2,0},{3,1},{4,6},{5,7},{6,4},{7,5},{8,10},{9,11},{10,... | collective-permute-start | bytes 589832 | tf_op jit(solution)/shard_map/ppermute | solution.py:28
  67.2 0.5 collective-permute-start.21
  67.7 5.2 %load.1 = (bf16[1,1152,3072]{2,1,0:T(8,128)(2,1)S(1)}, bf16[1,1152,3072]{2,1,0:T(8,128)(2,1)S(1)}) custom-call(bf16[1,1152,3072]{2,1,0:T(8,128)(2,1)} %gate_hbm.1, bf16[1,1152,3072]{2,1,0:T(8,128)(2,1)} %up_hbm.1, bf16[96,3072]{1,0:T(8,128)(2,1)S(1)} %get-tuple-element.58.after.refs_2_), custom_call_target="tpu_custom_call" | custom-call | flops 1 | bytes 14155776 | tf_op jit(solution)/shard_map/load/pallas_call | solution.py:490
  72.9 4.2 %collective-permute-done.16.two_ref.refs_2_ = bf16[96,3072]{1,0:T(8,128)(2,1)S(1)} collective-permute-done((bf16[96,3072]{1,0:T(8,128)(2,1)S(1)}, bf16[96,3072]{1,0:T(8,128)(2,1)S(1)}, u32[]{:S(2)}, u32[]{:S(2)}) %collective-permute-start.16) | collective-permute-done | bytes 589856 | tf_op jit(solution)/shard_map/ppermute | solution.py:28
  77.1 1.2 %collective-permute-done.15.one_ref.refs_4_ = bf16[96,3072]{1,0:T(8,128)(2,1)S(1)} collective-permute-done((bf16[96,3072]{1,0:T(8,128)(2,1)S(1)}, bf16[96,3072]{1,0:T(8,128)(2,1)S(1)}, u32[]{:S(2)}, u32[]{:S(2)}) %collective-permute-start.15) | collective-permute-done | bytes 589856 | tf_op jit(solution)/shard_map/ppermute | solution.py:28
  78.9 0.6 collective-permute-start.19
  79.5 1.5 %collective-permute-start.20 = (bf16[32,3072]{1,0:T(8,128)(2,1)S(1)}, bf16[32,3072]{1,0:T(8,128)(2,1)S(1)}, u32[]{:S(2)}, u32[]{:S(2)}) collective-permute-start(bf16[32,3072]{1,0:T(8,128)(2,1)S(1)} %get-tuple-element.67), channel_id=1, source_target_pairs={{0,8},{8,0},{16,24},{24,16},{1,9},{9,1},{17,25},{25,17},{2,10},{10... | collective-permute-start | bytes 589832 | tf_op jit(solution)/shard_map/ppermute | solution.py:28
  81.0 5.6 %experts.2.refs_10_ = f32[1,1152,512]{2,1,0:T(8,128)} custom-call(s32[4,256]{1,0:T(4,128)S(1)} %get-tuple-element.55.slot_ref, f32[4,256]{1,0:T(4,128)S(1)} %get-tuple-element.56.weight_ref, bf16[1,1152,3072]{2,1,0:T(8,128)(2,1)S(1)} %get-tuple-element.59.after.gate_ref, bf16[1,1152,3072]{2,1,0:T(8,128)(2,1)S(1)} %get-tuple-element.60.up_ref, ...), custom_call_target="tpu_custom_call" | custom-call | flops 3623878656 | bytes 1572864 | tf_op jit(solution)/shard_map/experts/pallas_call | solution.py:345
  87.2 0.9 collective-permute-done.24.refs_8_
  88.4 5.6 %experts.3 = f32[1,1152,512]{2,1,0:T(8,128)} custom-call(s32[4,256]{1,0:T(4,128)S(1)} %get-tuple-element.55.slot_ref, f32[4,256]{1,0:T(4,128)S(1)} %get-tuple-element.56.weight_ref, bf16[1,1152,3072]{2,1,0:T(8,128)(2,1)S(1)} %get-tuple-element.59.after.gate_ref, ...), custom_call_target="tpu_custom_call", output_to_operand_aliasing={{}: (14, {})} | custom-call | flops 3623878656 | bytes 1572864 | tf_op jit(solution)/shard_map/experts/pallas_call | solution.py:345
  (42 shorter events, 3.5 us)
Async XLA Ops:
  0.6 19.4 %copy-start = (f32[2,4,128]{2,1,0:T(4,128)S(1)}, f32[2,4,128]{2,1,0:T(4,128)}, u32[]{:S(2)}) copy-start(f32[2,4,128]{2,1,0:T(4,128)} %refs_2_.1) | copy-start | bytes 12292
  0.6 19.4 %copy-start.4 = (f32[512]{0:T(512)S(1)}, f32[512]{0:T(512)}, u32[]{:S(2)}) copy-start(f32[512]{0:T(512)} %param.17) | copy-start | bytes 6148
  2.8 19.6 %collective-permute-start.4 = (bf16[512,3072]{1,0:T(8,128)(2,1)S(1)}, bf16[512,3072]{1,0:T(8,128)(2,1)S(1)}, u32[]{:S(2)}, u32[]{:S(2)}) collective-permute-start(bf16[512,3072]{1,0:T(8,128)(2,1)S(1)} %get-tuple-element.42.proj_ref), channel_id=1, source_target_pairs={{0,1},{1,0},{2,3},{3,2},{4,5},{5,4},{6,7},{7,6},{8,9},{9,8},{10,11... | collective-permute-start | bytes 9437192 | tf_op jit(solution)/shard_map/ppermute | solution.py:28
  3.3 10.9 %collective-permute-start.2 = (bf16[1056,128]{1,0:T(8,128)(2,1)S(1)}, bf16[1056,128]{1,0:T(8,128)(2,1)S(1)}, u32[]{:S(2)}, u32[]{:S(2)}) collective-permute-start(bf16[1056,128]{1,0:T(8,128)(2,1)S(1)} %get-tuple-element.37.after), channel_id=1, source_target_pairs={{0,24},{8,16},{16,8},{24,0},{1,25},{9,17},{17,9},{25,1},{2,26},{10... | collective-permute-start | bytes 811016 | tf_op jit(solution)/shard_map/ppermute | solution.py:28
  6.8 12.9 %collective-permute-start.1 = (bf16[1056,128]{1,0:T(8,128)(2,1)S(1)}, bf16[1056,128]{1,0:T(8,128)(2,1)S(1)}, u32[]{:S(2)}, u32[]{:S(2)}) collective-permute-start(bf16[1056,128]{1,0:T(8,128)(2,1)S(1)} %get-tuple-element.37.after), channel_id=1, source_target_pairs={{0,16},{8,24},{16,0},{24,8},{1,17},{9,25},{17,1},{25,9},{2,18},{10... | collective-permute-start | bytes 811016 | tf_op jit(solution)/shard_map/ppermute | solution.py:28
  7.3 12.7 %collective-permute-start = (bf16[1056,128]{1,0:T(8,128)(2,1)S(1)}, bf16[1056,128]{1,0:T(8,128)(2,1)S(1)}, u32[]{:S(2)}, u32[]{:S(2)}) collective-permute-start(bf16[1056,128]{1,0:T(8,128)(2,1)S(1)} %get-tuple-element.37.after), channel_id=1, source_target_pairs={{0,8},{8,0},{16,24},{24,16},{1,9},{9,1},{17,25},{25,17},{2,10},{10... | collective-permute-start | bytes 811016 | tf_op jit(solution)/shard_map/ppermute | solution.py:28
  20.9 1.4 %collective-permute-start.3 = (bf16[128,512]{1,0:T(8,128)(2,1)S(1)}, bf16[128,512]{1,0:T(8,128)(2,1)S(1)}, u32[]{:S(2)}, u32[]{:S(2)}) collective-permute-start(bf16[128,512]{1,0:T(8,128)(2,1)S(1)} %get-tuple-element.41), channel_id=1, source_target_pairs={{0,1},{1,0},{2,3},{3,2},{4,5},{5,4},{6,7},{7,6},{8,9},{9,8},{10,11... | collective-permute-start | bytes 393224 | tf_op jit(solution)/shard_map/ppermute | solution.py:28
  22.4 5.5 %copy-start.2 = (s32[512,2,2]{0,2,1:T(2,128)S(1)}, s32[512,2,2]{0,2,1:T(2,128)}, u32[]{:S(2)}) copy-start(s32[512,2,2]{0,2,1:T(2,128)} %param.20) | copy-start | bytes 24580
  22.4 5.5 %copy-start.3 = (f32[512,2,2]{0,2,1:T(2,128)S(1)}, f32[512,2,2]{0,2,1:T(2,128)}, u32[]{:S(2)}) copy-start(f32[512,2,2]{0,2,1:T(2,128)} %param.21) | copy-start | bytes 24580
  22.4 19.8 %copy-start.1 = (f32[3072]{0:T(1024)S(1)}, f32[3072]{0:T(1024)}, u32[]{:S(2)}) copy-start(f32[3072]{0:T(1024)} %param.19) | copy-start | bytes 36868
  23.4 10.6 %collective-permute-start.5 = (bf16[32,3072]{1,0:T(8,128)(2,1)S(1)}, bf16[32,3072]{1,0:T(8,128)(2,1)S(1)}, u32[]{:S(2)}, u32[]{:S(2)}) collective-permute-start(bf16[32,3072]{1,0:T(8,128)(2,1)S(1)} %get-tuple-element.51), channel_id=1, source_target_pairs={{0,2},{1,3},{2,0},{3,1},{4,6},{5,7},{6,4},{7,5},{8,10},{9,11},{10,... | collective-permute-start | bytes 589832 | tf_op jit(solution)/shard_map/ppermute | solution.py:28
  25.0 17.1 %collective-permute-start.6 = (bf16[32,3072]{1,0:T(8,128)(2,1)S(1)}, bf16[32,3072]{1,0:T(8,128)(2,1)S(1)}, u32[]{:S(2)}, u32[]{:S(2)}) collective-permute-start(bf16[32,3072]{1,0:T(8,128)(2,1)S(1)} %get-tuple-element.52), channel_id=1, source_target_pairs={{0,4},{1,5},{2,6},{3,7},{4,0},{5,1},{6,2},{7,3},{8,12},{9,13},{10,... | collective-permute-start | bytes 589832 | tf_op jit(solution)/shard_map/ppermute | solution.py:28
  27.6 14.5 %collective-permute-start.7 = (bf16[32,3072]{1,0:T(8,128)(2,1)S(1)}, bf16[32,3072]{1,0:T(8,128)(2,1)S(1)}, u32[]{:S(2)}, u32[]{:S(2)}) collective-permute-start(bf16[32,3072]{1,0:T(8,128)(2,1)S(1)} %get-tuple-element.53), channel_id=1, source_target_pairs={{0,6},{1,7},{2,4},{3,5},{4,2},{5,3},{6,0},{7,1},{8,14},{9,15},{10,... | collective-permute-start | bytes 589832 | tf_op jit(solution)/shard_map/ppermute | solution.py:28
  42.4 10.5 %collective-permute-start.13 = (bf16[32,3072]{1,0:T(8,128)(2,1)S(1)}, bf16[32,3072]{1,0:T(8,128)(2,1)S(1)}, u32[]{:S(2)}, u32[]{:S(2)}) collective-permute-start(bf16[32,3072]{1,0:T(8,128)(2,1)S(1)} %get-tuple-element.57.refs_0_), channel_id=1, source_target_pairs={{0,6},{1,7},{2,4},{3,5},{4,2},{5,3},{6,0},{7,1},{8,14},{9,15},{10,... | collective-permute-start | bytes 589832 | tf_op jit(solution)/shard_map/ppermute | solution.py:28
  44.9 17.2 %collective-permute-start.12 = (bf16[32,3072]{1,0:T(8,128)(2,1)S(1)}, bf16[32,3072]{1,0:T(8,128)(2,1)S(1)}, u32[]{:S(2)}, u32[]{:S(2)}) collective-permute-start(bf16[32,3072]{1,0:T(8,128)(2,1)S(1)} %get-tuple-element.57.refs_0_), channel_id=1, source_target_pairs={{0,4},{1,5},{2,6},{3,7},{4,0},{5,1},{6,2},{7,3},{8,12},{9,13},{10,... | collective-permute-start | bytes 589832 | tf_op jit(solution)/shard_map/ppermute | solution.py:28
  49.8 12.3 %collective-permute-start.11 = (bf16[32,3072]{1,0:T(8,128)(2,1)S(1)}, bf16[32,3072]{1,0:T(8,128)(2,1)S(1)}, u32[]{:S(2)}, u32[]{:S(2)}) collective-permute-start(bf16[32,3072]{1,0:T(8,128)(2,1)S(1)} %get-tuple-element.57.refs_0_), channel_id=1, source_target_pairs={{0,2},{1,3},{2,0},{3,1},{4,6},{5,7},{6,4},{7,5},{8,10},{9,11},{10,... | collective-permute-start | bytes 589832 | tf_op jit(solution)/shard_map/ppermute | solution.py:28
  49.9 12.2 %collective-permute-start.10 = (bf16[32,3072]{1,0:T(8,128)(2,1)S(1)}, bf16[32,3072]{1,0:T(8,128)(2,1)S(1)}, u32[]{:S(2)}, u32[]{:S(2)}) collective-permute-start(bf16[32,3072]{1,0:T(8,128)(2,1)S(1)} %get-tuple-element.57.refs_0_), channel_id=1, source_target_pairs={{0,24},{8,16},{16,8},{24,0},{1,25},{9,17},{17,9},{25,1},{2,26},{10... | collective-permute-start | bytes 589832 | tf_op jit(solution)/shard_map/ppermute | solution.py:28
  51.6 10.5 %collective-permute-start.9 = (bf16[32,3072]{1,0:T(8,128)(2,1)S(1)}, bf16[32,3072]{1,0:T(8,128)(2,1)S(1)}, u32[]{:S(2)}, u32[]{:S(2)}) collective-permute-start(bf16[32,3072]{1,0:T(8,128)(2,1)S(1)} %get-tuple-element.57.refs_0_), channel_id=1, source_target_pairs={{0,16},{8,24},{16,0},{24,8},{1,17},{9,25},{17,1},{25,9},{2,18},{10... | collective-permute-start | bytes 589832 | tf_op jit(solution)/shard_map/ppermute | solution.py:28
  52.9 9.3 %collective-permute-start.8 = (bf16[32,3072]{1,0:T(8,128)(2,1)S(1)}, bf16[32,3072]{1,0:T(8,128)(2,1)S(1)}, u32[]{:S(2)}, u32[]{:S(2)}) collective-permute-start(bf16[32,3072]{1,0:T(8,128)(2,1)S(1)} %get-tuple-element.57.refs_0_), channel_id=1, source_target_pairs={{0,8},{8,0},{16,24},{24,16},{1,9},{9,1},{17,25},{25,17},{2,10},{10... | collective-permute-start | bytes 589832 | tf_op jit(solution)/shard_map/ppermute | solution.py:28
  62.2 14.8 %collective-permute-start.16 = (bf16[96,3072]{1,0:T(8,128)(2,1)S(1)}, bf16[96,3072]{1,0:T(8,128)(2,1)S(1)}, u32[]{:S(2)}, u32[]{:S(2)}) collective-permute-start(bf16[96,3072]{1,0:T(8,128)(2,1)S(1)} %get-tuple-element.58.after.refs_2_), channel_id=1, source_target_pairs={{0,16},{8,24},{16,0},{24,8},{1,17},{9,25},{17,1},{25,9},{2,18},{10... | collective-permute-start | bytes 1769480 | tf_op jit(solution)/shard_map/ppermute | solution.py:28
  63.7 14.5 %collective-permute-start.15 = (bf16[96,3072]{1,0:T(8,128)(2,1)S(1)}, bf16[96,3072]{1,0:T(8,128)(2,1)S(1)}, u32[]{:S(2)}, u32[]{:S(2)}) collective-permute-start(bf16[96,3072]{1,0:T(8,128)(2,1)S(1)} %get-tuple-element.58.after.refs_2_), channel_id=1, source_target_pairs={{0,8},{8,0},{16,24},{24,16},{1,9},{9,1},{17,25},{25,17},{2,10},{10... | collective-permute-start | bytes 1769480 | tf_op jit(solution)/shard_map/ppermute | solution.py:28
  64.5 8.3 %collective-permute-start.17 = (bf16[32,3072]{1,0:T(8,128)(2,1)S(1)}, bf16[32,3072]{1,0:T(8,128)(2,1)S(1)}, u32[]{:S(2)}, u32[]{:S(2)}) collective-permute-start(bf16[32,3072]{1,0:T(8,128)(2,1)S(1)} %get-tuple-element.62), channel_id=1, source_target_pairs={{0,2},{1,3},{2,0},{3,1},{4,6},{5,7},{6,4},{7,5},{8,10},{9,11},{10,... | collective-permute-start | bytes 589832 | tf_op jit(solution)/shard_map/ppermute | solution.py:28
  67.2 12.3 %collective-permute-start.14 = (bf16[128,3072]{1,0:T(8,128)(2,1)S(1)}, bf16[128,3072]{1,0:T(8,128)(2,1)S(1)}, u32[]{:S(2)}, u32[]{:S(2)}) collective-permute-start(bf16[128,3072]{1,0:T(8,128)(2,1)S(1)} %get-tuple-element.61.refs_0_), channel_id=1, source_target_pairs={{0,1},{1,0},{2,3},{3,2},{4,5},{5,4},{6,7},{7,6},{8,9},{9,8},{10,11... | collective-permute-start | bytes 2359304 | tf_op jit(solution)/shard_map/ppermute | solution.py:28
  67.2 11.7 %collective-permute-start.21 = (bf16[96,3072]{1,0:T(8,128)(2,1)S(1)}, bf16[96,3072]{1,0:T(8,128)(2,1)S(1)}, u32[]{:S(2)}, u32[]{:S(2)}) collective-permute-start(bf16[96,3072]{1,0:T(8,128)(2,1)S(1)} %get-tuple-element.58.after.refs_2_), channel_id=1, source_target_pairs={{0,1},{1,0},{2,3},{3,2},{4,5},{5,4},{6,7},{7,6},{8,9},{9,8},{10,11... | collective-permute-start | bytes 1769480 | tf_op jit(solution)/shard_map/ppermute | solution.py:28
  78.2 2.8 %collective-permute-start.22 = (bf16[96,3072]{1,0:T(8,128)(2,1)S(1)}, bf16[96,3072]{1,0:T(8,128)(2,1)S(1)}, u32[]{:S(2)}, u32[]{:S(2)}) collective-permute-start(bf16[96,3072]{1,0:T(8,128)(2,1)S(1)} %collective-permute-done.15.one_ref.refs_4_), channel_id=1, source_target_pairs={{0,1},{1,0},{2,3},{3,2},{4,5},{5,4},{6,7},{7,6},{8,9},{9,8},{10,11... | collective-permute-start | bytes 1769480 | tf_op jit(solution)/shard_map/ppermute | solution.py:28
  78.3 8.9 %collective-permute-start.18 = (bf16[96,3072]{1,0:T(8,128)(2,1)S(1)}, bf16[96,3072]{1,0:T(8,128)(2,1)S(1)}, u32[]{:S(2)}, u32[]{:S(2)}) collective-permute-start(bf16[96,3072]{1,0:T(8,128)(2,1)S(1)} %collective-permute-done.16.two_ref.refs_2_), channel_id=1, source_target_pairs={{0,1},{1,0},{2,3},{3,2},{4,5},{5,4},{6,7},{7,6},{8,9},{9,8},{10,11... | collective-permute-start | bytes 1769480 | tf_op jit(solution)/shard_map/ppermute | solution.py:28
  78.8 8.4 %collective-permute-start.23 = (bf16[32,3072]{1,0:T(8,128)(2,1)S(1)}, bf16[32,3072]{1,0:T(8,128)(2,1)S(1)}, u32[]{:S(2)}, u32[]{:S(2)}) collective-permute-start(bf16[32,3072]{1,0:T(8,128)(2,1)S(1)} %collective-permute-done.17.corner_ref.refs_4_), channel_id=1, source_target_pairs={{0,1},{1,0},{2,3},{3,2},{4,5},{5,4},{6,7},{7,6},{8,9},{9,8},{10,11... | collective-permute-start | bytes 589832 | tf_op jit(solution)/shard_map/ppermute | solution.py:28
  78.9 7.7 %collective-permute-start.19 = (bf16[32,3072]{1,0:T(8,128)(2,1)S(1)}, bf16[32,3072]{1,0:T(8,128)(2,1)S(1)}, u32[]{:S(2)}, u32[]{:S(2)}) collective-permute-start(bf16[32,3072]{1,0:T(8,128)(2,1)S(1)} %get-tuple-element.66), channel_id=1, source_target_pairs={{0,16},{8,24},{16,0},{24,8},{1,17},{9,25},{17,1},{25,9},{2,18},{10... | collective-permute-start | bytes 589832 | tf_op jit(solution)/shard_map/ppermute | solution.py:28
  79.5 7.1 %collective-permute-start.20 = (bf16[32,3072]{1,0:T(8,128)(2,1)S(1)}, bf16[32,3072]{1,0:T(8,128)(2,1)S(1)}, u32[]{:S(2)}, u32[]{:S(2)}) collective-permute-start(bf16[32,3072]{1,0:T(8,128)(2,1)S(1)} %get-tuple-element.67), channel_id=1, source_target_pairs={{0,8},{8,0},{16,24},{24,16},{1,9},{9,1},{17,25},{25,17},{2,10},{10... | collective-permute-start | bytes 589832 | tf_op jit(solution)/shard_map/ppermute | solution.py:28
  86.6 1.5 %collective-permute-start.24 = (bf16[32,3072]{1,0:T(8,128)(2,1)S(1)}, bf16[32,3072]{1,0:T(8,128)(2,1)S(1)}, u32[]{:S(2)}, u32[]{:S(2)}) collective-permute-start(bf16[32,3072]{1,0:T(8,128)(2,1)S(1)} %collective-permute-done.19.refs_5_), channel_id=1, source_target_pairs={{0,1},{1,0},{2,3},{3,2},{4,5},{5,4},{6,7},{7,6},{8,9},{9,8},{10,11... | collective-permute-start | bytes 589832 | tf_op jit(solution)/shard_map/ppermute | solution.py:28
  86.7 1.7 %collective-permute-start.25 = (bf16[32,3072]{1,0:T(8,128)(2,1)S(1)}, bf16[32,3072]{1,0:T(8,128)(2,1)S(1)}, u32[]{:S(2)}, u32[]{:S(2)}) collective-permute-start(bf16[32,3072]{1,0:T(8,128)(2,1)S(1)} %collective-permute-done.20.refs_6_), channel_id=1, source_target_pairs={{0,1},{1,0},{2,3},{3,2},{4,5},{5,4},{6,7},{7,6},{8,9},{9,8},{10,11... | collective-permute-start | bytes 589832 | tf_op jit(solution)/shard_map/ppermute | solution.py:28

commit v4 on v3

--- a/solution.py
+++ b/solution.py
@@ -255,7 +255,7 @@
     return [[one], [two], [corner, swap(low, "seq", 2), swap(high, "seq", 1)]]
 
 
-def route_kernel(capacity, own, routes_ref, weights_ref, slot_ref, weight_ref, a_ref, b_ref):
+def route_kernel(own, routes_ref, weights_ref, slot_ref, weight_ref, a_ref, b_ref):
     seqs, tops, _ = routes_ref.shape
     count, total = slot_ref.shape
     size = total // seqs
@@ -282,8 +282,7 @@
     rank = mm(chosen, (origin <= row).astype(BF)) - 1.0
     same = (origin == row).astype(BF)
     picked = mm(chosen, same) > 0.5
-    block = lax.broadcasted_iota(jnp.int32, (count, total), 0) % (count // 2)
-    a_ref[...] = jnp.where(picked, rank.astype(jnp.int32) + block * capacity, -1)
+    a_ref[...] = jnp.where(picked, rank.astype(jnp.int32), -1)
     high, middle, low = thirds(weight)
     b_ref[...] = mm(high, same) + mm(middle, same) + mm(low, same)
     for d in range(count):
@@ -291,35 +290,54 @@
         weight_ref[d : d + 1, :] = b_ref[pl.ds(me ^ d, 1), :]
 
 
-def expert_kernel(plan, arrays, later, slot_ref, weight_ref, gate_ref, up_ref, *refs):
+def expert_kernel(plan, arrays, lines, slot_ref, weight_ref, gate_ref, up_ref, *refs):
     array_refs, (out_hbm, rows_ref, out_ref, sems) = refs[:arrays], refs[-4:]
-    count, total = slot_ref.shape
-    blocks = count // 2
-    first_block = later * blocks
+    total = slot_ref.shape[1]
+    blocks = len(lines)
     slots, width = rows_ref.shape
+    me = lax.axis_index("seq")
     tile = out_ref.shape[1]
+    capacity = slots // blocks
+    apart = capacity % 128 == 0
     numbers = lax.broadcasted_iota(jnp.int32, (slots, total), 0)
-    lines = range(first_block, first_block + blocks)
-    pick = jnp.concatenate([(slot_ref[n : n + 1, :] == numbers).astype(BF) for n in lines], axis=1)
-    weight = jnp.concatenate([weight_ref[n : n + 1, :] for n in lines], axis=1)
+    picks = []
+    for n, line in enumerate(lines):
+        place = n if apart else (me ^ line) % blocks
+        slot = slot_ref[line : line + 1, :]
+        picks.append((jnp.where(slot < 0, slot, slot + place * capacity) == numbers).astype(BF))
+    weight = jnp.concatenate([weight_ref[line : line + 1, :] for line in lines], axis=1)
     parts = [part.astype(F32) for part in thirds(weight)] + [jnp.zeros((5, blocks * total), F32)]
-    scale = jnp.sum(mm(jnp.concatenate(parts, axis=0).astype(BF), pick, NT), axis=0, keepdims=True)
+    parts = jnp.concatenate(parts, axis=0).astype(BF)
+    scale = jnp.sum(mm(parts, jnp.concatenate(picks, axis=1), NT), axis=0, keepdims=True)
 
     step = column_tile(width)
-    for n in range(width // step):
-        part = slice(n * step, (n + 1) * step)
-        rows = [array_refs[number][first : first + height, part] for number, first, height in plan]
-        rows_ref[:, part] = mm(pick, jnp.concatenate(rows, axis=0)).astype(BF)
-    side = (lax.axis_index("seq") // blocks) ^ later
-    columns = pl.ds(pl.multiple_of(side * slots, slots), slots)
+    for at in range(0, width, step):
+        part = slice(at, at + step)
+        rows = []
+        for pieces in plan:
+            rows.append([array_refs[m][first : first + height, part] for m, first, height in pieces])
+        if apart:
+            for n, pick in enumerate(picks):
+                own = slice(n * capacity, (n + 1) * capacity)
+                rows_ref[own, part] = mm(pick[own], jnp.concatenate(rows[n], axis=0)).astype(BF)
+        else:
+            rows = jnp.concatenate([piece for pieces in rows for piece in pieces], axis=0)
+            rows_ref[:, part] = mm(jnp.concatenate(picks, axis=1), rows).astype(BF)
+
+    targets = [(slice(0, slots), (me ^ lines[0]) // blocks)]
+    if apart:
+        targets = [(slice(n * capacity, (n + 1) * capacity), me ^ line) for n, line in enumerate(lines)]
     copies = []
     for step in range(out_ref.shape[0]):
         part = slice(step * tile, (step + 1) * tile)
         gate = mm(gate_ref[0, part, :], rows_ref[...], NT)
         up = mm(up_ref[0, part, :], rows_ref[...], NT)
         out_ref[step] = scale * (gate / (1.0 + jnp.exp(-gate))) * up
-        copies.append(pltpu.make_async_copy(out_ref.at[step], out_hbm.at[0, part, columns], sems.at[step]))
-        copies[-1].start()
+        for columns, place in targets:
+            size = columns.stop - columns.start
+            to = out_hbm.at[0, part, pl.ds(pl.multiple_of(place * size, size), size)]
+            copies.append(pltpu.make_async_copy(out_ref.at[step, :, columns], to, sems.at[len(copies)]))
+            copies[-1].start()
     for copy in copies:
         copy.wait()
 
@@ -336,21 +354,22 @@
     return pl.BlockSpec(shape, lambda *_: (0,) * len(shape))
 
 
-def expert_half(later, slot, weight, w_gate, w_up, plan, arrays, previous, slots):
+def experts(lines, capacity, slot, weight, w_gate, w_up, plan, arrays, previous):
     units, width = w_gate.shape[1:]
     tile = max(size for size in range(16, 385, 16) if units % size == 0)
     steps = units // tile
+    slots = len(lines) * capacity
     carried = [] if previous is None else [previous]
     vmem, hbm = pl.BlockSpec(memory_space=pltpu.VMEM), pl.BlockSpec(memory_space=pltpu.HBM)
     return pl.pallas_call(
-        functools.partial(expert_kernel, plan, len(arrays), later),
+        functools.partial(expert_kernel, plan, len(arrays), lines),
         in_specs=[vmem] * (4 + len(arrays)) + [hbm] * len(carried),
         out_specs=hbm,
-        out_shape=jax.ShapeDtypeStruct((1, units, 2 * slots), F32),
+        out_shape=jax.ShapeDtypeStruct((1, units, slot.shape[0] * capacity), F32),
         scratch_shapes=[
             pltpu.VMEM((slots, width), BF),
             pltpu.VMEM((steps, tile, slots), F32),
-            pltpu.SemaphoreType.DMA((steps,)),
+            pltpu.SemaphoreType.DMA((steps * len(lines),)),
         ],
         input_output_aliases={4 + len(arrays): 0} if carried else {},
         compiler_params=params(),
@@ -451,7 +470,7 @@
 
     routes, route_weight, keep = lax.optimization_barrier((routes, route_weight, keep))
     slot, weight = pl.pallas_call(
-        functools.partial(route_kernel, capacity, own),
+        functools.partial(route_kernel, own),
         out_shape=[jax.ShapeDtypeStruct((count, total), jnp.int32), jax.ShapeDtypeStruct((count, total), F32)],
         scratch_shapes=[pltpu.VMEM((count, total), jnp.int32), pltpu.VMEM((count, total), F32)],
         compiler_params=params(),
@@ -466,7 +485,7 @@
         compiler_params=params(),
         cost_estimate=cost(10 * unit * model, 16 * unit * model),
         name="mix",
-    )(keep, residual_rows, norm_gain.reshape(1, model), *got)
+    )(keep, residual_rows, norm_gain.reshape(1, model), *reversed(got))
     attn_out = pl.pallas_call(
         place_kernel,
         out_shape=jax.ShapeDtypeStruct((own, seqs, model), F32),
@@ -497,27 +516,25 @@
         cost_estimate=cost(1, 4 * w_gate.size),
         name="load",
     )(*in_hbm(w_gate, w_up), rest)
+    near_partner = swap(near, "exp", 1)
+
+    def computed(lines, parts, previous):
+        plan, arrays = [], [near, near_partner]
+        for n, pieces in zip(lines, parts):
+            partners = [swap(piece, "exp", 1) for piece in pieces]
+            plan.append([])
+            for k, share in enumerate((pieces, partners)):
+                plan[-1].append((k, n * unit, unit))
+                for piece in share:
+                    plan[-1].append((len(arrays), 0, piece.shape[0]))
+                    arrays.append(piece)
+        return experts(lines, capacity, slot, weight, gate, up, plan, arrays, previous)
+
+    half = count // 2
     rests = [[rest]] + exchanged(rest, corner, count, *in_vmem(gate))
-    half = count // 2
-    slots = half * capacity
-
-    def planned(first, parts):
-        plan, arrays = [], [near, near_partner]
-        for n, pieces in enumerate(parts):
-            partners = [swap(piece, "exp", 1) for piece in pieces]
-            for k, share in enumerate((pieces, partners)):
-                plan.append((k, (first + n) * unit, unit))
-                for piece in share:
-                    plan.append((len(arrays), 0, piece.shape[0]))
-                    arrays.append(piece)
-        return plan, arrays
-
-    near_partner = swap(near, "exp", 1)
-    plan, arrays = planned(0, rests[:half])
-    hidden = expert_half(0, slot, weight, gate, up, plan, arrays, None, slots)
+    hidden = computed(range(half), rests[:half], None)
     *rests[-1][-2:], hidden = lax.optimization_barrier((*rests[-1][-2:], hidden))
-    plan, arrays = planned(half, rests[half:])
-    hidden = expert_half(1, slot, weight, gate, up, plan, arrays, hidden, slots)
+    hidden = computed(range(half, count), rests[half:], hidden)
     return (attn_out, hidden)
 
 

time: 94.2 us -> 92.9 us (0.986)
  transfers between devices with their start and end apart: 26 -> 26, of which waited for: 11 -> 13; matrix products, arithmetic and copies ran while one was open for 0% -> 0% of each run, Pallas kernels for 16% -> 16%
where the time goes in v4:
time: 92.9 us; the launch traced here: 92.7 us
  waiting for transfers between devices  39.6 us (43%)
  starting transfers between devices  28.6 us (31%)
  Pallas kernels  23.7 us (26%)
    ppermute x26, waiting for transfers between devices, swap(): return lax.ppermute(block, axis, route)  39.6 us
    ppermute x26, starting transfers between devices, swap(): return lax.ppermute(block, axis, route)  28.6 us
    pallas_call x2, Pallas kernels, experts(): pl.pallas_call(functools.partial(expert_kernel, plan, len(arrays), lines)...  10.4 us
    pallas_call x1, Pallas kernels, per_device(): pl.pallas_call(load_kernel, in_specs=[hbm, hbm, anywhere], out_specs=[vme...  5.15 us
    pallas_call x1, Pallas kernels, per_device(): pl.pallas_call(inner_kernel, in_specs=[hbm] * 5 + [anywhere], out_specs=[...  2.69 us
    pallas_call x1, Pallas kernels, per_device(): pl.pallas_call(state_kernel, in_specs=[hbm] * 4, out_specs=[vmem] * 2, ou...  2.12 us
  transfers between devices with their start and end apart: 26, of which 13 were waited for; matrix products, arithmetic and copies ran while one was open for 0% of the time, Pallas kernels for 16%

profile of v4, /device:TPU:0, one launch (start us, length us, event | category | flops | bytes accessed | tf_op | source)
XLA Modules:
  0.0 92.7 jit_solution(10067238212681316520)
XLA Ops:
  0.7 2.1 %states.1 = (bf16[1056,128]{1,0:T(8,128)(2,1)S(1)}, bf16[512,3072]{1,0:T(8,128)(2,1)S(1)}) custom-call(bf16[2,128,512]{2,1,0:T(8,128)(2,1)} %k_hbm.3, bf16[2,128,512]{2,1,0:T(8,128)(2,1)} %v_hbm.3, f32[2,4,128]{2,1,0:T(4,128)} %refs_2_.1, bf16[512,3072]{1,0:T(8,128)(2,1)} %proj_hbm.1), custom_call_target="tpu_custom_call" | custom-call | flops 67108864 | bytes 786432 | tf_op jit(solution)/shard_map/states/pallas_call | solution.py:408
  2.8 0.5 collective-permute-start.4
  3.3 3.5 %collective-permute-start.2 = (bf16[1056,128]{1,0:T(8,128)(2,1)S(1)}, bf16[1056,128]{1,0:T(8,128)(2,1)S(1)}, u32[]{:S(2)}, u32[]{:S(2)}) collective-permute-start(bf16[1056,128]{1,0:T(8,128)(2,1)S(1)} %get-tuple-element.37.after), channel_id=1, source_target_pairs={{0,24},{8,16},{16,8},{24,0},{1,25},{9,17},{17,9},{25,1},{2,26},{10... | collective-permute-start | bytes 811016 | tf_op jit(solution)/shard_map/ppermute | solution.py:28
  7.5 2.7 %inner.1 = (f32[2,128,512]{2,1,0:T(8,128)S(1)}, bf16[2,128,512]{2,1,0:T(8,128)(2,1)S(1)}, f32[32,3072]{1,0:T(8,128)S(1)}) custom-call(bf16[2,128,512]{2,1,0:T(8,128)(2,1)} %q_hbm.1, bf16[2,128,512]{2,1,0:T(8,128)(2,1)} %k_hbm.3, bf16[2,128,512]{2,1,0:T(8,128)(2,1)} %v_hbm.3, f32[2,4,128]{2,1,0:T(4,128)} %refs_2_.1, bf16[16,2,3072]{2,1,0:T(2,128)(2,1)} %residual_hbm.1, ...), custom_call_target="tpu_custom_call" | custom-call | flops 100663296 | bytes 1310720 | tf_op jit(solution)/shard_map/inner/pallas_call | solution.py:428
  10.2 4.0 %collective-permute-done.2.refs_6_ = bf16[1056,128]{1,0:T(8,128)(2,1)S(1)} collective-permute-done((bf16[1056,128]{1,0:T(8,128)(2,1)S(1)}, bf16[1056,128]{1,0:T(8,128)(2,1)S(1)}, u32[]{:S(2)}, u32[]{:S(2)}) %collective-permute-start.2) | collective-permute-done | bytes 270368 | tf_op jit(solution)/shard_map/ppermute | solution.py:28
  14.2 5.5 %collective-permute-done.1.refs_5_ = bf16[1056,128]{1,0:T(8,128)(2,1)S(1)} collective-permute-done((bf16[1056,128]{1,0:T(8,128)(2,1)S(1)}, bf16[1056,128]{1,0:T(8,128)(2,1)S(1)}, u32[]{:S(2)}, u32[]{:S(2)}) %collective-permute-start.1) | collective-permute-done | bytes 270368 | tf_op jit(solution)/shard_map/ppermute | solution.py:28
  20.0 0.9 attend.1
  21.0 1.3 %collective-permute-done.3.partner_ref = bf16[128,512]{1,0:T(8,128)(2,1)S(1)} collective-permute-done((bf16[128,512]{1,0:T(8,128)(2,1)S(1)}, bf16[128,512]{1,0:T(8,128)(2,1)S(1)}, u32[]{:S(2)}, u32[]{:S(2)}) %collective-permute-start.3) | collective-permute-done | bytes 131104 | tf_op jit(solution)/shard_map/ppermute | solution.py:28
  22.4 1.0 %project.1 = (f32[32,3072]{1,0:T(8,128)S(1)}, bf16[32,3072]{1,0:T(8,128)(2,1)S(1)}, bf16[32,3072]{1,0:T(8,128)(2,1)S(1)}, bf16[32,3072]{1,0:T(8,128)(2,1)S(1)}) custom-call(bf16[128,512]{1,0:T(8,128)(2,1)S(1)} %get-tuple-element.40.own_ref, bf16[128,512]{1,0:T(8,128)(2,1)S(1)} %collective-permute-done.3.partner_ref, ...), custom_call_target="tpu_custom_call" | custom-call | flops 805306368 | bytes 8650752 | tf_op jit(solution)/shard_map/project/pallas_call | solution.py:459
  23.4 3.7 %collective-permute-start.5 = (bf16[32,3072]{1,0:T(8,128)(2,1)S(1)}, bf16[32,3072]{1,0:T(8,128)(2,1)S(1)}, u32[]{:S(2)}, u32[]{:S(2)}) collective-permute-start(bf16[32,3072]{1,0:T(8,128)(2,1)S(1)} %get-tuple-element.51), channel_id=1, source_target_pairs={{0,6},{1,7},{2,4},{3,5},{4,2},{5,3},{6,0},{7,1},{8,14},{9,15},{10,... | collective-permute-start | bytes 589832 | tf_op jit(solution)/shard_map/ppermute | solution.py:28
  27.0 0.8 collective-permute-start.7
  28.1 5.0 %collective-permute-done.5.refs_0_ = bf16[32,3072]{1,0:T(8,128)(2,1)S(1)} collective-permute-done((bf16[32,3072]{1,0:T(8,128)(2,1)S(1)}, bf16[32,3072]{1,0:T(8,128)(2,1)S(1)}, u32[]{:S(2)}, u32[]{:S(2)}) %collective-permute-start.5) | collective-permute-done | bytes 196640 | tf_op jit(solution)/shard_map/ppermute | solution.py:28
  33.1 10.9 %collective-permute-done.6.refs_1_ = bf16[32,3072]{1,0:T(8,128)(2,1)S(1)} collective-permute-done((bf16[32,3072]{1,0:T(8,128)(2,1)S(1)}, bf16[32,3072]{1,0:T(8,128)(2,1)S(1)}, u32[]{:S(2)}, u32[]{:S(2)}) %collective-permute-start.6) | collective-permute-done | bytes 196640 | tf_op jit(solution)/shard_map/ppermute | solution.py:28
  44.3 2.5 %collective-permute-start.13 = (bf16[32,3072]{1,0:T(8,128)(2,1)S(1)}, bf16[32,3072]{1,0:T(8,128)(2,1)S(1)}, u32[]{:S(2)}, u32[]{:S(2)}) collective-permute-start(bf16[32,3072]{1,0:T(8,128)(2,1)S(1)} %get-tuple-element.57.refs_0_), channel_id=1, source_target_pairs={{0,6},{1,7},{2,4},{3,5},{4,2},{5,3},{6,0},{7,1},{8,14},{9,15},{10,... | collective-permute-start | bytes 589832 | tf_op jit(solution)/shard_map/ppermute | solution.py:28
  46.8 1.9 %collective-permute-start.11 = (bf16[32,3072]{1,0:T(8,128)(2,1)S(1)}, bf16[32,3072]{1,0:T(8,128)(2,1)S(1)}, u32[]{:S(2)}, u32[]{:S(2)}) collective-permute-start(bf16[32,3072]{1,0:T(8,128)(2,1)S(1)} %get-tuple-element.57.refs_0_), channel_id=1, source_target_pairs={{0,2},{1,3},{2,0},{3,1},{4,6},{5,7},{6,4},{7,5},{8,10},{9,11},{10,... | collective-permute-start | bytes 589832 | tf_op jit(solution)/shard_map/ppermute | solution.py:28
  48.7 1.7 %collective-permute-start.10 = (bf16[32,3072]{1,0:T(8,128)(2,1)S(1)}, bf16[32,3072]{1,0:T(8,128)(2,1)S(1)}, u32[]{:S(2)}, u32[]{:S(2)}) collective-permute-start(bf16[32,3072]{1,0:T(8,128)(2,1)S(1)} %get-tuple-element.57.refs_0_), channel_id=1, source_target_pairs={{0,24},{8,16},{16,8},{24,0},{1,25},{9,17},{17,9},{25,1},{2,26},{10... | collective-permute-start | bytes 589832 | tf_op jit(solution)/shard_map/ppermute | solution.py:28
  50.4 1.3 %collective-permute-start.9 = (bf16[32,3072]{1,0:T(8,128)(2,1)S(1)}, bf16[32,3072]{1,0:T(8,128)(2,1)S(1)}, u32[]{:S(2)}, u32[]{:S(2)}) collective-permute-start(bf16[32,3072]{1,0:T(8,128)(2,1)S(1)} %get-tuple-element.57.refs_0_), channel_id=1, source_target_pairs={{0,16},{8,24},{16,0},{24,8},{1,17},{9,25},{17,1},{25,9},{2,18},{10... | collective-permute-start | bytes 589832 | tf_op jit(solution)/shard_map/ppermute | solution.py:28
  51.7 2.4 %collective-permute-done.13.refs_6_ = bf16[32,3072]{1,0:T(8,128)(2,1)S(1)} collective-permute-done((bf16[32,3072]{1,0:T(8,128)(2,1)S(1)}, bf16[32,3072]{1,0:T(8,128)(2,1)S(1)}, u32[]{:S(2)}, u32[]{:S(2)}) %collective-permute-start.13) | collective-permute-done | bytes 196640 | tf_op jit(solution)/shard_map/ppermute | solution.py:28
  54.1 1.5 %collective-permute-start.8 = (bf16[32,3072]{1,0:T(8,128)(2,1)S(1)}, bf16[32,3072]{1,0:T(8,128)(2,1)S(1)}, u32[]{:S(2)}, u32[]{:S(2)}) collective-permute-start(bf16[32,3072]{1,0:T(8,128)(2,1)S(1)} %get-tuple-element.57.refs_0_), channel_id=1, source_target_pairs={{0,8},{8,0},{16,24},{24,16},{1,9},{9,1},{17,25},{25,17},{2,10},{10... | collective-permute-start | bytes 589832 | tf_op jit(solution)/shard_map/ppermute | solution.py:28
  55.6 0.8 place.1.refs_7_
  56.4 5.8 %collective-permute-done.12.refs_5_ = bf16[32,3072]{1,0:T(8,128)(2,1)S(1)} collective-permute-done((bf16[32,3072]{1,0:T(8,128)(2,1)S(1)}, bf16[32,3072]{1,0:T(8,128)(2,1)S(1)}, u32[]{:S(2)}, u32[]{:S(2)}) %collective-permute-start.12) | collective-permute-done | bytes 196640 | tf_op jit(solution)/shard_map/ppermute | solution.py:28
  62.3 1.5 %collective-permute-start.16 = (bf16[96,3072]{1,0:T(8,128)(2,1)S(1)}, bf16[96,3072]{1,0:T(8,128)(2,1)S(1)}, u32[]{:S(2)}, u32[]{:S(2)}) collective-permute-start(bf16[96,3072]{1,0:T(8,128)(2,1)S(1)} %get-tuple-element.58.after.refs_2_), channel_id=1, source_target_pairs={{0,16},{8,24},{16,0},{24,8},{1,17},{9,25},{17,1},{25,9},{2,18},{10... | collective-permute-start | bytes 1769480 | tf_op jit(solution)/shard_map/ppermute | solution.py:28
  63.8 0.8 collective-permute-start.15
  64.6 4.5 %collective-permute-start.17 = (bf16[32,3072]{1,0:T(8,128)(2,1)S(1)}, bf16[32,3072]{1,0:T(8,128)(2,1)S(1)}, u32[]{:S(2)}, u32[]{:S(2)}) collective-permute-start(bf16[32,3072]{1,0:T(8,128)(2,1)S(1)} %get-tuple-element.62), channel_id=1, source_target_pairs={{0,2},{1,3},{2,0},{3,1},{4,6},{5,7},{6,4},{7,5},{8,10},{9,11},{10,... | collective-permute-start | bytes 589832 | tf_op jit(solution)/shard_map/ppermute | solution.py:28
  69.6 5.2 %load.1 = (bf16[1,1152,3072]{2,1,0:T(8,128)(2,1)S(1)}, bf16[1,1152,3072]{2,1,0:T(8,128)(2,1)S(1)}) custom-call(bf16[1,1152,3072]{2,1,0:T(8,128)(2,1)} %gate_hbm.1, bf16[1,1152,3072]{2,1,0:T(8,128)(2,1)} %up_hbm.1, bf16[96,3072]{1,0:T(8,128)(2,1)S(1)} %get-tuple-element.58.after.refs_2_), custom_call_target="tpu_custom_call" | custom-call | flops 1 | bytes 14155776 | tf_op jit(solution)/shard_map/load/pallas_call | solution.py:509
  74.8 1.6 %collective-permute-done.16.two_ref.refs_2_ = bf16[96,3072]{1,0:T(8,128)(2,1)S(1)} collective-permute-done((bf16[96,3072]{1,0:T(8,128)(2,1)S(1)}, bf16[96,3072]{1,0:T(8,128)(2,1)S(1)}, u32[]{:S(2)}, u32[]{:S(2)}) %collective-permute-start.16) | collective-permute-done | bytes 589856 | tf_op jit(solution)/shard_map/ppermute | solution.py:28
  76.4 1.2 %collective-permute-done.15.one_ref.refs_4_ = bf16[96,3072]{1,0:T(8,128)(2,1)S(1)} collective-permute-done((bf16[96,3072]{1,0:T(8,128)(2,1)S(1)}, bf16[96,3072]{1,0:T(8,128)(2,1)S(1)}, u32[]{:S(2)}, u32[]{:S(2)}) %collective-permute-start.15) | collective-permute-done | bytes 589856 | tf_op jit(solution)/shard_map/ppermute | solution.py:28
  78.2 0.6 collective-permute-start.19
  78.8 1.5 %collective-permute-start.20 = (bf16[32,3072]{1,0:T(8,128)(2,1)S(1)}, bf16[32,3072]{1,0:T(8,128)(2,1)S(1)}, u32[]{:S(2)}, u32[]{:S(2)}) collective-permute-start(bf16[32,3072]{1,0:T(8,128)(2,1)S(1)} %get-tuple-element.67), channel_id=1, source_target_pairs={{0,8},{8,0},{16,24},{24,16},{1,9},{9,1},{17,25},{25,17},{2,10},{10... | collective-permute-start | bytes 589832 | tf_op jit(solution)/shard_map/ppermute | solution.py:28
  80.3 5.2 %experts.2.refs_10_ = f32[1,1152,512]{2,1,0:T(8,128)} custom-call(s32[4,256]{1,0:T(4,128)S(1)} %get-tuple-element.55.slot_ref, f32[4,256]{1,0:T(4,128)S(1)} %get-tuple-element.56.weight_ref, bf16[1,1152,3072]{2,1,0:T(8,128)(2,1)S(1)} %get-tuple-element.59.after.gate_ref, bf16[1,1152,3072]{2,1,0:T(8,128)(2,1)S(1)} %get-tuple-element.60.up_ref, ...), custom_call_target="tpu_custom_call" | custom-call | flops 3623878656 | bytes 1572864 | tf_op jit(solution)/shard_map/experts/pallas_call | solution.py:364
  86.3 0.9 collective-permute-done.24.refs_8_
  87.5 5.2 %experts.3 = f32[1,1152,512]{2,1,0:T(8,128)} custom-call(s32[4,256]{1,0:T(4,128)S(1)} %get-tuple-element.55.slot_ref, f32[4,256]{1,0:T(4,128)S(1)} %get-tuple-element.56.weight_ref, bf16[1,1152,3072]{2,1,0:T(8,128)(2,1)S(1)} %get-tuple-element.59.after.gate_ref, ...), custom_call_target="tpu_custom_call", output_to_operand_aliasing={{}: (14, {})} | custom-call | flops 3623878656 | bytes 1572864 | tf_op jit(solution)/shard_map/experts/pallas_call | solution.py:364
  (42 shorter events, 3.9 us)
Async XLA Ops:
  0.6 19.4 %copy-start = (f32[2,4,128]{2,1,0:T(4,128)S(1)}, f32[2,4,128]{2,1,0:T(4,128)}, u32[]{:S(2)}) copy-start(f32[2,4,128]{2,1,0:T(4,128)} %refs_2_.1) | copy-start | bytes 12292
  0.6 19.4 %copy-start.4 = (f32[512]{0:T(512)S(1)}, f32[512]{0:T(512)}, u32[]{:S(2)}) copy-start(f32[512]{0:T(512)} %param.17) | copy-start | bytes 6148
  2.8 19.6 %collective-permute-start.4 = (bf16[512,3072]{1,0:T(8,128)(2,1)S(1)}, bf16[512,3072]{1,0:T(8,128)(2,1)S(1)}, u32[]{:S(2)}, u32[]{:S(2)}) collective-permute-start(bf16[512,3072]{1,0:T(8,128)(2,1)S(1)} %get-tuple-element.42.proj_ref), channel_id=1, source_target_pairs={{0,1},{1,0},{2,3},{3,2},{4,5},{5,4},{6,7},{7,6},{8,9},{9,8},{10,11... | collective-permute-start | bytes 9437192 | tf_op jit(solution)/shard_map/ppermute | solution.py:28
  3.3 10.9 %collective-permute-start.2 = (bf16[1056,128]{1,0:T(8,128)(2,1)S(1)}, bf16[1056,128]{1,0:T(8,128)(2,1)S(1)}, u32[]{:S(2)}, u32[]{:S(2)}) collective-permute-start(bf16[1056,128]{1,0:T(8,128)(2,1)S(1)} %get-tuple-element.37.after), channel_id=1, source_target_pairs={{0,24},{8,16},{16,8},{24,0},{1,25},{9,17},{17,9},{25,1},{2,26},{10... | collective-permute-start | bytes 811016 | tf_op jit(solution)/shard_map/ppermute | solution.py:28
  6.8 12.9 %collective-permute-start.1 = (bf16[1056,128]{1,0:T(8,128)(2,1)S(1)}, bf16[1056,128]{1,0:T(8,128)(2,1)S(1)}, u32[]{:S(2)}, u32[]{:S(2)}) collective-permute-start(bf16[1056,128]{1,0:T(8,128)(2,1)S(1)} %get-tuple-element.37.after), channel_id=1, source_target_pairs={{0,16},{8,24},{16,0},{24,8},{1,17},{9,25},{17,1},{25,9},{2,18},{10... | collective-permute-start | bytes 811016 | tf_op jit(solution)/shard_map/ppermute | solution.py:28
  7.3 12.7 %collective-permute-start = (bf16[1056,128]{1,0:T(8,128)(2,1)S(1)}, bf16[1056,128]{1,0:T(8,128)(2,1)S(1)}, u32[]{:S(2)}, u32[]{:S(2)}) collective-permute-start(bf16[1056,128]{1,0:T(8,128)(2,1)S(1)} %get-tuple-element.37.after), channel_id=1, source_target_pairs={{0,8},{8,0},{16,24},{24,16},{1,9},{9,1},{17,25},{25,17},{2,10},{10... | collective-permute-start | bytes 811016 | tf_op jit(solution)/shard_map/ppermute | solution.py:28
  20.9 1.4 %collective-permute-start.3 = (bf16[128,512]{1,0:T(8,128)(2,1)S(1)}, bf16[128,512]{1,0:T(8,128)(2,1)S(1)}, u32[]{:S(2)}, u32[]{:S(2)}) collective-permute-start(bf16[128,512]{1,0:T(8,128)(2,1)S(1)} %get-tuple-element.41), channel_id=1, source_target_pairs={{0,1},{1,0},{2,3},{3,2},{4,5},{5,4},{6,7},{7,6},{8,9},{9,8},{10,11... | collective-permute-start | bytes 393224 | tf_op jit(solution)/shard_map/ppermute | solution.py:28
  22.4 5.5 %copy-start.2 = (s32[512,2,2]{0,2,1:T(2,128)S(1)}, s32[512,2,2]{0,2,1:T(2,128)}, u32[]{:S(2)}) copy-start(s32[512,2,2]{0,2,1:T(2,128)} %param.20) | copy-start | bytes 24580
  22.4 5.5 %copy-start.3 = (f32[512,2,2]{0,2,1:T(2,128)S(1)}, f32[512,2,2]{0,2,1:T(2,128)}, u32[]{:S(2)}) copy-start(f32[512,2,2]{0,2,1:T(2,128)} %param.21) | copy-start | bytes 24580
  22.4 21.7 %copy-start.1 = (f32[3072]{0:T(1024)S(1)}, f32[3072]{0:T(1024)}, u32[]{:S(2)}) copy-start(f32[3072]{0:T(1024)} %param.19) | copy-start | bytes 36868
  23.4 9.8 %collective-permute-start.5 = (bf16[32,3072]{1,0:T(8,128)(2,1)S(1)}, bf16[32,3072]{1,0:T(8,128)(2,1)S(1)}, u32[]{:S(2)}, u32[]{:S(2)}) collective-permute-start(bf16[32,3072]{1,0:T(8,128)(2,1)S(1)} %get-tuple-element.51), channel_id=1, source_target_pairs={{0,6},{1,7},{2,4},{3,5},{4,2},{5,3},{6,0},{7,1},{8,14},{9,15},{10,... | collective-permute-start | bytes 589832 | tf_op jit(solution)/shard_map/ppermute | solution.py:28
  27.0 17.0 %collective-permute-start.6 = (bf16[32,3072]{1,0:T(8,128)(2,1)S(1)}, bf16[32,3072]{1,0:T(8,128)(2,1)S(1)}, u32[]{:S(2)}, u32[]{:S(2)}) collective-permute-start(bf16[32,3072]{1,0:T(8,128)(2,1)S(1)} %get-tuple-element.52), channel_id=1, source_target_pairs={{0,4},{1,5},{2,6},{3,7},{4,0},{5,1},{6,2},{7,3},{8,12},{9,13},{10,... | collective-permute-start | bytes 589832 | tf_op jit(solution)/shard_map/ppermute | solution.py:28
  27.0 17.0 %collective-permute-start.7 = (bf16[32,3072]{1,0:T(8,128)(2,1)S(1)}, bf16[32,3072]{1,0:T(8,128)(2,1)S(1)}, u32[]{:S(2)}, u32[]{:S(2)}) collective-permute-start(bf16[32,3072]{1,0:T(8,128)(2,1)S(1)} %get-tuple-element.53), channel_id=1, source_target_pairs={{0,2},{1,3},{2,0},{3,1},{4,6},{5,7},{6,4},{7,5},{8,10},{9,11},{10,... | collective-permute-start | bytes 589832 | tf_op jit(solution)/shard_map/ppermute | solution.py:28
  44.3 9.8 %collective-permute-start.13 = (bf16[32,3072]{1,0:T(8,128)(2,1)S(1)}, bf16[32,3072]{1,0:T(8,128)(2,1)S(1)}, u32[]{:S(2)}, u32[]{:S(2)}) collective-permute-start(bf16[32,3072]{1,0:T(8,128)(2,1)S(1)} %get-tuple-element.57.refs_0_), channel_id=1, source_target_pairs={{0,6},{1,7},{2,4},{3,5},{4,2},{5,3},{6,0},{7,1},{8,14},{9,15},{10,... | collective-permute-start | bytes 589832 | tf_op jit(solution)/shard_map/ppermute | solution.py:28
  46.8 15.4 %collective-permute-start.12 = (bf16[32,3072]{1,0:T(8,128)(2,1)S(1)}, bf16[32,3072]{1,0:T(8,128)(2,1)S(1)}, u32[]{:S(2)}, u32[]{:S(2)}) collective-permute-start(bf16[32,3072]{1,0:T(8,128)(2,1)S(1)} %get-tuple-element.57.refs_0_), channel_id=1, source_target_pairs={{0,4},{1,5},{2,6},{3,7},{4,0},{5,1},{6,2},{7,3},{8,12},{9,13},{10,... | collective-permute-start | bytes 589832 | tf_op jit(solution)/shard_map/ppermute | solution.py:28
  46.8 15.4 %collective-permute-start.11 = (bf16[32,3072]{1,0:T(8,128)(2,1)S(1)}, bf16[32,3072]{1,0:T(8,128)(2,1)S(1)}, u32[]{:S(2)}, u32[]{:S(2)}) collective-permute-start(bf16[32,3072]{1,0:T(8,128)(2,1)S(1)} %get-tuple-element.57.refs_0_), channel_id=1, source_target_pairs={{0,2},{1,3},{2,0},{3,1},{4,6},{5,7},{6,4},{7,5},{8,10},{9,11},{10,... | collective-permute-start | bytes 589832 | tf_op jit(solution)/shard_map/ppermute | solution.py:28
  48.7 13.5 %collective-permute-start.10 = (bf16[32,3072]{1,0:T(8,128)(2,1)S(1)}, bf16[32,3072]{1,0:T(8,128)(2,1)S(1)}, u32[]{:S(2)}, u32[]{:S(2)}) collective-permute-start(bf16[32,3072]{1,0:T(8,128)(2,1)S(1)} %get-tuple-element.57.refs_0_), channel_id=1, source_target_pairs={{0,24},{8,16},{16,8},{24,0},{1,25},{9,17},{17,9},{25,1},{2,26},{10... | collective-permute-start | bytes 589832 | tf_op jit(solution)/shard_map/ppermute | solution.py:28
  50.4 11.8 %collective-permute-start.9 = (bf16[32,3072]{1,0:T(8,128)(2,1)S(1)}, bf16[32,3072]{1,0:T(8,128)(2,1)S(1)}, u32[]{:S(2)}, u32[]{:S(2)}) collective-permute-start(bf16[32,3072]{1,0:T(8,128)(2,1)S(1)} %get-tuple-element.57.refs_0_), channel_id=1, source_target_pairs={{0,16},{8,24},{16,0},{24,8},{1,17},{9,25},{17,1},{25,9},{2,18},{10... | collective-permute-start | bytes 589832 | tf_op jit(solution)/shard_map/ppermute | solution.py:28
  54.1 8.1 %collective-permute-start.8 = (bf16[32,3072]{1,0:T(8,128)(2,1)S(1)}, bf16[32,3072]{1,0:T(8,128)(2,1)S(1)}, u32[]{:S(2)}, u32[]{:S(2)}) collective-permute-start(bf16[32,3072]{1,0:T(8,128)(2,1)S(1)} %get-tuple-element.57.refs_0_), channel_id=1, source_target_pairs={{0,8},{8,0},{16,24},{24,16},{1,9},{9,1},{17,25},{25,17},{2,10},{10... | collective-permute-start | bytes 589832 | tf_op jit(solution)/shard_map/ppermute | solution.py:28
  62.3 14.1 %collective-permute-start.16 = (bf16[96,3072]{1,0:T(8,128)(2,1)S(1)}, bf16[96,3072]{1,0:T(8,128)(2,1)S(1)}, u32[]{:S(2)}, u32[]{:S(2)}) collective-permute-start(bf16[96,3072]{1,0:T(8,128)(2,1)S(1)} %get-tuple-element.58.after.refs_2_), channel_id=1, source_target_pairs={{0,16},{8,24},{16,0},{24,8},{1,17},{9,25},{17,1},{25,9},{2,18},{10... | collective-permute-start | bytes 1769480 | tf_op jit(solution)/shard_map/ppermute | solution.py:28
  63.8 13.7 %collective-permute-start.15 = (bf16[96,3072]{1,0:T(8,128)(2,1)S(1)}, bf16[96,3072]{1,0:T(8,128)(2,1)S(1)}, u32[]{:S(2)}, u32[]{:S(2)}) collective-permute-start(bf16[96,3072]{1,0:T(8,128)(2,1)S(1)} %get-tuple-element.58.after.refs_2_), channel_id=1, source_target_pairs={{0,8},{8,0},{16,24},{24,16},{1,9},{9,1},{17,25},{25,17},{2,10},{10... | collective-permute-start | bytes 1769480 | tf_op jit(solution)/shard_map/ppermute | solution.py:28
  64.6 10.2 %collective-permute-start.17 = (bf16[32,3072]{1,0:T(8,128)(2,1)S(1)}, bf16[32,3072]{1,0:T(8,128)(2,1)S(1)}, u32[]{:S(2)}, u32[]{:S(2)}) collective-permute-start(bf16[32,3072]{1,0:T(8,128)(2,1)S(1)} %get-tuple-element.62), channel_id=1, source_target_pairs={{0,2},{1,3},{2,0},{3,1},{4,6},{5,7},{6,4},{7,5},{8,10},{9,11},{10,... | collective-permute-start | bytes 589832 | tf_op jit(solution)/shard_map/ppermute | solution.py:28
  69.1 9.7 %collective-permute-start.14 = (bf16[128,3072]{1,0:T(8,128)(2,1)S(1)}, bf16[128,3072]{1,0:T(8,128)(2,1)S(1)}, u32[]{:S(2)}, u32[]{:S(2)}) collective-permute-start(bf16[128,3072]{1,0:T(8,128)(2,1)S(1)} %get-tuple-element.61.refs_0_), channel_id=1, source_target_pairs={{0,1},{1,0},{2,3},{3,2},{4,5},{5,4},{6,7},{7,6},{8,9},{9,8},{10,11... | collective-permute-start | bytes 2359304 | tf_op jit(solution)/shard_map/ppermute | solution.py:28
  69.1 9.1 %collective-permute-start.21 = (bf16[96,3072]{1,0:T(8,128)(2,1)S(1)}, bf16[96,3072]{1,0:T(8,128)(2,1)S(1)}, u32[]{:S(2)}, u32[]{:S(2)}) collective-permute-start(bf16[96,3072]{1,0:T(8,128)(2,1)S(1)} %get-tuple-element.58.after.refs_2_), channel_id=1, source_target_pairs={{0,1},{1,0},{2,3},{3,2},{4,5},{5,4},{6,7},{7,6},{8,9},{9,8},{10,11... | collective-permute-start | bytes 1769480 | tf_op jit(solution)/shard_map/ppermute | solution.py:28
  77.6 2.8 %collective-permute-start.22 = (bf16[96,3072]{1,0:T(8,128)(2,1)S(1)}, bf16[96,3072]{1,0:T(8,128)(2,1)S(1)}, u32[]{:S(2)}, u32[]{:S(2)}) collective-permute-start(bf16[96,3072]{1,0:T(8,128)(2,1)S(1)} %collective-permute-done.15.one_ref.refs_4_), channel_id=1, source_target_pairs={{0,1},{1,0},{2,3},{3,2},{4,5},{5,4},{6,7},{7,6},{8,9},{9,8},{10,11... | collective-permute-start | bytes 1769480 | tf_op jit(solution)/shard_map/ppermute | solution.py:28
  77.7 8.7 %collective-permute-start.18 = (bf16[96,3072]{1,0:T(8,128)(2,1)S(1)}, bf16[96,3072]{1,0:T(8,128)(2,1)S(1)}, u32[]{:S(2)}, u32[]{:S(2)}) collective-permute-start(bf16[96,3072]{1,0:T(8,128)(2,1)S(1)} %collective-permute-done.16.two_ref.refs_2_), channel_id=1, source_target_pairs={{0,1},{1,0},{2,3},{3,2},{4,5},{5,4},{6,7},{7,6},{8,9},{9,8},{10,11... | collective-permute-start | bytes 1769480 | tf_op jit(solution)/shard_map/ppermute | solution.py:28
  78.2 8.2 %collective-permute-start.23 = (bf16[32,3072]{1,0:T(8,128)(2,1)S(1)}, bf16[32,3072]{1,0:T(8,128)(2,1)S(1)}, u32[]{:S(2)}, u32[]{:S(2)}) collective-permute-start(bf16[32,3072]{1,0:T(8,128)(2,1)S(1)} %collective-permute-done.17.corner_ref.refs_4_), channel_id=1, source_target_pairs={{0,1},{1,0},{2,3},{3,2},{4,5},{5,4},{6,7},{7,6},{8,9},{9,8},{10,11... | collective-permute-start | bytes 589832 | tf_op jit(solution)/shard_map/ppermute | solution.py:28
  78.2 7.3 %collective-permute-start.19 = (bf16[32,3072]{1,0:T(8,128)(2,1)S(1)}, bf16[32,3072]{1,0:T(8,128)(2,1)S(1)}, u32[]{:S(2)}, u32[]{:S(2)}) collective-permute-start(bf16[32,3072]{1,0:T(8,128)(2,1)S(1)} %get-tuple-element.66), channel_id=1, source_target_pairs={{0,16},{8,24},{16,0},{24,8},{1,17},{9,25},{17,1},{25,9},{2,18},{10... | collective-permute-start | bytes 589832 | tf_op jit(solution)/shard_map/ppermute | solution.py:28
  78.8 7.0 %collective-permute-start.20 = (bf16[32,3072]{1,0:T(8,128)(2,1)S(1)}, bf16[32,3072]{1,0:T(8,128)(2,1)S(1)}, u32[]{:S(2)}, u32[]{:S(2)}) collective-permute-start(bf16[32,3072]{1,0:T(8,128)(2,1)S(1)} %get-tuple-element.67), channel_id=1, source_target_pairs={{0,8},{8,0},{16,24},{24,16},{1,9},{9,1},{17,25},{25,17},{2,10},{10... | collective-permute-start | bytes 589832 | tf_op jit(solution)/shard_map/ppermute | solution.py:28
  85.8 1.4 %collective-permute-start.24 = (bf16[32,3072]{1,0:T(8,128)(2,1)S(1)}, bf16[32,3072]{1,0:T(8,128)(2,1)S(1)}, u32[]{:S(2)}, u32[]{:S(2)}) collective-permute-start(bf16[32,3072]{1,0:T(8,128)(2,1)S(1)} %collective-permute-done.19.refs_5_), channel_id=1, source_target_pairs={{0,1},{1,0},{2,3},{3,2},{4,5},{5,4},{6,7},{7,6},{8,9},{9,8},{10,11... | collective-permute-start | bytes 589832 | tf_op jit(solution)/shard_map/ppermute | solution.py:28
  85.8 1.7 %collective-permute-start.25 = (bf16[32,3072]{1,0:T(8,128)(2,1)S(1)}, bf16[32,3072]{1,0:T(8,128)(2,1)S(1)}, u32[]{:S(2)}, u32[]{:S(2)}) collective-permute-start(bf16[32,3072]{1,0:T(8,128)(2,1)S(1)} %collective-permute-done.20.refs_6_), channel_id=1, source_target_pairs={{0,1},{1,0},{2,3},{3,2},{4,5},{5,4},{6,7},{7,6},{8,9},{9,8},{10,11... | collective-permute-start | bytes 589832 | tf_op jit(solution)/shard_map/ppermute | solution.py:28

commit v5 on v4

--- a/solution.py
+++ b/solution.py
@@ -189,7 +189,7 @@
     return own * (2 * ((index // 2) ^ distance) + ((index % 2) ^ flip)) + place
 
 
-def mix_kernel(kept_ref, residual_ref, gain_ref, *refs):
+def mix_kernel(kept_ref, residual_ref, gain_ref, after, *refs):
     mixed_ref, normed_ref = refs[-2:]
     mixed = residual_ref[...] + kept_ref[...]
     for got_ref in refs[:-2]:
@@ -218,14 +218,12 @@
         copy.wait()
 
 
-def gather_kernel(first, second, *refs):
-    near_ref, rest_ref, corner_ref = refs[-3:]
-    for to, sources in ((near_ref, refs[:first]), (rest_ref, refs[first : first + second])):
+def gather_kernel(plans, *refs):
+    for to, plan in zip(refs[-len(plans) :], plans):
         at = 0
-        for source in sources:
-            to[at : at + source.shape[0], :] = source[...]
-            at += source.shape[0]
-    corner_ref[...] = refs[first - 1][...]
+        for number, first, height in plan:
+            to[at : at + height, :] = refs[number][first : first + height, :]
+            at += height
 
 
 def halves_kernel(one_ref, two_ref, corner_ref, after, low_ref, high_ref):
@@ -235,10 +233,9 @@
     high_ref[...] = two_ref[first + half :, :]
 
 
-def exchanged(block, corner, count, after):
-    rows, unit = block.shape[0], corner.shape[0]
-    if count != 4 or unit % 16 != 0 or (rows - unit) % 32 != 0 or rows == unit:
-        return [[swap(block, "seq", d)] for d in range(1, count)]
+def exchanged(block, corner, unit, after):
+    rows, head = block.shape[0], unit // 2
+    half = (rows - head) // 2
     one, two = swap(block, "seq", 1), swap(block, "seq", 2)
     corner = swap(corner, "exp", 2)
     vmem, anywhere = pl.BlockSpec(memory_space=pltpu.VMEM), pl.BlockSpec(memory_space=pl.ANY)
@@ -246,13 +243,18 @@
         halves_kernel,
         in_specs=[vmem] * 3 + [anywhere],
         out_specs=[vmem] * 2,
-        out_shape=[jax.ShapeDtypeStruct(((rows - unit) // 2, block.shape[1]), block.dtype)] * 2,
+        out_shape=[jax.ShapeDtypeStruct((half, block.shape[1]), block.dtype)] * 2,
         compiler_params=params(VMEM_BYTES // 8),
         cost_estimate=cost(1, 4 * block.size),
         name="halves",
     )(one, two, corner, after)
     one, two, low, high = lax.optimization_barrier((one, two, low, high))
-    return [[one], [two], [corner, swap(low, "seq", 2), swap(high, "seq", 1)]]
+    far = [(swap(low, "seq", 2), 0, half), (swap(high, "seq", 1), 0, half)]
+    return [
+        [(corner, 0, head), (one, 0, rows)],
+        [(corner, head, head), (two, 0, rows)],
+        [(corner, 2 * head, unit)] + far,
+    ]
 
 
 def route_kernel(own, routes_ref, weights_ref, slot_ref, weight_ref, a_ref, b_ref):
@@ -479,33 +481,6 @@
     )(jnp.transpose(routes, (1, 2, 0)), jnp.transpose(route_weight, (1, 2, 0)))
 
     keep, slot, weight = lax.optimization_barrier((keep, slot, weight))
-    mixed, normed = pl.pallas_call(
-        mix_kernel,
-        out_shape=[jax.ShapeDtypeStruct((unit, model), F32), jax.ShapeDtypeStruct((unit, model), BF)],
-        compiler_params=params(),
-        cost_estimate=cost(10 * unit * model, 16 * unit * model),
-        name="mix",
-    )(keep, residual_rows, norm_gain.reshape(1, model), *reversed(got))
-    attn_out = pl.pallas_call(
-        place_kernel,
-        out_shape=jax.ShapeDtypeStruct((own, seqs, model), F32),
-        compiler_params=params(VMEM_BYTES // 8),
-        cost_estimate=cost(1, 8 * unit * model),
-        name="place",
-    )(mixed)
-
-    along = [swap(normed, "exp", 2 * d) for d in range(1, line)]
-    across = [normed] + [swap(normed, "seq", d) for d in range(1, count)]
-    rows = [len(arrays) * unit for arrays in (across, along)]
-    near, rest, corner = pl.pallas_call(
-        functools.partial(gather_kernel, count, line - 1),
-        in_specs=[vmem] * (count + line - 1) + [anywhere],
-        out_specs=[vmem] * 3,
-        out_shape=[jax.ShapeDtypeStruct((n, model), BF) for n in (*rows, unit)],
-        compiler_params=params(VMEM_BYTES // 8),
-        cost_estimate=cost(1, 4 * sum(rows) * model),
-        name="gather",
-    )(*across, *along, *in_hbm(attn_out))
     gate, up = pl.pallas_call(
         load_kernel,
         in_specs=[hbm, hbm, anywhere],
@@ -515,26 +490,73 @@
         compiler_params=params(VMEM_BYTES // 8),
         cost_estimate=cost(1, 4 * w_gate.size),
         name="load",
-    )(*in_hbm(w_gate, w_up), rest)
-    near_partner = swap(near, "exp", 1)
-
-    def computed(lines, parts, previous):
-        plan, arrays = [], [near, near_partner]
-        for n, pieces in zip(lines, parts):
-            partners = [swap(piece, "exp", 1) for piece in pieces]
+    )(*in_hbm(w_gate, w_up), keep)
+    mixed, normed = pl.pallas_call(
+        mix_kernel,
+        in_specs=[vmem] * 3 + [anywhere] + [vmem] * (line - 1),
+        out_shape=[jax.ShapeDtypeStruct((unit, model), F32), jax.ShapeDtypeStruct((unit, model), BF)],
+        compiler_params=params(),
+        cost_estimate=cost(10 * unit * model, 16 * unit * model),
+        name="mix",
+    )(keep, residual_rows, norm_gain.reshape(1, model), *in_vmem(gate), *reversed(got))
+    attn_out = pl.pallas_call(
+        place_kernel,
+        out_shape=jax.ShapeDtypeStruct((own, seqs, model), F32),
+        compiler_params=params(VMEM_BYTES // 8),
+        cost_estimate=cost(1, 8 * unit * model),
+        name="place",
+    )(mixed)
+
+    along = [swap(normed, "exp", 2 * d) for d in range(1, line)]
+    across = [normed] + [swap(normed, "seq", d) for d in range(1, count)]
+    arrays = along[:1] + across[1:] + along[1:] + [normed]
+
+    def parts_of(some, first=0):
+        return [(next(n for n, a in enumerate(arrays) if a is one), first, unit - first) for one in some]
+
+    plans = [parts_of(across), parts_of(along)]
+    head = unit // 2
+    square = count == 4 and unit % 32 == 0 and line > 2
+    if square:
+        plans.append(parts_of(along[:1], head) + parts_of(along[1:]))
+        plans.append([(n, 0, head) for n, *_ in parts_of(across[1:3])] + parts_of(across[3:]))
+    rows = [sum(height for _, _, height in plan) for plan in plans]
+    near, rest, *going = pl.pallas_call(
+        functools.partial(gather_kernel, plans),
+        in_specs=[vmem] * len(arrays) + [anywhere],
+        out_specs=[vmem] * len(plans),
+        out_shape=[jax.ShapeDtypeStruct((n, model), BF) for n in rows],
+        compiler_params=params(VMEM_BYTES // 8),
+        cost_estimate=cost(1, 4 * sum(rows) * model),
+        name="gather",
+    )(*arrays, *in_hbm(attn_out))
+    def computed(lines, blocks, previous):
+        plan, arrays = [], []
+        for n, pieces in zip(lines, blocks):
             plan.append([])
-            for k, share in enumerate((pieces, partners)):
-                plan[-1].append((k, n * unit, unit))
-                for piece in share:
-                    plan[-1].append((len(arrays), 0, piece.shape[0]))
-                    arrays.append(piece)
-        return experts(lines, capacity, slot, weight, gate, up, plan, arrays, previous)
+            for partner in (False, True):
+                for piece, first, height in [(near, n * unit, unit)] + pieces:
+                    number = next((m for m, one in enumerate(arrays) if one is piece), len(arrays))
+                    if number == len(arrays):
+                        arrays.append(piece)
+                    plan[-1].append((2 * number + partner, first, height))
+        for piece in arrays:
+            if not any(one is piece for one, _ in swapped):
+                swapped.append((piece, swap(piece, "exp", 1)))
+        both = [pair for piece in arrays for pair in next(pair for pair in swapped if pair[0] is piece)]
+        return experts(lines, capacity, slot, weight, gate, up, plan, both, previous)
 
     half = count // 2
-    rests = [[rest]] + exchanged(rest, corner, count, *in_vmem(gate))
-    hidden = computed(range(half), rests[:half], None)
-    *rests[-1][-2:], hidden = lax.optimization_barrier((*rests[-1][-2:], hidden))
-    hidden = computed(range(half, count), rests[half:], hidden)
+    swapped = []
+    blocks = [[(rest, 0, rest.shape[0])]]
+    if square:
+        blocks += exchanged(*going, unit, *in_vmem(gate))
+    else:
+        blocks += [[(swap(rest, "seq", d), 0, rest.shape[0])] for d in range(1, count)]
+    hidden = computed(range(half), blocks[:half], None)
+    *last, hidden = lax.optimization_barrier((*(piece for piece, *_ in blocks[-1][-2:]), hidden))
+    blocks[-1][-2:] = [(piece, *place) for piece, (_, *place) in zip(last, blocks[-1][-2:])]
+    hidden = computed(range(half, count), blocks[half:], hidden)
     return (attn_out, hidden)
 
 

time: 92.9 us -> 90.8 us (0.977)
  waiting for transfers between devices: 39.6 us -> 37.5 us
    ppermute x26, waiting for transfers between devices: 39.6 us -> 37.5 us  [swap(): return lax.ppermute(block, axis, route)]
  transfers between devices with their start and end apart: 26 -> 26, of which waited for: 13 -> 12; matrix products, arithmetic and copies ran while one was open for 0% -> 0% of each run, Pallas kernels for 16% -> 17%
where the time goes in v5:
time: 90.8 us; the launch traced here: 90.7 us
  waiting for transfers between devices  37.5 us (41%)
  starting transfers between devices  28.5 us (31%)
  Pallas kernels  23.8 us (26%)
    ppermute x26, waiting for transfers between devices, swap(): return lax.ppermute(block, axis, route)  37.5 us
    ppermute x26, starting transfers between devices, swap(): return lax.ppermute(block, axis, route)  28.5 us
    pallas_call x2, Pallas kernels, experts(): pl.pallas_call(functools.partial(expert_kernel, plan, len(arrays), lines)...  10.4 us
    pallas_call x1, Pallas kernels, per_device(): pl.pallas_call(load_kernel, in_specs=[hbm, hbm, anywhere], out_specs=[vme...  5.18 us
    pallas_call x1, Pallas kernels, per_device(): pl.pallas_call(inner_kernel, in_specs=[hbm] * 5 + [anywhere], out_specs=[...  2.69 us
    pallas_call x1, Pallas kernels, per_device(): pl.pallas_call(state_kernel, in_specs=[hbm] * 4, out_specs=[vmem] * 2, ou...  2.12 us
  transfers between devices with their start and end apart: 26, of which 12 were waited for; matrix products, arithmetic and copies ran while one was open for 0% of the time, Pallas kernels for 17%

profile of v5, /device:TPU:0, one launch (start us, length us, event | category | flops | bytes accessed | tf_op | source)
XLA Modules:
  0.0 90.7 jit_solution(15208571198326767145)
XLA Ops:
  0.7 2.1 %states.1 = (bf16[1056,128]{1,0:T(8,128)(2,1)S(1)}, bf16[512,3072]{1,0:T(8,128)(2,1)S(1)}) custom-call(bf16[2,128,512]{2,1,0:T(8,128)(2,1)} %k_hbm.3, bf16[2,128,512]{2,1,0:T(8,128)(2,1)} %v_hbm.3, f32[2,4,128]{2,1,0:T(4,128)} %refs_2_.1, bf16[512,3072]{1,0:T(8,128)(2,1)} %proj_hbm.1), custom_call_target="tpu_custom_call" | custom-call | flops 67108864 | bytes 786432 | tf_op jit(solution)/shard_map/states/pallas_call | solution.py:410
  3.3 3.5 %collective-permute-start.2 = (bf16[1056,128]{1,0:T(8,128)(2,1)S(1)}, bf16[1056,128]{1,0:T(8,128)(2,1)S(1)}, u32[]{:S(2)}, u32[]{:S(2)}) collective-permute-start(bf16[1056,128]{1,0:T(8,128)(2,1)S(1)} %get-tuple-element.38.after), channel_id=1, source_target_pairs={{0,24},{8,16},{16,8},{24,0},{1,25},{9,17},{17,9},{25,1},{2,26},{10... | collective-permute-start | bytes 811016 | tf_op jit(solution)/shard_map/ppermute | solution.py:28
  7.5 2.7 %inner.1 = (f32[2,128,512]{2,1,0:T(8,128)S(1)}, bf16[2,128,512]{2,1,0:T(8,128)(2,1)S(1)}, f32[32,3072]{1,0:T(8,128)S(1)}) custom-call(bf16[2,128,512]{2,1,0:T(8,128)(2,1)} %q_hbm.1, bf16[2,128,512]{2,1,0:T(8,128)(2,1)} %k_hbm.3, bf16[2,128,512]{2,1,0:T(8,128)(2,1)} %v_hbm.3, f32[2,4,128]{2,1,0:T(4,128)} %refs_2_.1, bf16[16,2,3072]{2,1,0:T(2,128)(2,1)} %residual_hbm.1, ...), custom_call_target="tpu_custom_call" | custom-call | flops 100663296 | bytes 1310720 | tf_op jit(solution)/shard_map/inner/pallas_call | solution.py:430
  10.2 4.0 %collective-permute-done.2.refs_6_ = bf16[1056,128]{1,0:T(8,128)(2,1)S(1)} collective-permute-done((bf16[1056,128]{1,0:T(8,128)(2,1)S(1)}, bf16[1056,128]{1,0:T(8,128)(2,1)S(1)}, u32[]{:S(2)}, u32[]{:S(2)}) %collective-permute-start.2) | collective-permute-done | bytes 270368 | tf_op jit(solution)/shard_map/ppermute | solution.py:28
  14.2 5.5 %collective-permute-done.1.refs_5_ = bf16[1056,128]{1,0:T(8,128)(2,1)S(1)} collective-permute-done((bf16[1056,128]{1,0:T(8,128)(2,1)S(1)}, bf16[1056,128]{1,0:T(8,128)(2,1)S(1)}, u32[]{:S(2)}, u32[]{:S(2)}) %collective-permute-start.1) | collective-permute-done | bytes 270368 | tf_op jit(solution)/shard_map/ppermute | solution.py:28
  20.0 0.9 %attend.1 = (bf16[128,512]{1,0:T(8,128)(2,1)S(1)}, bf16[128,512]{1,0:T(8,128)(2,1)S(1)}) custom-call(bf16[2,128,512]{2,1,0:T(8,128)(2,1)S(1)} %get-tuple-element.39.refs_0_, f32[2,128,512]{2,1,0:T(8,128)S(1)} %get-tuple-element.40.refs_1_, f32[2,4,128]{2,1,0:T(4,128)S(1)} %copy-done, f32[1,512]{1,0:T(1,128)S(1)} %bitcast.7, ...), custom_call_target="tpu_custom_call" | custom-call | flops 100663296 | bytes 1310720 | tf_op jit(solution)/shard_map/attend/pallas_call | solution.py:451
  21.0 1.3 %collective-permute-done.3.partner_ref = bf16[128,512]{1,0:T(8,128)(2,1)S(1)} collective-permute-done((bf16[128,512]{1,0:T(8,128)(2,1)S(1)}, bf16[128,512]{1,0:T(8,128)(2,1)S(1)}, u32[]{:S(2)}, u32[]{:S(2)}) %collective-permute-start.3) | collective-permute-done | bytes 131104 | tf_op jit(solution)/shard_map/ppermute | solution.py:28
  22.4 1.0 %project.1 = (f32[32,3072]{1,0:T(8,128)S(1)}, bf16[32,3072]{1,0:T(8,128)(2,1)S(1)}, bf16[32,3072]{1,0:T(8,128)(2,1)S(1)}, bf16[32,3072]{1,0:T(8,128)(2,1)S(1)}) custom-call(bf16[128,512]{1,0:T(8,128)(2,1)S(1)} %get-tuple-element.41.own_ref, bf16[128,512]{1,0:T(8,128)(2,1)S(1)} %collective-permute-done.3.partner_ref, ...), custom_call_target="tpu_custom_call" | custom-call | flops 805306368 | bytes 8650752 | tf_op jit(solution)/shard_map/project/pallas_call | solution.py:461
  23.4 3.7 %collective-permute-start.5 = (bf16[32,3072]{1,0:T(8,128)(2,1)S(1)}, bf16[32,3072]{1,0:T(8,128)(2,1)S(1)}, u32[]{:S(2)}, u32[]{:S(2)}) collective-permute-start(bf16[32,3072]{1,0:T(8,128)(2,1)S(1)} %get-tuple-element.53), channel_id=1, source_target_pairs={{0,6},{1,7},{2,4},{3,5},{4,2},{5,3},{6,0},{7,1},{8,14},{9,15},{10,... | collective-permute-start | bytes 589832 | tf_op jit(solution)/shard_map/ppermute | solution.py:28
  27.0 0.8 collective-permute-start.7
  28.1 5.2 %load.1 = (bf16[1,1152,3072]{2,1,0:T(8,128)(2,1)S(1)}, bf16[1,1152,3072]{2,1,0:T(8,128)(2,1)S(1)}) custom-call(bf16[1,1152,3072]{2,1,0:T(8,128)(2,1)} %gate_hbm.1, bf16[1,1152,3072]{2,1,0:T(8,128)(2,1)} %up_hbm.1, f32[32,3072]{1,0:T(8,128)S(1)} %get-tuple-element.50.after.kept_ref), custom_call_target="tpu_custom_call" | custom-call | flops 1 | bytes 14155776 | tf_op jit(solution)/shard_map/load/pallas_call | solution.py:484
  33.3 10.8 %collective-permute-done.6.refs_1_ = bf16[32,3072]{1,0:T(8,128)(2,1)S(1)} collective-permute-done((bf16[32,3072]{1,0:T(8,128)(2,1)S(1)}, bf16[32,3072]{1,0:T(8,128)(2,1)S(1)}, u32[]{:S(2)}, u32[]{:S(2)}) %collective-permute-start.6) | collective-permute-done | bytes 196640 | tf_op jit(solution)/shard_map/ppermute | solution.py:28
  44.3 2.5 %collective-permute-start.13 = (bf16[32,3072]{1,0:T(8,128)(2,1)S(1)}, bf16[32,3072]{1,0:T(8,128)(2,1)S(1)}, u32[]{:S(2)}, u32[]{:S(2)}) collective-permute-start(bf16[32,3072]{1,0:T(8,128)(2,1)S(1)} %get-tuple-element.60.refs_6_), channel_id=1, source_target_pairs={{0,6},{1,7},{2,4},{3,5},{4,2},{5,3},{6,0},{7,1},{8,14},{9,15},{10,... | collective-permute-start | bytes 589832 | tf_op jit(solution)/shard_map/ppermute | solution.py:28
  46.8 1.7 %collective-permute-start.11 = (bf16[32,3072]{1,0:T(8,128)(2,1)S(1)}, bf16[32,3072]{1,0:T(8,128)(2,1)S(1)}, u32[]{:S(2)}, u32[]{:S(2)}) collective-permute-start(bf16[32,3072]{1,0:T(8,128)(2,1)S(1)} %get-tuple-element.60.refs_6_), channel_id=1, source_target_pairs={{0,24},{8,16},{16,8},{24,0},{1,25},{9,17},{17,9},{25,1},{2,26},{10... | collective-permute-start | bytes 589832 | tf_op jit(solution)/shard_map/ppermute | solution.py:28
  48.5 1.3 %collective-permute-start.10 = (bf16[32,3072]{1,0:T(8,128)(2,1)S(1)}, bf16[32,3072]{1,0:T(8,128)(2,1)S(1)}, u32[]{:S(2)}, u32[]{:S(2)}) collective-permute-start(bf16[32,3072]{1,0:T(8,128)(2,1)S(1)} %get-tuple-element.60.refs_6_), channel_id=1, source_target_pairs={{0,16},{8,24},{16,0},{24,8},{1,17},{9,25},{17,1},{25,9},{2,18},{10... | collective-permute-start | bytes 589832 | tf_op jit(solution)/shard_map/ppermute | solution.py:28
  49.8 0.5 collective-permute-start.9
  50.3 3.7 %collective-permute-done.13.refs_5_ = bf16[32,3072]{1,0:T(8,128)(2,1)S(1)} collective-permute-done((bf16[32,3072]{1,0:T(8,128)(2,1)S(1)}, bf16[32,3072]{1,0:T(8,128)(2,1)S(1)}, u32[]{:S(2)}, u32[]{:S(2)}) %collective-permute-start.13) | collective-permute-done | bytes 196640 | tf_op jit(solution)/shard_map/ppermute | solution.py:28
  54.0 5.9 %collective-permute-start.8 = (bf16[32,3072]{1,0:T(8,128)(2,1)S(1)}, bf16[32,3072]{1,0:T(8,128)(2,1)S(1)}, u32[]{:S(2)}, u32[]{:S(2)}) collective-permute-start(bf16[32,3072]{1,0:T(8,128)(2,1)S(1)} %get-tuple-element.60.refs_6_), channel_id=1, source_target_pairs={{0,2},{1,3},{2,0},{3,1},{4,6},{5,7},{6,4},{7,5},{8,10},{9,11},{10,... | collective-permute-start | bytes 589832 | tf_op jit(solution)/shard_map/ppermute | solution.py:28
  59.9 0.8 place.1.refs_7_
  60.7 1.6 %collective-permute-done.12.refs_4_ = bf16[32,3072]{1,0:T(8,128)(2,1)S(1)} collective-permute-done((bf16[32,3072]{1,0:T(8,128)(2,1)S(1)}, bf16[32,3072]{1,0:T(8,128)(2,1)S(1)}, u32[]{:S(2)}, u32[]{:S(2)}) %collective-permute-start.12) | collective-permute-done | bytes 196640 | tf_op jit(solution)/shard_map/ppermute | solution.py:28
  62.3 2.0 %collective-permute-done.8.refs_0_ = bf16[32,3072]{1,0:T(8,128)(2,1)S(1)} collective-permute-done((bf16[32,3072]{1,0:T(8,128)(2,1)S(1)}, bf16[32,3072]{1,0:T(8,128)(2,1)S(1)}, u32[]{:S(2)}, u32[]{:S(2)}) %collective-permute-start.8) | collective-permute-done | bytes 196640 | tf_op jit(solution)/shard_map/ppermute | solution.py:28
  64.4 1.5 %collective-permute-start.18 = (bf16[80,3072]{1,0:T(8,128)(2,1)S(1)}, bf16[80,3072]{1,0:T(8,128)(2,1)S(1)}, u32[]{:S(2)}, u32[]{:S(2)}) collective-permute-start(bf16[80,3072]{1,0:T(8,128)(2,1)S(1)} %get-tuple-element.63), channel_id=1, source_target_pairs={{0,16},{8,24},{16,0},{24,8},{1,17},{9,25},{17,1},{25,9},{2,18},{10... | collective-permute-start | bytes 1474568 | tf_op jit(solution)/shard_map/ppermute | solution.py:28
  65.9 0.8 collective-permute-start.17
  66.7 1.4 %collective-permute-start.15 = (bf16[64,3072]{1,0:T(8,128)(2,1)S(1)}, bf16[64,3072]{1,0:T(8,128)(2,1)S(1)}, u32[]{:S(2)}, u32[]{:S(2)}) collective-permute-start(bf16[64,3072]{1,0:T(8,128)(2,1)S(1)} %get-tuple-element.62), channel_id=1, source_target_pairs={{0,2},{1,3},{2,0},{3,1},{4,6},{5,7},{6,4},{7,5},{8,10},{9,11},{10,... | collective-permute-start | bytes 1179656 | tf_op jit(solution)/shard_map/ppermute | solution.py:28
  68.6 5.9 %collective-permute-done.15.corner_ref.refs_4_.refs_2_ = bf16[64,3072]{1,0:T(8,128)(2,1)S(1)} collective-permute-done((bf16[64,3072]{1,0:T(8,128)(2,1)S(1)}, bf16[64,3072]{1,0:T(8,128)(2,1)S(1)}, u32[]{:S(2)}, u32[]{:S(2)}) %collective-permute-start.15) | collective-permute-done | bytes 393248 | tf_op jit(solution)/shard_map/ppermute | solution.py:28
  74.5 1.0 %collective-permute-done.17.one_ref.refs_6_ = bf16[80,3072]{1,0:T(8,128)(2,1)S(1)} collective-permute-done((bf16[80,3072]{1,0:T(8,128)(2,1)S(1)}, bf16[80,3072]{1,0:T(8,128)(2,1)S(1)}, u32[]{:S(2)}, u32[]{:S(2)}) %collective-permute-start.17) | collective-permute-done | bytes 491552 | tf_op jit(solution)/shard_map/ppermute | solution.py:28
  76.1 0.6 collective-permute-start.20
  76.7 1.5 %collective-permute-start.21 = (bf16[32,3072]{1,0:T(8,128)(2,1)S(1)}, bf16[32,3072]{1,0:T(8,128)(2,1)S(1)}, u32[]{:S(2)}, u32[]{:S(2)}) collective-permute-start(bf16[32,3072]{1,0:T(8,128)(2,1)S(1)} %get-tuple-element.68), channel_id=1, source_target_pairs={{0,8},{8,0},{16,24},{24,16},{1,9},{9,1},{17,25},{25,17},{2,10},{10... | collective-permute-start | bytes 589832 | tf_op jit(solution)/shard_map/ppermute | solution.py:28
  78.2 5.2 %experts.2.refs_10_ = f32[1,1152,512]{2,1,0:T(8,128)} custom-call(s32[4,256]{1,0:T(4,128)S(1)} %get-tuple-element.57.slot_ref, f32[4,256]{1,0:T(4,128)S(1)} %get-tuple-element.58.weight_ref, bf16[1,1152,3072]{2,1,0:T(8,128)(2,1)S(1)} %get-tuple-element.52.after.gate_ref, bf16[1,1152,3072]{2,1,0:T(8,128)(2,1)S(1)} %get-tuple-element.59.up_ref, ...), custom_call_target="tpu_custom_call" | custom-call | flops 3623878656 | bytes 1572864 | tf_op jit(solution)/shard_map/experts/pallas_call | solution.py:366
  83.5 0.6 collective-permute-start.24
  84.1 1.0 %collective-permute-done.24.refs_7_ = bf16[32,3072]{1,0:T(8,128)(2,1)S(1)} collective-permute-done((bf16[32,3072]{1,0:T(8,128)(2,1)S(1)}, bf16[32,3072]{1,0:T(8,128)(2,1)S(1)}, u32[]{:S(2)}, u32[]{:S(2)}) %collective-permute-start.24) | collective-permute-done | bytes 196640 | tf_op jit(solution)/shard_map/ppermute | solution.py:28
  85.5 5.2 %experts.3 = f32[1,1152,512]{2,1,0:T(8,128)} custom-call(s32[4,256]{1,0:T(4,128)S(1)} %get-tuple-element.57.slot_ref, f32[4,256]{1,0:T(4,128)S(1)} %get-tuple-element.58.weight_ref, bf16[1,1152,3072]{2,1,0:T(8,128)(2,1)S(1)} %get-tuple-element.52.after.gate_ref, ...), custom_call_target="tpu_custom_call", output_to_operand_aliasing={{}: (14, {})} | custom-call | flops 3623878656 | bytes 1572864 | tf_op jit(solution)/shard_map/experts/pallas_call | solution.py:366
  (42 shorter events, 3.8 us)
Async XLA Ops:
  0.6 19.4 %copy-start = (f32[2,4,128]{2,1,0:T(4,128)S(1)}, f32[2,4,128]{2,1,0:T(4,128)}, u32[]{:S(2)}) copy-start(f32[2,4,128]{2,1,0:T(4,128)} %refs_2_.1) | copy-start | bytes 12292
  0.6 19.4 %copy-start.4 = (f32[512]{0:T(512)S(1)}, f32[512]{0:T(512)}, u32[]{:S(2)}) copy-start(f32[512]{0:T(512)} %param.17) | copy-start | bytes 6148
  2.8 19.6 %collective-permute-start.4 = (bf16[512,3072]{1,0:T(8,128)(2,1)S(1)}, bf16[512,3072]{1,0:T(8,128)(2,1)S(1)}, u32[]{:S(2)}, u32[]{:S(2)}) collective-permute-start(bf16[512,3072]{1,0:T(8,128)(2,1)S(1)} %get-tuple-element.43.proj_ref), channel_id=1, source_target_pairs={{0,1},{1,0},{2,3},{3,2},{4,5},{5,4},{6,7},{7,6},{8,9},{9,8},{10,11... | collective-permute-start | bytes 9437192 | tf_op jit(solution)/shard_map/ppermute | solution.py:28
  3.3 10.9 %collective-permute-start.2 = (bf16[1056,128]{1,0:T(8,128)(2,1)S(1)}, bf16[1056,128]{1,0:T(8,128)(2,1)S(1)}, u32[]{:S(2)}, u32[]{:S(2)}) collective-permute-start(bf16[1056,128]{1,0:T(8,128)(2,1)S(1)} %get-tuple-element.38.after), channel_id=1, source_target_pairs={{0,24},{8,16},{16,8},{24,0},{1,25},{9,17},{17,9},{25,1},{2,26},{10... | collective-permute-start | bytes 811016 | tf_op jit(solution)/shard_map/ppermute | solution.py:28
  6.8 12.9 %collective-permute-start.1 = (bf16[1056,128]{1,0:T(8,128)(2,1)S(1)}, bf16[1056,128]{1,0:T(8,128)(2,1)S(1)}, u32[]{:S(2)}, u32[]{:S(2)}) collective-permute-start(bf16[1056,128]{1,0:T(8,128)(2,1)S(1)} %get-tuple-element.38.after), channel_id=1, source_target_pairs={{0,16},{8,24},{16,0},{24,8},{1,17},{9,25},{17,1},{25,9},{2,18},{10... | collective-permute-start | bytes 811016 | tf_op jit(solution)/shard_map/ppermute | solution.py:28
  7.3 12.7 %collective-permute-start = (bf16[1056,128]{1,0:T(8,128)(2,1)S(1)}, bf16[1056,128]{1,0:T(8,128)(2,1)S(1)}, u32[]{:S(2)}, u32[]{:S(2)}) collective-permute-start(bf16[1056,128]{1,0:T(8,128)(2,1)S(1)} %get-tuple-element.38.after), channel_id=1, source_target_pairs={{0,8},{8,0},{16,24},{24,16},{1,9},{9,1},{17,25},{25,17},{2,10},{10... | collective-permute-start | bytes 811016 | tf_op jit(solution)/shard_map/ppermute | solution.py:28
  20.9 1.4 %collective-permute-start.3 = (bf16[128,512]{1,0:T(8,128)(2,1)S(1)}, bf16[128,512]{1,0:T(8,128)(2,1)S(1)}, u32[]{:S(2)}, u32[]{:S(2)}) collective-permute-start(bf16[128,512]{1,0:T(8,128)(2,1)S(1)} %get-tuple-element.42), channel_id=1, source_target_pairs={{0,1},{1,0},{2,3},{3,2},{4,5},{5,4},{6,7},{7,6},{8,9},{9,8},{10,11... | collective-permute-start | bytes 393224 | tf_op jit(solution)/shard_map/ppermute | solution.py:28
  22.4 5.5 %copy-start.2 = (s32[512,2,2]{0,2,1:T(2,128)S(1)}, s32[512,2,2]{0,2,1:T(2,128)}, u32[]{:S(2)}) copy-start(s32[512,2,2]{0,2,1:T(2,128)} %param.20) | copy-start | bytes 24580
  22.4 5.5 %copy-start.3 = (f32[512,2,2]{0,2,1:T(2,128)S(1)}, f32[512,2,2]{0,2,1:T(2,128)}, u32[]{:S(2)}) copy-start(f32[512,2,2]{0,2,1:T(2,128)} %param.21) | copy-start | bytes 24580
  23.4 9.9 %collective-permute-start.5 = (bf16[32,3072]{1,0:T(8,128)(2,1)S(1)}, bf16[32,3072]{1,0:T(8,128)(2,1)S(1)}, u32[]{:S(2)}, u32[]{:S(2)}) collective-permute-start(bf16[32,3072]{1,0:T(8,128)(2,1)S(1)} %get-tuple-element.53), channel_id=1, source_target_pairs={{0,6},{1,7},{2,4},{3,5},{4,2},{5,3},{6,0},{7,1},{8,14},{9,15},{10,... | collective-permute-start | bytes 589832 | tf_op jit(solution)/shard_map/ppermute | solution.py:28
  27.0 17.0 %collective-permute-start.6 = (bf16[32,3072]{1,0:T(8,128)(2,1)S(1)}, bf16[32,3072]{1,0:T(8,128)(2,1)S(1)}, u32[]{:S(2)}, u32[]{:S(2)}) collective-permute-start(bf16[32,3072]{1,0:T(8,128)(2,1)S(1)} %get-tuple-element.54), channel_id=1, source_target_pairs={{0,4},{1,5},{2,6},{3,7},{4,0},{5,1},{6,2},{7,3},{8,12},{9,13},{10,... | collective-permute-start | bytes 589832 | tf_op jit(solution)/shard_map/ppermute | solution.py:28
  27.0 17.0 %collective-permute-start.7 = (bf16[32,3072]{1,0:T(8,128)(2,1)S(1)}, bf16[32,3072]{1,0:T(8,128)(2,1)S(1)}, u32[]{:S(2)}, u32[]{:S(2)}) collective-permute-start(bf16[32,3072]{1,0:T(8,128)(2,1)S(1)} %get-tuple-element.55), channel_id=1, source_target_pairs={{0,2},{1,3},{2,0},{3,1},{4,6},{5,7},{6,4},{7,5},{8,10},{9,11},{10,... | collective-permute-start | bytes 589832 | tf_op jit(solution)/shard_map/ppermute | solution.py:28
  28.1 16.0 %copy-start.1 = (f32[3072]{0:T(1024)S(1)}, f32[3072]{0:T(1024)}, u32[]{:S(2)}) copy-start(f32[3072]{0:T(1024)} %param.19) | copy-start | bytes 36868
  44.3 9.8 %collective-permute-start.13 = (bf16[32,3072]{1,0:T(8,128)(2,1)S(1)}, bf16[32,3072]{1,0:T(8,128)(2,1)S(1)}, u32[]{:S(2)}, u32[]{:S(2)}) collective-permute-start(bf16[32,3072]{1,0:T(8,128)(2,1)S(1)} %get-tuple-element.60.refs_6_), channel_id=1, source_target_pairs={{0,6},{1,7},{2,4},{3,5},{4,2},{5,3},{6,0},{7,1},{8,14},{9,15},{10,... | collective-permute-start | bytes 589832 | tf_op jit(solution)/shard_map/ppermute | solution.py:28
  46.8 15.5 %collective-permute-start.12 = (bf16[32,3072]{1,0:T(8,128)(2,1)S(1)}, bf16[32,3072]{1,0:T(8,128)(2,1)S(1)}, u32[]{:S(2)}, u32[]{:S(2)}) collective-permute-start(bf16[32,3072]{1,0:T(8,128)(2,1)S(1)} %get-tuple-element.60.refs_6_), channel_id=1, source_target_pairs={{0,4},{1,5},{2,6},{3,7},{4,0},{5,1},{6,2},{7,3},{8,12},{9,13},{10,... | collective-permute-start | bytes 589832 | tf_op jit(solution)/shard_map/ppermute | solution.py:28
  46.8 15.5 %collective-permute-start.11 = (bf16[32,3072]{1,0:T(8,128)(2,1)S(1)}, bf16[32,3072]{1,0:T(8,128)(2,1)S(1)}, u32[]{:S(2)}, u32[]{:S(2)}) collective-permute-start(bf16[32,3072]{1,0:T(8,128)(2,1)S(1)} %get-tuple-element.60.refs_6_), channel_id=1, source_target_pairs={{0,24},{8,16},{16,8},{24,0},{1,25},{9,17},{17,9},{25,1},{2,26},{10... | collective-permute-start | bytes 589832 | tf_op jit(solution)/shard_map/ppermute | solution.py:28
  48.5 13.8 %collective-permute-start.10 = (bf16[32,3072]{1,0:T(8,128)(2,1)S(1)}, bf16[32,3072]{1,0:T(8,128)(2,1)S(1)}, u32[]{:S(2)}, u32[]{:S(2)}) collective-permute-start(bf16[32,3072]{1,0:T(8,128)(2,1)S(1)} %get-tuple-element.60.refs_6_), channel_id=1, source_target_pairs={{0,16},{8,24},{16,0},{24,8},{1,17},{9,25},{17,1},{25,9},{2,18},{10... | collective-permute-start | bytes 589832 | tf_op jit(solution)/shard_map/ppermute | solution.py:28
  49.8 12.5 %collective-permute-start.9 = (bf16[32,3072]{1,0:T(8,128)(2,1)S(1)}, bf16[32,3072]{1,0:T(8,128)(2,1)S(1)}, u32[]{:S(2)}, u32[]{:S(2)}) collective-permute-start(bf16[32,3072]{1,0:T(8,128)(2,1)S(1)} %get-tuple-element.60.refs_6_), channel_id=1, source_target_pairs={{0,8},{8,0},{16,24},{24,16},{1,9},{9,1},{17,25},{25,17},{2,10},{10... | collective-permute-start | bytes 589832 | tf_op jit(solution)/shard_map/ppermute | solution.py:28
  54.0 10.3 %collective-permute-start.8 = (bf16[32,3072]{1,0:T(8,128)(2,1)S(1)}, bf16[32,3072]{1,0:T(8,128)(2,1)S(1)}, u32[]{:S(2)}, u32[]{:S(2)}) collective-permute-start(bf16[32,3072]{1,0:T(8,128)(2,1)S(1)} %get-tuple-element.60.refs_6_), channel_id=1, source_target_pairs={{0,2},{1,3},{2,0},{3,1},{4,6},{5,7},{6,4},{7,5},{8,10},{9,11},{10,... | collective-permute-start | bytes 589832 | tf_op jit(solution)/shard_map/ppermute | solution.py:28
  64.4 10.1 %collective-permute-start.18 = (bf16[80,3072]{1,0:T(8,128)(2,1)S(1)}, bf16[80,3072]{1,0:T(8,128)(2,1)S(1)}, u32[]{:S(2)}, u32[]{:S(2)}) collective-permute-start(bf16[80,3072]{1,0:T(8,128)(2,1)S(1)} %get-tuple-element.63), channel_id=1, source_target_pairs={{0,16},{8,24},{16,0},{24,8},{1,17},{9,25},{17,1},{25,9},{2,18},{10... | collective-permute-start | bytes 1474568 | tf_op jit(solution)/shard_map/ppermute | solution.py:28
  65.9 9.5 %collective-permute-start.17 = (bf16[80,3072]{1,0:T(8,128)(2,1)S(1)}, bf16[80,3072]{1,0:T(8,128)(2,1)S(1)}, u32[]{:S(2)}, u32[]{:S(2)}) collective-permute-start(bf16[80,3072]{1,0:T(8,128)(2,1)S(1)} %get-tuple-element.63), channel_id=1, source_target_pairs={{0,8},{8,0},{16,24},{24,16},{1,9},{9,1},{17,25},{25,17},{2,10},{10... | collective-permute-start | bytes 1474568 | tf_op jit(solution)/shard_map/ppermute | solution.py:28
  66.7 7.8 %collective-permute-start.15 = (bf16[64,3072]{1,0:T(8,128)(2,1)S(1)}, bf16[64,3072]{1,0:T(8,128)(2,1)S(1)}, u32[]{:S(2)}, u32[]{:S(2)}) collective-permute-start(bf16[64,3072]{1,0:T(8,128)(2,1)S(1)} %get-tuple-element.62), channel_id=1, source_target_pairs={{0,2},{1,3},{2,0},{3,1},{4,6},{5,7},{6,4},{7,5},{8,10},{9,11},{10,... | collective-permute-start | bytes 1179656 | tf_op jit(solution)/shard_map/ppermute | solution.py:28
  68.1 10.1 %collective-permute-start.14 = (bf16[128,3072]{1,0:T(8,128)(2,1)S(1)}, bf16[128,3072]{1,0:T(8,128)(2,1)S(1)}, u32[]{:S(2)}, u32[]{:S(2)}) collective-permute-start(bf16[128,3072]{1,0:T(8,128)(2,1)S(1)} %get-tuple-element.61.refs_0_), channel_id=1, source_target_pairs={{0,1},{1,0},{2,3},{3,2},{4,5},{5,4},{6,7},{7,6},{8,9},{9,8},{10,11... | collective-permute-start | bytes 2359304 | tf_op jit(solution)/shard_map/ppermute | solution.py:28
  68.1 8.6 %collective-permute-start.22 = (bf16[96,3072]{1,0:T(8,128)(2,1)S(1)}, bf16[96,3072]{1,0:T(8,128)(2,1)S(1)}, u32[]{:S(2)}, u32[]{:S(2)}) collective-permute-start(bf16[96,3072]{1,0:T(8,128)(2,1)S(1)} %get-tuple-element.69.refs_2_), channel_id=1, source_target_pairs={{0,1},{1,0},{2,3},{3,2},{4,5},{5,4},{6,7},{7,6},{8,9},{9,8},{10,11... | collective-permute-start | bytes 1769480 | tf_op jit(solution)/shard_map/ppermute | solution.py:28
  75.5 2.7 %collective-permute-start.23 = (bf16[80,3072]{1,0:T(8,128)(2,1)S(1)}, bf16[80,3072]{1,0:T(8,128)(2,1)S(1)}, u32[]{:S(2)}, u32[]{:S(2)}) collective-permute-start(bf16[80,3072]{1,0:T(8,128)(2,1)S(1)} %collective-permute-done.17.one_ref.refs_6_), channel_id=1, source_target_pairs={{0,1},{1,0},{2,3},{3,2},{4,5},{5,4},{6,7},{7,6},{8,9},{9,8},{10,11... | collective-permute-start | bytes 1474568 | tf_op jit(solution)/shard_map/ppermute | solution.py:28
  75.6 2.6 %collective-permute-start.16 = (bf16[64,3072]{1,0:T(8,128)(2,1)S(1)}, bf16[64,3072]{1,0:T(8,128)(2,1)S(1)}, u32[]{:S(2)}, u32[]{:S(2)}) collective-permute-start(bf16[64,3072]{1,0:T(8,128)(2,1)S(1)} %collective-permute-done.15.corner_ref.refs_4_.refs_2_), channel_id=1, source_target_pairs={{0,1},{1,0},{2,3},{3,2},{4,5},{5,4},{6,7},{7,6},{8,9},{9,8},{10,11... | collective-permute-start | bytes 1179656 | tf_op jit(solution)/shard_map/ppermute | solution.py:28
  76.1 7.3 %collective-permute-start.20 = (bf16[32,3072]{1,0:T(8,128)(2,1)S(1)}, bf16[32,3072]{1,0:T(8,128)(2,1)S(1)}, u32[]{:S(2)}, u32[]{:S(2)}) collective-permute-start(bf16[32,3072]{1,0:T(8,128)(2,1)S(1)} %get-tuple-element.67), channel_id=1, source_target_pairs={{0,16},{8,24},{16,0},{24,8},{1,17},{9,25},{17,1},{25,9},{2,18},{10... | collective-permute-start | bytes 589832 | tf_op jit(solution)/shard_map/ppermute | solution.py:28
  76.7 6.8 %collective-permute-start.21 = (bf16[32,3072]{1,0:T(8,128)(2,1)S(1)}, bf16[32,3072]{1,0:T(8,128)(2,1)S(1)}, u32[]{:S(2)}, u32[]{:S(2)}) collective-permute-start(bf16[32,3072]{1,0:T(8,128)(2,1)S(1)} %get-tuple-element.68), channel_id=1, source_target_pairs={{0,8},{8,0},{16,24},{24,16},{1,9},{9,1},{17,25},{25,17},{2,10},{10... | collective-permute-start | bytes 589832 | tf_op jit(solution)/shard_map/ppermute | solution.py:28
  78.2 5.9 %collective-permute-start.19 = (bf16[80,3072]{1,0:T(8,128)(2,1)S(1)}, bf16[80,3072]{1,0:T(8,128)(2,1)S(1)}, u32[]{:S(2)}, u32[]{:S(2)}) collective-permute-start(bf16[80,3072]{1,0:T(8,128)(2,1)S(1)} %collective-permute-done.18.two_ref.refs_4_), channel_id=1, source_target_pairs={{0,1},{1,0},{2,3},{3,2},{4,5},{5,4},{6,7},{7,6},{8,9},{9,8},{10,11... | collective-permute-start | bytes 1474568 | tf_op jit(solution)/shard_map/ppermute | solution.py:28
  83.5 1.6 %collective-permute-start.24 = (bf16[32,3072]{1,0:T(8,128)(2,1)S(1)}, bf16[32,3072]{1,0:T(8,128)(2,1)S(1)}, u32[]{:S(2)}, u32[]{:S(2)}) collective-permute-start(bf16[32,3072]{1,0:T(8,128)(2,1)S(1)} %collective-permute-done.20.refs_6_), channel_id=1, source_target_pairs={{0,1},{1,0},{2,3},{3,2},{4,5},{5,4},{6,7},{7,6},{8,9},{9,8},{10,11... | collective-permute-start | bytes 589832 | tf_op jit(solution)/shard_map/ppermute | solution.py:28
  84.0 1.4 %collective-permute-start.25 = (bf16[32,3072]{1,0:T(8,128)(2,1)S(1)}, bf16[32,3072]{1,0:T(8,128)(2,1)S(1)}, u32[]{:S(2)}, u32[]{:S(2)}) collective-permute-start(bf16[32,3072]{1,0:T(8,128)(2,1)S(1)} %collective-permute-done.21.refs_8_), channel_id=1, source_target_pairs={{0,1},{1,0},{2,3},{3,2},{4,5},{5,4},{6,7},{7,6},{8,9},{9,8},{10,11... | collective-permute-start | bytes 589832 | tf_op jit(solution)/shard_map/ppermute | solution.py:28

commit v6 on v5

--- a/solution.py
+++ b/solution.py
@@ -61,19 +61,24 @@
 
 
 def state_kernel(k_hbm, v_hbm, decay_hbm, proj_hbm, out_ref, proj_ref, k_ref, v_ref, decay_ref, sems):
-    pairs = ((decay_hbm, decay_ref), (k_hbm, k_ref), (v_hbm, v_ref), (proj_hbm, proj_ref))
+    seqs, heads, size = decay_ref.shape
+    width = k_ref.shape[2] // heads
+    pairs = [(decay_hbm, decay_ref)]
+    for b in range(seqs):
+        pairs += [(k_hbm.at[b], k_ref.at[b]), (v_hbm.at[b], v_ref.at[b])]
+    pairs.append((proj_hbm, proj_ref))
     copies = [pltpu.make_async_copy(source, to, sems.at[n]) for n, (source, to) in enumerate(pairs)]
     for copy in copies:
         copy.start()
-    for copy in copies[:-1]:
-        copy.wait()
-    seqs, heads, size = decay_ref.shape
-    width = k_ref.shape[2] // heads
-    totals = []
+    copies[0].wait()
+    totals, tails = [], []
     for b in range(seqs):
         columns = running_columns(decay_ref[b])
-        tail = jnp.exp(columns[size - 1 : size, :] - columns)
-        totals.append(jnp.broadcast_to(running_rows(decay_ref[b])[:, size - 1 : size], (heads, width)))
+        tails.append(jnp.exp(columns[size - 1 : size, :] - columns))
+        totals.append(jnp.broadcast_to(jnp.sum(decay_ref[b], axis=1, keepdims=True), (heads, width)))
+    for b, tail in enumerate(tails):
+        copies[1 + 2 * b].wait()
+        copies[2 + 2 * b].wait()
         for h in range(heads):
             part = slice(h * width, (h + 1) * width)
             value = v_ref[b, :, part]
@@ -87,7 +92,9 @@
     copies[-1].wait()
 
 
-def inner_kernel(q_hbm, k_hbm, v_hbm, decay_hbm, residual_hbm, after, out_ref, q_ref, rows_ref, *scratch):
+def inner_kernel(line, q_hbm, k_hbm, v_hbm, decay_hbm, residual_hbm, after, *refs):
+    out_ref, q_ref, rows_ref, grown_ref, order_ref = refs[:5]
+    scratch = refs[5:]
     k_ref, v_ref, decay_ref, residual_ref, sems = scratch
     pairs = (
         (decay_hbm, decay_ref),
@@ -99,9 +106,15 @@
     copies = [pltpu.make_async_copy(source, to, sems.at[n]) for n, (source, to) in enumerate(pairs)]
     for copy in copies:
         copy.start()
+    own, seqs, _ = residual_ref.shape
+    index = lax.axis_index("exp")
+    total = order_ref.shape[0]
+    to = lax.broadcasted_iota(jnp.int32, (total, total), 0)
+    source = source_position(to // (total // 2), (to // (seqs * own)) % line, to % own, index, own)
+    source = source + (total // seqs) * ((to // own) % seqs)
+    order_ref[...] = (source == lax.broadcasted_iota(jnp.int32, (total, total), 1)).astype(BF)
     for copy in copies:
         copy.wait()
-    own, seqs, _ = residual_ref.shape
     for b in range(seqs):
         rows_ref[b * own : (b + 1) * own, :] = residual_ref[:, b, :].astype(F32)
     _, heads, size = decay_ref.shape
@@ -110,6 +123,7 @@
     for b in range(seqs):
         columns = running_columns(decay_ref[b])
         rows = running_rows(decay_ref[b])
+        grown_ref[b] = jnp.exp(columns)
         for h in range(heads):
             part = slice(h * width, (h + 1) * width)
             spread = columns[:, h : h + 1] - rows[h : h + 1, :]
@@ -120,15 +134,14 @@
             out_ref[b, :, part] = mm(high, value) + mm(low, value)
 
 
-def attend_kernel(count, line, *refs):
-    q_ref, inner_ref, decay_ref, gain_ref = refs[:4]
-    states = refs[4 : 3 + count]
-    own_ref, partner_ref = refs[3 + count :]
+def attend_kernel(count, *refs):
+    q_ref, inner_ref, grown_ref, order_ref, gain_ref = refs[:5]
+    states = refs[5 : 4 + count]
+    own_ref, partner_ref = refs[4 + count :]
     seqs, size, feat = q_ref.shape
-    heads = decay_ref.shape[1]
+    heads = grown_ref.shape[2]
     width = feat // heads
     me = lax.axis_index("seq")
-    index = lax.axis_index("exp")
     each = seqs * heads
     base = each * width
     totals = []
@@ -144,7 +157,7 @@
         factors.append(jnp.where((me ^ first) < me, jnp.exp(later), 0.0))
     rows = []
     for b in range(seqs):
-        grown = jnp.exp(running_columns(decay_ref[b]))
+        grown = grown_ref[b]
         parts = []
         for h in range(heads):
             part = slice(h * width, (h + 1) * width)
@@ -160,12 +173,7 @@
         rows.append(jnp.concatenate(parts, axis=1))
     attention = jnp.concatenate(rows, axis=0)
     total = seqs * size
-    own = size // (2 * line)
-    to = lax.broadcasted_iota(jnp.int32, (total, total), 0)
-    source = source_position(to // (total // 2), (to // (seqs * own)) % line, to % own, index, own)
-    source = source + size * ((to // own) % seqs)
-    pick = (source == lax.broadcasted_iota(jnp.int32, (total, total), 1)).astype(BF)
-    attention = mm(pick, attention).astype(BF)
+    attention = mm(order_ref[...], attention).astype(BF)
     own_ref[...] = attention[: total // 2, :]
     partner_ref[...] = attention[total // 2 :, :]
 
@@ -419,7 +427,7 @@
             pltpu.VMEM(key_vecs.shape, BF),
             pltpu.VMEM(value_vecs.shape, BF),
             pltpu.VMEM(log_decay.shape, F32),
-            pltpu.SemaphoreType.DMA((4,)),
+            pltpu.SemaphoreType.DMA((2 + 2 * seqs,)),
         ],
         compiler_params=params(),
         cost_estimate=cost(4 * total * feat * width, 6 * total * feat),
@@ -427,14 +435,16 @@
     )(*in_hbm(key_vecs, value_vecs, log_decay, out_proj))
     arrived = [swap(states, "seq", d) for d in range(1, count)]
 
-    inner, query, residual_rows = pl.pallas_call(
-        inner_kernel,
+    inner, query, residual_rows, grown, order = pl.pallas_call(
+        functools.partial(inner_kernel, line),
         in_specs=[hbm] * 5 + [anywhere],
-        out_specs=[vmem] * 3,
+        out_specs=[vmem] * 5,
         out_shape=[
             pltpu.VMEM((seqs, size, feat), F32),
             pltpu.VMEM(queries.shape, BF),
             pltpu.VMEM((unit, model), F32),
+            pltpu.VMEM((seqs, size, heads), F32),
+            pltpu.VMEM((total, total), BF),
         ],
         scratch_shapes=[
             pltpu.VMEM(key_vecs.shape, BF),
@@ -449,14 +459,14 @@
     )(*in_hbm(queries, key_vecs, value_vecs, log_decay, residual), *in_vmem(states))
 
     mine, theirs = pl.pallas_call(
-        functools.partial(attend_kernel, count, line),
-        in_specs=[vmem] * (4 + count - 1),
+        functools.partial(attend_kernel, count),
+        in_specs=[vmem] * (5 + count - 1),
         out_specs=[vmem] * 2,
         out_shape=[jax.ShapeDtypeStruct((total // 2, feat), BF)] * 2,
         compiler_params=params(),
         cost_estimate=cost(6 * total * feat * width, 10 * total * feat),
         name="attend",
-    )(*in_vmem(query, inner), log_decay, head_gain.reshape(1, feat), *arrived)
+    )(*in_vmem(query, inner, grown, order), head_gain.reshape(1, feat), *arrived)
 
     keep, *sends = pl.pallas_call(
         project_kernel,
@@ -498,7 +508,7 @@
         compiler_params=params(),
         cost_estimate=cost(10 * unit * model, 16 * unit * model),
         name="mix",
-    )(keep, residual_rows, norm_gain.reshape(1, model), *in_vmem(gate), *reversed(got))
+    )(keep, residual_rows, norm_gain.reshape(1, model), *in_vmem(gate), *got[1:2], *got[:1], *got[2:])
     attn_out = pl.pallas_call(
         place_kernel,
         out_shape=jax.ShapeDtypeStruct((own, seqs, model), F32),

time: 90.8 us -> 89.9 us (0.990)
  waiting for transfers between devices: 37.5 us -> 30.7 us
  starting transfers between devices: 28.5 us -> 33.8 us
    ppermute x26, waiting for transfers between devices: 37.5 us -> 30.7 us  [swap(): return lax.ppermute(block, axis, route)]
    ppermute x26, starting transfers between devices: 28.5 us -> 33.8 us  [swap(): return lax.ppermute(block, axis, route)]
where the time goes in v6:
time: 89.9 us; the launch traced here: 89.2 us
  starting transfers between devices  33.8 us (38%)
  waiting for transfers between devices  30.7 us (34%)
  Pallas kernels  23.9 us (27%)
    ppermute x26, starting transfers between devices, swap(): return lax.ppermute(block, axis, route)  33.8 us
    ppermute x26, waiting for transfers between devices, swap(): return lax.ppermute(block, axis, route)  30.7 us
    pallas_call x2, Pallas kernels, experts(): pl.pallas_call(functools.partial(expert_kernel, plan, len(arrays), lines)...  10.4 us
    pallas_call x1, Pallas kernels, per_device(): pl.pallas_call(load_kernel, in_specs=[hbm, hbm, anywhere], out_specs=[vme...  5.18 us
    pallas_call x1, Pallas kernels, per_device(): pl.pallas_call(functools.partial(inner_kernel, line), in_specs=[hbm] * 5...  2.7 us
    pallas_call x1, Pallas kernels, per_device(): pl.pallas_call(state_kernel, in_specs=[hbm] * 4, out_specs=[vmem] * 2, ou...  2.24 us
  transfers between devices with their start and end apart: 26, of which 12 were waited for; matrix products, arithmetic and copies ran while one was open for 0% of the time, Pallas kernels for 17%

profile of v6, /device:TPU:0, one launch (start us, length us, event | category | flops | bytes accessed | tf_op | source)
XLA Modules:
  0.0 89.2 jit_solution(12226765983910109006)
XLA Ops:
  0.6 2.2 %states.1 = (bf16[1056,128]{1,0:T(8,128)(2,1)S(1)}, bf16[512,3072]{1,0:T(8,128)(2,1)S(1)}) custom-call(bf16[2,128,512]{2,1,0:T(8,128)(2,1)} %k_hbm.3, bf16[2,128,512]{2,1,0:T(8,128)(2,1)} %v_hbm.3, f32[2,4,128]{2,1,0:T(4,128)} %decay_hbm.3, bf16[512,3072]{1,0:T(8,128)(2,1)} %proj_hbm.1), custom_call_target="tpu_custom_call" | custom-call | flops 67108864 | bytes 786432 | tf_op jit(solution)/shard_map/states/pallas_call | solution.py:418
  2.9 0.5 collective-permute-start.4
  3.4 3.5 %collective-permute-start.2 = (bf16[1056,128]{1,0:T(8,128)(2,1)S(1)}, bf16[1056,128]{1,0:T(8,128)(2,1)S(1)}, u32[]{:S(2)}, u32[]{:S(2)}) collective-permute-start(bf16[1056,128]{1,0:T(8,128)(2,1)S(1)} %get-tuple-element.40.after), channel_id=1, source_target_pairs={{0,24},{8,16},{16,8},{24,0},{1,25},{9,17},{17,9},{25,1},{2,26},{10... | collective-permute-start | bytes 811016 | tf_op jit(solution)/shard_map/ppermute | solution.py:28
  7.6 2.7 %inner.1 = (f32[2,128,512]{2,1,0:T(8,128)S(1)}, bf16[2,128,512]{2,1,0:T(8,128)(2,1)S(1)}, f32[32,3072]{1,0:T(8,128)S(1)}, f32[2,128,4]{2,1,0:T(8,128)S(1)}, bf16[256,256]{1,0:T(8,128)(2,1)S(1)}) custom-call(bf16[2,128,512]{2,1,0:T(8,128)(2,1)} %q_hbm.1, bf16[2,128,512]{2,1,0:T(8,128)(2,1)} %k_hbm.3, bf16[2,128,512]{2,1,0:T(8,128)(2,1)} %v_hbm.3, ...), custom_call_target="tpu_custom_call" | custom-call | flops 100663296 | bytes 1310720 | tf_op jit(solution)/shard_map/inner/pallas_call | solution.py:438
  10.3 4.0 %collective-permute-done.2.refs_7_ = bf16[1056,128]{1,0:T(8,128)(2,1)S(1)} collective-permute-done((bf16[1056,128]{1,0:T(8,128)(2,1)S(1)}, bf16[1056,128]{1,0:T(8,128)(2,1)S(1)}, u32[]{:S(2)}, u32[]{:S(2)}) %collective-permute-start.2) | collective-permute-done | bytes 270368 | tf_op jit(solution)/shard_map/ppermute | solution.py:28
  14.3 5.5 %collective-permute-done.1.refs_6_ = bf16[1056,128]{1,0:T(8,128)(2,1)S(1)} collective-permute-done((bf16[1056,128]{1,0:T(8,128)(2,1)S(1)}, bf16[1056,128]{1,0:T(8,128)(2,1)S(1)}, u32[]{:S(2)}, u32[]{:S(2)}) %collective-permute-start.1) | collective-permute-done | bytes 270368 | tf_op jit(solution)/shard_map/ppermute | solution.py:28
  20.1 0.8 attend.1
  21.0 1.3 %collective-permute-done.3.partner_ref = bf16[128,512]{1,0:T(8,128)(2,1)S(1)} collective-permute-done((bf16[128,512]{1,0:T(8,128)(2,1)S(1)}, bf16[128,512]{1,0:T(8,128)(2,1)S(1)}, u32[]{:S(2)}, u32[]{:S(2)}) %collective-permute-start.3) | collective-permute-done | bytes 131104 | tf_op jit(solution)/shard_map/ppermute | solution.py:28
  22.4 1.0 %project.1 = (f32[32,3072]{1,0:T(8,128)S(1)}, bf16[32,3072]{1,0:T(8,128)(2,1)S(1)}, bf16[32,3072]{1,0:T(8,128)(2,1)S(1)}, bf16[32,3072]{1,0:T(8,128)(2,1)S(1)}) custom-call(bf16[128,512]{1,0:T(8,128)(2,1)S(1)} %get-tuple-element.45.own_ref, bf16[128,512]{1,0:T(8,128)(2,1)S(1)} %collective-permute-done.3.partner_ref, ...), custom_call_target="tpu_custom_call" | custom-call | flops 805306368 | bytes 8650752 | tf_op jit(solution)/shard_map/project/pallas_call | solution.py:471
  23.4 2.7 %collective-permute-start.5 = (bf16[32,3072]{1,0:T(8,128)(2,1)S(1)}, bf16[32,3072]{1,0:T(8,128)(2,1)S(1)}, u32[]{:S(2)}, u32[]{:S(2)}) collective-permute-start(bf16[32,3072]{1,0:T(8,128)(2,1)S(1)} %get-tuple-element.57), channel_id=1, source_target_pairs={{0,4},{1,5},{2,6},{3,7},{4,0},{5,1},{6,2},{7,3},{8,12},{9,13},{10,... | collective-permute-start | bytes 589832 | tf_op jit(solution)/shard_map/ppermute | solution.py:28
  26.0 1.6 %collective-permute-start.6 = (bf16[32,3072]{1,0:T(8,128)(2,1)S(1)}, bf16[32,3072]{1,0:T(8,128)(2,1)S(1)}, u32[]{:S(2)}, u32[]{:S(2)}) collective-permute-start(bf16[32,3072]{1,0:T(8,128)(2,1)S(1)} %get-tuple-element.58), channel_id=1, source_target_pairs={{0,2},{1,3},{2,0},{3,1},{4,6},{5,7},{6,4},{7,5},{8,10},{9,11},{10,... | collective-permute-start | bytes 589832 | tf_op jit(solution)/shard_map/ppermute | solution.py:28
  28.1 5.2 %load.1 = (bf16[1,1152,3072]{2,1,0:T(8,128)(2,1)S(1)}, bf16[1,1152,3072]{2,1,0:T(8,128)(2,1)S(1)}) custom-call(bf16[1,1152,3072]{2,1,0:T(8,128)(2,1)} %gate_hbm.1, bf16[1,1152,3072]{2,1,0:T(8,128)(2,1)} %up_hbm.1, f32[32,3072]{1,0:T(8,128)S(1)} %get-tuple-element.54.after.kept_ref), custom_call_target="tpu_custom_call" | custom-call | flops 1 | bytes 14155776 | tf_op jit(solution)/shard_map/load/pallas_call | solution.py:494
  33.3 3.6 %collective-permute-done.5.refs_0_ = bf16[32,3072]{1,0:T(8,128)(2,1)S(1)} collective-permute-done((bf16[32,3072]{1,0:T(8,128)(2,1)S(1)}, bf16[32,3072]{1,0:T(8,128)(2,1)S(1)}, u32[]{:S(2)}, u32[]{:S(2)}) %collective-permute-start.5) | collective-permute-done | bytes 196640 | tf_op jit(solution)/shard_map/ppermute | solution.py:28
  36.9 4.0 %collective-permute-done.7.refs_2_ = bf16[32,3072]{1,0:T(8,128)(2,1)S(1)} collective-permute-done((bf16[32,3072]{1,0:T(8,128)(2,1)S(1)}, bf16[32,3072]{1,0:T(8,128)(2,1)S(1)}, u32[]{:S(2)}, u32[]{:S(2)}) %collective-permute-start.7) | collective-permute-done | bytes 196640 | tf_op jit(solution)/shard_map/ppermute | solution.py:28
  41.1 2.5 %collective-permute-start.13 = (bf16[32,3072]{1,0:T(8,128)(2,1)S(1)}, bf16[32,3072]{1,0:T(8,128)(2,1)S(1)}, u32[]{:S(2)}, u32[]{:S(2)}) collective-permute-start(bf16[32,3072]{1,0:T(8,128)(2,1)S(1)} %get-tuple-element.64.refs_6_), channel_id=1, source_target_pairs={{0,6},{1,7},{2,4},{3,5},{4,2},{5,3},{6,0},{7,1},{8,14},{9,15},{10,... | collective-permute-start | bytes 589832 | tf_op jit(solution)/shard_map/ppermute | solution.py:28
  43.7 9.6 %collective-permute-start.12 = (bf16[32,3072]{1,0:T(8,128)(2,1)S(1)}, bf16[32,3072]{1,0:T(8,128)(2,1)S(1)}, u32[]{:S(2)}, u32[]{:S(2)}) collective-permute-start(bf16[32,3072]{1,0:T(8,128)(2,1)S(1)} %get-tuple-element.64.refs_6_), channel_id=1, source_target_pairs={{0,4},{1,5},{2,6},{3,7},{4,0},{5,1},{6,2},{7,3},{8,12},{9,13},{10,... | collective-permute-start | bytes 589832 | tf_op jit(solution)/shard_map/ppermute | solution.py:28
  53.2 1.7 %collective-permute-start.11 = (bf16[32,3072]{1,0:T(8,128)(2,1)S(1)}, bf16[32,3072]{1,0:T(8,128)(2,1)S(1)}, u32[]{:S(2)}, u32[]{:S(2)}) collective-permute-start(bf16[32,3072]{1,0:T(8,128)(2,1)S(1)} %get-tuple-element.64.refs_6_), channel_id=1, source_target_pairs={{0,24},{8,16},{16,8},{24,0},{1,25},{9,17},{17,9},{25,1},{2,26},{10... | collective-permute-start | bytes 589832 | tf_op jit(solution)/shard_map/ppermute | solution.py:28
  54.9 1.3 %collective-permute-start.10 = (bf16[32,3072]{1,0:T(8,128)(2,1)S(1)}, bf16[32,3072]{1,0:T(8,128)(2,1)S(1)}, u32[]{:S(2)}, u32[]{:S(2)}) collective-permute-start(bf16[32,3072]{1,0:T(8,128)(2,1)S(1)} %get-tuple-element.64.refs_6_), channel_id=1, source_target_pairs={{0,16},{8,24},{16,0},{24,8},{1,17},{9,25},{17,1},{25,9},{2,18},{10... | collective-permute-start | bytes 589832 | tf_op jit(solution)/shard_map/ppermute | solution.py:28
  56.2 0.5 collective-permute-start.9
  56.7 1.9 %collective-permute-start.8 = (bf16[32,3072]{1,0:T(8,128)(2,1)S(1)}, bf16[32,3072]{1,0:T(8,128)(2,1)S(1)}, u32[]{:S(2)}, u32[]{:S(2)}) collective-permute-start(bf16[32,3072]{1,0:T(8,128)(2,1)S(1)} %get-tuple-element.64.refs_6_), channel_id=1, source_target_pairs={{0,2},{1,3},{2,0},{3,1},{4,6},{5,7},{6,4},{7,5},{8,10},{9,11},{10,... | collective-permute-start | bytes 589832 | tf_op jit(solution)/shard_map/ppermute | solution.py:28
  58.7 0.8 place.1.refs_7_
  59.5 2.3 %collective-permute-done.12.refs_4_ = bf16[32,3072]{1,0:T(8,128)(2,1)S(1)} collective-permute-done((bf16[32,3072]{1,0:T(8,128)(2,1)S(1)}, bf16[32,3072]{1,0:T(8,128)(2,1)S(1)}, u32[]{:S(2)}, u32[]{:S(2)}) %collective-permute-start.12) | collective-permute-done | bytes 196640 | tf_op jit(solution)/shard_map/ppermute | solution.py:28
  61.8 1.5 %collective-permute-done.10.refs_2_ = bf16[32,3072]{1,0:T(8,128)(2,1)S(1)} collective-permute-done((bf16[32,3072]{1,0:T(8,128)(2,1)S(1)}, bf16[32,3072]{1,0:T(8,128)(2,1)S(1)}, u32[]{:S(2)}, u32[]{:S(2)}) %collective-permute-start.10) | collective-permute-done | bytes 196640 | tf_op jit(solution)/shard_map/ppermute | solution.py:28
  63.5 1.6 %collective-permute-start.18 = (bf16[80,3072]{1,0:T(8,128)(2,1)S(1)}, bf16[80,3072]{1,0:T(8,128)(2,1)S(1)}, u32[]{:S(2)}, u32[]{:S(2)}) collective-permute-start(bf16[80,3072]{1,0:T(8,128)(2,1)S(1)} %get-tuple-element.67), channel_id=1, source_target_pairs={{0,16},{8,24},{16,0},{24,8},{1,17},{9,25},{17,1},{25,9},{2,18},{10... | collective-permute-start | bytes 1474568 | tf_op jit(solution)/shard_map/ppermute | solution.py:28
  65.0 1.0 %collective-permute-start.17 = (bf16[80,3072]{1,0:T(8,128)(2,1)S(1)}, bf16[80,3072]{1,0:T(8,128)(2,1)S(1)}, u32[]{:S(2)}, u32[]{:S(2)}) collective-permute-start(bf16[80,3072]{1,0:T(8,128)(2,1)S(1)} %get-tuple-element.67), channel_id=1, source_target_pairs={{0,8},{8,0},{16,24},{24,16},{1,9},{9,1},{17,25},{25,17},{2,10},{10... | collective-permute-start | bytes 1474568 | tf_op jit(solution)/shard_map/ppermute | solution.py:28
  66.1 0.7 collective-permute-start.15
  67.3 6.5 %collective-permute-done.15.corner_ref.refs_4_.refs_2_ = bf16[64,3072]{1,0:T(8,128)(2,1)S(1)} collective-permute-done((bf16[64,3072]{1,0:T(8,128)(2,1)S(1)}, bf16[64,3072]{1,0:T(8,128)(2,1)S(1)}, u32[]{:S(2)}, u32[]{:S(2)}) %collective-permute-start.15) | collective-permute-done | bytes 393248 | tf_op jit(solution)/shard_map/ppermute | solution.py:28
  74.5 1.1 %collective-permute-start.20 = (bf16[32,3072]{1,0:T(8,128)(2,1)S(1)}, bf16[32,3072]{1,0:T(8,128)(2,1)S(1)}, u32[]{:S(2)}, u32[]{:S(2)}) collective-permute-start(bf16[32,3072]{1,0:T(8,128)(2,1)S(1)} %get-tuple-element.71), channel_id=1, source_target_pairs={{0,16},{8,24},{16,0},{24,8},{1,17},{9,25},{17,1},{25,9},{2,18},{10... | collective-permute-start | bytes 589832 | tf_op jit(solution)/shard_map/ppermute | solution.py:28
  75.6 1.0 %collective-permute-start.21 = (bf16[32,3072]{1,0:T(8,128)(2,1)S(1)}, bf16[32,3072]{1,0:T(8,128)(2,1)S(1)}, u32[]{:S(2)}, u32[]{:S(2)}) collective-permute-start(bf16[32,3072]{1,0:T(8,128)(2,1)S(1)} %get-tuple-element.72), channel_id=1, source_target_pairs={{0,8},{8,0},{16,24},{24,16},{1,9},{9,1},{17,25},{25,17},{2,10},{10... | collective-permute-start | bytes 589832 | tf_op jit(solution)/shard_map/ppermute | solution.py:28
  76.7 5.2 %experts.2.refs_10_ = f32[1,1152,512]{2,1,0:T(8,128)} custom-call(s32[4,256]{1,0:T(4,128)S(1)} %get-tuple-element.61.slot_ref, f32[4,256]{1,0:T(4,128)S(1)} %get-tuple-element.62.weight_ref, bf16[1,1152,3072]{2,1,0:T(8,128)(2,1)S(1)} %get-tuple-element.56.after.gate_ref, bf16[1,1152,3072]{2,1,0:T(8,128)(2,1)S(1)} %get-tuple-element.63.up_ref, ...), custom_call_target="tpu_custom_call" | custom-call | flops 3623878656 | bytes 1572864 | tf_op jit(solution)/shard_map/experts/pallas_call | solution.py:374
  82.7 0.9 %collective-permute-done.24.refs_7_ = bf16[32,3072]{1,0:T(8,128)(2,1)S(1)} collective-permute-done((bf16[32,3072]{1,0:T(8,128)(2,1)S(1)}, bf16[32,3072]{1,0:T(8,128)(2,1)S(1)}, u32[]{:S(2)}, u32[]{:S(2)}) %collective-permute-start.24) | collective-permute-done | bytes 196640 | tf_op jit(solution)/shard_map/ppermute | solution.py:28
  83.9 5.2 %experts.3 = f32[1,1152,512]{2,1,0:T(8,128)} custom-call(s32[4,256]{1,0:T(4,128)S(1)} %get-tuple-element.61.slot_ref, f32[4,256]{1,0:T(4,128)S(1)} %get-tuple-element.62.weight_ref, bf16[1,1152,3072]{2,1,0:T(8,128)(2,1)S(1)} %get-tuple-element.56.after.gate_ref, ...), custom_call_target="tpu_custom_call", output_to_operand_aliasing={{}: (14, {})} | custom-call | flops 3623878656 | bytes 1572864 | tf_op jit(solution)/shard_map/experts/pallas_call | solution.py:374
  (40 shorter events, 4.1 us)
Async XLA Ops:
  0.6 19.5 %copy-start.3 = (f32[512]{0:T(512)S(1)}, f32[512]{0:T(512)}, u32[]{:S(2)}) copy-start(f32[512]{0:T(512)} %param.17) | copy-start | bytes 6148
  2.9 19.5 %collective-permute-start.4 = (bf16[512,3072]{1,0:T(8,128)(2,1)S(1)}, bf16[512,3072]{1,0:T(8,128)(2,1)S(1)}, u32[]{:S(2)}, u32[]{:S(2)}) collective-permute-start(bf16[512,3072]{1,0:T(8,128)(2,1)S(1)} %get-tuple-element.47.proj_ref), channel_id=1, source_target_pairs={{0,1},{1,0},{2,3},{3,2},{4,5},{5,4},{6,7},{7,6},{8,9},{9,8},{10,11... | collective-permute-start | bytes 9437192 | tf_op jit(solution)/shard_map/ppermute | solution.py:28
  3.4 10.9 %collective-permute-start.2 = (bf16[1056,128]{1,0:T(8,128)(2,1)S(1)}, bf16[1056,128]{1,0:T(8,128)(2,1)S(1)}, u32[]{:S(2)}, u32[]{:S(2)}) collective-permute-start(bf16[1056,128]{1,0:T(8,128)(2,1)S(1)} %get-tuple-element.40.after), channel_id=1, source_target_pairs={{0,24},{8,16},{16,8},{24,0},{1,25},{9,17},{17,9},{25,1},{2,26},{10... | collective-permute-start | bytes 811016 | tf_op jit(solution)/shard_map/ppermute | solution.py:28
  6.9 12.9 %collective-permute-start.1 = (bf16[1056,128]{1,0:T(8,128)(2,1)S(1)}, bf16[1056,128]{1,0:T(8,128)(2,1)S(1)}, u32[]{:S(2)}, u32[]{:S(2)}) collective-permute-start(bf16[1056,128]{1,0:T(8,128)(2,1)S(1)} %get-tuple-element.40.after), channel_id=1, source_target_pairs={{0,16},{8,24},{16,0},{24,8},{1,17},{9,25},{17,1},{25,9},{2,18},{10... | collective-permute-start | bytes 811016 | tf_op jit(solution)/shard_map/ppermute | solution.py:28
  7.4 12.7 %collective-permute-start = (bf16[1056,128]{1,0:T(8,128)(2,1)S(1)}, bf16[1056,128]{1,0:T(8,128)(2,1)S(1)}, u32[]{:S(2)}, u32[]{:S(2)}) collective-permute-start(bf16[1056,128]{1,0:T(8,128)(2,1)S(1)} %get-tuple-element.40.after), channel_id=1, source_target_pairs={{0,8},{8,0},{16,24},{24,16},{1,9},{9,1},{17,25},{25,17},{2,10},{10... | collective-permute-start | bytes 811016 | tf_op jit(solution)/shard_map/ppermute | solution.py:28
  20.9 1.4 %collective-permute-start.3 = (bf16[128,512]{1,0:T(8,128)(2,1)S(1)}, bf16[128,512]{1,0:T(8,128)(2,1)S(1)}, u32[]{:S(2)}, u32[]{:S(2)}) collective-permute-start(bf16[128,512]{1,0:T(8,128)(2,1)S(1)} %get-tuple-element.46), channel_id=1, source_target_pairs={{0,1},{1,0},{2,3},{3,2},{4,5},{5,4},{6,7},{7,6},{8,9},{9,8},{10,11... | collective-permute-start | bytes 393224 | tf_op jit(solution)/shard_map/ppermute | solution.py:28
  22.4 5.5 %copy-start.1 = (s32[512,2,2]{0,2,1:T(2,128)S(1)}, s32[512,2,2]{0,2,1:T(2,128)}, u32[]{:S(2)}) copy-start(s32[512,2,2]{0,2,1:T(2,128)} %param.20) | copy-start | bytes 24580
  22.4 5.5 %copy-start.2 = (f32[512,2,2]{0,2,1:T(2,128)S(1)}, f32[512,2,2]{0,2,1:T(2,128)}, u32[]{:S(2)}) copy-start(f32[512,2,2]{0,2,1:T(2,128)} %param.21) | copy-start | bytes 24580
  23.4 13.5 %collective-permute-start.5 = (bf16[32,3072]{1,0:T(8,128)(2,1)S(1)}, bf16[32,3072]{1,0:T(8,128)(2,1)S(1)}, u32[]{:S(2)}, u32[]{:S(2)}) collective-permute-start(bf16[32,3072]{1,0:T(8,128)(2,1)S(1)} %get-tuple-element.57), channel_id=1, source_target_pairs={{0,4},{1,5},{2,6},{3,7},{4,0},{5,1},{6,2},{7,3},{8,12},{9,13},{10,... | collective-permute-start | bytes 589832 | tf_op jit(solution)/shard_map/ppermute | solution.py:28
  26.0 10.9 %collective-permute-start.6 = (bf16[32,3072]{1,0:T(8,128)(2,1)S(1)}, bf16[32,3072]{1,0:T(8,128)(2,1)S(1)}, u32[]{:S(2)}, u32[]{:S(2)}) collective-permute-start(bf16[32,3072]{1,0:T(8,128)(2,1)S(1)} %get-tuple-element.58), channel_id=1, source_target_pairs={{0,2},{1,3},{2,0},{3,1},{4,6},{5,7},{6,4},{7,5},{8,10},{9,11},{10,... | collective-permute-start | bytes 589832 | tf_op jit(solution)/shard_map/ppermute | solution.py:28
  27.6 13.3 %collective-permute-start.7 = (bf16[32,3072]{1,0:T(8,128)(2,1)S(1)}, bf16[32,3072]{1,0:T(8,128)(2,1)S(1)}, u32[]{:S(2)}, u32[]{:S(2)}) collective-permute-start(bf16[32,3072]{1,0:T(8,128)(2,1)S(1)} %get-tuple-element.59), channel_id=1, source_target_pairs={{0,6},{1,7},{2,4},{3,5},{4,2},{5,3},{6,0},{7,1},{8,14},{9,15},{10,... | collective-permute-start | bytes 589832 | tf_op jit(solution)/shard_map/ppermute | solution.py:28
  28.1 12.8 %copy-start = (f32[3072]{0:T(1024)S(1)}, f32[3072]{0:T(1024)}, u32[]{:S(2)}) copy-start(f32[3072]{0:T(1024)} %param.19) | copy-start | bytes 36868
  41.1 15.6 %collective-permute-start.13 = (bf16[32,3072]{1,0:T(8,128)(2,1)S(1)}, bf16[32,3072]{1,0:T(8,128)(2,1)S(1)}, u32[]{:S(2)}, u32[]{:S(2)}) collective-permute-start(bf16[32,3072]{1,0:T(8,128)(2,1)S(1)} %get-tuple-element.64.refs_6_), channel_id=1, source_target_pairs={{0,6},{1,7},{2,4},{3,5},{4,2},{5,3},{6,0},{7,1},{8,14},{9,15},{10,... | collective-permute-start | bytes 589832 | tf_op jit(solution)/shard_map/ppermute | solution.py:28
  43.7 18.1 %collective-permute-start.12 = (bf16[32,3072]{1,0:T(8,128)(2,1)S(1)}, bf16[32,3072]{1,0:T(8,128)(2,1)S(1)}, u32[]{:S(2)}, u32[]{:S(2)}) collective-permute-start(bf16[32,3072]{1,0:T(8,128)(2,1)S(1)} %get-tuple-element.64.refs_6_), channel_id=1, source_target_pairs={{0,4},{1,5},{2,6},{3,7},{4,0},{5,1},{6,2},{7,3},{8,12},{9,13},{10,... | collective-permute-start | bytes 589832 | tf_op jit(solution)/shard_map/ppermute | solution.py:28
  53.2 8.6 %collective-permute-start.11 = (bf16[32,3072]{1,0:T(8,128)(2,1)S(1)}, bf16[32,3072]{1,0:T(8,128)(2,1)S(1)}, u32[]{:S(2)}, u32[]{:S(2)}) collective-permute-start(bf16[32,3072]{1,0:T(8,128)(2,1)S(1)} %get-tuple-element.64.refs_6_), channel_id=1, source_target_pairs={{0,24},{8,16},{16,8},{24,0},{1,25},{9,17},{17,9},{25,1},{2,26},{10... | collective-permute-start | bytes 589832 | tf_op jit(solution)/shard_map/ppermute | solution.py:28
  54.9 8.4 %collective-permute-start.10 = (bf16[32,3072]{1,0:T(8,128)(2,1)S(1)}, bf16[32,3072]{1,0:T(8,128)(2,1)S(1)}, u32[]{:S(2)}, u32[]{:S(2)}) collective-permute-start(bf16[32,3072]{1,0:T(8,128)(2,1)S(1)} %get-tuple-element.64.refs_6_), channel_id=1, source_target_pairs={{0,16},{8,24},{16,0},{24,8},{1,17},{9,25},{17,1},{25,9},{2,18},{10... | collective-permute-start | bytes 589832 | tf_op jit(solution)/shard_map/ppermute | solution.py:28
  56.2 7.1 %collective-permute-start.9 = (bf16[32,3072]{1,0:T(8,128)(2,1)S(1)}, bf16[32,3072]{1,0:T(8,128)(2,1)S(1)}, u32[]{:S(2)}, u32[]{:S(2)}) collective-permute-start(bf16[32,3072]{1,0:T(8,128)(2,1)S(1)} %get-tuple-element.64.refs_6_), channel_id=1, source_target_pairs={{0,8},{8,0},{16,24},{24,16},{1,9},{9,1},{17,25},{25,17},{2,10},{10... | collective-permute-start | bytes 589832 | tf_op jit(solution)/shard_map/ppermute | solution.py:28
  56.7 6.6 %collective-permute-start.8 = (bf16[32,3072]{1,0:T(8,128)(2,1)S(1)}, bf16[32,3072]{1,0:T(8,128)(2,1)S(1)}, u32[]{:S(2)}, u32[]{:S(2)}) collective-permute-start(bf16[32,3072]{1,0:T(8,128)(2,1)S(1)} %get-tuple-element.64.refs_6_), channel_id=1, source_target_pairs={{0,2},{1,3},{2,0},{3,1},{4,6},{5,7},{6,4},{7,5},{8,10},{9,11},{10,... | collective-permute-start | bytes 589832 | tf_op jit(solution)/shard_map/ppermute | solution.py:28
  63.5 10.4 %collective-permute-start.18 = (bf16[80,3072]{1,0:T(8,128)(2,1)S(1)}, bf16[80,3072]{1,0:T(8,128)(2,1)S(1)}, u32[]{:S(2)}, u32[]{:S(2)}) collective-permute-start(bf16[80,3072]{1,0:T(8,128)(2,1)S(1)} %get-tuple-element.67), channel_id=1, source_target_pairs={{0,16},{8,24},{16,0},{24,8},{1,17},{9,25},{17,1},{25,9},{2,18},{10... | collective-permute-start | bytes 1474568 | tf_op jit(solution)/shard_map/ppermute | solution.py:28
  65.0 8.8 %collective-permute-start.17 = (bf16[80,3072]{1,0:T(8,128)(2,1)S(1)}, bf16[80,3072]{1,0:T(8,128)(2,1)S(1)}, u32[]{:S(2)}, u32[]{:S(2)}) collective-permute-start(bf16[80,3072]{1,0:T(8,128)(2,1)S(1)} %get-tuple-element.67), channel_id=1, source_target_pairs={{0,8},{8,0},{16,24},{24,16},{1,9},{9,1},{17,25},{25,17},{2,10},{10... | collective-permute-start | bytes 1474568 | tf_op jit(solution)/shard_map/ppermute | solution.py:28
  66.1 7.8 %collective-permute-start.15 = (bf16[64,3072]{1,0:T(8,128)(2,1)S(1)}, bf16[64,3072]{1,0:T(8,128)(2,1)S(1)}, u32[]{:S(2)}, u32[]{:S(2)}) collective-permute-start(bf16[64,3072]{1,0:T(8,128)(2,1)S(1)} %get-tuple-element.66), channel_id=1, source_target_pairs={{0,2},{1,3},{2,0},{3,1},{4,6},{5,7},{6,4},{7,5},{8,10},{9,11},{10,... | collective-permute-start | bytes 1179656 | tf_op jit(solution)/shard_map/ppermute | solution.py:28
  66.8 9.8 %collective-permute-start.14 = (bf16[128,3072]{1,0:T(8,128)(2,1)S(1)}, bf16[128,3072]{1,0:T(8,128)(2,1)S(1)}, u32[]{:S(2)}, u32[]{:S(2)}) collective-permute-start(bf16[128,3072]{1,0:T(8,128)(2,1)S(1)} %get-tuple-element.65.refs_0_), channel_id=1, source_target_pairs={{0,1},{1,0},{2,3},{3,2},{4,5},{5,4},{6,7},{7,6},{8,9},{9,8},{10,11... | collective-permute-start | bytes 2359304 | tf_op jit(solution)/shard_map/ppermute | solution.py:28
  66.8 8.8 %collective-permute-start.22 = (bf16[96,3072]{1,0:T(8,128)(2,1)S(1)}, bf16[96,3072]{1,0:T(8,128)(2,1)S(1)}, u32[]{:S(2)}, u32[]{:S(2)}) collective-permute-start(bf16[96,3072]{1,0:T(8,128)(2,1)S(1)} %get-tuple-element.73.refs_2_), channel_id=1, source_target_pairs={{0,1},{1,0},{2,3},{3,2},{4,5},{5,4},{6,7},{7,6},{8,9},{9,8},{10,11... | collective-permute-start | bytes 1769480 | tf_op jit(solution)/shard_map/ppermute | solution.py:28
  73.9 2.8 %collective-permute-start.23 = (bf16[80,3072]{1,0:T(8,128)(2,1)S(1)}, bf16[80,3072]{1,0:T(8,128)(2,1)S(1)}, u32[]{:S(2)}, u32[]{:S(2)}) collective-permute-start(bf16[80,3072]{1,0:T(8,128)(2,1)S(1)} %collective-permute-done.17.one_ref.refs_6_), channel_id=1, source_target_pairs={{0,1},{1,0},{2,3},{3,2},{4,5},{5,4},{6,7},{7,6},{8,9},{9,8},{10,11... | collective-permute-start | bytes 1474568 | tf_op jit(solution)/shard_map/ppermute | solution.py:28
  74.0 2.7 %collective-permute-start.16 = (bf16[64,3072]{1,0:T(8,128)(2,1)S(1)}, bf16[64,3072]{1,0:T(8,128)(2,1)S(1)}, u32[]{:S(2)}, u32[]{:S(2)}) collective-permute-start(bf16[64,3072]{1,0:T(8,128)(2,1)S(1)} %collective-permute-done.15.corner_ref.refs_4_.refs_2_), channel_id=1, source_target_pairs={{0,1},{1,0},{2,3},{3,2},{4,5},{5,4},{6,7},{7,6},{8,9},{9,8},{10,11... | collective-permute-start | bytes 1179656 | tf_op jit(solution)/shard_map/ppermute | solution.py:28
  74.5 7.4 %collective-permute-start.20 = (bf16[32,3072]{1,0:T(8,128)(2,1)S(1)}, bf16[32,3072]{1,0:T(8,128)(2,1)S(1)}, u32[]{:S(2)}, u32[]{:S(2)}) collective-permute-start(bf16[32,3072]{1,0:T(8,128)(2,1)S(1)} %get-tuple-element.71), channel_id=1, source_target_pairs={{0,16},{8,24},{16,0},{24,8},{1,17},{9,25},{17,1},{25,9},{2,18},{10... | collective-permute-start | bytes 589832 | tf_op jit(solution)/shard_map/ppermute | solution.py:28
  75.6 6.6 %collective-permute-start.21 = (bf16[32,3072]{1,0:T(8,128)(2,1)S(1)}, bf16[32,3072]{1,0:T(8,128)(2,1)S(1)}, u32[]{:S(2)}, u32[]{:S(2)}) collective-permute-start(bf16[32,3072]{1,0:T(8,128)(2,1)S(1)} %get-tuple-element.72), channel_id=1, source_target_pairs={{0,8},{8,0},{16,24},{24,16},{1,9},{9,1},{17,25},{25,17},{2,10},{10... | collective-permute-start | bytes 589832 | tf_op jit(solution)/shard_map/ppermute | solution.py:28
  76.7 6.1 %collective-permute-start.19 = (bf16[80,3072]{1,0:T(8,128)(2,1)S(1)}, bf16[80,3072]{1,0:T(8,128)(2,1)S(1)}, u32[]{:S(2)}, u32[]{:S(2)}) collective-permute-start(bf16[80,3072]{1,0:T(8,128)(2,1)S(1)} %collective-permute-done.18.two_ref.refs_4_), channel_id=1, source_target_pairs={{0,1},{1,0},{2,3},{3,2},{4,5},{5,4},{6,7},{7,6},{8,9},{9,8},{10,11... | collective-permute-start | bytes 1474568 | tf_op jit(solution)/shard_map/ppermute | solution.py:28
  82.2 1.4 %collective-permute-start.24 = (bf16[32,3072]{1,0:T(8,128)(2,1)S(1)}, bf16[32,3072]{1,0:T(8,128)(2,1)S(1)}, u32[]{:S(2)}, u32[]{:S(2)}) collective-permute-start(bf16[32,3072]{1,0:T(8,128)(2,1)S(1)} %collective-permute-done.20.refs_6_), channel_id=1, source_target_pairs={{0,1},{1,0},{2,3},{3,2},{4,5},{5,4},{6,7},{7,6},{8,9},{9,8},{10,11... | collective-permute-start | bytes 589832 | tf_op jit(solution)/shard_map/ppermute | solution.py:28
  82.5 1.5 %collective-permute-start.25 = (bf16[32,3072]{1,0:T(8,128)(2,1)S(1)}, bf16[32,3072]{1,0:T(8,128)(2,1)S(1)}, u32[]{:S(2)}, u32[]{:S(2)}) collective-permute-start(bf16[32,3072]{1,0:T(8,128)(2,1)S(1)} %collective-permute-done.21.refs_8_), channel_id=1, source_target_pairs={{0,1},{1,0},{2,3},{3,2},{4,5},{5,4},{6,7},{7,6},{8,9},{9,8},{10,11... | collective-permute-start | bytes 589832 | tf_op jit(solution)/shard_map/ppermute | solution.py:28

commit v7 on v6

--- a/solution.py
+++ b/solution.py
@@ -267,7 +267,7 @@
 
 def route_kernel(own, routes_ref, weights_ref, slot_ref, weight_ref, a_ref, b_ref):
     seqs, tops, _ = routes_ref.shape
-    count, total = slot_ref.shape
+    count, total = a_ref.shape
     size = total // seqs
     me = lax.axis_index("seq")
     index = lax.axis_index("exp")
@@ -295,9 +295,23 @@
     a_ref[...] = jnp.where(picked, rank.astype(jnp.int32), -1)
     high, middle, low = thirds(weight)
     b_ref[...] = mm(high, same) + mm(middle, same) + mm(low, same)
+    capacity = weight_ref.shape[1]
+    numbers = lax.broadcasted_iota(jnp.int32, (capacity, total), 0)
     for d in range(count):
-        slot_ref[d : d + 1, :] = a_ref[pl.ds(me ^ d, 1), :]
-        weight_ref[d : d + 1, :] = b_ref[pl.ds(me ^ d, 1), :]
+        slot, weight = a_ref[pl.ds(me ^ d, 1), :], b_ref[pl.ds(me ^ d, 1), :]
+        if slot_ref.shape[0] == count:
+            slot_ref[d : d + 1, :] = slot
+            weight_ref[d : d + 1, :] = weight
+            continue
+        pick = (slot == numbers).astype(BF)
+        slot_ref[d * capacity : (d + 1) * capacity, :] = pick
+        weight_ref[d : d + 1, :] = weighed([weight], pick)
+
+
+def weighed(weights, pick):
+    weight = jnp.concatenate(weights, axis=1)
+    parts = [part.astype(F32) for part in thirds(weight)] + [jnp.zeros((5, weight.shape[1]), F32)]
+    return jnp.sum(mm(jnp.concatenate(parts, axis=0).astype(BF), pick, NT), axis=0, keepdims=True)
 
 
 def expert_kernel(plan, arrays, lines, slot_ref, weight_ref, gate_ref, up_ref, *refs):
@@ -309,16 +323,17 @@
     tile = out_ref.shape[1]
     capacity = slots // blocks
     apart = capacity % 128 == 0
-    numbers = lax.broadcasted_iota(jnp.int32, (slots, total), 0)
     picks = []
-    for n, line in enumerate(lines):
-        place = n if apart else (me ^ line) % blocks
-        slot = slot_ref[line : line + 1, :]
-        picks.append((jnp.where(slot < 0, slot, slot + place * capacity) == numbers).astype(BF))
-    weight = jnp.concatenate([weight_ref[line : line + 1, :] for line in lines], axis=1)
-    parts = [part.astype(F32) for part in thirds(weight)] + [jnp.zeros((5, blocks * total), F32)]
-    parts = jnp.concatenate(parts, axis=0).astype(BF)
-    scale = jnp.sum(mm(parts, jnp.concatenate(picks, axis=1), NT), axis=0, keepdims=True)
+    if apart:
+        picks = [slot_ref[line * capacity : (line + 1) * capacity, :] for line in lines]
+        scale = jnp.concatenate([weight_ref[line : line + 1, :] for line in lines], axis=1)
+    else:
+        numbers = lax.broadcasted_iota(jnp.int32, (slots, total), 0)
+        for line in lines:
+            slot = slot_ref[line : line + 1, :]
+            place = (me ^ line) % blocks
+            picks.append((jnp.where(slot < 0, slot, slot + place * capacity) == numbers).astype(BF))
+        scale = weighed([weight_ref[line : line + 1, :] for line in lines], jnp.concatenate(picks, axis=1))
 
     step = column_tile(width)
     for at in range(0, width, step):
@@ -329,7 +344,7 @@
         if apart:
             for n, pick in enumerate(picks):
                 own = slice(n * capacity, (n + 1) * capacity)
-                rows_ref[own, part] = mm(pick[own], jnp.concatenate(rows[n], axis=0)).astype(BF)
+                rows_ref[own, part] = mm(pick, jnp.concatenate(rows[n], axis=0)).astype(BF)
         else:
             rows = jnp.concatenate([piece for pieces in rows for piece in pieces], axis=0)
             rows_ref[:, part] = mm(jnp.concatenate(picks, axis=1), rows).astype(BF)
@@ -375,7 +390,7 @@
         functools.partial(expert_kernel, plan, len(arrays), lines),
         in_specs=[vmem] * (4 + len(arrays)) + [hbm] * len(carried),
         out_specs=hbm,
-        out_shape=jax.ShapeDtypeStruct((1, units, slot.shape[0] * capacity), F32),
+        out_shape=jax.ShapeDtypeStruct((1, units, weight.shape[0] * capacity), F32),
         scratch_shapes=[
             pltpu.VMEM((slots, width), BF),
             pltpu.VMEM((steps, tile, slots), F32),
@@ -481,9 +496,15 @@
     got = [swap(send, "exp", 2 * d) for d, send in enumerate(sends, start=1)]
 
     routes, route_weight, keep = lax.optimization_barrier((routes, route_weight, keep))
+    tables = [jax.ShapeDtypeStruct((count, total), jnp.int32), jax.ShapeDtypeStruct((count, total), F32)]
+    if capacity % 128 == 0:
+        tables = [
+            jax.ShapeDtypeStruct((count * capacity, total), BF),
+            jax.ShapeDtypeStruct((count, capacity), F32),
+        ]
     slot, weight = pl.pallas_call(
         functools.partial(route_kernel, own),
-        out_shape=[jax.ShapeDtypeStruct((count, total), jnp.int32), jax.ShapeDtypeStruct((count, total), F32)],
+        out_shape=tables,
         scratch_shapes=[pltpu.VMEM((count, total), jnp.int32), pltpu.VMEM((count, total), F32)],
         compiler_params=params(),
         cost_estimate=cost(10 * count * total * total, 16 * count * total),
@@ -496,7 +517,7 @@
         in_specs=[hbm, hbm, anywhere],
         out_specs=[vmem] * 2,
         out_shape=[pltpu.VMEM(w_gate.shape, BF), pltpu.VMEM(w_up.shape, BF)],
-        scratch_shapes=[pltpu.SemaphoreType.DMA((2, 4))],
+        scratch_shapes=[pltpu.SemaphoreType.DMA((2, max(n for n in (4, 2, 1) if w_gate.shape[1] % (16 * n) == 0)))],
         compiler_params=params(VMEM_BYTES // 8),
         cost_estimate=cost(1, 4 * w_gate.size),
         name="load",

time: 89.9 us -> 89.8 us (level)
  no operation moved by 1% of the time
where the time goes in v7:
time: 89.8 us; the launch traced here: 89.1 us
  starting transfers between devices  33.8 us (38%)
  waiting for transfers between devices  30.5 us (34%)
  Pallas kernels  24 us (27%)
    ppermute x26, starting transfers between devices, swap(): return lax.ppermute(block, axis, route)  33.8 us
    ppermute x26, waiting for transfers between devices, swap(): return lax.ppermute(block, axis, route)  30.5 us
    pallas_call x2, Pallas kernels, experts(): pl.pallas_call(functools.partial(expert_kernel, plan, len(arrays), lines)...  10.4 us
    pallas_call x1, Pallas kernels, per_device(): pl.pallas_call(load_kernel, in_specs=[hbm, hbm, anywhere], out_specs=[vme...  5.19 us
    pallas_call x1, Pallas kernels, per_device(): pl.pallas_call(functools.partial(inner_kernel, line), in_specs=[hbm] * 5...  2.7 us
    pallas_call x1, Pallas kernels, per_device(): pl.pallas_call(state_kernel, in_specs=[hbm] * 4, out_specs=[vmem] * 2, ou...  2.24 us
  transfers between devices with their start and end apart: 26, of which 12 were waited for; matrix products, arithmetic and copies ran while one was open for 0% of the time, Pallas kernels for 17%

profile of v7, /device:TPU:0, one launch (start us, length us, event | category | flops | bytes accessed | tf_op | source)
XLA Modules:
  0.0 89.1 jit_solution(6178489643991025996)
XLA Ops:
  0.6 2.2 %states.1 = (bf16[1056,128]{1,0:T(8,128)(2,1)S(1)}, bf16[512,3072]{1,0:T(8,128)(2,1)S(1)}) custom-call(bf16[2,128,512]{2,1,0:T(8,128)(2,1)} %k_hbm.3, bf16[2,128,512]{2,1,0:T(8,128)(2,1)} %v_hbm.3, f32[2,4,128]{2,1,0:T(4,128)} %decay_hbm.3, bf16[512,3072]{1,0:T(8,128)(2,1)} %proj_hbm.1), custom_call_target="tpu_custom_call" | custom-call | flops 67108864 | bytes 786432 | tf_op jit(solution)/shard_map/states/pallas_call | solution.py:433
  2.9 0.5 collective-permute-start.4
  3.4 3.5 %collective-permute-start.2 = (bf16[1056,128]{1,0:T(8,128)(2,1)S(1)}, bf16[1056,128]{1,0:T(8,128)(2,1)S(1)}, u32[]{:S(2)}, u32[]{:S(2)}) collective-permute-start(bf16[1056,128]{1,0:T(8,128)(2,1)S(1)} %get-tuple-element.40.after), channel_id=1, source_target_pairs={{0,24},{8,16},{16,8},{24,0},{1,25},{9,17},{17,9},{25,1},{2,26},{10... | collective-permute-start | bytes 811016 | tf_op jit(solution)/shard_map/ppermute | solution.py:28
  7.6 2.7 %inner.1 = (f32[2,128,512]{2,1,0:T(8,128)S(1)}, bf16[2,128,512]{2,1,0:T(8,128)(2,1)S(1)}, f32[32,3072]{1,0:T(8,128)S(1)}, f32[2,128,4]{2,1,0:T(8,128)S(1)}, bf16[256,256]{1,0:T(8,128)(2,1)S(1)}) custom-call(bf16[2,128,512]{2,1,0:T(8,128)(2,1)} %q_hbm.1, bf16[2,128,512]{2,1,0:T(8,128)(2,1)} %k_hbm.3, bf16[2,128,512]{2,1,0:T(8,128)(2,1)} %v_hbm.3, ...), custom_call_target="tpu_custom_call" | custom-call | flops 100663296 | bytes 1310720 | tf_op jit(solution)/shard_map/inner/pallas_call | solution.py:453
  10.3 4.0 %collective-permute-done.2.refs_7_ = bf16[1056,128]{1,0:T(8,128)(2,1)S(1)} collective-permute-done((bf16[1056,128]{1,0:T(8,128)(2,1)S(1)}, bf16[1056,128]{1,0:T(8,128)(2,1)S(1)}, u32[]{:S(2)}, u32[]{:S(2)}) %collective-permute-start.2) | collective-permute-done | bytes 270368 | tf_op jit(solution)/shard_map/ppermute | solution.py:28
  14.3 5.5 %collective-permute-done.1.refs_6_ = bf16[1056,128]{1,0:T(8,128)(2,1)S(1)} collective-permute-done((bf16[1056,128]{1,0:T(8,128)(2,1)S(1)}, bf16[1056,128]{1,0:T(8,128)(2,1)S(1)}, u32[]{:S(2)}, u32[]{:S(2)}) %collective-permute-start.1) | collective-permute-done | bytes 270368 | tf_op jit(solution)/shard_map/ppermute | solution.py:28
  20.1 0.8 attend.1
  21.0 1.3 %collective-permute-done.3.partner_ref = bf16[128,512]{1,0:T(8,128)(2,1)S(1)} collective-permute-done((bf16[128,512]{1,0:T(8,128)(2,1)S(1)}, bf16[128,512]{1,0:T(8,128)(2,1)S(1)}, u32[]{:S(2)}, u32[]{:S(2)}) %collective-permute-start.3) | collective-permute-done | bytes 131104 | tf_op jit(solution)/shard_map/ppermute | solution.py:28
  22.4 1.0 %project.1 = (f32[32,3072]{1,0:T(8,128)S(1)}, bf16[32,3072]{1,0:T(8,128)(2,1)S(1)}, bf16[32,3072]{1,0:T(8,128)(2,1)S(1)}, bf16[32,3072]{1,0:T(8,128)(2,1)S(1)}) custom-call(bf16[128,512]{1,0:T(8,128)(2,1)S(1)} %get-tuple-element.45.own_ref, bf16[128,512]{1,0:T(8,128)(2,1)S(1)} %collective-permute-done.3.partner_ref, ...), custom_call_target="tpu_custom_call" | custom-call | flops 805306368 | bytes 8650752 | tf_op jit(solution)/shard_map/project/pallas_call | solution.py:486
  23.4 2.7 %collective-permute-start.5 = (bf16[32,3072]{1,0:T(8,128)(2,1)S(1)}, bf16[32,3072]{1,0:T(8,128)(2,1)S(1)}, u32[]{:S(2)}, u32[]{:S(2)}) collective-permute-start(bf16[32,3072]{1,0:T(8,128)(2,1)S(1)} %get-tuple-element.57), channel_id=1, source_target_pairs={{0,4},{1,5},{2,6},{3,7},{4,0},{5,1},{6,2},{7,3},{8,12},{9,13},{10,... | collective-permute-start | bytes 589832 | tf_op jit(solution)/shard_map/ppermute | solution.py:28
  26.0 1.6 %collective-permute-start.6 = (bf16[32,3072]{1,0:T(8,128)(2,1)S(1)}, bf16[32,3072]{1,0:T(8,128)(2,1)S(1)}, u32[]{:S(2)}, u32[]{:S(2)}) collective-permute-start(bf16[32,3072]{1,0:T(8,128)(2,1)S(1)} %get-tuple-element.58), channel_id=1, source_target_pairs={{0,2},{1,3},{2,0},{3,1},{4,6},{5,7},{6,4},{7,5},{8,10},{9,11},{10,... | collective-permute-start | bytes 589832 | tf_op jit(solution)/shard_map/ppermute | solution.py:28
  28.3 5.2 %load.1 = (bf16[1,1152,3072]{2,1,0:T(8,128)(2,1)S(1)}, bf16[1,1152,3072]{2,1,0:T(8,128)(2,1)S(1)}) custom-call(bf16[1,1152,3072]{2,1,0:T(8,128)(2,1)} %gate_hbm.1, bf16[1,1152,3072]{2,1,0:T(8,128)(2,1)} %up_hbm.1, f32[32,3072]{1,0:T(8,128)S(1)} %get-tuple-element.54.after.kept_ref), custom_call_target="tpu_custom_call" | custom-call | flops 1 | bytes 14155776 | tf_op jit(solution)/shard_map/load/pallas_call | solution.py:515
  33.5 3.4 %collective-permute-done.5.refs_0_ = bf16[32,3072]{1,0:T(8,128)(2,1)S(1)} collective-permute-done((bf16[32,3072]{1,0:T(8,128)(2,1)S(1)}, bf16[32,3072]{1,0:T(8,128)(2,1)S(1)}, u32[]{:S(2)}, u32[]{:S(2)}) %collective-permute-start.5) | collective-permute-done | bytes 196640 | tf_op jit(solution)/shard_map/ppermute | solution.py:28
  36.9 4.0 %collective-permute-done.7.refs_2_ = bf16[32,3072]{1,0:T(8,128)(2,1)S(1)} collective-permute-done((bf16[32,3072]{1,0:T(8,128)(2,1)S(1)}, bf16[32,3072]{1,0:T(8,128)(2,1)S(1)}, u32[]{:S(2)}, u32[]{:S(2)}) %collective-permute-start.7) | collective-permute-done | bytes 196640 | tf_op jit(solution)/shard_map/ppermute | solution.py:28
  41.1 2.5 %collective-permute-start.13 = (bf16[32,3072]{1,0:T(8,128)(2,1)S(1)}, bf16[32,3072]{1,0:T(8,128)(2,1)S(1)}, u32[]{:S(2)}, u32[]{:S(2)}) collective-permute-start(bf16[32,3072]{1,0:T(8,128)(2,1)S(1)} %get-tuple-element.64.refs_6_), channel_id=1, source_target_pairs={{0,6},{1,7},{2,4},{3,5},{4,2},{5,3},{6,0},{7,1},{8,14},{9,15},{10,... | collective-permute-start | bytes 589832 | tf_op jit(solution)/shard_map/ppermute | solution.py:28
  43.7 9.6 %collective-permute-start.12 = (bf16[32,3072]{1,0:T(8,128)(2,1)S(1)}, bf16[32,3072]{1,0:T(8,128)(2,1)S(1)}, u32[]{:S(2)}, u32[]{:S(2)}) collective-permute-start(bf16[32,3072]{1,0:T(8,128)(2,1)S(1)} %get-tuple-element.64.refs_6_), channel_id=1, source_target_pairs={{0,4},{1,5},{2,6},{3,7},{4,0},{5,1},{6,2},{7,3},{8,12},{9,13},{10,... | collective-permute-start | bytes 589832 | tf_op jit(solution)/shard_map/ppermute | solution.py:28
  53.2 1.7 %collective-permute-start.11 = (bf16[32,3072]{1,0:T(8,128)(2,1)S(1)}, bf16[32,3072]{1,0:T(8,128)(2,1)S(1)}, u32[]{:S(2)}, u32[]{:S(2)}) collective-permute-start(bf16[32,3072]{1,0:T(8,128)(2,1)S(1)} %get-tuple-element.64.refs_6_), channel_id=1, source_target_pairs={{0,24},{8,16},{16,8},{24,0},{1,25},{9,17},{17,9},{25,1},{2,26},{10... | collective-permute-start | bytes 589832 | tf_op jit(solution)/shard_map/ppermute | solution.py:28
  54.9 1.3 %collective-permute-start.10 = (bf16[32,3072]{1,0:T(8,128)(2,1)S(1)}, bf16[32,3072]{1,0:T(8,128)(2,1)S(1)}, u32[]{:S(2)}, u32[]{:S(2)}) collective-permute-start(bf16[32,3072]{1,0:T(8,128)(2,1)S(1)} %get-tuple-element.64.refs_6_), channel_id=1, source_target_pairs={{0,16},{8,24},{16,0},{24,8},{1,17},{9,25},{17,1},{25,9},{2,18},{10... | collective-permute-start | bytes 589832 | tf_op jit(solution)/shard_map/ppermute | solution.py:28
  56.2 0.5 collective-permute-start.9
  56.7 1.9 %collective-permute-start.8 = (bf16[32,3072]{1,0:T(8,128)(2,1)S(1)}, bf16[32,3072]{1,0:T(8,128)(2,1)S(1)}, u32[]{:S(2)}, u32[]{:S(2)}) collective-permute-start(bf16[32,3072]{1,0:T(8,128)(2,1)S(1)} %get-tuple-element.64.refs_6_), channel_id=1, source_target_pairs={{0,2},{1,3},{2,0},{3,1},{4,6},{5,7},{6,4},{7,5},{8,10},{9,11},{10,... | collective-permute-start | bytes 589832 | tf_op jit(solution)/shard_map/ppermute | solution.py:28
  58.7 0.8 place.1.refs_7_
  59.5 2.3 %collective-permute-done.12.refs_4_ = bf16[32,3072]{1,0:T(8,128)(2,1)S(1)} collective-permute-done((bf16[32,3072]{1,0:T(8,128)(2,1)S(1)}, bf16[32,3072]{1,0:T(8,128)(2,1)S(1)}, u32[]{:S(2)}, u32[]{:S(2)}) %collective-permute-start.12) | collective-permute-done | bytes 196640 | tf_op jit(solution)/shard_map/ppermute | solution.py:28
  61.8 1.5 %collective-permute-done.10.refs_2_ = bf16[32,3072]{1,0:T(8,128)(2,1)S(1)} collective-permute-done((bf16[32,3072]{1,0:T(8,128)(2,1)S(1)}, bf16[32,3072]{1,0:T(8,128)(2,1)S(1)}, u32[]{:S(2)}, u32[]{:S(2)}) %collective-permute-start.10) | collective-permute-done | bytes 196640 | tf_op jit(solution)/shard_map/ppermute | solution.py:28
  63.5 1.6 %collective-permute-start.18 = (bf16[80,3072]{1,0:T(8,128)(2,1)S(1)}, bf16[80,3072]{1,0:T(8,128)(2,1)S(1)}, u32[]{:S(2)}, u32[]{:S(2)}) collective-permute-start(bf16[80,3072]{1,0:T(8,128)(2,1)S(1)} %get-tuple-element.67), channel_id=1, source_target_pairs={{0,16},{8,24},{16,0},{24,8},{1,17},{9,25},{17,1},{25,9},{2,18},{10... | collective-permute-start | bytes 1474568 | tf_op jit(solution)/shard_map/ppermute | solution.py:28
  65.0 1.0 %collective-permute-start.17 = (bf16[80,3072]{1,0:T(8,128)(2,1)S(1)}, bf16[80,3072]{1,0:T(8,128)(2,1)S(1)}, u32[]{:S(2)}, u32[]{:S(2)}) collective-permute-start(bf16[80,3072]{1,0:T(8,128)(2,1)S(1)} %get-tuple-element.67), channel_id=1, source_target_pairs={{0,8},{8,0},{16,24},{24,16},{1,9},{9,1},{17,25},{25,17},{2,10},{10... | collective-permute-start | bytes 1474568 | tf_op jit(solution)/shard_map/ppermute | solution.py:28
  66.1 0.8 collective-permute-start.15
  67.3 6.5 %collective-permute-done.15.corner_ref.refs_4_.refs_2_ = bf16[64,3072]{1,0:T(8,128)(2,1)S(1)} collective-permute-done((bf16[64,3072]{1,0:T(8,128)(2,1)S(1)}, bf16[64,3072]{1,0:T(8,128)(2,1)S(1)}, u32[]{:S(2)}, u32[]{:S(2)}) %collective-permute-start.15) | collective-permute-done | bytes 393248 | tf_op jit(solution)/shard_map/ppermute | solution.py:28
  74.5 1.1 %collective-permute-start.20 = (bf16[32,3072]{1,0:T(8,128)(2,1)S(1)}, bf16[32,3072]{1,0:T(8,128)(2,1)S(1)}, u32[]{:S(2)}, u32[]{:S(2)}) collective-permute-start(bf16[32,3072]{1,0:T(8,128)(2,1)S(1)} %get-tuple-element.71), channel_id=1, source_target_pairs={{0,16},{8,24},{16,0},{24,8},{1,17},{9,25},{17,1},{25,9},{2,18},{10... | collective-permute-start | bytes 589832 | tf_op jit(solution)/shard_map/ppermute | solution.py:28
  75.6 1.0 %collective-permute-start.21 = (bf16[32,3072]{1,0:T(8,128)(2,1)S(1)}, bf16[32,3072]{1,0:T(8,128)(2,1)S(1)}, u32[]{:S(2)}, u32[]{:S(2)}) collective-permute-start(bf16[32,3072]{1,0:T(8,128)(2,1)S(1)} %get-tuple-element.72), channel_id=1, source_target_pairs={{0,8},{8,0},{16,24},{24,16},{1,9},{9,1},{17,25},{25,17},{2,10},{10... | collective-permute-start | bytes 589832 | tf_op jit(solution)/shard_map/ppermute | solution.py:28
  76.7 5.2 %experts.2.refs_10_ = f32[1,1152,512]{2,1,0:T(8,128)} custom-call(bf16[512,256]{1,0:T(8,128)(2,1)S(1)} %get-tuple-element.61.slot_ref, f32[4,128]{1,0:T(4,128)S(1)} %get-tuple-element.62.weight_ref, bf16[1,1152,3072]{2,1,0:T(8,128)(2,1)S(1)} %get-tuple-element.56.after.gate_ref, bf16[1,1152,3072]{2,1,0:T(8,128)(2,1)S(1)} %get-tuple-element.63.up_ref, ...), custom_call_target="tpu_custom_call" | custom-call | flops 3623878656 | bytes 1572864 | tf_op jit(solution)/shard_map/experts/pallas_call | solution.py:389
  82.7 0.9 %collective-permute-done.24.refs_7_ = bf16[32,3072]{1,0:T(8,128)(2,1)S(1)} collective-permute-done((bf16[32,3072]{1,0:T(8,128)(2,1)S(1)}, bf16[32,3072]{1,0:T(8,128)(2,1)S(1)}, u32[]{:S(2)}, u32[]{:S(2)}) %collective-permute-start.24) | collective-permute-done | bytes 196640 | tf_op jit(solution)/shard_map/ppermute | solution.py:28
  83.9 5.2 %experts.3 = f32[1,1152,512]{2,1,0:T(8,128)} custom-call(bf16[512,256]{1,0:T(8,128)(2,1)S(1)} %get-tuple-element.61.slot_ref, f32[4,128]{1,0:T(4,128)S(1)} %get-tuple-element.62.weight_ref, bf16[1,1152,3072]{2,1,0:T(8,128)(2,1)S(1)} %get-tuple-element.56.after.gate_ref, ...), custom_call_target="tpu_custom_call", output_to_operand_aliasing={{}: (14, {})} | custom-call | flops 3623878656 | bytes 1572864 | tf_op jit(solution)/shard_map/experts/pallas_call | solution.py:389
  (40 shorter events, 4.4 us)
Async XLA Ops:
  0.6 19.5 %copy-start.3 = (f32[512]{0:T(512)S(1)}, f32[512]{0:T(512)}, u32[]{:S(2)}) copy-start(f32[512]{0:T(512)} %param.17) | copy-start | bytes 6148
  2.9 19.5 %collective-permute-start.4 = (bf16[512,3072]{1,0:T(8,128)(2,1)S(1)}, bf16[512,3072]{1,0:T(8,128)(2,1)S(1)}, u32[]{:S(2)}, u32[]{:S(2)}) collective-permute-start(bf16[512,3072]{1,0:T(8,128)(2,1)S(1)} %get-tuple-element.47.proj_ref), channel_id=1, source_target_pairs={{0,1},{1,0},{2,3},{3,2},{4,5},{5,4},{6,7},{7,6},{8,9},{9,8},{10,11... | collective-permute-start | bytes 9437192 | tf_op jit(solution)/shard_map/ppermute | solution.py:28
  3.4 10.9 %collective-permute-start.2 = (bf16[1056,128]{1,0:T(8,128)(2,1)S(1)}, bf16[1056,128]{1,0:T(8,128)(2,1)S(1)}, u32[]{:S(2)}, u32[]{:S(2)}) collective-permute-start(bf16[1056,128]{1,0:T(8,128)(2,1)S(1)} %get-tuple-element.40.after), channel_id=1, source_target_pairs={{0,24},{8,16},{16,8},{24,0},{1,25},{9,17},{17,9},{25,1},{2,26},{10... | collective-permute-start | bytes 811016 | tf_op jit(solution)/shard_map/ppermute | solution.py:28
  6.9 12.9 %collective-permute-start.1 = (bf16[1056,128]{1,0:T(8,128)(2,1)S(1)}, bf16[1056,128]{1,0:T(8,128)(2,1)S(1)}, u32[]{:S(2)}, u32[]{:S(2)}) collective-permute-start(bf16[1056,128]{1,0:T(8,128)(2,1)S(1)} %get-tuple-element.40.after), channel_id=1, source_target_pairs={{0,16},{8,24},{16,0},{24,8},{1,17},{9,25},{17,1},{25,9},{2,18},{10... | collective-permute-start | bytes 811016 | tf_op jit(solution)/shard_map/ppermute | solution.py:28
  7.4 12.7 %collective-permute-start = (bf16[1056,128]{1,0:T(8,128)(2,1)S(1)}, bf16[1056,128]{1,0:T(8,128)(2,1)S(1)}, u32[]{:S(2)}, u32[]{:S(2)}) collective-permute-start(bf16[1056,128]{1,0:T(8,128)(2,1)S(1)} %get-tuple-element.40.after), channel_id=1, source_target_pairs={{0,8},{8,0},{16,24},{24,16},{1,9},{9,1},{17,25},{25,17},{2,10},{10... | collective-permute-start | bytes 811016 | tf_op jit(solution)/shard_map/ppermute | solution.py:28
  20.9 1.4 %collective-permute-start.3 = (bf16[128,512]{1,0:T(8,128)(2,1)S(1)}, bf16[128,512]{1,0:T(8,128)(2,1)S(1)}, u32[]{:S(2)}, u32[]{:S(2)}) collective-permute-start(bf16[128,512]{1,0:T(8,128)(2,1)S(1)} %get-tuple-element.46), channel_id=1, source_target_pairs={{0,1},{1,0},{2,3},{3,2},{4,5},{5,4},{6,7},{7,6},{8,9},{9,8},{10,11... | collective-permute-start | bytes 393224 | tf_op jit(solution)/shard_map/ppermute | solution.py:28
  22.4 5.5 %copy-start.1 = (s32[512,2,2]{0,2,1:T(2,128)S(1)}, s32[512,2,2]{0,2,1:T(2,128)}, u32[]{:S(2)}) copy-start(s32[512,2,2]{0,2,1:T(2,128)} %param.20) | copy-start | bytes 24580
  22.4 5.5 %copy-start.2 = (f32[512,2,2]{0,2,1:T(2,128)S(1)}, f32[512,2,2]{0,2,1:T(2,128)}, u32[]{:S(2)}) copy-start(f32[512,2,2]{0,2,1:T(2,128)} %param.21) | copy-start | bytes 24580
  23.4 13.5 %collective-permute-start.5 = (bf16[32,3072]{1,0:T(8,128)(2,1)S(1)}, bf16[32,3072]{1,0:T(8,128)(2,1)S(1)}, u32[]{:S(2)}, u32[]{:S(2)}) collective-permute-start(bf16[32,3072]{1,0:T(8,128)(2,1)S(1)} %get-tuple-element.57), channel_id=1, source_target_pairs={{0,4},{1,5},{2,6},{3,7},{4,0},{5,1},{6,2},{7,3},{8,12},{9,13},{10,... | collective-permute-start | bytes 589832 | tf_op jit(solution)/shard_map/ppermute | solution.py:28
  26.0 10.9 %collective-permute-start.6 = (bf16[32,3072]{1,0:T(8,128)(2,1)S(1)}, bf16[32,3072]{1,0:T(8,128)(2,1)S(1)}, u32[]{:S(2)}, u32[]{:S(2)}) collective-permute-start(bf16[32,3072]{1,0:T(8,128)(2,1)S(1)} %get-tuple-element.58), channel_id=1, source_target_pairs={{0,2},{1,3},{2,0},{3,1},{4,6},{5,7},{6,4},{7,5},{8,10},{9,11},{10,... | collective-permute-start | bytes 589832 | tf_op jit(solution)/shard_map/ppermute | solution.py:28
  27.6 13.3 %collective-permute-start.7 = (bf16[32,3072]{1,0:T(8,128)(2,1)S(1)}, bf16[32,3072]{1,0:T(8,128)(2,1)S(1)}, u32[]{:S(2)}, u32[]{:S(2)}) collective-permute-start(bf16[32,3072]{1,0:T(8,128)(2,1)S(1)} %get-tuple-element.59), channel_id=1, source_target_pairs={{0,6},{1,7},{2,4},{3,5},{4,2},{5,3},{6,0},{7,1},{8,14},{9,15},{10,... | collective-permute-start | bytes 589832 | tf_op jit(solution)/shard_map/ppermute | solution.py:28
  28.3 12.6 %copy-start = (f32[3072]{0:T(1024)S(1)}, f32[3072]{0:T(1024)}, u32[]{:S(2)}) copy-start(f32[3072]{0:T(1024)} %param.19) | copy-start | bytes 36868
  41.1 15.6 %collective-permute-start.13 = (bf16[32,3072]{1,0:T(8,128)(2,1)S(1)}, bf16[32,3072]{1,0:T(8,128)(2,1)S(1)}, u32[]{:S(2)}, u32[]{:S(2)}) collective-permute-start(bf16[32,3072]{1,0:T(8,128)(2,1)S(1)} %get-tuple-element.64.refs_6_), channel_id=1, source_target_pairs={{0,6},{1,7},{2,4},{3,5},{4,2},{5,3},{6,0},{7,1},{8,14},{9,15},{10,... | collective-permute-start | bytes 589832 | tf_op jit(solution)/shard_map/ppermute | solution.py:28
  43.7 18.1 %collective-permute-start.12 = (bf16[32,3072]{1,0:T(8,128)(2,1)S(1)}, bf16[32,3072]{1,0:T(8,128)(2,1)S(1)}, u32[]{:S(2)}, u32[]{:S(2)}) collective-permute-start(bf16[32,3072]{1,0:T(8,128)(2,1)S(1)} %get-tuple-element.64.refs_6_), channel_id=1, source_target_pairs={{0,4},{1,5},{2,6},{3,7},{4,0},{5,1},{6,2},{7,3},{8,12},{9,13},{10,... | collective-permute-start | bytes 589832 | tf_op jit(solution)/shard_map/ppermute | solution.py:28
  53.2 8.6 %collective-permute-start.11 = (bf16[32,3072]{1,0:T(8,128)(2,1)S(1)}, bf16[32,3072]{1,0:T(8,128)(2,1)S(1)}, u32[]{:S(2)}, u32[]{:S(2)}) collective-permute-start(bf16[32,3072]{1,0:T(8,128)(2,1)S(1)} %get-tuple-element.64.refs_6_), channel_id=1, source_target_pairs={{0,24},{8,16},{16,8},{24,0},{1,25},{9,17},{17,9},{25,1},{2,26},{10... | collective-permute-start | bytes 589832 | tf_op jit(solution)/shard_map/ppermute | solution.py:28
  54.9 8.4 %collective-permute-start.10 = (bf16[32,3072]{1,0:T(8,128)(2,1)S(1)}, bf16[32,3072]{1,0:T(8,128)(2,1)S(1)}, u32[]{:S(2)}, u32[]{:S(2)}) collective-permute-start(bf16[32,3072]{1,0:T(8,128)(2,1)S(1)} %get-tuple-element.64.refs_6_), channel_id=1, source_target_pairs={{0,16},{8,24},{16,0},{24,8},{1,17},{9,25},{17,1},{25,9},{2,18},{10... | collective-permute-start | bytes 589832 | tf_op jit(solution)/shard_map/ppermute | solution.py:28
  56.2 7.1 %collective-permute-start.9 = (bf16[32,3072]{1,0:T(8,128)(2,1)S(1)}, bf16[32,3072]{1,0:T(8,128)(2,1)S(1)}, u32[]{:S(2)}, u32[]{:S(2)}) collective-permute-start(bf16[32,3072]{1,0:T(8,128)(2,1)S(1)} %get-tuple-element.64.refs_6_), channel_id=1, source_target_pairs={{0,8},{8,0},{16,24},{24,16},{1,9},{9,1},{17,25},{25,17},{2,10},{10... | collective-permute-start | bytes 589832 | tf_op jit(solution)/shard_map/ppermute | solution.py:28
  56.7 6.6 %collective-permute-start.8 = (bf16[32,3072]{1,0:T(8,128)(2,1)S(1)}, bf16[32,3072]{1,0:T(8,128)(2,1)S(1)}, u32[]{:S(2)}, u32[]{:S(2)}) collective-permute-start(bf16[32,3072]{1,0:T(8,128)(2,1)S(1)} %get-tuple-element.64.refs_6_), channel_id=1, source_target_pairs={{0,2},{1,3},{2,0},{3,1},{4,6},{5,7},{6,4},{7,5},{8,10},{9,11},{10,... | collective-permute-start | bytes 589832 | tf_op jit(solution)/shard_map/ppermute | solution.py:28
  63.5 10.4 %collective-permute-start.18 = (bf16[80,3072]{1,0:T(8,128)(2,1)S(1)}, bf16[80,3072]{1,0:T(8,128)(2,1)S(1)}, u32[]{:S(2)}, u32[]{:S(2)}) collective-permute-start(bf16[80,3072]{1,0:T(8,128)(2,1)S(1)} %get-tuple-element.67), channel_id=1, source_target_pairs={{0,16},{8,24},{16,0},{24,8},{1,17},{9,25},{17,1},{25,9},{2,18},{10... | collective-permute-start | bytes 1474568 | tf_op jit(solution)/shard_map/ppermute | solution.py:28
  65.0 8.8 %collective-permute-start.17 = (bf16[80,3072]{1,0:T(8,128)(2,1)S(1)}, bf16[80,3072]{1,0:T(8,128)(2,1)S(1)}, u32[]{:S(2)}, u32[]{:S(2)}) collective-permute-start(bf16[80,3072]{1,0:T(8,128)(2,1)S(1)} %get-tuple-element.67), channel_id=1, source_target_pairs={{0,8},{8,0},{16,24},{24,16},{1,9},{9,1},{17,25},{25,17},{2,10},{10... | collective-permute-start | bytes 1474568 | tf_op jit(solution)/shard_map/ppermute | solution.py:28
  66.1 7.8 %collective-permute-start.15 = (bf16[64,3072]{1,0:T(8,128)(2,1)S(1)}, bf16[64,3072]{1,0:T(8,128)(2,1)S(1)}, u32[]{:S(2)}, u32[]{:S(2)}) collective-permute-start(bf16[64,3072]{1,0:T(8,128)(2,1)S(1)} %get-tuple-element.66), channel_id=1, source_target_pairs={{0,2},{1,3},{2,0},{3,1},{4,6},{5,7},{6,4},{7,5},{8,10},{9,11},{10,... | collective-permute-start | bytes 1179656 | tf_op jit(solution)/shard_map/ppermute | solution.py:28
  66.8 9.8 %collective-permute-start.14 = (bf16[128,3072]{1,0:T(8,128)(2,1)S(1)}, bf16[128,3072]{1,0:T(8,128)(2,1)S(1)}, u32[]{:S(2)}, u32[]{:S(2)}) collective-permute-start(bf16[128,3072]{1,0:T(8,128)(2,1)S(1)} %get-tuple-element.65.refs_0_), channel_id=1, source_target_pairs={{0,1},{1,0},{2,3},{3,2},{4,5},{5,4},{6,7},{7,6},{8,9},{9,8},{10,11... | collective-permute-start | bytes 2359304 | tf_op jit(solution)/shard_map/ppermute | solution.py:28
  66.8 8.8 %collective-permute-start.22 = (bf16[96,3072]{1,0:T(8,128)(2,1)S(1)}, bf16[96,3072]{1,0:T(8,128)(2,1)S(1)}, u32[]{:S(2)}, u32[]{:S(2)}) collective-permute-start(bf16[96,3072]{1,0:T(8,128)(2,1)S(1)} %get-tuple-element.73.refs_2_), channel_id=1, source_target_pairs={{0,1},{1,0},{2,3},{3,2},{4,5},{5,4},{6,7},{7,6},{8,9},{9,8},{10,11... | collective-permute-start | bytes 1769480 | tf_op jit(solution)/shard_map/ppermute | solution.py:28
  73.9 2.8 %collective-permute-start.23 = (bf16[80,3072]{1,0:T(8,128)(2,1)S(1)}, bf16[80,3072]{1,0:T(8,128)(2,1)S(1)}, u32[]{:S(2)}, u32[]{:S(2)}) collective-permute-start(bf16[80,3072]{1,0:T(8,128)(2,1)S(1)} %collective-permute-done.17.one_ref.refs_6_), channel_id=1, source_target_pairs={{0,1},{1,0},{2,3},{3,2},{4,5},{5,4},{6,7},{7,6},{8,9},{9,8},{10,11... | collective-permute-start | bytes 1474568 | tf_op jit(solution)/shard_map/ppermute | solution.py:28
  74.0 2.7 %collective-permute-start.16 = (bf16[64,3072]{1,0:T(8,128)(2,1)S(1)}, bf16[64,3072]{1,0:T(8,128)(2,1)S(1)}, u32[]{:S(2)}, u32[]{:S(2)}) collective-permute-start(bf16[64,3072]{1,0:T(8,128)(2,1)S(1)} %collective-permute-done.15.corner_ref.refs_4_.refs_2_), channel_id=1, source_target_pairs={{0,1},{1,0},{2,3},{3,2},{4,5},{5,4},{6,7},{7,6},{8,9},{9,8},{10,11... | collective-permute-start | bytes 1179656 | tf_op jit(solution)/shard_map/ppermute | solution.py:28
  74.5 7.4 %collective-permute-start.20 = (bf16[32,3072]{1,0:T(8,128)(2,1)S(1)}, bf16[32,3072]{1,0:T(8,128)(2,1)S(1)}, u32[]{:S(2)}, u32[]{:S(2)}) collective-permute-start(bf16[32,3072]{1,0:T(8,128)(2,1)S(1)} %get-tuple-element.71), channel_id=1, source_target_pairs={{0,16},{8,24},{16,0},{24,8},{1,17},{9,25},{17,1},{25,9},{2,18},{10... | collective-permute-start | bytes 589832 | tf_op jit(solution)/shard_map/ppermute | solution.py:28
  75.6 6.6 %collective-permute-start.21 = (bf16[32,3072]{1,0:T(8,128)(2,1)S(1)}, bf16[32,3072]{1,0:T(8,128)(2,1)S(1)}, u32[]{:S(2)}, u32[]{:S(2)}) collective-permute-start(bf16[32,3072]{1,0:T(8,128)(2,1)S(1)} %get-tuple-element.72), channel_id=1, source_target_pairs={{0,8},{8,0},{16,24},{24,16},{1,9},{9,1},{17,25},{25,17},{2,10},{10... | collective-permute-start | bytes 589832 | tf_op jit(solution)/shard_map/ppermute | solution.py:28
  76.6 6.1 %collective-permute-start.19 = (bf16[80,3072]{1,0:T(8,128)(2,1)S(1)}, bf16[80,3072]{1,0:T(8,128)(2,1)S(1)}, u32[]{:S(2)}, u32[]{:S(2)}) collective-permute-start(bf16[80,3072]{1,0:T(8,128)(2,1)S(1)} %collective-permute-done.18.two_ref.refs_4_), channel_id=1, source_target_pairs={{0,1},{1,0},{2,3},{3,2},{4,5},{5,4},{6,7},{7,6},{8,9},{9,8},{10,11... | collective-permute-start | bytes 1474568 | tf_op jit(solution)/shard_map/ppermute | solution.py:28
  82.2 1.4 %collective-permute-start.24 = (bf16[32,3072]{1,0:T(8,128)(2,1)S(1)}, bf16[32,3072]{1,0:T(8,128)(2,1)S(1)}, u32[]{:S(2)}, u32[]{:S(2)}) collective-permute-start(bf16[32,3072]{1,0:T(8,128)(2,1)S(1)} %collective-permute-done.20.refs_6_), channel_id=1, source_target_pairs={{0,1},{1,0},{2,3},{3,2},{4,5},{5,4},{6,7},{7,6},{8,9},{9,8},{10,11... | collective-permute-start | bytes 589832 | tf_op jit(solution)/shard_map/ppermute | solution.py:28
  82.4 1.5 %collective-permute-start.25 = (bf16[32,3072]{1,0:T(8,128)(2,1)S(1)}, bf16[32,3072]{1,0:T(8,128)(2,1)S(1)}, u32[]{:S(2)}, u32[]{:S(2)}) collective-permute-start(bf16[32,3072]{1,0:T(8,128)(2,1)S(1)} %collective-permute-done.21.refs_8_), channel_id=1, source_target_pairs={{0,1},{1,0},{2,3},{3,2},{4,5},{5,4},{6,7},{7,6},{8,9},{9,8},{10,11... | collective-permute-start | bytes 589832 | tf_op jit(solution)/shard_map/ppermute | solution.py:28

commit v8 on v7

--- a/solution.py
+++ b/solution.py
@@ -586,7 +586,20 @@
         blocks += [[(swap(rest, "seq", d), 0, rest.shape[0])] for d in range(1, count)]
     hidden = computed(range(half), blocks[:half], None)
     *last, hidden = lax.optimization_barrier((*(piece for piece, *_ in blocks[-1][-2:]), hidden))
-    blocks[-1][-2:] = [(piece, *place) for piece, (_, *place) in zip(last, blocks[-1][-2:])]
+    if square:
+        height = last[0].shape[0]
+        joined = pl.pallas_call(
+            functools.partial(gather_kernel, [[(0, 0, height), (1, 0, height)]]),
+            in_specs=[vmem] * 2,
+            out_specs=vmem,
+            out_shape=jax.ShapeDtypeStruct((2 * height, model), BF),
+            compiler_params=params(VMEM_BYTES // 8),
+            cost_estimate=cost(1, 8 * height * model),
+            name="join",
+        )(*last)
+        blocks[-1][-2:] = [(joined, 0, 2 * height)]
+    else:
+        blocks[-1][-2:] = [(piece, *place) for piece, (_, *place) in zip(last, blocks[-1][-2:])]
     hidden = computed(range(half, count), blocks[half:], hidden)
     return (attn_out, hidden)
 

time: 89.8 us -> 95.7 us (1.066)
  waiting for transfers between devices: 30.5 us -> 38.5 us
  starting transfers between devices: 33.8 us -> 32.2 us
    ppermute x26 -> x25, waiting for transfers between devices: 30.5 us -> 38.5 us  [swap(): return lax.ppermute(block, axis, route)]
    ppermute x26 -> x25, starting transfers between devices: 33.8 us -> 32.2 us  [swap(): return lax.ppermute(block, axis, route)]
  transfers between devices with their start and end apart: 26 -> 25, of which waited for: 12 -> 12; matrix products, arithmetic and copies ran while one was open for 0% -> 0% of each run, Pallas kernels for 17% -> 16%
where the time goes in v8:
time: 95.7 us; the launch traced here: 95.5 us
  waiting for transfers between devices  38.5 us (40%)
  starting transfers between devices  32.2 us (34%)
  Pallas kernels  24 us (25%)
    ppermute x25, waiting for transfers between devices, swap(): return lax.ppermute(block, axis, route)  38.5 us
    ppermute x25, starting transfers between devices, swap(): return lax.ppermute(block, axis, route)  32.2 us
    pallas_call x2, Pallas kernels, experts(): pl.pallas_call(functools.partial(expert_kernel, plan, len(arrays), lines)...  10.3 us
    pallas_call x1, Pallas kernels, per_device(): pl.pallas_call(load_kernel, in_specs=[hbm, hbm, anywhere], out_specs=[vme...  5.19 us
    pallas_call x1, Pallas kernels, per_device(): pl.pallas_call(functools.partial(inner_kernel, line), in_specs=[hbm] * 5...  2.7 us
    pallas_call x1, Pallas kernels, per_device(): pl.pallas_call(state_kernel, in_specs=[hbm] * 4, out_specs=[vmem] * 2, ou...  2.24 us
  transfers between devices with their start and end apart: 25, of which 12 were waited for; matrix products, arithmetic and copies ran while one was open for 0% of the time, Pallas kernels for 16%

profile of v8, /device:TPU:0, one launch (start us, length us, event | category | flops | bytes accessed | tf_op | source)
XLA Modules:
  0.0 95.5 jit_solution(11583590093134995441)
XLA Ops:
  0.6 2.2 %states.1 = (bf16[1056,128]{1,0:T(8,128)(2,1)S(1)}, bf16[512,3072]{1,0:T(8,128)(2,1)S(1)}) custom-call(bf16[2,128,512]{2,1,0:T(8,128)(2,1)} %k_hbm.3, bf16[2,128,512]{2,1,0:T(8,128)(2,1)} %v_hbm.3, f32[2,4,128]{2,1,0:T(4,128)} %decay_hbm.3, bf16[512,3072]{1,0:T(8,128)(2,1)} %proj_hbm.1), custom_call_target="tpu_custom_call" | custom-call | flops 67108864 | bytes 786432 | tf_op jit(solution)/shard_map/states/pallas_call | solution.py:433
  3.4 3.5 %collective-permute-start.2 = (bf16[1056,128]{1,0:T(8,128)(2,1)S(1)}, bf16[1056,128]{1,0:T(8,128)(2,1)S(1)}, u32[]{:S(2)}, u32[]{:S(2)}) collective-permute-start(bf16[1056,128]{1,0:T(8,128)(2,1)S(1)} %get-tuple-element.40.after), channel_id=1, source_target_pairs={{0,24},{8,16},{16,8},{24,0},{1,25},{9,17},{17,9},{25,1},{2,26},{10... | collective-permute-start | bytes 811016 | tf_op jit(solution)/shard_map/ppermute | solution.py:28
  7.6 2.7 %inner.1 = (f32[2,128,512]{2,1,0:T(8,128)S(1)}, bf16[2,128,512]{2,1,0:T(8,128)(2,1)S(1)}, f32[32,3072]{1,0:T(8,128)S(1)}, f32[2,128,4]{2,1,0:T(8,128)S(1)}, bf16[256,256]{1,0:T(8,128)(2,1)S(1)}) custom-call(bf16[2,128,512]{2,1,0:T(8,128)(2,1)} %q_hbm.1, bf16[2,128,512]{2,1,0:T(8,128)(2,1)} %k_hbm.3, bf16[2,128,512]{2,1,0:T(8,128)(2,1)} %v_hbm.3, ...), custom_call_target="tpu_custom_call" | custom-call | flops 100663296 | bytes 1310720 | tf_op jit(solution)/shard_map/inner/pallas_call | solution.py:453
  10.3 4.0 %collective-permute-done.2.refs_7_ = bf16[1056,128]{1,0:T(8,128)(2,1)S(1)} collective-permute-done((bf16[1056,128]{1,0:T(8,128)(2,1)S(1)}, bf16[1056,128]{1,0:T(8,128)(2,1)S(1)}, u32[]{:S(2)}, u32[]{:S(2)}) %collective-permute-start.2) | collective-permute-done | bytes 270368 | tf_op jit(solution)/shard_map/ppermute | solution.py:28
  14.3 5.5 %collective-permute-done.1.refs_6_ = bf16[1056,128]{1,0:T(8,128)(2,1)S(1)} collective-permute-done((bf16[1056,128]{1,0:T(8,128)(2,1)S(1)}, bf16[1056,128]{1,0:T(8,128)(2,1)S(1)}, u32[]{:S(2)}, u32[]{:S(2)}) %collective-permute-start.1) | collective-permute-done | bytes 270368 | tf_op jit(solution)/shard_map/ppermute | solution.py:28
  20.1 0.8 attend.1
  21.0 1.3 %collective-permute-done.3.partner_ref = bf16[128,512]{1,0:T(8,128)(2,1)S(1)} collective-permute-done((bf16[128,512]{1,0:T(8,128)(2,1)S(1)}, bf16[128,512]{1,0:T(8,128)(2,1)S(1)}, u32[]{:S(2)}, u32[]{:S(2)}) %collective-permute-start.3) | collective-permute-done | bytes 131104 | tf_op jit(solution)/shard_map/ppermute | solution.py:28
  22.4 1.0 %project.1 = (f32[32,3072]{1,0:T(8,128)S(1)}, bf16[32,3072]{1,0:T(8,128)(2,1)S(1)}, bf16[32,3072]{1,0:T(8,128)(2,1)S(1)}, bf16[32,3072]{1,0:T(8,128)(2,1)S(1)}) custom-call(bf16[128,512]{1,0:T(8,128)(2,1)S(1)} %get-tuple-element.45.own_ref, bf16[128,512]{1,0:T(8,128)(2,1)S(1)} %collective-permute-done.3.partner_ref, ...), custom_call_target="tpu_custom_call" | custom-call | flops 805306368 | bytes 8650752 | tf_op jit(solution)/shard_map/project/pallas_call | solution.py:486
  23.4 2.7 %collective-permute-start.5 = (bf16[32,3072]{1,0:T(8,128)(2,1)S(1)}, bf16[32,3072]{1,0:T(8,128)(2,1)S(1)}, u32[]{:S(2)}, u32[]{:S(2)}) collective-permute-start(bf16[32,3072]{1,0:T(8,128)(2,1)S(1)} %get-tuple-element.57), channel_id=1, source_target_pairs={{0,4},{1,5},{2,6},{3,7},{4,0},{5,1},{6,2},{7,3},{8,12},{9,13},{10,... | collective-permute-start | bytes 589832 | tf_op jit(solution)/shard_map/ppermute | solution.py:28
  26.0 1.6 %collective-permute-start.6 = (bf16[32,3072]{1,0:T(8,128)(2,1)S(1)}, bf16[32,3072]{1,0:T(8,128)(2,1)S(1)}, u32[]{:S(2)}, u32[]{:S(2)}) collective-permute-start(bf16[32,3072]{1,0:T(8,128)(2,1)S(1)} %get-tuple-element.58), channel_id=1, source_target_pairs={{0,2},{1,3},{2,0},{3,1},{4,6},{5,7},{6,4},{7,5},{8,10},{9,11},{10,... | collective-permute-start | bytes 589832 | tf_op jit(solution)/shard_map/ppermute | solution.py:28
  28.3 5.2 %load.1 = (bf16[1,1152,3072]{2,1,0:T(8,128)(2,1)S(1)}, bf16[1,1152,3072]{2,1,0:T(8,128)(2,1)S(1)}) custom-call(bf16[1,1152,3072]{2,1,0:T(8,128)(2,1)} %gate_hbm.1, bf16[1,1152,3072]{2,1,0:T(8,128)(2,1)} %up_hbm.1, f32[32,3072]{1,0:T(8,128)S(1)} %get-tuple-element.54.after.kept_ref), custom_call_target="tpu_custom_call" | custom-call | flops 1 | bytes 14155776 | tf_op jit(solution)/shard_map/load/pallas_call | solution.py:515
  33.5 3.4 %collective-permute-done.5.refs_0_ = bf16[32,3072]{1,0:T(8,128)(2,1)S(1)} collective-permute-done((bf16[32,3072]{1,0:T(8,128)(2,1)S(1)}, bf16[32,3072]{1,0:T(8,128)(2,1)S(1)}, u32[]{:S(2)}, u32[]{:S(2)}) %collective-permute-start.5) | collective-permute-done | bytes 196640 | tf_op jit(solution)/shard_map/ppermute | solution.py:28
  36.9 4.0 %collective-permute-done.7.refs_2_ = bf16[32,3072]{1,0:T(8,128)(2,1)S(1)} collective-permute-done((bf16[32,3072]{1,0:T(8,128)(2,1)S(1)}, bf16[32,3072]{1,0:T(8,128)(2,1)S(1)}, u32[]{:S(2)}, u32[]{:S(2)}) %collective-permute-start.7) | collective-permute-done | bytes 196640 | tf_op jit(solution)/shard_map/ppermute | solution.py:28
  41.1 2.5 %collective-permute-start.13 = (bf16[32,3072]{1,0:T(8,128)(2,1)S(1)}, bf16[32,3072]{1,0:T(8,128)(2,1)S(1)}, u32[]{:S(2)}, u32[]{:S(2)}) collective-permute-start(bf16[32,3072]{1,0:T(8,128)(2,1)S(1)} %get-tuple-element.64.refs_6_), channel_id=1, source_target_pairs={{0,6},{1,7},{2,4},{3,5},{4,2},{5,3},{6,0},{7,1},{8,14},{9,15},{10,... | collective-permute-start | bytes 589832 | tf_op jit(solution)/shard_map/ppermute | solution.py:28
  43.7 3.3 %collective-permute-start.12 = (bf16[32,3072]{1,0:T(8,128)(2,1)S(1)}, bf16[32,3072]{1,0:T(8,128)(2,1)S(1)}, u32[]{:S(2)}, u32[]{:S(2)}) collective-permute-start(bf16[32,3072]{1,0:T(8,128)(2,1)S(1)} %get-tuple-element.64.refs_6_), channel_id=1, source_target_pairs={{0,4},{1,5},{2,6},{3,7},{4,0},{5,1},{6,2},{7,3},{8,12},{9,13},{10,... | collective-permute-start | bytes 589832 | tf_op jit(solution)/shard_map/ppermute | solution.py:28
  46.9 1.7 %collective-permute-start.11 = (bf16[32,3072]{1,0:T(8,128)(2,1)S(1)}, bf16[32,3072]{1,0:T(8,128)(2,1)S(1)}, u32[]{:S(2)}, u32[]{:S(2)}) collective-permute-start(bf16[32,3072]{1,0:T(8,128)(2,1)S(1)} %get-tuple-element.64.refs_6_), channel_id=1, source_target_pairs={{0,24},{8,16},{16,8},{24,0},{1,25},{9,17},{17,9},{25,1},{2,26},{10... | collective-permute-start | bytes 589832 | tf_op jit(solution)/shard_map/ppermute | solution.py:28
  48.6 1.3 %collective-permute-start.10 = (bf16[32,3072]{1,0:T(8,128)(2,1)S(1)}, bf16[32,3072]{1,0:T(8,128)(2,1)S(1)}, u32[]{:S(2)}, u32[]{:S(2)}) collective-permute-start(bf16[32,3072]{1,0:T(8,128)(2,1)S(1)} %get-tuple-element.64.refs_6_), channel_id=1, source_target_pairs={{0,16},{8,24},{16,0},{24,8},{1,17},{9,25},{17,1},{25,9},{2,18},{10... | collective-permute-start | bytes 589832 | tf_op jit(solution)/shard_map/ppermute | solution.py:28
  49.9 0.5 collective-permute-start.9
  50.4 7.7 %collective-permute-start.8 = (bf16[32,3072]{1,0:T(8,128)(2,1)S(1)}, bf16[32,3072]{1,0:T(8,128)(2,1)S(1)}, u32[]{:S(2)}, u32[]{:S(2)}) collective-permute-start(bf16[32,3072]{1,0:T(8,128)(2,1)S(1)} %get-tuple-element.64.refs_6_), channel_id=1, source_target_pairs={{0,2},{1,3},{2,0},{3,1},{4,6},{5,7},{6,4},{7,5},{8,10},{9,11},{10,... | collective-permute-start | bytes 589832 | tf_op jit(solution)/shard_map/ppermute | solution.py:28
  58.1 0.8 place.1.refs_7_
  58.9 2.9 %collective-permute-done.12.refs_4_ = bf16[32,3072]{1,0:T(8,128)(2,1)S(1)} collective-permute-done((bf16[32,3072]{1,0:T(8,128)(2,1)S(1)}, bf16[32,3072]{1,0:T(8,128)(2,1)S(1)}, u32[]{:S(2)}, u32[]{:S(2)}) %collective-permute-start.12) | collective-permute-done | bytes 196640 | tf_op jit(solution)/shard_map/ppermute | solution.py:28
  61.8 4.1 %collective-permute-done.8.refs_0_ = bf16[32,3072]{1,0:T(8,128)(2,1)S(1)} collective-permute-done((bf16[32,3072]{1,0:T(8,128)(2,1)S(1)}, bf16[32,3072]{1,0:T(8,128)(2,1)S(1)}, u32[]{:S(2)}, u32[]{:S(2)}) %collective-permute-start.8) | collective-permute-done | bytes 196640 | tf_op jit(solution)/shard_map/ppermute | solution.py:28
  66.1 1.5 %collective-permute-start.18 = (bf16[80,3072]{1,0:T(8,128)(2,1)S(1)}, bf16[80,3072]{1,0:T(8,128)(2,1)S(1)}, u32[]{:S(2)}, u32[]{:S(2)}) collective-permute-start(bf16[80,3072]{1,0:T(8,128)(2,1)S(1)} %get-tuple-element.67), channel_id=1, source_target_pairs={{0,16},{8,24},{16,0},{24,8},{1,17},{9,25},{17,1},{25,9},{2,18},{10... | collective-permute-start | bytes 1474568 | tf_op jit(solution)/shard_map/ppermute | solution.py:28
  67.6 0.8 collective-permute-start.17
  68.9 10.0 %collective-permute-done.15.corner_ref.refs_4_.refs_2_ = bf16[64,3072]{1,0:T(8,128)(2,1)S(1)} collective-permute-done((bf16[64,3072]{1,0:T(8,128)(2,1)S(1)}, bf16[64,3072]{1,0:T(8,128)(2,1)S(1)}, u32[]{:S(2)}, u32[]{:S(2)}) %collective-permute-start.15) | collective-permute-done | bytes 393248 | tf_op jit(solution)/shard_map/ppermute | solution.py:28
  79.3 1.2 %collective-permute-done.17.one_ref.refs_6_ = bf16[80,3072]{1,0:T(8,128)(2,1)S(1)} collective-permute-done((bf16[80,3072]{1,0:T(8,128)(2,1)S(1)}, bf16[80,3072]{1,0:T(8,128)(2,1)S(1)}, u32[]{:S(2)}, u32[]{:S(2)}) %collective-permute-start.17) | collective-permute-done | bytes 491552 | tf_op jit(solution)/shard_map/ppermute | solution.py:28
  81.1 0.6 collective-permute-start.20
  81.7 1.5 %collective-permute-start.21 = (bf16[32,3072]{1,0:T(8,128)(2,1)S(1)}, bf16[32,3072]{1,0:T(8,128)(2,1)S(1)}, u32[]{:S(2)}, u32[]{:S(2)}) collective-permute-start(bf16[32,3072]{1,0:T(8,128)(2,1)S(1)} %get-tuple-element.72), channel_id=1, source_target_pairs={{0,8},{8,0},{16,24},{24,16},{1,9},{9,1},{17,25},{25,17},{2,10},{10... | collective-permute-start | bytes 589832 | tf_op jit(solution)/shard_map/ppermute | solution.py:28
  83.2 5.2 %experts.2.refs_8_ = f32[1,1152,512]{2,1,0:T(8,128)} custom-call(bf16[512,256]{1,0:T(8,128)(2,1)S(1)} %get-tuple-element.61.slot_ref, f32[4,128]{1,0:T(4,128)S(1)} %get-tuple-element.62.weight_ref, bf16[1,1152,3072]{2,1,0:T(8,128)(2,1)S(1)} %get-tuple-element.56.after.gate_ref, bf16[1,1152,3072]{2,1,0:T(8,128)(2,1)S(1)} %get-tuple-element.63.up_ref, ...), custom_call_target="tpu_custom_call" | custom-call | flops 3623878656 | bytes 1572864 | tf_op jit(solution)/shard_map/experts/pallas_call | solution.py:389
  88.4 0.5 collective-permute-start.24
  89.0 1.3 %collective-permute-done.24.refs_7_ = bf16[64,3072]{1,0:T(8,128)(2,1)S(1)} collective-permute-done((bf16[64,3072]{1,0:T(8,128)(2,1)S(1)}, bf16[64,3072]{1,0:T(8,128)(2,1)S(1)}, u32[]{:S(2)}, u32[]{:S(2)}) %collective-permute-start.24) | collective-permute-done | bytes 393248 | tf_op jit(solution)/shard_map/ppermute | solution.py:28
  90.3 5.2 %experts.3 = f32[1,1152,512]{2,1,0:T(8,128)} custom-call(bf16[512,256]{1,0:T(8,128)(2,1)S(1)} %get-tuple-element.61.slot_ref, f32[4,128]{1,0:T(4,128)S(1)} %get-tuple-element.62.weight_ref, bf16[1,1152,3072]{2,1,0:T(8,128)(2,1)S(1)} %get-tuple-element.56.after.gate_ref, ...), custom_call_target="tpu_custom_call", output_to_operand_aliasing={{}: (12, {})} | custom-call | flops 3623878656 | bytes 1572864 | tf_op jit(solution)/shard_map/experts/pallas_call | solution.py:389
  (39 shorter events, 4.2 us)
Async XLA Ops:
  0.6 19.5 %copy-start.3 = (f32[512]{0:T(512)S(1)}, f32[512]{0:T(512)}, u32[]{:S(2)}) copy-start(f32[512]{0:T(512)} %param.17) | copy-start | bytes 6148
  2.9 19.5 %collective-permute-start.4 = (bf16[512,3072]{1,0:T(8,128)(2,1)S(1)}, bf16[512,3072]{1,0:T(8,128)(2,1)S(1)}, u32[]{:S(2)}, u32[]{:S(2)}) collective-permute-start(bf16[512,3072]{1,0:T(8,128)(2,1)S(1)} %get-tuple-element.47.proj_ref), channel_id=1, source_target_pairs={{0,1},{1,0},{2,3},{3,2},{4,5},{5,4},{6,7},{7,6},{8,9},{9,8},{10,11... | collective-permute-start | bytes 9437192 | tf_op jit(solution)/shard_map/ppermute | solution.py:28
  3.4 10.9 %collective-permute-start.2 = (bf16[1056,128]{1,0:T(8,128)(2,1)S(1)}, bf16[1056,128]{1,0:T(8,128)(2,1)S(1)}, u32[]{:S(2)}, u32[]{:S(2)}) collective-permute-start(bf16[1056,128]{1,0:T(8,128)(2,1)S(1)} %get-tuple-element.40.after), channel_id=1, source_target_pairs={{0,24},{8,16},{16,8},{24,0},{1,25},{9,17},{17,9},{25,1},{2,26},{10... | collective-permute-start | bytes 811016 | tf_op jit(solution)/shard_map/ppermute | solution.py:28
  6.9 12.9 %collective-permute-start.1 = (bf16[1056,128]{1,0:T(8,128)(2,1)S(1)}, bf16[1056,128]{1,0:T(8,128)(2,1)S(1)}, u32[]{:S(2)}, u32[]{:S(2)}) collective-permute-start(bf16[1056,128]{1,0:T(8,128)(2,1)S(1)} %get-tuple-element.40.after), channel_id=1, source_target_pairs={{0,16},{8,24},{16,0},{24,8},{1,17},{9,25},{17,1},{25,9},{2,18},{10... | collective-permute-start | bytes 811016 | tf_op jit(solution)/shard_map/ppermute | solution.py:28
  7.4 12.7 %collective-permute-start = (bf16[1056,128]{1,0:T(8,128)(2,1)S(1)}, bf16[1056,128]{1,0:T(8,128)(2,1)S(1)}, u32[]{:S(2)}, u32[]{:S(2)}) collective-permute-start(bf16[1056,128]{1,0:T(8,128)(2,1)S(1)} %get-tuple-element.40.after), channel_id=1, source_target_pairs={{0,8},{8,0},{16,24},{24,16},{1,9},{9,1},{17,25},{25,17},{2,10},{10... | collective-permute-start | bytes 811016 | tf_op jit(solution)/shard_map/ppermute | solution.py:28
  20.9 1.4 %collective-permute-start.3 = (bf16[128,512]{1,0:T(8,128)(2,1)S(1)}, bf16[128,512]{1,0:T(8,128)(2,1)S(1)}, u32[]{:S(2)}, u32[]{:S(2)}) collective-permute-start(bf16[128,512]{1,0:T(8,128)(2,1)S(1)} %get-tuple-element.46), channel_id=1, source_target_pairs={{0,1},{1,0},{2,3},{3,2},{4,5},{5,4},{6,7},{7,6},{8,9},{9,8},{10,11... | collective-permute-start | bytes 393224 | tf_op jit(solution)/shard_map/ppermute | solution.py:28
  22.4 5.5 %copy-start.1 = (s32[512,2,2]{0,2,1:T(2,128)S(1)}, s32[512,2,2]{0,2,1:T(2,128)}, u32[]{:S(2)}) copy-start(s32[512,2,2]{0,2,1:T(2,128)} %param.20) | copy-start | bytes 24580
  22.4 5.5 %copy-start.2 = (f32[512,2,2]{0,2,1:T(2,128)S(1)}, f32[512,2,2]{0,2,1:T(2,128)}, u32[]{:S(2)}) copy-start(f32[512,2,2]{0,2,1:T(2,128)} %param.21) | copy-start | bytes 24580
  23.4 13.5 %collective-permute-start.5 = (bf16[32,3072]{1,0:T(8,128)(2,1)S(1)}, bf16[32,3072]{1,0:T(8,128)(2,1)S(1)}, u32[]{:S(2)}, u32[]{:S(2)}) collective-permute-start(bf16[32,3072]{1,0:T(8,128)(2,1)S(1)} %get-tuple-element.57), channel_id=1, source_target_pairs={{0,4},{1,5},{2,6},{3,7},{4,0},{5,1},{6,2},{7,3},{8,12},{9,13},{10,... | collective-permute-start | bytes 589832 | tf_op jit(solution)/shard_map/ppermute | solution.py:28
  26.0 10.9 %collective-permute-start.6 = (bf16[32,3072]{1,0:T(8,128)(2,1)S(1)}, bf16[32,3072]{1,0:T(8,128)(2,1)S(1)}, u32[]{:S(2)}, u32[]{:S(2)}) collective-permute-start(bf16[32,3072]{1,0:T(8,128)(2,1)S(1)} %get-tuple-element.58), channel_id=1, source_target_pairs={{0,2},{1,3},{2,0},{3,1},{4,6},{5,7},{6,4},{7,5},{8,10},{9,11},{10,... | collective-permute-start | bytes 589832 | tf_op jit(solution)/shard_map/ppermute | solution.py:28
  27.6 13.3 %collective-permute-start.7 = (bf16[32,3072]{1,0:T(8,128)(2,1)S(1)}, bf16[32,3072]{1,0:T(8,128)(2,1)S(1)}, u32[]{:S(2)}, u32[]{:S(2)}) collective-permute-start(bf16[32,3072]{1,0:T(8,128)(2,1)S(1)} %get-tuple-element.59), channel_id=1, source_target_pairs={{0,6},{1,7},{2,4},{3,5},{4,2},{5,3},{6,0},{7,1},{8,14},{9,15},{10,... | collective-permute-start | bytes 589832 | tf_op jit(solution)/shard_map/ppermute | solution.py:28
  28.3 12.6 %copy-start = (f32[3072]{0:T(1024)S(1)}, f32[3072]{0:T(1024)}, u32[]{:S(2)}) copy-start(f32[3072]{0:T(1024)} %param.19) | copy-start | bytes 36868
  41.1 9.3 %collective-permute-start.13 = (bf16[32,3072]{1,0:T(8,128)(2,1)S(1)}, bf16[32,3072]{1,0:T(8,128)(2,1)S(1)}, u32[]{:S(2)}, u32[]{:S(2)}) collective-permute-start(bf16[32,3072]{1,0:T(8,128)(2,1)S(1)} %get-tuple-element.64.refs_6_), channel_id=1, source_target_pairs={{0,6},{1,7},{2,4},{3,5},{4,2},{5,3},{6,0},{7,1},{8,14},{9,15},{10,... | collective-permute-start | bytes 589832 | tf_op jit(solution)/shard_map/ppermute | solution.py:28
  43.7 18.1 %collective-permute-start.12 = (bf16[32,3072]{1,0:T(8,128)(2,1)S(1)}, bf16[32,3072]{1,0:T(8,128)(2,1)S(1)}, u32[]{:S(2)}, u32[]{:S(2)}) collective-permute-start(bf16[32,3072]{1,0:T(8,128)(2,1)S(1)} %get-tuple-element.64.refs_6_), channel_id=1, source_target_pairs={{0,4},{1,5},{2,6},{3,7},{4,0},{5,1},{6,2},{7,3},{8,12},{9,13},{10,... | collective-permute-start | bytes 589832 | tf_op jit(solution)/shard_map/ppermute | solution.py:28
  46.9 14.9 %collective-permute-start.11 = (bf16[32,3072]{1,0:T(8,128)(2,1)S(1)}, bf16[32,3072]{1,0:T(8,128)(2,1)S(1)}, u32[]{:S(2)}, u32[]{:S(2)}) collective-permute-start(bf16[32,3072]{1,0:T(8,128)(2,1)S(1)} %get-tuple-element.64.refs_6_), channel_id=1, source_target_pairs={{0,24},{8,16},{16,8},{24,0},{1,25},{9,17},{17,9},{25,1},{2,26},{10... | collective-permute-start | bytes 589832 | tf_op jit(solution)/shard_map/ppermute | solution.py:28
  48.6 13.2 %collective-permute-start.10 = (bf16[32,3072]{1,0:T(8,128)(2,1)S(1)}, bf16[32,3072]{1,0:T(8,128)(2,1)S(1)}, u32[]{:S(2)}, u32[]{:S(2)}) collective-permute-start(bf16[32,3072]{1,0:T(8,128)(2,1)S(1)} %get-tuple-element.64.refs_6_), channel_id=1, source_target_pairs={{0,16},{8,24},{16,0},{24,8},{1,17},{9,25},{17,1},{25,9},{2,18},{10... | collective-permute-start | bytes 589832 | tf_op jit(solution)/shard_map/ppermute | solution.py:28
  49.9 11.9 %collective-permute-start.9 = (bf16[32,3072]{1,0:T(8,128)(2,1)S(1)}, bf16[32,3072]{1,0:T(8,128)(2,1)S(1)}, u32[]{:S(2)}, u32[]{:S(2)}) collective-permute-start(bf16[32,3072]{1,0:T(8,128)(2,1)S(1)} %get-tuple-element.64.refs_6_), channel_id=1, source_target_pairs={{0,8},{8,0},{16,24},{24,16},{1,9},{9,1},{17,25},{25,17},{2,10},{10... | collective-permute-start | bytes 589832 | tf_op jit(solution)/shard_map/ppermute | solution.py:28
  50.4 15.5 %collective-permute-start.8 = (bf16[32,3072]{1,0:T(8,128)(2,1)S(1)}, bf16[32,3072]{1,0:T(8,128)(2,1)S(1)}, u32[]{:S(2)}, u32[]{:S(2)}) collective-permute-start(bf16[32,3072]{1,0:T(8,128)(2,1)S(1)} %get-tuple-element.64.refs_6_), channel_id=1, source_target_pairs={{0,2},{1,3},{2,0},{3,1},{4,6},{5,7},{6,4},{7,5},{8,10},{9,11},{10,... | collective-permute-start | bytes 589832 | tf_op jit(solution)/shard_map/ppermute | solution.py:28
  66.1 13.2 %collective-permute-start.18 = (bf16[80,3072]{1,0:T(8,128)(2,1)S(1)}, bf16[80,3072]{1,0:T(8,128)(2,1)S(1)}, u32[]{:S(2)}, u32[]{:S(2)}) collective-permute-start(bf16[80,3072]{1,0:T(8,128)(2,1)S(1)} %get-tuple-element.67), channel_id=1, source_target_pairs={{0,16},{8,24},{16,0},{24,8},{1,17},{9,25},{17,1},{25,9},{2,18},{10... | collective-permute-start | bytes 1474568 | tf_op jit(solution)/shard_map/ppermute | solution.py:28
  67.6 12.9 %collective-permute-start.17 = (bf16[80,3072]{1,0:T(8,128)(2,1)S(1)}, bf16[80,3072]{1,0:T(8,128)(2,1)S(1)}, u32[]{:S(2)}, u32[]{:S(2)}) collective-permute-start(bf16[80,3072]{1,0:T(8,128)(2,1)S(1)} %get-tuple-element.67), channel_id=1, source_target_pairs={{0,8},{8,0},{16,24},{24,16},{1,9},{9,1},{17,25},{25,17},{2,10},{10... | collective-permute-start | bytes 1474568 | tf_op jit(solution)/shard_map/ppermute | solution.py:28
  68.4 10.5 %collective-permute-start.15 = (bf16[64,3072]{1,0:T(8,128)(2,1)S(1)}, bf16[64,3072]{1,0:T(8,128)(2,1)S(1)}, u32[]{:S(2)}, u32[]{:S(2)}) collective-permute-start(bf16[64,3072]{1,0:T(8,128)(2,1)S(1)} %get-tuple-element.66), channel_id=1, source_target_pairs={{0,2},{1,3},{2,0},{3,1},{4,6},{5,7},{6,4},{7,5},{8,10},{9,11},{10,... | collective-permute-start | bytes 1179656 | tf_op jit(solution)/shard_map/ppermute | solution.py:28
  68.4 14.8 %collective-permute-start.14 = (bf16[128,3072]{1,0:T(8,128)(2,1)S(1)}, bf16[128,3072]{1,0:T(8,128)(2,1)S(1)}, u32[]{:S(2)}, u32[]{:S(2)}) collective-permute-start(bf16[128,3072]{1,0:T(8,128)(2,1)S(1)} %get-tuple-element.65.refs_0_), channel_id=1, source_target_pairs={{0,1},{1,0},{2,3},{3,2},{4,5},{5,4},{6,7},{7,6},{8,9},{9,8},{10,11... | collective-permute-start | bytes 2359304 | tf_op jit(solution)/shard_map/ppermute | solution.py:28
  68.4 13.3 %collective-permute-start.22 = (bf16[96,3072]{1,0:T(8,128)(2,1)S(1)}, bf16[96,3072]{1,0:T(8,128)(2,1)S(1)}, u32[]{:S(2)}, u32[]{:S(2)}) collective-permute-start(bf16[96,3072]{1,0:T(8,128)(2,1)S(1)} %get-tuple-element.73.refs_2_), channel_id=1, source_target_pairs={{0,1},{1,0},{2,3},{3,2},{4,5},{5,4},{6,7},{7,6},{8,9},{9,8},{10,11... | collective-permute-start | bytes 1769480 | tf_op jit(solution)/shard_map/ppermute | solution.py:28
  80.5 2.7 %collective-permute-start.23 = (bf16[80,3072]{1,0:T(8,128)(2,1)S(1)}, bf16[80,3072]{1,0:T(8,128)(2,1)S(1)}, u32[]{:S(2)}, u32[]{:S(2)}) collective-permute-start(bf16[80,3072]{1,0:T(8,128)(2,1)S(1)} %collective-permute-done.17.one_ref.refs_6_), channel_id=1, source_target_pairs={{0,1},{1,0},{2,3},{3,2},{4,5},{5,4},{6,7},{7,6},{8,9},{9,8},{10,11... | collective-permute-start | bytes 1474568 | tf_op jit(solution)/shard_map/ppermute | solution.py:28
  80.6 2.6 %collective-permute-start.16 = (bf16[64,3072]{1,0:T(8,128)(2,1)S(1)}, bf16[64,3072]{1,0:T(8,128)(2,1)S(1)}, u32[]{:S(2)}, u32[]{:S(2)}) collective-permute-start(bf16[64,3072]{1,0:T(8,128)(2,1)S(1)} %collective-permute-done.15.corner_ref.refs_4_.refs_2_), channel_id=1, source_target_pairs={{0,1},{1,0},{2,3},{3,2},{4,5},{5,4},{6,7},{7,6},{8,9},{9,8},{10,11... | collective-permute-start | bytes 1179656 | tf_op jit(solution)/shard_map/ppermute | solution.py:28
  81.1 7.3 %collective-permute-start.20 = (bf16[32,3072]{1,0:T(8,128)(2,1)S(1)}, bf16[32,3072]{1,0:T(8,128)(2,1)S(1)}, u32[]{:S(2)}, u32[]{:S(2)}) collective-permute-start(bf16[32,3072]{1,0:T(8,128)(2,1)S(1)} %get-tuple-element.71), channel_id=1, source_target_pairs={{0,16},{8,24},{16,0},{24,8},{1,17},{9,25},{17,1},{25,9},{2,18},{10... | collective-permute-start | bytes 589832 | tf_op jit(solution)/shard_map/ppermute | solution.py:28
  81.7 6.7 %collective-permute-start.21 = (bf16[32,3072]{1,0:T(8,128)(2,1)S(1)}, bf16[32,3072]{1,0:T(8,128)(2,1)S(1)}, u32[]{:S(2)}, u32[]{:S(2)}) collective-permute-start(bf16[32,3072]{1,0:T(8,128)(2,1)S(1)} %get-tuple-element.72), channel_id=1, source_target_pairs={{0,8},{8,0},{16,24},{24,16},{1,9},{9,1},{17,25},{25,17},{2,10},{10... | collective-permute-start | bytes 589832 | tf_op jit(solution)/shard_map/ppermute | solution.py:28
  83.2 5.8 %collective-permute-start.19 = (bf16[80,3072]{1,0:T(8,128)(2,1)S(1)}, bf16[80,3072]{1,0:T(8,128)(2,1)S(1)}, u32[]{:S(2)}, u32[]{:S(2)}) collective-permute-start(bf16[80,3072]{1,0:T(8,128)(2,1)S(1)} %collective-permute-done.18.two_ref.refs_4_), channel_id=1, source_target_pairs={{0,1},{1,0},{2,3},{3,2},{4,5},{5,4},{6,7},{7,6},{8,9},{9,8},{10,11... | collective-permute-start | bytes 1474568 | tf_op jit(solution)/shard_map/ppermute | solution.py:28
  88.4 1.9 %collective-permute-start.24 = (bf16[64,3072]{1,0:T(8,128)(2,1)S(1)}, bf16[64,3072]{1,0:T(8,128)(2,1)S(1)}, u32[]{:S(2)}, u32[]{:S(2)}) collective-permute-start(bf16[64,3072]{1,0:T(8,128)(2,1)S(1)} %join.1.refs_6_), channel_id=1, source_target_pairs={{0,1},{1,0},{2,3},{3,2},{4,5},{5,4},{6,7},{7,6},{8,9},{9,8},{10,11... | collective-permute-start | bytes 1179656 | tf_op jit(solution)/shard_map/ppermute | solution.py:28
